TPU v7x, 256 devices: a whole 4x4x8 slice. The times are simulated.
256 devices in a mesh: fsdp: 8 (over y, core), tile: 32 (over x, z).
Axes of the slice: x: 4, y: 4, z: 8, core: 2. Of those that a mesh axis runs over, the one named last changes fastest.
Arguments:
- tokens: bfloat16 [8, 4096, 1024], P('fsdp', 'tile'), may hold values from -8 to 8
- context: bfloat16 [8, 1024, 1024], P('fsdp', 'tile'), may hold values from -8 to 8
- pattern: int32 [8, 64, 16], P('fsdp', 'tile'), may hold values from 0 to 1, as said below
- w_query: bfloat16 [1024, 1024], P('fsdp'), may hold values from -0.125 to 0.125
- w_key: bfloat16 [1024, 1024], P('fsdp'), may hold values from -0.125 to 0.125
- w_value: bfloat16 [1024, 1024], P('fsdp'), may hold values from -0.1875 to 0.1875
- w_out: bfloat16 [1024, 1024], P('fsdp'), may hold values from -0.1875 to 0.1875
- cotangent: bfloat16 [8, 4096, 1024], P('fsdp', 'tile'), may hold values from -6 to 6
Outputs:
- mixed: bfloat16 [8, 4096, 1024], P('fsdp', 'tile')
- d_tokens: bfloat16 [8, 4096, 1024], P('fsdp', 'tile')
- d_context: bfloat16 [8, 1024, 1024], P('fsdp', 'tile')
- g_query: float32 [1024, 1024], P(('fsdp', 'tile'))
- g_out: float32 [1024, 1024], P(('fsdp', 'tile'))
Inputs may be any that keep to these rules, and one draw needn't show every extreme that they name: `pattern`: every query block may attend at least one context block.
All inputs are finite; a program needn't handle non-finite values.
Results may differ from a plain program's by a relative error of at most 0.03.
The roundings to bfloat16 on the way count: a program that leaves them out, or rounds other values in their place, can miss the bound.
Values may be sent and summed in bfloat16 or wider, within the bound.
No kernel may reach another device: no remote copies, remote signals or barrier semaphores. Data moves between devices by JAX's collectives and lax.ppermute only.
A program may use at most 128 MiB of HBM per device.

v0:
```python
import jax
import jax.numpy as jnp
from jax import lax
from jax.sharding import PartitionSpec as P

HEADS = 16


def expand_mask(pattern_rows, block_size):
    q_blocks, k_blocks = pattern_rows.shape
    grid = pattern_rows[:, None, :, None] > 0
    grid = jnp.broadcast_to(grid, (q_blocks, block_size, k_blocks, block_size))
    return grid.reshape(q_blocks * block_size, k_blocks * block_size)


def local(tokens, context, pattern, w_query, w_key, w_value, w_out, cotangent):
    f32 = jnp.float32
    bf16 = jnp.bfloat16
    tok = tokens[0]
    ctx = context[0]
    cot = cotangent[0]
    full_query, full_key, full_value, full_out = (
        lax.all_gather(w_query, "fsdp", axis=0, tiled=True),
        lax.all_gather(w_key, "fsdp", axis=0, tiled=True),
        lax.all_gather(w_value, "fsdp", axis=0, tiled=True),
        lax.all_gather(w_out, "fsdp", axis=0, tiled=True),
    )
    model_width = full_query.shape[1]
    head_count = HEADS
    head_size = model_width // head_count
    own_keys = jnp.dot(ctx, full_key, preferred_element_type=f32).astype(bf16)
    own_values = jnp.dot(ctx, full_value, preferred_element_type=f32).astype(bf16)
    keys, values = (
        lax.all_gather(own_keys, "tile", axis=0, tiled=True),
        lax.all_gather(own_values, "tile", axis=0, tiled=True),
    )
    key_count = keys.shape[0]
    tok_count = tok.shape[0]
    queries = jnp.dot(tok, full_query, preferred_element_type=f32).astype(bf16)
    d_attended = jnp.dot(cot, full_out.T, preferred_element_type=f32).astype(bf16)
    allowed = expand_mask(pattern[0], key_count // pattern.shape[2])
    q_heads = queries.reshape(tok_count, head_count, head_size)
    k_heads = keys.reshape(key_count, head_count, head_size)
    v_heads = values.reshape(key_count, head_count, head_size)
    da_heads = d_attended.reshape(tok_count, head_count, head_size)
    scores = 0.125 * jnp.einsum("qhd,khd->hqk", q_heads, k_heads, preferred_element_type=f32)
    scores = jnp.where(allowed[None, :, :], scores, -jnp.inf)
    top = jnp.max(scores, axis=2, keepdims=True)
    expo = jnp.exp(scores - top)
    attn_prob = expo / jnp.sum(expo, axis=2, keepdims=True)
    prob_low = attn_prob.astype(bf16)
    attended = jnp.einsum("hqk,khd->qhd", prob_low, v_heads, preferred_element_type=f32).astype(
        bf16
    )
    attended = attended.reshape(tok_count, model_width)
    mixed = (tok.astype(f32) + jnp.dot(attended, full_out, preferred_element_type=f32)).astype(bf16)
    d_prob = jnp.einsum("qhd,khd->hqk", da_heads, v_heads, preferred_element_type=f32)
    row_delta = jnp.sum(attn_prob * d_prob, axis=2, keepdims=True)
    d_score = (0.125 * attn_prob * (d_prob - row_delta)).astype(bf16)
    d_queries = jnp.einsum("hqk,khd->qhd", d_score, k_heads, preferred_element_type=f32).astype(
        bf16
    )
    d_queries = d_queries.reshape(tok_count, model_width)
    dk_part = jnp.einsum("hqk,qhd->khd", d_score, q_heads, preferred_element_type=f32).reshape(
        key_count, model_width
    )
    dv_part = jnp.einsum("hqk,qhd->khd", prob_low, da_heads, preferred_element_type=f32).reshape(
        key_count, model_width
    )
    dk_terms = lax.optimization_barrier(dk_part.astype(bf16)).astype(f32)
    dv_terms = lax.optimization_barrier(dv_part.astype(bf16)).astype(f32)
    d_keys, d_values = (
        lax.psum_scatter(
            dk_terms.astype(jnp.bfloat16), "tile", scatter_dimension=0, tiled=True
        ).astype(jnp.float32),
        lax.psum_scatter(
            dv_terms.astype(jnp.bfloat16), "tile", scatter_dimension=0, tiled=True
        ).astype(jnp.float32),
    )
    key_share = jnp.dot(d_keys, full_key.astype(f32).T, precision=lax.Precision.HIGHEST)
    value_share = jnp.dot(d_values, full_value.astype(f32).T, precision=lax.Precision.HIGHEST)
    d_context = (key_share + value_share).astype(bf16)
    d_tokens = (
        cot.astype(f32) + jnp.dot(d_queries, full_query.T, preferred_element_type=f32)
    ).astype(bf16)
    gq_part = jnp.dot(tok.T, d_queries, preferred_element_type=f32)
    go_part = jnp.dot(attended.T, cot, preferred_element_type=f32)
    g_query, g_out = (
        lax.psum_scatter(gq_part, ("fsdp", "tile"), scatter_dimension=0, tiled=True),
        lax.psum_scatter(go_part, ("fsdp", "tile"), scatter_dimension=0, tiled=True),
    )
    return (mixed[None], d_tokens[None], d_context[None], g_query, g_out)


def solution(mesh):
    in_specs = (
        P("fsdp", "tile", None),
        P("fsdp", "tile", None),
        P("fsdp", "tile", None),
        P("fsdp", None),
        P("fsdp", None),
        P("fsdp", None),
        P("fsdp", None),
        P("fsdp", "tile", None),
    )
    out_specs = (
        P("fsdp", "tile", None),
        P("fsdp", "tile", None),
        P("fsdp", "tile", None),
        P(("fsdp", "tile"), None),
        P(("fsdp", "tile"), None),
    )
    return jax.shard_map(local, mesh=mesh, in_specs=in_specs, out_specs=out_specs, check_vma=False)
```

profile of v0, /device:TPU:8, one launch (start us, length us, event | category | flops | bytes accessed | tf_op | source)
XLA Modules:
  0.0 1035.5 jit_solution(17711123839599553506)
XLA Ops:
  10.1 29.6 %all-gather.13.cloned.1.call-done = bf16[1024,1024]{1,0:T(8,128)(2,1)} async-done(((bf16[128,1024]{1,0:T(8,128)(2,1)}), bf16[1024,1024]{1,0:T(8,128)(2,1)}) %all-gather.13.cloned.1.call-update) | async-done | bytes 2097168 | tf_op jit(solution)/shard_map/all_gather | solution.py:24
  39.6 2.7 convolution_convert_fusion.4
  42.4 27.2 %all-gather.7.cloned.1.call-done = bf16[1024,1024]{1,0:T(8,128)(2,1)} async-done(((bf16[128,1024]{1,0:T(8,128)(2,1)}), bf16[1024,1024]{1,0:T(8,128)(2,1)}) %all-gather.7.cloned.1.call-update) | async-done | bytes 2097168 | tf_op jit(solution)/shard_map/all_gather | solution.py:25
  69.5 2.7 convolution_convert_fusion.5
  72.9 26.6 %all-gather.11.cloned.1.call-done = bf16[1024,1024]{1,0:T(8,128)(2,1)} async-done(((bf16[128,1024]{1,0:T(8,128)(2,1)}), bf16[1024,1024]{1,0:T(8,128)(2,1)}) %all-gather.11.cloned.1.call-update) | async-done | bytes 2097168 | tf_op jit(solution)/shard_map/all_gather | solution.py:23
  99.5 2.0 convolution_convert_fusion.3
  101.7 27.6 %all-gather.17.cloned.1.call-done = bf16[1024,1024]{1,0:T(8,128)(2,1)} async-done(((bf16[128,1024]{1,0:T(8,128)(2,1)}), bf16[1024,1024]{1,0:T(8,128)(2,1)}) %all-gather.17.cloned.1.call-update) | async-done | bytes 2097168 | tf_op jit(solution)/shard_map/all_gather | solution.py:26
  129.3 2.4 convolution_convert_fusion.2
  132.5 78.9 %all-gather.15.cloned.1.call-done = bf16[1024,1024]{1,0:T(8,128)(2,1)} async-done(((bf16[32,1024]{1,0:T(8,128)(2,1)}), bf16[1024,1024]{1,0:T(8,128)(2,1)}) %all-gather.15.cloned.1.call-update) | async-done | bytes 2097168 | tf_op jit(solution)/shard_map/all_gather | solution.py:34
  211.4 2.9 copy.29
  214.3 5.4 fusion.32
  219.7 70.0 %all-gather.9.cloned.1.call-done = bf16[1024,1024]{1,0:T(8,128)(2,1)} async-done(((bf16[32,1024]{1,0:T(8,128)(2,1)}), bf16[1024,1024]{1,0:T(8,128)(2,1)}) %all-gather.9.cloned.1.call-update) | async-done | bytes 2097168 | tf_op jit(solution)/shard_map/all_gather | solution.py:35
  289.6 3.9 copy.27
  293.6 5.8 fusion.12
  300.6 2.3 multiply_reduce_fusion
  302.9 1.6 multiply_convert_fusion
  304.5 1.5 convolution_convert_fusion.1
  306.1 2.6 convolution_bitcast_fusion
  308.7 2.7 fusion.23
  311.5 2.9 convolution_convert_fusion
  314.4 2.6 copy.32
  317.3 6.2 fusion.9
  323.4 4.1 copy.34
  327.6 2.8 fusion.18
  330.4 1.5 fusion.17
  332.0 256.4 %all-reduce.5.cloned.1.call-done = (f32[1024,1024]{0,1:T(8,128)}, f32[1024,1024]{1,0:T(8,128)}) async-done(((f32[1024,1024]{0,1:T(8,128)}, f32[1024,1024]{1,0:T(8,128)}), (f32[1024,1024]{0,1:T(8,128)}, f32[1024,1024]{1,0:T(8,128)})) %all-reduce.5.cloned.1.call-update) | async-done | bytes 8388624
  588.4 1.2 constant_dynamic-slice_fusion.1
  590.4 1.4 constant_dynamic-slice_fusion
  591.8 215.8 %reduce-scatter.8.cloned.1.call-done = bf16[32,1024]{1,0:T(8,128)(2,1)} async-done(((bf16[1024,1024]{1,0:T(8,128)(2,1)}), bf16[32,1024]{1,0:T(8,128)(2,1)}) %reduce-scatter.8.cloned.1.call-update) | async-done | bytes 65552
  807.6 2.3 fusion.33
  810.0 216.0 %reduce-scatter.10.cloned.1.call-done = bf16[32,1024]{1,0:T(8,128)(2,1)} async-done(((bf16[1024,1024]{1,0:T(8,128)(2,1)}), bf16[32,1024]{1,0:T(8,128)(2,1)}) %reduce-scatter.10.cloned.1.call-update) | async-done | bytes 65552
  1025.9 3.0 fusion.20
  (46 shorter events, 6.8 us)
Async XLA Ops:
  7.2 32.4 %copy-start = (bf16[1,32,1024]{2,1,0:T(8,128)(2,1)S(1)}, bf16[1,32,1024]{2,1,0:T(8,128)(2,1)}, u32[]{:S(2)}) copy-start(bf16[1,32,1024]{2,1,0:T(8,128)(2,1)} %param.9) | copy-start | bytes 196612
  7.2 65.1 %copy-start.10 = (s32[1,2,16]{2,1,0:T(2,128)S(1)}, s32[1,2,16]{2,1,0:T(2,128)}, u32[]{:S(2)}) copy-start(s32[1,2,16]{2,1,0:T(2,128)} %param.10) | copy-start | bytes 388
  7.2 92.3 %copy-start.5 = (bf16[1,128,1024]{2,1,0:T(8,128)(2,1)S(1)}, bf16[1,128,1024]{2,1,0:T(8,128)(2,1)}, u32[]{:S(2)}) copy-start(bf16[1,128,1024]{2,1,0:T(8,128)(2,1)} %param.8) | copy-start | bytes 786436
  7.2 32.4 %all-gather.13.cloned.1.call-start = ((), (), s32[]{:S(2)}) async-start(), calls=%async_computation.5 | async-start | bytes 2359296 | tf_op jit(solution)/shard_map/all_gather | solution.py:24
  7.9 61.6 %all-gather.7.cloned.1.call-start = ((), (), s32[]{:S(2)}) async-start(), calls=%async_computation.2 | async-start | bytes 2359296 | tf_op jit(solution)/shard_map/all_gather | solution.py:25
  8.7 90.8 %all-gather.11.cloned.1.call-start = ((), (), s32[]{:S(2)}) async-start(), calls=%async_computation.4 | async-start | bytes 2359296 | tf_op jit(solution)/shard_map/all_gather | solution.py:23
  9.4 119.9 %all-gather.17.cloned.1.call-start = ((), (), s32[]{:S(2)}) async-start(), calls=%async_computation.7 | async-start | bytes 2359296 | tf_op jit(solution)/shard_map/all_gather | solution.py:26
  10.0 119.3 %copy-start.6 = (bf16[1,128,1024]{2,1,0:T(8,128)(2,1)S(1)}, bf16[1,128,1024]{2,1,0:T(8,128)(2,1)}, u32[]{:S(2)}) copy-start(bf16[1,128,1024]{2,1,0:T(8,128)(2,1)} %param.15) | copy-start | bytes 786436
  10.0 201.4 %all-gather.15.cloned.1.call-start = ((), (), s32[]{:S(2)}) async-start(), calls=%async_computation.6 | async-start | bytes 2162688 | tf_op jit(solution)/shard_map/all_gather | solution.py:34
  42.3 247.3 %all-gather.9.cloned.1.call-start = ((), (), s32[]{:S(2)}) async-start(), calls=%async_computation.3 | async-start | bytes 2162688 | tf_op jit(solution)/shard_map/all_gather | solution.py:35
  72.3 516.1 %all-reduce.5.cloned.1.call-start = ((), (), s32[]{:S(2)}) async-start(), calls=%async_computation.10 | async-start | bytes 16777216
  293.6 6.4 copy-start.4
  293.6 7.0 copy-start.7
  293.6 7.0 copy-start.8
  304.5 4.2 copy-start.2
  311.4 496.2 %reduce-scatter.8.cloned.1.call-start = ((), (), s32[]{:S(2)}) async-start(), calls=%async_computation.8 | async-start | bytes 2162688
  314.4 2.9 copy-start.9
  317.0 708.9 %reduce-scatter.10.cloned.1.call-start = ((), (), s32[]{:S(2)}) async-start(), calls=%async_computation.9 | async-start | bytes 2162688
  323.4 7.0 copy-start.3
  327.6 701.3 %copy-start.1 = (bf16[1,32,1024]{2,1,0:T(8,128)(2,1)S(1)}, bf16[1,32,1024]{2,1,0:T(8,128)(2,1)}, u32[]{:S(2)}) copy-start(bf16[1,32,1024]{2,1,0:T(8,128)(2,1)} %param.9) | copy-start | bytes 196612
Sparse Core Ops, SparseCore 0:
  9.9 29.6 all-gather.12
  41.5 28.0 all-gather.6
  71.4 28.0 all-gather.10
  101.2 28.0 all-gather.16
  132.3 79.1 all-gather.14
  214.5 75.1 all-gather.8
  311.6 276.7 all-reduce.4
  592.7 214.8 reduce-scatter.7
  811.5 214.4 reduce-scatter.9
where the time goes:
time: 1040 us
  waiting for transfers between devices  951 us (91%)
  matrix products  48.9 us (5%)
  local copies, waits for them, and re-layouts  19.7 us (2%)
  between operations  14 us (1%)
    unnamed x12, waiting for transfers between devices  691 us
    all_gather x1, waiting for transfers between devices, local(): lax.all_gather(own_keys, 'tile', axis=0, tiled=True)  78.9 us
    all_gather x1, waiting for transfers between devices, local(): lax.all_gather(own_values, 'tile', axis=0, tiled=True)  70 us
    all_gather x1, waiting for transfers between devices, local(): lax.all_gather(w_key, 'fsdp', axis=0, tiled=True)  29.6 us
    all_gather x1, waiting for transfers between devices, local(): lax.all_gather(w_out, 'fsdp', axis=0, tiled=True)  27.6 us
    all_gather x1, waiting for transfers between devices, local(): lax.all_gather(w_value, 'fsdp', axis=0, tiled=True)  27.2 us
    all_gather x1, waiting for transfers between devices, local(): lax.all_gather(w_query, 'fsdp', axis=0, tiled=True)  26.6 us
  transfers between devices with their start and end apart: 9, of which 9 were waited for; matrix products, arithmetic and copies ran while one was open for 4% of the time, Pallas kernels for 0%

commit v1 on v0

v1 whole, which is shorter than its diff:
```python
import functools

import jax
import jax.numpy as jnp
from jax import lax
from jax.experimental import pallas as pl
from jax.experimental.pallas import tpu as pltpu
from jax.sharding import Mesh, PartitionSpec as P

BF = jnp.bfloat16
F32 = jnp.float32
X_SHIFTS = (0, 1, -1, 2)
Z_SHIFTS = (0, 4, 3, -3, 2, -2, 1, -1)
SIZES = {"y": 4, "c": 2, "x": 4, "z": 8}


def dot(a, b, da, db):
    return lax.dot_general(a, b, (((da,), (db,)), ((), ())), preferred_element_type=F32)


def shift(value, axis, by):
    n = SIZES[axis]
    return lax.ppermute(value, axis, [(i, (i + by) % n) for i in range(n)])


def mod(a, n):
    return lax.rem(a + n, n)


def kv_kernel(pos, c0, c1, c2, c3, wa, wb, kv_out, w_out, wo_out, ctx):
    y, c, x = pos[0], pos[1], pos[2]
    for src, by in zip((c0, c1, c2, c3), X_SHIFTS):
        at = pl.multiple_of(32 * mod(x - by, 4), 32)
        ctx[pl.ds(at, 32), :] = src[...]
    for half, core in ((wa, c), (wb, 1 - c)):
        for slot, by in enumerate(X_SHIFTS):
            at = pl.multiple_of(128 * (2 * mod(y - by, 4) + core), 128)
            w_out[pl.ds(at, 128), :] = half[128 * slot : 128 * slot + 128, 0:768]
        at = pl.multiple_of(128 * core, 128)
        for j in range(4):
            wo_out[pl.ds(at, 128), 256 * j : 256 * j + 256] = half[128 * j : 128 * j + 128, 768:1024]
    kv_out[...] = dot(ctx[...], w_out[:, 0:512], 1, 0).astype(BF)


def attn_kernel(pos, xg, kv0, kv1, kv2, kv3, kv4, kv5, kv6, kv7, w, wo, pay, att_out, dq_out,
                k_s, v_s, kt_s, vt_s, q_s, da_s, dk_s, dv_s, at_s, dqt_s, gq_s, go_s):
    z = pos[3]
    for src, by in zip((kv0, kv1, kv2, kv3, kv4, kv5, kv6, kv7), Z_SHIFTS):
        zs = mod(z - by, 8)
        for xs in range(4):
            at = pl.multiple_of(256 * xs + 32 * zs, 32)
            k_s[pl.ds(at, 32), :] = src[32 * xs : 32 * xs + 32, 0:256]
            v_s[pl.ds(at, 32), :] = src[32 * xs : 32 * xs + 32, 256:512]
    kt_s[...] = k_s[...].T
    vt_s[...] = v_s[...].T
    wq = w[:, 512:768]
    for t in range(4):
        rows = slice(128 * t, 128 * t + 128)
        q_s[rows, :] = dot(xg[t, 0:128, :], wq, 1, 0).astype(BF) * jnp.asarray(0.125, BF)
        da_s[rows, :] = dot(xg[t, 128:256, :], wo[...], 1, 1).astype(BF)
    dk_s[...] = jnp.zeros_like(dk_s)
    dv_s[...] = jnp.zeros_like(dv_s)
    lane = lax.broadcasted_iota(jnp.int32, (256, 128), 1) // 64
    row16 = lax.broadcasted_iota(jnp.int32, (16, 128), 0)
    col16 = lax.broadcasted_iota(jnp.int32, (16, 128), 1) // 64
    pick = jnp.where(row16 == col16, 1.0, 0.0).astype(BF)
    for u in range(2):
        allowed = jnp.concatenate(
            [dot(xg[2 * u + s, 256:272, :], pick, 0, 0) for s in range(2)], axis=1
        ) > 0.5
        for h in range(4):
            pair = slice(128 * (h // 2), 128 * (h // 2) + 128)
            head = slice(64 * h, 64 * h + 64)
            qrows = slice(256 * u, 256 * u + 256)
            own = lane == (h % 2)
            zero = jnp.zeros((256, 128), BF)
            qm = jnp.where(own, q_s[qrows, pair], zero)
            dam = jnp.where(own, da_s[qrows, pair], zero)
            s = jnp.where(allowed, dot(k_s[:, pair], qm, 1, 1), -jnp.inf)
            e = jnp.exp(s - jnp.max(s, axis=0, keepdims=True))
            p = e * (1.0 / jnp.sum(e, axis=0, keepdims=True))
            plow = p.astype(BF)
            at_s[head, qrows] = dot(vt_s[head, :], plow, 1, 0).astype(BF)
            dv_s[:, pair] += dot(plow, dam, 1, 0)
            dp = dot(v_s[:, pair], dam, 1, 1)
            delta = jnp.sum(p * dp, axis=0, keepdims=True)
            ds = (p * (dp - delta)).astype(BF)
            dqt_s[head, qrows] = (0.125 * dot(kt_s[head, :], ds, 1, 0)).astype(BF)
            dk_s[:, pair] += dot(ds, qm, 1, 0)
    att_out[...] = at_s[...].T
    dq_out[...] = dqt_s[...].T
    go = jnp.zeros((256, 1024), F32)
    gq = jnp.zeros((256, 1024), F32)
    for t in range(4):
        rows = slice(128 * t, 128 * t + 128)
        go += dot(at_s[:, rows], xg[t, 128:256, :], 1, 0)
        gq += dot(dqt_s[:, rows], xg[t, 0:128, :], 1, 0)
    for j in range(8):
        go_s[j] = go[:, 128 * j : 128 * j + 128]
    for j in range(2):
        gq_s[j] = gq[128 * j : 128 * j + 128, :].T
    for zd in range(8):
        base = 128 * zd
        for b in range(4):
            rows = slice(base + 32 * b, base + 32 * b + 32)
            keys = slice(256 * b + 32 * zd, 256 * b + 32 * zd + 32)
            pay[rows, 0:256] = dk_s[keys, :].astype(BF)
            pay[rows, 256:512] = dv_s[keys, :].astype(BF)
            for j in range(2):
                lanes = slice(512 + 128 * j, 640 + 128 * j)
                pay[rows, lanes] = gq_s[j, pl.ds(4 * zd + b, 32, stride=32), :].astype(BF)
                part = [go_s[2 * b + j, pl.ds(4 * zd + i, 8, stride=32), :] for i in range(4)]
                lanes = slice(768 + 128 * j, 896 + 128 * j)
                pay[rows, lanes] = jnp.concatenate(part, axis=0).astype(BF)


def md_kernel(att, dq, w, wo, out):
    for t in range(4):
        rows = slice(128 * t, 128 * t + 128)
        out[t, 0:128, :] = dot(att[rows, :], wo[...], 1, 0).astype(BF)
        out[t, 128:256, :] = dot(dq[rows, :], w[:, 512:768], 1, 1).astype(BF)


VM = pl.BlockSpec(memory_space=pltpu.VMEM)
SM = pl.BlockSpec(memory_space=pltpu.SMEM)


def call(kernel, n_in, outs, scratch, flops, nbytes, limit, name):
    return pl.pallas_call(
        kernel,
        out_shape=outs,
        in_specs=[SM] + [VM] * (n_in - 1) if name != "md" else [VM] * n_in,
        out_specs=[VM] * len(outs),
        scratch_shapes=scratch,
        compiler_params=pltpu.CompilerParams(vmem_limit_bytes=limit * 2**20),
        cost_estimate=pl.CostEstimate(flops=flops, bytes_accessed=nbytes, transcendentals=0),
        name=name,
    )


def local(tokens, context, pattern, w_query, w_key, w_value, w_out, cotangent):
    y, c, x, z = (lax.axis_index(n) for n in ("y", "c", "x", "z"))
    pos = jnp.stack([y, c, x, z]).astype(jnp.int32)
    tok, ctx, cot = tokens[0], context[0], cotangent[0]
    mask = jnp.repeat(pattern[0].astype(BF), 64, axis=1)
    own = jnp.concatenate([tok, cot, mask, jnp.zeros((14, 1024), BF)], axis=0)
    xg = lax.all_gather(own, "x", axis=0, tiled=False)

    ctxs = [ctx] + [shift(ctx, "x", by) for by in X_SHIFTS[1:]]
    col = 256 * x
    cut = lambda w: lax.dynamic_slice(w, (0, col), (128, 256))
    mine = jnp.concatenate([cut(w_key), cut(w_value), cut(w_query)], axis=1)
    slots = [mine] + [shift(mine, "y", by) for by in X_SHIFTS[1:]]
    wo = lax.ppermute(
        w_out, ("y", "x"), [(a * 4 + b, b * 4 + a) for a in range(4) for b in range(4)]
    )
    wo4 = jnp.concatenate([wo[:, 256 * j : 256 * j + 256] for j in range(4)], axis=0)
    wa = jnp.concatenate([jnp.concatenate(slots, axis=0), wo4], axis=1)
    wb = shift(wa, "c", 1)
    kv, w, wo_g = call(
        kv_kernel, 7,
        [jax.ShapeDtypeStruct((128, 512), BF), jax.ShapeDtypeStruct((1024, 768), BF),
         jax.ShapeDtypeStruct((256, 1024), BF)],
        [pltpu.VMEM((128, 1024), BF)], 2 * 128 * 1024 * 512, 4 * 2**20, 16, "kv",
    )(pos, *ctxs, wa, wb)

    kvs = [kv] + [shift(kv, "z", by) for by in Z_SHIFTS[1:]]
    pay, att, dq = call(
        attn_kernel, 12,
        [jax.ShapeDtypeStruct((1024, 1024), BF), jax.ShapeDtypeStruct((512, 256), BF),
         jax.ShapeDtypeStruct((512, 256), BF)],
        [pltpu.VMEM((1024, 256), BF), pltpu.VMEM((1024, 256), BF),
         pltpu.VMEM((256, 1024), BF), pltpu.VMEM((256, 1024), BF),
         pltpu.VMEM((512, 256), BF), pltpu.VMEM((512, 256), BF),
         pltpu.VMEM((1024, 256), F32), pltpu.VMEM((1024, 256), F32),
         pltpu.VMEM((256, 512), BF), pltpu.VMEM((256, 512), BF),
         pltpu.VMEM((2, 1024, 128), F32), pltpu.VMEM((8, 256, 128), F32)],
        2 * 1300 * 10**6, 8 * 2**20, 48, "attention",
    )(pos, xg, *kvs, w, wo_g)

    red = lax.psum_scatter(pay, "z", scatter_dimension=0, tiled=True)
    (md,) = call(
        md_kernel, 4, [jax.ShapeDtypeStruct((4, 256, 1024), BF)], [],
        2 * 2 * 512 * 256 * 1024, 4 * 2**20, 16, "md",
    )(att, dq, w, wo_g)
    md = lax.all_to_all(md, "x", split_axis=0, concat_axis=0, tiled=True)
    md = jnp.sum(md.astype(F32), axis=0)
    mixed = (tok.astype(F32) + md[0:128]).astype(BF)
    d_tokens = (cot.astype(F32) + md[128:256]).astype(BF)

    part = (dot(red[:, 0:256], w[:, 0:256], 1, 1) + dot(red[:, 256:512], w[:, 256:512], 1, 1)).astype(BF)
    part = lax.all_to_all(part.reshape(4, 32, 1024), "x", split_axis=0, concat_axis=0, tiled=True)
    d_context = jnp.sum(part.astype(F32), axis=0).astype(BF)

    gq = jnp.transpose(red[:, 512:768].reshape(4, 32, 256), (1, 0, 2))
    go = jnp.transpose(red[:, 768:1024].reshape(4, 4, 8, 256), (2, 1, 0, 3)).reshape(1, 8, 4, 1024)
    there = (jnp.arange(4) == x).reshape(4, 1, 1, 1)
    go = jnp.where(there, go, jnp.zeros((), BF)).reshape(32, 4, 1024)
    g = jnp.concatenate([gq, go], axis=2)
    g = lax.all_to_all(g, ("y", "c", "x"), split_axis=0, concat_axis=0, tiled=True).astype(F32)
    g_query = jnp.sum(g[:, :, 0:256].reshape(8, 4, 4, 256), axis=0)
    g_query = jnp.transpose(g_query, (1, 0, 2)).reshape(4, 1024)
    g_out = jnp.sum(g[:, :, 256:1280], axis=0)
    return mixed[None], d_tokens[None], d_context[None], g_query, g_out


def solution(mesh):
    fine = Mesh(mesh.devices.reshape(4, 2, 4, 8), ("y", "c", "x", "z"))
    seq = P(("y", "c"), ("x", "z"), None)
    wts = P(("y", "c"), None)
    grad = P(("y", "c", "x", "z"), None)
    return jax.shard_map(
        local,
        mesh=fine,
        in_specs=(seq, seq, seq, wts, wts, wts, wts, seq),
        out_specs=(seq, seq, seq, grad, grad),
        check_vma=False,
    )
```

time: 1040 us -> 186 us (0.18)
  waiting for transfers between devices: 951 us -> 79 us
  matrix products: 48.9 us -> 2.99 us
  starting transfers between devices: 0.54 us -> 42.2 us
  Pallas kernels: 0 us -> 20 us
    unnamed x12 -> x2, waiting for transfers between devices: 691 us -> 0.03 us
    all_gather x6 -> x1, waiting for transfers between devices: 260 us -> 0.01 us  [local(): xg = lax.all_gather(own, 'x', axis=0, tiled=False)]
    dot_general x15 -> x2, matrix products: 43.5 us -> 2.99 us  [dot(): lax.dot_general(a, b, (((da,), (db,)), ((), ())), preferred_element_type=...]
    reduce_scatter x0 -> x1, waiting for transfers between devices: none -> 35.4 us  [local(): red = lax.psum_scatter(pay, 'z', scatter_dimension=0, tiled=True)]
    ppermute x0 -> x15, waiting for transfers between devices: none -> 33 us  [the longest x14 28 us: shift(): return lax.ppermute(value, axis, [(i, (i + by) % n) for i in range(n)])]
    ppermute x0 -> x15, starting transfers between devices: none -> 27.9 us  [the longest x14 24.6 us: shift(): return lax.ppermute(value, axis, [(i, (i + by) % n) for i in range(n)])]
    pallas_call x0 -> x3, Pallas kernels: none -> 20 us  [the longest x1 16.5 us: local(): call(attn_kernel, 12, [jax.ShapeDtypeStruct((1024, 1024), BF), jax.ShapeD...]
    all_to_all x0 -> x3, starting transfers between devices: none -> 14.2 us  [the longest x1 5.39 us: local(): lax.all_to_all(g, ('y', 'c', 'x'), split_axis=0, concat_axis=0, tiled=True)]
  transfers between devices with their start and end apart: 9 -> 20, of which waited for: 9 -> 12; matrix products, arithmetic and copies ran while one was open for 4% -> 6% of each run, Pallas kernels for 0% -> 2%
where the time goes in v1:
time: 186 us; the launch traced here: 183 us
  waiting for transfers between devices  79 us (42%)
  starting transfers between devices  42.2 us (23%)
  Pallas kernels  20 us (11%)
  local copies, waits for them, and re-layouts  15.2 us (8%)
  between operations  14.3 us (8%)
  other arithmetic  9.1 us (5%)
  matrix products  2.99 us (2%)
    reduce_scatter x1, waiting for transfers between devices, local(): red = lax.psum_scatter(pay, 'z', scatter_dimension=0, tiled=True)  35.4 us
    ppermute x14, waiting for transfers between devices, shift(): return lax.ppermute(value, axis, [(i, (i + by) % n) for i in range(n)])  28 us
    ppermute x14, starting transfers between devices, shift(): return lax.ppermute(value, axis, [(i, (i + by) % n) for i in range(n)])  24.6 us
    pallas_call x1, Pallas kernels, local(): call(attn_kernel, 12, [jax.ShapeDtypeStruct((1024, 1024), BF), jax.ShapeD...  16.5 us
    unnamed x38, local copies, waits for them, and re-layouts  12.8 us
    all_to_all x1, waiting for transfers between devices, local(): lax.all_to_all(part.reshape(4, 32, 1024), 'x', split_axis=0, concat_axis=...  5.79 us
    all_to_all x1, starting transfers between devices, local(): lax.all_to_all(g, ('y', 'c', 'x'), split_axis=0, concat_axis=0, tiled=True)  5.39 us
    ppermute x1, waiting for transfers between devices, local(): lax.ppermute(w_out, ('y', 'x'), [(a * 4 + b, b * 4 + a) for a in range(4)...  5.06 us
  transfers between devices with their start and end apart: 20, of which 12 were waited for; matrix products, arithmetic and copies ran while one was open for 6% of the time, Pallas kernels for 2%

profile of v1, /device:TPU:8, one launch (start us, length us, event | category | flops | bytes accessed | tf_op | source)
XLA Modules:
  0.0 182.8 jit_solution(11529037087629059264)
XLA Ops:
  8.2 2.0 %maximum_maximum_fusion.1 = bf16[272,1024]{1,0:T(8,128)(2,1)} fusion(bf16[2,1024]{1,0:T(2,128)(2,1)S(1)} %reshape.39, bf16[128,1024]{1,0:T(8,128)(2,1)} %bitcast.38, bf16[128,1024]{1,0:T(8,128)(2,1)} %bitcast.39, bf16[272]{0:T(512)(128)(2,1)S(1)} %pad.18.clone), kind=kLoop, calls=%fused_computation.4 | loop fusion | flops 2228224 | bytes 1085984 | tf_op jit(solution)/shard_map/concatenate | solution.py:146
  10.3 3.3 %collective-permute-start.6 = (bf16[128,1024]{1,0:T(8,128)(2,1)}, bf16[128,1024]{1,0:T(8,128)(2,1)S(1)}, u32[]{:S(2)}, u32[]{:S(2)}) collective-permute-start(bf16[128,1024]{1,0:T(8,128)(2,1)} %param.14), channel_id=1, source_target_pairs={{0,0},{8,64},{16,128},{24,192},{64,8},{72,72},{80,136},{88,200},{1... | collective-permute-start | bytes 786440 | tf_op jit(solution)/shard_map/ppermute | solution.py:154
  14.5 3.4 %collective-permute-start.5 = (bf16[128,768]{1,0:T(8,128)(2,1)S(1)}, bf16[128,768]{1,0:T(8,128)(2,1)S(1)}, u32[]{:S(2)}, u32[]{:S(2)}) collective-permute-start(bf16[128,768]{1,0:T(8,128)(2,1)S(1)} %pad_maximum_fusion.1), channel_id=1, source_target_pairs={{0,128},{64,192},{128,0},{192,64},{1,129},{65,193},{129,1},{193,65... | collective-permute-start | bytes 589832 | tf_op jit(solution)/shard_map/ppermute | solution.py:23
  17.9 1.7 collective-permute-start.4
  20.0 5.1 %collective-permute-done.6 = bf16[128,1024]{1,0:T(8,128)(2,1)S(1)} collective-permute-done((bf16[128,1024]{1,0:T(8,128)(2,1)}, bf16[128,1024]{1,0:T(8,128)(2,1)S(1)}, u32[]{:S(2)}, u32[]{:S(2)}) %collective-permute-start.6) | collective-permute-done | bytes 262176 | tf_op jit(solution)/shard_map/ppermute | solution.py:154
  25.1 1.7 collective-permute-done.4
  26.8 8.6 %collective-permute-done.3 = bf16[128,768]{1,0:T(8,128)(2,1)S(1)} collective-permute-done((bf16[128,768]{1,0:T(8,128)(2,1)S(1)}, bf16[128,768]{1,0:T(8,128)(2,1)S(1)}, u32[]{:S(2)}, u32[]{:S(2)}) %collective-permute-start.3) | collective-permute-done | bytes 196640 | tf_op jit(solution)/shard_map/ppermute | solution.py:23
  35.7 2.1 %collective-permute-start.1 = (bf16[32,1024]{1,0:T(8,128)(2,1)S(1)}, bf16[32,1024]{1,0:T(8,128)(2,1)S(1)}, u32[]{:S(2)}, u32[]{:S(2)}) collective-permute-start(bf16[32,1024]{1,0:T(8,128)(2,1)S(1)} %bitcast.35), channel_id=1, source_target_pairs={{0,24},{8,0},{16,8},{24,16},{1,25},{9,1},{17,9},{25,17},{2,26},{10... | collective-permute-start | bytes 196616 | tf_op jit(solution)/shard_map/ppermute | solution.py:23
  37.9 5.7 %collective-permute-done.2.c3 = bf16[32,1024]{1,0:T(8,128)(2,1)S(1)} collective-permute-done((bf16[32,1024]{1,0:T(8,128)(2,1)S(1)}, bf16[32,1024]{1,0:T(8,128)(2,1)S(1)}, u32[]{:S(2)}, u32[]{:S(2)}) %collective-permute-start.2) | collective-permute-done | bytes 65568 | tf_op jit(solution)/shard_map/ppermute | solution.py:23
  44.2 1.3 collective-permute-done.c1
  46.1 1.0 copy-done.2
  47.1 1.2 copy-done.3
  50.0 1.0 kv.1
  51.0 5.9 %collective-permute-start.14 = (bf16[128,512]{1,0:T(8,128)(2,1)S(1)}, bf16[128,512]{1,0:T(8,128)(2,1)S(1)}, u32[]{:S(2)}, u32[]{:S(2)}) collective-permute-start(bf16[128,512]{1,0:T(8,128)(2,1)S(1)} %get-tuple-element.11.kv0), channel_id=1, source_target_pairs={{0,7},{1,0},{2,1},{3,2},{4,3},{5,4},{6,5},{7,6},{8,15},{9,8},{10,9... | collective-permute-start | bytes 393224 | tf_op jit(solution)/shard_map/ppermute | solution.py:23
  57.0 2.5 %collective-permute-start.12 = (bf16[128,512]{1,0:T(8,128)(2,1)S(1)}, bf16[128,512]{1,0:T(8,128)(2,1)S(1)}, u32[]{:S(2)}, u32[]{:S(2)}) collective-permute-start(bf16[128,512]{1,0:T(8,128)(2,1)S(1)} %get-tuple-element.11.kv0), channel_id=1, source_target_pairs={{0,6},{1,7},{2,0},{3,1},{4,2},{5,3},{6,4},{7,5},{8,14},{9,15},{10,... | collective-permute-start | bytes 393224 | tf_op jit(solution)/shard_map/ppermute | solution.py:23
  59.9 2.9 %collective-permute-start.10 = (bf16[128,512]{1,0:T(8,128)(2,1)S(1)}, bf16[128,512]{1,0:T(8,128)(2,1)S(1)}, u32[]{:S(2)}, u32[]{:S(2)}) collective-permute-start(bf16[128,512]{1,0:T(8,128)(2,1)S(1)} %get-tuple-element.11.kv0), channel_id=1, source_target_pairs={{0,5},{1,6},{2,7},{3,0},{4,1},{5,2},{6,3},{7,4},{8,13},{9,14},{10,... | collective-permute-start | bytes 393224 | tf_op jit(solution)/shard_map/ppermute | solution.py:23
  63.7 4.1 %collective-permute-start.8 = (bf16[128,512]{1,0:T(8,128)(2,1)S(1)}, bf16[128,512]{1,0:T(8,128)(2,1)S(1)}, u32[]{:S(2)}, u32[]{:S(2)}) collective-permute-start(bf16[128,512]{1,0:T(8,128)(2,1)S(1)} %get-tuple-element.11.kv0), channel_id=1, source_target_pairs={{0,4},{1,5},{2,6},{3,7},{4,0},{5,1},{6,2},{7,3},{8,12},{9,13},{10,... | collective-permute-start | bytes 393224 | tf_op jit(solution)/shard_map/ppermute | solution.py:23
  68.9 1.6 collective-permute-done.11.kv4
  71.1 8.0 %collective-permute-done.9.kv2 = bf16[128,512]{1,0:T(8,128)(2,1)S(1)} collective-permute-done((bf16[128,512]{1,0:T(8,128)(2,1)S(1)}, bf16[128,512]{1,0:T(8,128)(2,1)S(1)}, u32[]{:S(2)}, u32[]{:S(2)}) %collective-permute-start.9) | collective-permute-done | bytes 131104 | tf_op jit(solution)/shard_map/ppermute | solution.py:23
  84.8 16.5 %attention.1 = (bf16[1024,1024]{1,0:T(8,128)(2,1)S(1)}, bf16[512,256]{1,0:T(8,128)(2,1)S(1)}, bf16[512,256]{1,0:T(8,128)(2,1)S(1)}) custom-call(s32[4]{0:T(128)S(1)} %pad_add_fusion.pos, bf16[4,272,1024]{2,1,0:T(8,128)(2,1)} %bitcast.47, bf16[128,512]{1,0:T(8,128)(2,1)S(1)} %copy-done.10, bf16[128,512]{1,0:T(8,128)(2,1)S(1)} %copy-done.16, ...), custom_call_target="tpu_custom_call" | custom-call | flops 2600000000 | bytes 8388608 | tf_op jit(solution)/shard_map/attention/pallas_call | solution.py:168
  101.3 1.4 copy-done.1
  102.7 2.5 %md.1 = bf16[4,256,1024]{2,1,0:T(8,128)(2,1)} custom-call(bf16[512,256]{1,0:T(8,128)(2,1)S(1)} %get-tuple-element.14.att, bf16[512,256]{1,0:T(8,128)(2,1)S(1)} %get-tuple-element.15.dq, bf16[1024,768]{1,0:T(8,128)(2,1)S(1)} %get-tuple-element.12.w, bf16[256,1024]{1,0:T(8,128)(2,1)S(1)} %get-tuple-element.13.wo), custom_call_target="tpu_custom_call" | custom-call | flops 536870912 | bytes 4194304 | tf_op jit(solution)/shard_map/md/pallas_call | solution.py:182
  105.2 4.4 %all-to-all-start = ((bf16[4,256,1024]{2,1,0:T(8,128)(2,1)}), bf16[4,256,1024]{2,1,0:T(8,128)(2,1)}, u32[]{:S(2)}, u32[]{:S(2)}) async-start(bf16[4,256,1024]{2,1,0:T(8,128)(2,1)} %md.1), calls=%async_computation | async-start | bytes 4194304 | tf_op jit(solution)/shard_map/all_to_all | solution.py:186
  109.9 35.4 %reduce-scatter.2.cloned.1.call-done = bf16[128,1024]{1,0:T(8,128)(2,1)} async-done(((bf16[1024,1024]{1,0:T(8,128)(2,1)}), bf16[128,1024]{1,0:T(8,128)(2,1)}) %reduce-scatter.2.cloned.1.call-update) | async-done | bytes 262160 | tf_op jit(solution)/shard_map/reduce_scatter | solution.py:181
  146.5 1.1 fusion.3
  147.7 1.9 %fusion = bf16[128,1024]{1,0:T(8,128)(2,1)} fusion(f32[128,1024]{1,0:T(8,128)S(1)} %fusion.3, bf16[1024,768]{1,0:T(8,128)(2,1)S(1)} %get-tuple-element.12.w, bf16[128,1024]{1,0:T(8,128)(2,1)} %reduce-scatter.2.cloned.1.call-done), kind=kOutput, calls=%fused_computation.2 | convolution fusion | flops 67371008 | bytes 1376256 | tf_op jit(solution)/shard_map/dot_general | solution.py:18
  149.5 4.4 %all-to-all-start.1 = ((bf16[4,32,1024]{2,1,0:T(8,128)(2,1)}), bf16[4,32,1024]{2,1,0:T(8,128)(2,1)S(1)}, u32[]{:S(2)}, u32[]{:S(2)}) async-start(bf16[4,32,1024]{2,1,0:T(8,128)(2,1)} %bitcast.11), calls=%async_computation.2 | async-start | bytes 524288 | tf_op jit(solution)/shard_map/all_to_all | solution.py:192
  154.8 5.8 %all-to-all-done.1 = bf16[4,32,1024]{2,1,0:T(8,128)(2,1)S(1)} async-done(((bf16[4,32,1024]{2,1,0:T(8,128)(2,1)}), bf16[4,32,1024]{2,1,0:T(8,128)(2,1)S(1)}, u32[]{:S(2)}, u32[]{:S(2)}) %all-to-all-start.1) | async-done | bytes 262176 | tf_op jit(solution)/shard_map/all_to_all | solution.py:192
  160.6 5.4 %all-to-all-start.2 = ((bf16[32,4,1280]{2,1,0:T(4,128)(2,1)}), bf16[32,4,1280]{2,1,0:T(4,128)(2,1)S(1)}, u32[]{:S(2)}, u32[]{:S(2)}) async-start(bf16[32,4,1280]{2,1,0:T(4,128)(2,1)} %pad_maximum_fusion), calls=%async_computation.3 | async-start | bytes 655360 | tf_op jit(solution)/shard_map/all_to_all | solution.py:200
  166.0 2.1 %convert_reduce_fusion = f32[256,1024]{1,0:T(8,128)S(1)} fusion(bf16[4,256,1024]{2,1,0:T(8,128)(2,1)} %all-to-all-done), kind=kLoop, calls=%fused_computation | loop fusion | flops 1835008 | bytes 3145728 | tf_op jit(solution)/shard_map/reduce_sum | solution.py:187
  168.2 1.0 fusion.7
  169.8 4.8 %all-to-all-done.2 = bf16[32,4,1280]{2,1,0:T(4,128)(2,1)S(1)} async-done(((bf16[32,4,1280]{2,1,0:T(4,128)(2,1)}), bf16[32,4,1280]{2,1,0:T(4,128)(2,1)S(1)}, u32[]{:S(2)}, u32[]{:S(2)}) %all-to-all-start.2) | async-done | bytes 327712 | tf_op jit(solution)/shard_map/all_to_all | solution.py:200
  (82 shorter events, 18.8 us)
Async XLA Ops:
  7.2 6.4 %copy-start = (bf16[128,1024]{1,0:T(8,128)(2,1)S(1)}, bf16[128,1024]{1,0:T(8,128)(2,1)}, u32[]{:S(2)}) copy-start(bf16[128,1024]{1,0:T(8,128)(2,1)} %param.12) | copy-start | bytes 786436
  7.2 74.0 %all-gather.3.cloned.1.call-start = ((), (), s32[]{:S(2)}) async-start(), calls=%async_computation.5 | async-start | bytes 2785280 | tf_op jit(solution)/shard_map/all_gather | solution.py:147
  10.2 25.5 %copy-start.4 = (bf16[1,32,1024]{2,1,0:T(8,128)(2,1)S(1)}, bf16[1,32,1024]{2,1,0:T(8,128)(2,1)}, u32[]{:S(2)}) copy-start(bf16[1,32,1024]{2,1,0:T(8,128)(2,1)} %param.9) | copy-start | bytes 196612
  10.2 135.0 %reduce-scatter.2.cloned.1.call-start = ((), (), s32[]{:S(2)}) async-start(), calls=%async_computation.4 | async-start | bytes 2359296 | tf_op jit(solution)/shard_map/reduce_scatter | solution.py:181
  10.3 14.8 %collective-permute-start.6 = (bf16[128,1024]{1,0:T(8,128)(2,1)}, bf16[128,1024]{1,0:T(8,128)(2,1)S(1)}, u32[]{:S(2)}, u32[]{:S(2)}) collective-permute-start(bf16[128,1024]{1,0:T(8,128)(2,1)} %param.14), channel_id=1, source_target_pairs={{0,0},{8,64},{16,128},{24,192},{64,8},{72,72},{80,136},{88,200},{1... | collective-permute-start | bytes 786440 | tf_op jit(solution)/shard_map/ppermute | solution.py:154
  14.5 10.5 %collective-permute-start.5 = (bf16[128,768]{1,0:T(8,128)(2,1)S(1)}, bf16[128,768]{1,0:T(8,128)(2,1)S(1)}, u32[]{:S(2)}, u32[]{:S(2)}) collective-permute-start(bf16[128,768]{1,0:T(8,128)(2,1)S(1)} %pad_maximum_fusion.1), channel_id=1, source_target_pairs={{0,128},{64,192},{128,0},{192,64},{1,129},{65,193},{129,1},{193,65... | collective-permute-start | bytes 589832 | tf_op jit(solution)/shard_map/ppermute | solution.py:23
  17.9 8.8 %collective-permute-start.4 = (bf16[128,768]{1,0:T(8,128)(2,1)S(1)}, bf16[128,768]{1,0:T(8,128)(2,1)S(1)}, u32[]{:S(2)}, u32[]{:S(2)}) collective-permute-start(bf16[128,768]{1,0:T(8,128)(2,1)S(1)} %pad_maximum_fusion.1), channel_id=1, source_target_pairs={{0,192},{64,0},{128,64},{192,128},{1,193},{65,1},{129,65},{193,129... | collective-permute-start | bytes 589832 | tf_op jit(solution)/shard_map/ppermute | solution.py:23
  19.7 15.7 %collective-permute-start.3 = (bf16[128,768]{1,0:T(8,128)(2,1)S(1)}, bf16[128,768]{1,0:T(8,128)(2,1)S(1)}, u32[]{:S(2)}, u32[]{:S(2)}) collective-permute-start(bf16[128,768]{1,0:T(8,128)(2,1)S(1)} %pad_maximum_fusion.1), channel_id=1, source_target_pairs={{0,64},{64,128},{128,192},{192,0},{1,65},{65,129},{129,193},{193,1... | collective-permute-start | bytes 589832 | tf_op jit(solution)/shard_map/ppermute | solution.py:23
  35.5 10.6 %collective-permute-start.7 = (bf16[512,1024]{1,0:T(8,128)(2,1)S(1)}, bf16[512,1024]{1,0:T(8,128)(2,1)S(1)}, u32[]{:S(2)}, u32[]{:S(2)}) collective-permute-start(bf16[512,1024]{1,0:T(8,128)(2,1)S(1)} %maximum_maximum_fusion.wa), channel_id=1, source_target_pairs={{0,32},{32,0},{1,33},{33,1},{2,34},{34,2},{3,35},{35,3},{4,36},{36... | collective-permute-start | bytes 3145736 | tf_op jit(solution)/shard_map/ppermute | solution.py:23
  35.7 7.9 %collective-permute-start.2 = (bf16[32,1024]{1,0:T(8,128)(2,1)S(1)}, bf16[32,1024]{1,0:T(8,128)(2,1)S(1)}, u32[]{:S(2)}, u32[]{:S(2)}) collective-permute-start(bf16[32,1024]{1,0:T(8,128)(2,1)S(1)} %bitcast.34), channel_id=1, source_target_pairs={{0,16},{8,24},{16,0},{24,8},{1,17},{9,25},{17,1},{25,9},{2,18},{10... | collective-permute-start | bytes 196616 | tf_op jit(solution)/shard_map/ppermute | solution.py:23
  35.7 7.9 %collective-permute-start.1 = (bf16[32,1024]{1,0:T(8,128)(2,1)S(1)}, bf16[32,1024]{1,0:T(8,128)(2,1)S(1)}, u32[]{:S(2)}, u32[]{:S(2)}) collective-permute-start(bf16[32,1024]{1,0:T(8,128)(2,1)S(1)} %bitcast.35), channel_id=1, source_target_pairs={{0,24},{8,0},{16,8},{24,16},{1,25},{9,1},{17,9},{25,17},{2,26},{10... | collective-permute-start | bytes 196616 | tf_op jit(solution)/shard_map/ppermute | solution.py:23
  37.8 7.6 %collective-permute-start = (bf16[32,1024]{1,0:T(8,128)(2,1)S(1)}, bf16[32,1024]{1,0:T(8,128)(2,1)S(1)}, u32[]{:S(2)}, u32[]{:S(2)}) collective-permute-start(bf16[32,1024]{1,0:T(8,128)(2,1)S(1)} %bitcast.36), channel_id=1, source_target_pairs={{0,8},{8,16},{16,24},{24,0},{1,9},{9,17},{17,25},{25,1},{2,10},{10... | collective-permute-start | bytes 196616 | tf_op jit(solution)/shard_map/ppermute | solution.py:23
  46.1 1.0 copy-start.2
  47.1 1.2 copy-start.3
  48.3 0.8 copy-start.6
  51.0 11.8 %collective-permute-start.14 = (bf16[128,512]{1,0:T(8,128)(2,1)S(1)}, bf16[128,512]{1,0:T(8,128)(2,1)S(1)}, u32[]{:S(2)}, u32[]{:S(2)}) collective-permute-start(bf16[128,512]{1,0:T(8,128)(2,1)S(1)} %get-tuple-element.11.kv0), channel_id=1, source_target_pairs={{0,7},{1,0},{2,1},{3,2},{4,3},{5,4},{6,5},{7,6},{8,15},{9,8},{10,9... | collective-permute-start | bytes 393224 | tf_op jit(solution)/shard_map/ppermute | solution.py:23
  57.0 6.8 %collective-permute-start.13 = (bf16[128,512]{1,0:T(8,128)(2,1)S(1)}, bf16[128,512]{1,0:T(8,128)(2,1)S(1)}, u32[]{:S(2)}, u32[]{:S(2)}) collective-permute-start(bf16[128,512]{1,0:T(8,128)(2,1)S(1)} %get-tuple-element.11.kv0), channel_id=1, source_target_pairs={{0,1},{1,2},{2,3},{3,4},{4,5},{5,6},{6,7},{7,0},{8,9},{9,10},{10,1... | collective-permute-start | bytes 393224 | tf_op jit(solution)/shard_map/ppermute | solution.py:23
  57.0 11.9 %collective-permute-start.12 = (bf16[128,512]{1,0:T(8,128)(2,1)S(1)}, bf16[128,512]{1,0:T(8,128)(2,1)S(1)}, u32[]{:S(2)}, u32[]{:S(2)}) collective-permute-start(bf16[128,512]{1,0:T(8,128)(2,1)S(1)} %get-tuple-element.11.kv0), channel_id=1, source_target_pairs={{0,6},{1,7},{2,0},{3,1},{4,2},{5,3},{6,4},{7,5},{8,14},{9,15},{10,... | collective-permute-start | bytes 393224 | tf_op jit(solution)/shard_map/ppermute | solution.py:23
  59.4 11.0 %collective-permute-start.11 = (bf16[128,512]{1,0:T(8,128)(2,1)S(1)}, bf16[128,512]{1,0:T(8,128)(2,1)S(1)}, u32[]{:S(2)}, u32[]{:S(2)}) collective-permute-start(bf16[128,512]{1,0:T(8,128)(2,1)S(1)} %get-tuple-element.11.kv0), channel_id=1, source_target_pairs={{0,2},{1,3},{2,4},{3,5},{4,6},{5,7},{6,0},{7,1},{8,10},{9,11},{10,... | collective-permute-start | bytes 393224 | tf_op jit(solution)/shard_map/ppermute | solution.py:23
  59.9 10.6 %collective-permute-start.10 = (bf16[128,512]{1,0:T(8,128)(2,1)S(1)}, bf16[128,512]{1,0:T(8,128)(2,1)S(1)}, u32[]{:S(2)}, u32[]{:S(2)}) collective-permute-start(bf16[128,512]{1,0:T(8,128)(2,1)S(1)} %get-tuple-element.11.kv0), channel_id=1, source_target_pairs={{0,5},{1,6},{2,7},{3,0},{4,1},{5,2},{6,3},{7,4},{8,13},{9,14},{10,... | collective-permute-start | bytes 393224 | tf_op jit(solution)/shard_map/ppermute | solution.py:23
  62.8 16.3 %collective-permute-start.9 = (bf16[128,512]{1,0:T(8,128)(2,1)S(1)}, bf16[128,512]{1,0:T(8,128)(2,1)S(1)}, u32[]{:S(2)}, u32[]{:S(2)}) collective-permute-start(bf16[128,512]{1,0:T(8,128)(2,1)S(1)} %get-tuple-element.11.kv0), channel_id=1, source_target_pairs={{0,3},{1,4},{2,5},{3,6},{4,7},{5,0},{6,1},{7,2},{8,11},{9,12},{10,... | collective-permute-start | bytes 393224 | tf_op jit(solution)/shard_map/ppermute | solution.py:23
  63.7 16.8 %collective-permute-start.8 = (bf16[128,512]{1,0:T(8,128)(2,1)S(1)}, bf16[128,512]{1,0:T(8,128)(2,1)S(1)}, u32[]{:S(2)}, u32[]{:S(2)}) collective-permute-start(bf16[128,512]{1,0:T(8,128)(2,1)S(1)} %get-tuple-element.11.kv0), channel_id=1, source_target_pairs={{0,4},{1,5},{2,6},{3,7},{4,0},{5,1},{6,2},{7,3},{8,12},{9,13},{10,... | collective-permute-start | bytes 393224 | tf_op jit(solution)/shard_map/ppermute | solution.py:23
  81.2 0.9 copy-start.10
  82.1 0.9 copy-start.12
  83.0 0.9 copy-start.14
  83.9 0.9 copy-start.16
  101.3 1.4 copy-start.1
  105.2 44.3 %all-to-all-start = ((bf16[4,256,1024]{2,1,0:T(8,128)(2,1)}), bf16[4,256,1024]{2,1,0:T(8,128)(2,1)}, u32[]{:S(2)}, u32[]{:S(2)}) async-start(bf16[4,256,1024]{2,1,0:T(8,128)(2,1)} %md.1), calls=%async_computation | async-start | bytes 4194304 | tf_op jit(solution)/shard_map/all_to_all | solution.py:186
  149.5 11.1 %all-to-all-start.1 = ((bf16[4,32,1024]{2,1,0:T(8,128)(2,1)}), bf16[4,32,1024]{2,1,0:T(8,128)(2,1)S(1)}, u32[]{:S(2)}, u32[]{:S(2)}) async-start(bf16[4,32,1024]{2,1,0:T(8,128)(2,1)} %bitcast.11), calls=%async_computation.2 | async-start | bytes 524288 | tf_op jit(solution)/shard_map/all_to_all | solution.py:192
  153.9 14.2 %copy-start.17 = (bf16[1,128,1024]{2,1,0:T(8,128)(2,1)S(1)}, bf16[1,128,1024]{2,1,0:T(8,128)(2,1)}, u32[]{:S(2)}) copy-start(bf16[1,128,1024]{2,1,0:T(8,128)(2,1)} %param.15) | copy-start | bytes 786436
  153.9 14.2 %copy-start.18 = (bf16[1,128,1024]{2,1,0:T(8,128)(2,1)S(1)}, bf16[1,128,1024]{2,1,0:T(8,128)(2,1)}, u32[]{:S(2)}) copy-start(bf16[1,128,1024]{2,1,0:T(8,128)(2,1)} %param.8) | copy-start | bytes 786436
  160.6 13.9 %all-to-all-start.2 = ((bf16[32,4,1280]{2,1,0:T(4,128)(2,1)}), bf16[32,4,1280]{2,1,0:T(4,128)(2,1)S(1)}, u32[]{:S(2)}, u32[]{:S(2)}) async-start(bf16[32,4,1280]{2,1,0:T(4,128)(2,1)} %pad_maximum_fusion), calls=%async_computation.3 | async-start | bytes 655360 | tf_op jit(solution)/shard_map/all_to_all | solution.py:200
  (7 other events, 4.7 us)
Sparse Core Ops, SparseCore 0:
  10.3 40.1 all-gather.2
  102.9 42.3 reduce-scatter.1

commit v2 on v1

v2 whole, which is shorter than its diff:
```python
import jax
import jax.numpy as jnp
from jax import lax
from jax.experimental import pallas as pl
from jax.experimental.pallas import tpu as pltpu
from jax.sharding import Mesh, PartitionSpec as P

BF = jnp.bfloat16
F32 = jnp.float32
SHIFTS = (0, 1, -1, 2)
SIZES = {"y": 4, "c": 2, "x": 4, "z": 8}


def dot(a, b, da, db):
    return lax.dot_general(a, b, (((da,), (db,)), ((), ())), preferred_element_type=F32)


def shift(value, axis, by):
    n = SIZES[axis]
    return lax.ppermute(value, axis, [(i, (i + by) % n) for i in range(n)])


def mod(a, n):
    return lax.rem(a + n, n)


def pack_kernel(tok, cot, pattern, out):
    out[0:128, :] = tok[...]
    out[128:256, :] = cot[...]
    block = lax.broadcasted_iota(jnp.int32, (16, 1024), 0)
    key = lax.broadcasted_iota(jnp.int32, (16, 1024), 1)
    grow = jnp.where(block == 4 * ((key // 32) % 4) + key // 256, 1.0, 0.0).astype(BF)
    rows = jnp.where(pattern[...] == 1, 1.0, 0.0).astype(BF)
    rows = jnp.concatenate([rows, jnp.zeros((14, 16), BF)], axis=0)
    out[256:272, :] = dot(rows, grow, 1, 0).astype(BF)


def kv_kernel(pos, c0, c1, c2, c3, wa, wb, kv_out, w_out, ctx, sems):
    y, c, x = pos[0], pos[1], pos[2]
    copies = []
    for src, by in zip((c0, c1, c2, c3), SHIFTS):
        at = pl.multiple_of(32 * mod(x - by, 4), 32)
        copies.append((src, ctx.at[pl.ds(at, 32), :]))
    for half, core in ((wa, c), (wb, 1 - c)):
        for slot, by in enumerate(SHIFTS):
            at = pl.multiple_of(128 * (2 * mod(y - by, 4) + core), 128)
            copies.append((half.at[pl.ds(128 * slot, 128), :], w_out.at[pl.ds(at, 128), :]))
    copies = [pltpu.make_async_copy(a, b, sems.at[i]) for i, (a, b) in enumerate(copies)]
    for copy in copies:
        copy.start()
    for copy in copies:
        copy.wait()
    kv = dot(ctx[...], w_out[...], 1, 0).astype(BF)
    for zd in range(8):
        kv_out[zd] = kv


def qd_kernel(pos, xg, wa, wb, q_out, da_out, wq_out, wo_out, sems):
    y, c = pos[0], pos[1]
    copies = []
    for half, core in ((wa, c), (wb, 1 - c)):
        for slot, by in enumerate(SHIFTS):
            at = pl.multiple_of(128 * (2 * mod(y - by, 4) + core), 128)
            copies.append(
                (half.at[pl.ds(128 * slot, 128), 0:256], wq_out.at[pl.ds(at, 128), :])
            )
            at = pl.multiple_of(128 * core, 128)
            copies.append(
                (
                    half.at[pl.ds(128 * slot, 128), 256:512],
                    wo_out.at[pl.ds(at, 128), 256 * slot : 256 * slot + 256],
                )
            )
    copies = [pltpu.make_async_copy(a, b, sems.at[i]) for i, (a, b) in enumerate(copies)]
    for copy in copies:
        copy.start()
    for copy in copies:
        copy.wait()
    for t in range(4):
        rows = slice(128 * t, 128 * t + 128)
        q = dot(xg[t, 0:128, :], wq_out[...], 1, 0).astype(BF)
        q_out[rows, :] = q * jnp.asarray(0.125, BF)
        da_out[rows, :] = dot(xg[t, 128:256, :], wo_out[...], 1, 1).astype(BF)


def attn_kernel(xg, q_s, da_s, kv, pay, att_out, dq_out,
                kt_s, vt_s, dk_s, dv_s, at_s, dqt_s, gq_s, go_s, pay_s, mask_s, x_s, sems):
    mask_copies = [
        pltpu.make_async_copy(xg.at[t, pl.ds(256, 16), :], mask_s.at[t], sems.at[t])
        for t in range(4)
    ]
    x_copies = [
        pltpu.make_async_copy(xg.at[t, pl.ds(0, 256), :], x_s.at[t], sems.at[4 + t])
        for t in range(4)
    ]
    for copy in mask_copies + x_copies:
        copy.start()
    kt_s[...] = kv[:, 0:256].T
    vt_s[...] = kv[:, 256:512].T
    dk_s[...] = jnp.zeros_like(dk_s)
    dv_s[...] = jnp.zeros_like(dv_s)
    for copy in mask_copies:
        copy.wait()
    lane = lax.broadcasted_iota(jnp.int32, (256, 128), 1) // 64
    row16 = lax.broadcasted_iota(jnp.int32, (16, 128), 0)
    col16 = lax.broadcasted_iota(jnp.int32, (16, 128), 1) // 64
    pick = jnp.where(row16 == col16, 1.0, 0.0).astype(BF)
    for u in range(2):
        allowed = jnp.concatenate(
            [dot(mask_s[2 * u + s], pick, 0, 0) for s in range(2)], axis=1
        ) > 0.5
        for h in range(4):
            pair = slice(128 * (h // 2), 128 * (h // 2) + 128)
            vpair = slice(256 + 128 * (h // 2), 384 + 128 * (h // 2))
            head = slice(64 * h, 64 * h + 64)
            qrows = slice(256 * u, 256 * u + 256)
            own = lane == (h % 2)
            zero = jnp.zeros((256, 128), BF)
            qm = jnp.where(own, q_s[qrows, pair], zero)
            dam = jnp.where(own, da_s[qrows, pair], zero)
            s = jnp.where(allowed, dot(kv[:, pair], qm, 1, 1), -jnp.inf)
            e = jnp.exp(s - jnp.max(s, axis=0, keepdims=True))
            p = e * (1.0 / jnp.sum(e, axis=0, keepdims=True))
            plow = p.astype(BF)
            at_s[head, qrows] = dot(vt_s[head, :], plow, 1, 0).astype(BF)
            dv_s[:, pair] += dot(plow, dam, 1, 0)
            dp = dot(kv[:, vpair], dam, 1, 1)
            delta = jnp.sum(p * dp, axis=0, keepdims=True)
            ds = (p * (dp - delta)).astype(BF)
            dqt_s[head, qrows] = (0.125 * dot(kt_s[head, :], ds, 1, 0)).astype(BF)
            dk_s[:, pair] += dot(ds, qm, 1, 0)
    for copy in x_copies:
        copy.wait()
    go = jnp.zeros((256, 1024), F32)
    gq = jnp.zeros((256, 1024), F32)
    for t in range(4):
        rows = slice(128 * t, 128 * t + 128)
        go += dot(at_s[:, rows], x_s[t, 128:256, :], 1, 0)
        gq += dot(dqt_s[:, rows], x_s[t, 0:128, :], 1, 0)
    for j in range(8):
        go_s[j] = go[:, 128 * j : 128 * j + 128]
    for j in range(2):
        gq_s[j] = gq[128 * j : 128 * j + 128, :].T
    outs = []
    for zd in range(8):
        block = slice(128 * zd, 128 * zd + 128)
        pay_s[block, 0:256] = dk_s[block, :].astype(BF)
        pay_s[block, 256:512] = dv_s[block, :].astype(BF)
        for b in range(4):
            rows = slice(128 * zd + 32 * b, 128 * zd + 32 * b + 32)
            for j in range(2):
                lanes = slice(512 + 128 * j, 640 + 128 * j)
                pay_s[rows, lanes] = gq_s[j, pl.ds(4 * zd + b, 32, stride=32), :].astype(BF)
                part = [go_s[2 * b + j, pl.ds(4 * zd + i, 8, stride=32), :] for i in range(4)]
                lanes = slice(768 + 128 * j, 896 + 128 * j)
                pay_s[rows, lanes] = jnp.concatenate(part, axis=0).astype(BF)
        outs.append(pltpu.make_async_copy(pay_s.at[block, :], pay.at[block, :], sems.at[8 + zd]))
        outs[-1].start()
    att_out[...] = at_s[...].T
    dq_out[...] = dqt_s[...].T
    for copy in outs:
        copy.wait()


def md_kernel(att, dq, wq, wo, out):
    for t in range(4):
        rows = slice(128 * t, 128 * t + 128)
        out[t, 0:128, :] = dot(att[rows, :], wo[...], 1, 0).astype(BF)
        out[t, 128:256, :] = dot(dq[rows, :], wq[...], 1, 1).astype(BF)


def split_kernel(pos, red, w, p0, p1, p2, p3, g_out, part, g_s):
    x = pos[2]
    part[...] = dot(red[:, 0:256], w[:, 0:256], 1, 1) + dot(red[:, 256:512], w[:, 256:512], 1, 1)
    for out, by in zip((p0, p1, p2, p3), SHIFTS):
        at = pl.multiple_of(32 * mod(x + by, 4), 32)
        out[...] = part[pl.ds(at, 32), :].astype(BF)
    g_s[...] = jnp.zeros_like(g_s)
    for i in range(4):
        for j in range(2):
            lanes = slice(512 + 128 * j, 640 + 128 * j)
            rows = slice(32 * i, 32 * i + 32)
            g_s[pl.ds(2 * i + j, 32, stride=40), :] = red[rows, lanes].astype(F32)
    for b in range(4):
        for j in range(2):
            block = red[32 * b : 32 * b + 32, 768 + 128 * j : 896 + 128 * j].astype(F32)
            for i in range(4):
                at = 320 * x + 8 + 8 * i + 2 * b + j
                g_s[pl.ds(at, 8, stride=40), :] = block[8 * i : 8 * i + 8, :]
    g_out[...] = g_s[...].astype(BF)


def finish_kernel(g, p0, p1, p2, p3, dctx, g_query, g_out):
    total = p0[...].astype(F32)
    for p in (p1, p2, p3):
        total += p[...].astype(F32)
    dctx[...] = total.astype(BF)
    for xs in range(4):
        acc = jnp.zeros((8, 128), F32)
        for yc in range(8):
            at = 40 * (4 * yc + xs)
            acc += g[at : at + 8, :].astype(F32)
        for i in range(4):
            for j in range(2):
                row = 2 * i + j
                lanes = slice(256 * xs + 128 * j, 256 * xs + 128 * j + 128)
                g_query[i : i + 1, lanes] = acc[row : row + 1, :]
    acc = jnp.zeros((32, 128), F32)
    for src in range(32):
        acc += g[40 * src + 8 : 40 * src + 40, :].astype(F32)
    for i in range(4):
        for m in range(8):
            row = 8 * i + m
            g_out[i : i + 1, 128 * m : 128 * m + 128] = acc[row : row + 1, :]


V = pl.BlockSpec(memory_space=pltpu.VMEM)
S = pl.BlockSpec(memory_space=pltpu.SMEM)
A = pl.BlockSpec(memory_space=pl.ANY)


def sds(shape, dtype=BF):
    return jax.ShapeDtypeStruct(shape, dtype)


def call(kernel, in_specs, outs, scratch, mflop, kib, limit, name, out_specs=None):
    return pl.pallas_call(
        kernel,
        out_shape=outs,
        in_specs=in_specs,
        out_specs=out_specs or [V] * len(outs),
        scratch_shapes=scratch,
        compiler_params=pltpu.CompilerParams(vmem_limit_bytes=limit * 2**20),
        cost_estimate=pl.CostEstimate(
            flops=mflop * 10**6, bytes_accessed=kib * 1024, transcendentals=0
        ),
        name=name,
    )


def local(tokens, context, pattern, w_query, w_key, w_value, w_out, cotangent):
    y, c, x, z = (lax.axis_index(n) for n in ("y", "c", "x", "z"))
    pos = jnp.stack([y, c, x, z]).astype(jnp.int32)
    tok, ctx, cot = tokens[0], context[0], cotangent[0]
    (own,) = call(pack_kernel, [V, V, V], [sds((272, 1024))], [], 1, 1100, 8, "pack")(
        tok, cot, pattern[0]
    )
    xg = lax.all_gather(own, "x", axis=0, tiled=False)

    col = 256 * x
    cut = lambda w: lax.dynamic_slice(w, (0, col), (128, 256))
    mine = jnp.concatenate([cut(w_key), cut(w_value)], axis=1)
    wa = jnp.concatenate([mine] + [shift(mine, "y", by) for by in SHIFTS[1:]], axis=0)
    wb = shift(wa, "c", 1)
    ctxs = [ctx] + [shift(ctx, "x", by) for by in SHIFTS[1:]]
    kv8, wkv = call(
        kv_kernel, [S] + [A] * 6, [sds((8, 128, 512)), sds((1024, 512))],
        [pltpu.VMEM((128, 1024), BF), pltpu.SemaphoreType.DMA((12,))], 134, 3000, 16, "kv",
    )(pos, *ctxs, wa, wb)
    kvg = lax.all_to_all(kv8, "z", split_axis=0, concat_axis=0, tiled=True).reshape(1024, 512)

    w_query, w_out, kv8 = lax.optimization_barrier((w_query, w_out, kv8))
    mine = cut(w_query)
    wo = lax.ppermute(
        w_out, ("y", "x"), [(a * 4 + b, b * 4 + a) for a in range(4) for b in range(4)]
    )
    wo4 = jnp.concatenate([wo[:, 256 * j : 256 * j + 256] for j in range(4)], axis=0)
    wq4 = jnp.concatenate([mine] + [shift(mine, "y", by) for by in SHIFTS[1:]], axis=0)
    wa = jnp.concatenate([wq4, wo4], axis=1)
    wb = shift(wa, "c", 1)
    q, da, wq, wo = call(
        qd_kernel, [S, V, A, A],
        [sds((512, 256)), sds((512, 256)), sds((1024, 256)), sds((256, 1024))],
        [pltpu.SemaphoreType.DMA((16,))], 540, 5000, 24, "queries",
    )(pos, xg, wa, wb)

    pay, att, dq = call(
        attn_kernel, [A, V, V, V],
        [sds((1024, 1024)), sds((512, 256)), sds((512, 256))],
        [pltpu.VMEM((256, 1024), BF), pltpu.VMEM((256, 1024), BF),
         pltpu.VMEM((1024, 256), F32), pltpu.VMEM((1024, 256), F32),
         pltpu.VMEM((256, 512), BF), pltpu.VMEM((256, 512), BF),
         pltpu.VMEM((2, 1024, 128), F32), pltpu.VMEM((8, 256, 128), F32),
         pltpu.VMEM((1024, 1024), BF), pltpu.VMEM((4, 16, 1024), BF),
         pltpu.VMEM((4, 256, 1024), BF), pltpu.SemaphoreType.DMA((16,))],
        2200, 8000, 48, "attention", [A, V, V],
    )(xg, q, da, kvg)

    red = lax.psum_scatter(pay, "z", scatter_dimension=0, tiled=True)
    (md,) = call(md_kernel, [V] * 4, [sds((4, 256, 1024))], [], 540, 4000, 16, "md")(
        att, dq, wq, wo
    )
    md = lax.all_to_all(md, "x", split_axis=0, concat_axis=0, tiled=True)
    md = jnp.sum(md.astype(F32), axis=0)
    mixed = (tok.astype(F32) + md[0:128]).astype(BF)
    d_tokens = (cot.astype(F32) + md[128:256]).astype(BF)
    red, mixed, d_tokens = lax.optimization_barrier((red, mixed, d_tokens))

    *parts, g = call(
        split_kernel, [S, V, V], [sds((32, 1024))] * 4 + [sds((1280, 128))],
        [pltpu.VMEM((128, 1024), F32), pltpu.VMEM((1280, 128), F32)], 134, 2000, 16, "split",
    )(pos, red, wkv)
    parts = [parts[0]] + [shift(p, "x", by) for p, by in zip(parts[1:], SHIFTS[1:])]
    g = lax.all_to_all(
        g.reshape(32, 40, 128), ("y", "c", "x"), split_axis=0, concat_axis=0, tiled=True
    ).reshape(1280, 128)
    d_context, g_query, g_out = call(
        finish_kernel, [V] * 5, [sds((32, 1024)), sds((4, 1024), F32), sds((4, 1024), F32)],
        [], 1, 700, 8, "finish",
    )(g, *parts)
    return mixed[None], d_tokens[None], d_context[None], g_query, g_out


def solution(mesh):
    fine = Mesh(mesh.devices.reshape(4, 2, 4, 8), ("y", "c", "x", "z"))
    seq = P(("y", "c"), ("x", "z"), None)
    wts = P(("y", "c"), None)
    grad = P(("y", "c", "x", "z"), None)
    return jax.shard_map(
        local,
        mesh=fine,
        in_specs=(seq, seq, seq, wts, wts, wts, wts, seq),
        out_specs=(seq, seq, seq, grad, grad),
        check_vma=False,
    )
```

time: 186 us -> 163 us (0.88); the launches traced: 183 us -> 162 us
  waiting for transfers between devices: 79 us -> 37.2 us
  blocking collectives: 0 us -> 29.4 us
  other arithmetic: 9.1 us -> 1.47 us
  Pallas kernels: 20 us -> 27.1 us
  starting transfers between devices: 42.2 us -> 38.6 us
  matrix products: 2.99 us -> 0 us
    all_to_all x0 -> x1, blocking collectives: none -> 29.4 us  [local(): md = lax.all_to_all(md, 'x', split_axis=0, concat_axis=0, tiled=True)]
    reduce_scatter x1, waiting for transfers between devices: 35.4 us -> 8.48 us  [local(): red = lax.psum_scatter(pay, 'z', scatter_dimension=0, tiled=True)]
    all_to_all x3 -> x2, waiting for transfers between devices: 10.5 us -> 0.01 us  [the longest x1 0.01 us: local(): lax.all_to_all(kv8, 'z', split_axis=0, concat_axis=0, tiled=True)]
    pallas_call x3 -> x7, Pallas kernels: 20 us -> 27.1 us  [the longest x1 16.6 us: local(): call(attn_kernel, [A, V, V, V], [sds((1024, 1024)), sds((512, 256)), sds(...]
    ppermute x14, waiting for transfers between devices: 28 us -> 22.6 us  [shift(): return lax.ppermute(value, axis, [(i, (i + by) % n) for i in range(n)])]
    ppermute x14, starting transfers between devices: 24.6 us -> 19.2 us  [shift(): return lax.ppermute(value, axis, [(i, (i + by) % n) for i in range(n)])]
    dot_general x2 -> x0, matrix products: 2.99 us -> none  [dot(): lax.dot_general(a, b, (((da,), (db,)), ((), ())), preferred_element_type=...]
    concatenate x4 -> x3, other arithmetic: 3.02 us -> 0.08 us  [the longest x1 0.03 us: local(): jnp.concatenate([mine] + [shift(mine, 'y', by) for by in SHIFTS[1:]], axi...]
  transfers between devices with their start and end apart: 20 -> 19, of which waited for: 12 -> 12; matrix products, arithmetic and copies ran while one was open for 6% -> 1% of each run, Pallas kernels for 2% -> 4%
where the time goes in v2:
time: 163 us; the launch traced here: 162 us
  starting transfers between devices  38.6 us (24%)
  waiting for transfers between devices  37.2 us (23%)
  blocking collectives  29.4 us (18%)
  Pallas kernels  27.1 us (17%)
  between operations  14.2 us (9%)
  local copies, waits for them, and re-layouts  13.7 us (8%)
    all_to_all x1, blocking collectives, local(): md = lax.all_to_all(md, 'x', split_axis=0, concat_axis=0, tiled=True)  29.4 us
    ppermute x14, waiting for transfers between devices, shift(): return lax.ppermute(value, axis, [(i, (i + by) % n) for i in range(n)])  22.6 us
    ppermute x14, starting transfers between devices, shift(): return lax.ppermute(value, axis, [(i, (i + by) % n) for i in range(n)])  19.2 us
    pallas_call x1, Pallas kernels, local(): call(attn_kernel, [A, V, V, V], [sds((1024, 1024)), sds((512, 256)), sds(...  16.6 us
    unnamed x36, local copies, waits for them, and re-layouts  12.8 us
    all_to_all x1, starting transfers between devices, local(): lax.all_to_all(kv8, 'z', split_axis=0, concat_axis=0, tiled=True)  9.01 us
    reduce_scatter x1, waiting for transfers between devices, local(): red = lax.psum_scatter(pay, 'z', scatter_dimension=0, tiled=True)  8.48 us
    all_to_all x1, starting transfers between devices, local(): lax.all_to_all(g.reshape(32, 40, 128), ('y', 'c', 'x'), split_axis=0, con...  7.38 us
  transfers between devices with their start and end apart: 19, of which 12 were waited for; matrix products, arithmetic and copies ran while one was open for 1% of the time, Pallas kernels for 4%

profile of v2, /device:TPU:8, one launch (start us, length us, event | category | flops | bytes accessed | tf_op | source)
XLA Modules:
  0.0 161.8 jit_solution(12246920026976255493)
XLA Ops:
  7.2 1.0 copy-done.2
  11.7 2.4 %collective-permute-start.5 = (bf16[128,512]{1,0:T(8,128)(2,1)S(1)}, bf16[128,512]{1,0:T(8,128)(2,1)S(1)}, u32[]{:S(2)}, u32[]{:S(2)}) collective-permute-start(bf16[128,512]{1,0:T(8,128)(2,1)S(1)} %pad_maximum_fusion.1), channel_id=1, source_target_pairs={{0,128},{64,192},{128,0},{192,64},{1,129},{65,193},{129,1},{193,65... | collective-permute-start | bytes 393224 | tf_op jit(solution)/shard_map/ppermute | solution.py:20
  14.1 1.3 collective-permute-start.4
  16.1 3.6 %collective-permute-done.5 = bf16[128,512]{1,0:T(8,128)(2,1)S(1)} collective-permute-done((bf16[128,512]{1,0:T(8,128)(2,1)S(1)}, bf16[128,512]{1,0:T(8,128)(2,1)S(1)}, u32[]{:S(2)}, u32[]{:S(2)}) %collective-permute-start.5) | collective-permute-done | bytes 131104 | tf_op jit(solution)/shard_map/ppermute | solution.py:20
  19.7 1.7 %collective-permute-done.4 = bf16[128,512]{1,0:T(8,128)(2,1)S(1)} collective-permute-done((bf16[128,512]{1,0:T(8,128)(2,1)S(1)}, bf16[128,512]{1,0:T(8,128)(2,1)S(1)}, u32[]{:S(2)}, u32[]{:S(2)}) %collective-permute-start.4) | collective-permute-done | bytes 131104 | tf_op jit(solution)/shard_map/ppermute | solution.py:20
  21.6 3.1 %collective-permute-start.2 = (bf16[32,1024]{1,0:T(8,128)(2,1)S(1)}, bf16[32,1024]{1,0:T(8,128)(2,1)S(1)}, u32[]{:S(2)}, u32[]{:S(2)}) collective-permute-start(bf16[32,1024]{1,0:T(8,128)(2,1)S(1)} %bitcast.23), channel_id=1, source_target_pairs={{0,16},{8,24},{16,0},{24,8},{1,17},{9,25},{17,1},{25,9},{2,18},{10... | collective-permute-start | bytes 196616 | tf_op jit(solution)/shard_map/ppermute | solution.py:20
  24.7 1.1 collective-permute-start.1
  27.7 1.7 %collective-permute-done.1.c2 = bf16[32,1024]{1,0:T(8,128)(2,1)S(1)} collective-permute-done((bf16[32,1024]{1,0:T(8,128)(2,1)S(1)}, bf16[32,1024]{1,0:T(8,128)(2,1)S(1)}, u32[]{:S(2)}, u32[]{:S(2)}) %collective-permute-start.1) | collective-permute-done | bytes 65568 | tf_op jit(solution)/shard_map/ppermute | solution.py:20
  29.4 3.1 %collective-permute-done.c1 = bf16[32,1024]{1,0:T(8,128)(2,1)S(1)} collective-permute-done((bf16[32,1024]{1,0:T(8,128)(2,1)S(1)}, bf16[32,1024]{1,0:T(8,128)(2,1)S(1)}, u32[]{:S(2)}, u32[]{:S(2)}) %collective-permute-start) | collective-permute-done | bytes 65568 | tf_op jit(solution)/shard_map/ppermute | solution.py:20
  32.4 3.9 %kv.1 = (bf16[8,128,512]{2,1,0:T(8,128)(2,1)}, bf16[1024,512]{1,0:T(8,128)(2,1)S(1)}) custom-call(s32[4]{0:T(128)S(1)} %pad_add_fusion.pos, bf16[32,1024]{1,0:T(8,128)(2,1)S(1)} %bitcast.26, bf16[32,1024]{1,0:T(8,128)(2,1)S(1)} %collective-permute-done.c1, bf16[32,1024]{1,0:T(8,128)(2,1)S(1)} %collective-permute-done.1.c2, ...), custom_call_target="tpu_custom_call" | custom-call | flops 134000000 | bytes 3072000 | tf_op jit(solution)/shard_map/kv/pallas_call | solution.py:256
  36.3 9.0 %all-to-all-start = ((bf16[8,128,512]{2,1,0:T(8,128)(2,1)}), bf16[8,128,512]{2,1,0:T(8,128)(2,1)S(1)}, u32[]{:S(2)}, u32[]{:S(2)}) async-start(bf16[8,128,512]{2,1,0:T(8,128)(2,1)} %get-tuple-element.27), calls=%async_computation | async-start | bytes 2097152 | tf_op jit(solution)/shard_map/all_to_all | solution.py:260
  45.4 2.9 %collective-permute-start.10 = (bf16[128,1024]{1,0:T(8,128)(2,1)S(1)}, bf16[128,1024]{1,0:T(8,128)(2,1)S(1)}, u32[]{:S(2)}, u32[]{:S(2)}) collective-permute-start(bf16[128,1024]{1,0:T(8,128)(2,1)S(1)} %copy-done.17), channel_id=1, source_target_pairs={{0,0},{8,64},{16,128},{24,192},{64,8},{72,72},{80,136},{88,200},{1... | collective-permute-start | bytes 786440 | tf_op jit(solution)/shard_map/ppermute | solution.py:264
  48.4 2.4 %collective-permute-start.9 = (bf16[128,256]{1,0:T(8,128)(2,1)S(1)}, bf16[128,256]{1,0:T(8,128)(2,1)S(1)}, u32[]{:S(2)}, u32[]{:S(2)}) collective-permute-start(bf16[128,256]{1,0:T(8,128)(2,1)S(1)} %constant_dynamic-slice_fusion), channel_id=1, source_target_pairs={{0,128},{64,192},{128,0},{192,64},{1,129},{65,193},{129,1},{193,65... | collective-permute-start | bytes 196616 | tf_op jit(solution)/shard_map/ppermute | solution.py:20
  50.7 1.8 %collective-permute-start.8 = (bf16[128,256]{1,0:T(8,128)(2,1)S(1)}, bf16[128,256]{1,0:T(8,128)(2,1)S(1)}, u32[]{:S(2)}, u32[]{:S(2)}) collective-permute-start(bf16[128,256]{1,0:T(8,128)(2,1)S(1)} %constant_dynamic-slice_fusion), channel_id=1, source_target_pairs={{0,192},{64,0},{128,64},{192,128},{1,193},{65,1},{129,65},{193,129... | collective-permute-start | bytes 196616 | tf_op jit(solution)/shard_map/ppermute | solution.py:20
  52.8 6.1 %collective-permute-done.10 = bf16[128,1024]{1,0:T(8,128)(2,1)S(1)} collective-permute-done((bf16[128,1024]{1,0:T(8,128)(2,1)S(1)}, bf16[128,1024]{1,0:T(8,128)(2,1)S(1)}, u32[]{:S(2)}, u32[]{:S(2)}) %collective-permute-start.10) | collective-permute-done | bytes 262176 | tf_op jit(solution)/shard_map/ppermute | solution.py:264
  58.9 4.5 %collective-permute-done.7 = bf16[128,256]{1,0:T(8,128)(2,1)S(1)} collective-permute-done((bf16[128,256]{1,0:T(8,128)(2,1)S(1)}, bf16[128,256]{1,0:T(8,128)(2,1)S(1)}, u32[]{:S(2)}, u32[]{:S(2)}) %collective-permute-start.7) | collective-permute-done | bytes 65568 | tf_op jit(solution)/shard_map/ppermute | solution.py:20
  63.5 1.9 %collective-permute-done.11.wb = bf16[512,512]{1,0:T(8,128)(2,1)S(1)} collective-permute-done((bf16[512,512]{1,0:T(8,128)(2,1)S(1)}, bf16[512,512]{1,0:T(8,128)(2,1)S(1)}, u32[]{:S(2)}, u32[]{:S(2)}) %collective-permute-start.11) | collective-permute-done | bytes 524320 | tf_op jit(solution)/shard_map/ppermute | solution.py:20
  66.2 1.6 %copy-done.1 = bf16[1088,1024]{1,0:T(8,128)(2,1)S(1)} copy-done((bf16[1088,1024]{1,0:T(8,128)(2,1)S(1)}, bf16[1088,1024]{1,0:T(8,128)(2,1)}, u32[]{:S(2)}) %copy-start.1) | copy-done | bytes 2228248
  67.8 1.0 copy-done.9
  68.9 2.1 %queries.1 = (bf16[512,256]{1,0:T(8,128)(2,1)S(1)}, bf16[512,256]{1,0:T(8,128)(2,1)S(1)}, bf16[1024,256]{1,0:T(8,128)(2,1)S(1)}, bf16[256,1024]{1,0:T(8,128)(2,1)S(1)}) custom-call(s32[4]{0:T(128)S(1)} %pad_add_fusion.pos, bf16[4,272,1024]{2,1,0:T(8,128)(2,1)S(1)} %bitcast.18, bf16[512,512]{1,0:T(8,128)(2,1)S(1)} %maximum_maximum_fusion.wa, ...), custom_call_target="tpu_custom_call" | custom-call | flops 540000000 | bytes 5120000 | tf_op jit(solution)/shard_map/queries/pallas_call | solution.py:271
  75.1 16.6 %attention.1 = (bf16[1024,1024]{1,0:T(8,128)(2,1)}, bf16[512,256]{1,0:T(8,128)(2,1)S(1)}, bf16[512,256]{1,0:T(8,128)(2,1)S(1)}) custom-call(bf16[4,272,1024]{2,1,0:T(8,128)(2,1)} %bitcast.17, bf16[512,256]{1,0:T(8,128)(2,1)S(1)} %copy-done.14, bf16[512,256]{1,0:T(8,128)(2,1)S(1)} %copy-done.16, bf16[1024,512]{1,0:T(8,128)(2,1)S(1)} %bitcast.20), custom_call_target="tpu_custom_call" | custom-call | flops 2200000000 | bytes 8192000 | tf_op jit(solution)/shard_map/attention/pallas_call | solution.py:277
  91.7 1.0 copy-done.7
  92.7 1.1 md.1
  93.9 29.4 %all_to_all.15 = bf16[4,256,1024]{2,1,0:T(8,128)(2,1)S(1)} all-to-all(bf16[4,256,1024]{2,1,0:T(8,128)(2,1)S(1)} %md.1), channel_id=1, replica_groups=mesh['y'=4,'c'=2,'x'=4,'z'=8] {'x'}, dimensions={0} | all-to-all | bytes 4194304 | tf_op jit(solution)/shard_map/all_to_all | solution.py:293
  125.3 8.5 %reduce-scatter.2.cloned.1.call-done.red = bf16[128,1024]{1,0:T(8,128)(2,1)} async-done(((bf16[1024,1024]{1,0:T(8,128)(2,1)}), bf16[128,1024]{1,0:T(8,128)(2,1)}) %reduce-scatter.2.cloned.1.call-update) | async-done | bytes 262160 | tf_op jit(solution)/shard_map/reduce_scatter | solution.py:289
  134.7 1.8 %split.1 = (bf16[32,1024]{1,0:T(8,128)(2,1)S(1)}, bf16[32,1024]{1,0:T(8,128)(2,1)S(1)}, bf16[32,1024]{1,0:T(8,128)(2,1)S(1)}, bf16[32,1024]{1,0:T(8,128)(2,1)S(1)}, bf16[1280,128]{1,0:T(8,128)(2,1)}) custom-call(s32[4]{0:T(128)S(1)} %pad_add_fusion.pos, bf16[128,1024]{1,0:T(8,128)(2,1)S(1)} %copy-done.10, bf16[1024,512]{1,0:T(8,128)(2,1)S(1)} %get-tuple-element.40.w), custom_call_target="tpu_custom_call" | custom-call | flops 134000000 | bytes 2048000 | tf_op jit(solution)/shard_map/split/pallas_call | solution.py:299
  136.5 7.4 %all-to-all-start.2 = ((bf16[32,40,128]{2,1,0:T(8,128)(2,1)}), bf16[32,40,128]{2,1,0:T(8,128)(2,1)S(1)}, u32[]{:S(2)}, u32[]{:S(2)}) async-start(bf16[32,40,128]{2,1,0:T(8,128)(2,1)} %bitcast.12), calls=%async_computation.3 | async-start | bytes 655360 | tf_op jit(solution)/shard_map/all_to_all | solution.py:304
  143.9 1.5 collective-permute-start.12
  145.4 1.8 %collective-permute-start.13 = (bf16[32,1024]{1,0:T(8,128)(2,1)S(1)}, bf16[32,1024]{1,0:T(8,128)(2,1)S(1)}, u32[]{:S(2)}, u32[]{:S(2)}) collective-permute-start(bf16[32,1024]{1,0:T(8,128)(2,1)S(1)} %get-tuple-element.44), channel_id=1, source_target_pairs={{0,24},{8,0},{16,8},{24,16},{1,25},{9,1},{17,9},{25,17},{2,26},{10... | collective-permute-start | bytes 196616 | tf_op jit(solution)/shard_map/ppermute | solution.py:20
  147.2 1.8 %collective-permute-start.14 = (bf16[32,1024]{1,0:T(8,128)(2,1)S(1)}, bf16[32,1024]{1,0:T(8,128)(2,1)S(1)}, u32[]{:S(2)}, u32[]{:S(2)}) collective-permute-start(bf16[32,1024]{1,0:T(8,128)(2,1)S(1)} %get-tuple-element.45), channel_id=1, source_target_pairs={{0,16},{8,24},{16,0},{24,8},{1,17},{9,25},{17,1},{25,9},{2,18},{10... | collective-permute-start | bytes 196616 | tf_op jit(solution)/shard_map/ppermute | solution.py:20
  148.9 3.8 %collective-permute-done.12.p1 = bf16[32,1024]{1,0:T(8,128)(2,1)S(1)} collective-permute-done((bf16[32,1024]{1,0:T(8,128)(2,1)S(1)}, bf16[32,1024]{1,0:T(8,128)(2,1)S(1)}, u32[]{:S(2)}, u32[]{:S(2)}) %collective-permute-start.12) | collective-permute-done | bytes 65568 | tf_op jit(solution)/shard_map/ppermute | solution.py:20
  152.7 1.5 collective-permute-done.14.p3
  (61 shorter events, 15.2 us)
Async XLA Ops:
  7.2 41.1 %copy-start = (bf16[128,1024]{1,0:T(8,128)(2,1)S(1)}, bf16[128,1024]{1,0:T(8,128)(2,1)}, u32[]{:S(2)}) copy-start(bf16[128,1024]{1,0:T(8,128)(2,1)} %param.11) | copy-start | bytes 786436
  7.2 59.0 %all-gather.3.cloned.1.call-start = ((), (), s32[]{:S(2)}) async-start(), calls=%async_computation.5 | async-start | bytes 2785280 | tf_op jit(solution)/shard_map/all_gather | solution.py:248
  7.2 1.0 copy-start.2
  8.2 0.9 copy-start.4
  9.8 11.8 %copy-start.11 = (bf16[1,32,1024]{2,1,0:T(8,128)(2,1)S(1)}, bf16[1,32,1024]{2,1,0:T(8,128)(2,1)}, u32[]{:S(2)}) copy-start(bf16[1,32,1024]{2,1,0:T(8,128)(2,1)} %param.9) | copy-start | bytes 196612
  11.7 33.6 %copy-start.17 = (bf16[128,1024]{1,0:T(8,128)(2,1)S(1)}, bf16[128,1024]{1,0:T(8,128)(2,1)}, u32[]{:S(2)}) copy-start(bf16[128,1024]{1,0:T(8,128)(2,1)} %param.14) | copy-start | bytes 786436
  11.7 8.0 %collective-permute-start.5 = (bf16[128,512]{1,0:T(8,128)(2,1)S(1)}, bf16[128,512]{1,0:T(8,128)(2,1)S(1)}, u32[]{:S(2)}, u32[]{:S(2)}) collective-permute-start(bf16[128,512]{1,0:T(8,128)(2,1)S(1)} %pad_maximum_fusion.1), channel_id=1, source_target_pairs={{0,128},{64,192},{128,0},{192,64},{1,129},{65,193},{129,1},{193,65... | collective-permute-start | bytes 393224 | tf_op jit(solution)/shard_map/ppermute | solution.py:20
  14.1 7.3 %collective-permute-start.4 = (bf16[128,512]{1,0:T(8,128)(2,1)S(1)}, bf16[128,512]{1,0:T(8,128)(2,1)S(1)}, u32[]{:S(2)}, u32[]{:S(2)}) collective-permute-start(bf16[128,512]{1,0:T(8,128)(2,1)S(1)} %pad_maximum_fusion.1), channel_id=1, source_target_pairs={{0,192},{64,0},{128,64},{192,128},{1,193},{65,1},{129,65},{193,129... | collective-permute-start | bytes 393224 | tf_op jit(solution)/shard_map/ppermute | solution.py:20
  15.5 6.0 %collective-permute-start.3 = (bf16[128,512]{1,0:T(8,128)(2,1)S(1)}, bf16[128,512]{1,0:T(8,128)(2,1)S(1)}, u32[]{:S(2)}, u32[]{:S(2)}) collective-permute-start(bf16[128,512]{1,0:T(8,128)(2,1)S(1)} %pad_maximum_fusion.1), channel_id=1, source_target_pairs={{0,64},{64,128},{128,192},{192,0},{1,65},{65,129},{129,193},{193,1... | collective-permute-start | bytes 393224 | tf_op jit(solution)/shard_map/ppermute | solution.py:20
  21.5 10.9 %collective-permute-start.6 = (bf16[512,512]{1,0:T(8,128)(2,1)S(1)}, bf16[512,512]{1,0:T(8,128)(2,1)S(1)}, u32[]{:S(2)}, u32[]{:S(2)}) collective-permute-start(bf16[512,512]{1,0:T(8,128)(2,1)S(1)} %pad_maximum_fusion.wa), channel_id=1, source_target_pairs={{0,32},{32,0},{1,33},{33,1},{2,34},{34,2},{3,35},{35,3},{4,36},{36... | collective-permute-start | bytes 1572872 | tf_op jit(solution)/shard_map/ppermute | solution.py:20
  21.6 6.0 %collective-permute-start.2 = (bf16[32,1024]{1,0:T(8,128)(2,1)S(1)}, bf16[32,1024]{1,0:T(8,128)(2,1)S(1)}, u32[]{:S(2)}, u32[]{:S(2)}) collective-permute-start(bf16[32,1024]{1,0:T(8,128)(2,1)S(1)} %bitcast.23), channel_id=1, source_target_pairs={{0,16},{8,24},{16,0},{24,8},{1,17},{9,25},{17,1},{25,9},{2,18},{10... | collective-permute-start | bytes 196616 | tf_op jit(solution)/shard_map/ppermute | solution.py:20
  24.7 4.6 %collective-permute-start.1 = (bf16[32,1024]{1,0:T(8,128)(2,1)S(1)}, bf16[32,1024]{1,0:T(8,128)(2,1)S(1)}, u32[]{:S(2)}, u32[]{:S(2)}) collective-permute-start(bf16[32,1024]{1,0:T(8,128)(2,1)S(1)} %bitcast.24), channel_id=1, source_target_pairs={{0,24},{8,0},{16,8},{24,16},{1,25},{9,1},{17,9},{25,17},{2,26},{10... | collective-permute-start | bytes 196616 | tf_op jit(solution)/shard_map/ppermute | solution.py:20
  25.9 6.5 %collective-permute-start = (bf16[32,1024]{1,0:T(8,128)(2,1)S(1)}, bf16[32,1024]{1,0:T(8,128)(2,1)S(1)}, u32[]{:S(2)}, u32[]{:S(2)}) collective-permute-start(bf16[32,1024]{1,0:T(8,128)(2,1)S(1)} %bitcast.25), channel_id=1, source_target_pairs={{0,8},{8,16},{16,24},{24,0},{1,9},{9,17},{17,25},{25,1},{2,10},{10... | collective-permute-start | bytes 196616 | tf_op jit(solution)/shard_map/ppermute | solution.py:20
  36.3 36.9 %all-to-all-start = ((bf16[8,128,512]{2,1,0:T(8,128)(2,1)}), bf16[8,128,512]{2,1,0:T(8,128)(2,1)S(1)}, u32[]{:S(2)}, u32[]{:S(2)}) async-start(bf16[8,128,512]{2,1,0:T(8,128)(2,1)} %get-tuple-element.27), calls=%async_computation | async-start | bytes 2097152 | tf_op jit(solution)/shard_map/all_to_all | solution.py:260
  45.3 88.4 %reduce-scatter.2.cloned.1.call-start = ((), (), s32[]{:S(2)}) async-start(), calls=%async_computation.4 | async-start | bytes 2359296 | tf_op jit(solution)/shard_map/reduce_scatter | solution.py:289
  45.4 13.5 %collective-permute-start.10 = (bf16[128,1024]{1,0:T(8,128)(2,1)S(1)}, bf16[128,1024]{1,0:T(8,128)(2,1)S(1)}, u32[]{:S(2)}, u32[]{:S(2)}) collective-permute-start(bf16[128,1024]{1,0:T(8,128)(2,1)S(1)} %copy-done.17), channel_id=1, source_target_pairs={{0,0},{8,64},{16,128},{24,192},{64,8},{72,72},{80,136},{88,200},{1... | collective-permute-start | bytes 786440 | tf_op jit(solution)/shard_map/ppermute | solution.py:264
  48.4 10.5 %collective-permute-start.9 = (bf16[128,256]{1,0:T(8,128)(2,1)S(1)}, bf16[128,256]{1,0:T(8,128)(2,1)S(1)}, u32[]{:S(2)}, u32[]{:S(2)}) collective-permute-start(bf16[128,256]{1,0:T(8,128)(2,1)S(1)} %constant_dynamic-slice_fusion), channel_id=1, source_target_pairs={{0,128},{64,192},{128,0},{192,64},{1,129},{65,193},{129,1},{193,65... | collective-permute-start | bytes 196616 | tf_op jit(solution)/shard_map/ppermute | solution.py:20
  50.7 8.2 %collective-permute-start.8 = (bf16[128,256]{1,0:T(8,128)(2,1)S(1)}, bf16[128,256]{1,0:T(8,128)(2,1)S(1)}, u32[]{:S(2)}, u32[]{:S(2)}) collective-permute-start(bf16[128,256]{1,0:T(8,128)(2,1)S(1)} %constant_dynamic-slice_fusion), channel_id=1, source_target_pairs={{0,192},{64,0},{128,64},{192,128},{1,193},{65,1},{129,65},{193,129... | collective-permute-start | bytes 196616 | tf_op jit(solution)/shard_map/ppermute | solution.py:20
  52.6 10.8 %collective-permute-start.7 = (bf16[128,256]{1,0:T(8,128)(2,1)S(1)}, bf16[128,256]{1,0:T(8,128)(2,1)S(1)}, u32[]{:S(2)}, u32[]{:S(2)}) collective-permute-start(bf16[128,256]{1,0:T(8,128)(2,1)S(1)} %constant_dynamic-slice_fusion), channel_id=1, source_target_pairs={{0,64},{64,128},{128,192},{192,0},{1,65},{65,129},{129,193},{193,1... | collective-permute-start | bytes 196616 | tf_op jit(solution)/shard_map/ppermute | solution.py:20
  63.4 2.0 %collective-permute-start.11 = (bf16[512,512]{1,0:T(8,128)(2,1)S(1)}, bf16[512,512]{1,0:T(8,128)(2,1)S(1)}, u32[]{:S(2)}, u32[]{:S(2)}) collective-permute-start(bf16[512,512]{1,0:T(8,128)(2,1)S(1)} %maximum_maximum_fusion.wa), channel_id=1, source_target_pairs={{0,32},{32,0},{1,33},{33,1},{2,34},{34,2},{3,35},{35,3},{4,36},{36... | collective-permute-start | bytes 1572872 | tf_op jit(solution)/shard_map/ppermute | solution.py:20
  66.2 1.6 %copy-start.1 = (bf16[1088,1024]{1,0:T(8,128)(2,1)S(1)}, bf16[1088,1024]{1,0:T(8,128)(2,1)}, u32[]{:S(2)}) copy-start(bf16[1088,1024]{1,0:T(8,128)(2,1)} %all-gather.3.cloned.1.call-done) | copy-start | bytes 6684676
  67.8 1.0 copy-start.9
  73.2 1.0 copy-start.14
  74.1 0.9 copy-start.16
  91.7 1.0 copy-start.7
  123.3 1.0 copy-start.3
  123.3 1.0 copy-start.5
  133.7 0.9 copy-start.10
  136.5 17.8 %all-to-all-start.2 = ((bf16[32,40,128]{2,1,0:T(8,128)(2,1)}), bf16[32,40,128]{2,1,0:T(8,128)(2,1)S(1)}, u32[]{:S(2)}, u32[]{:S(2)}) async-start(bf16[32,40,128]{2,1,0:T(8,128)(2,1)} %bitcast.12), calls=%async_computation.3 | async-start | bytes 655360 | tf_op jit(solution)/shard_map/all_to_all | solution.py:304
  143.9 8.9 %collective-permute-start.12 = (bf16[32,1024]{1,0:T(8,128)(2,1)S(1)}, bf16[32,1024]{1,0:T(8,128)(2,1)S(1)}, u32[]{:S(2)}, u32[]{:S(2)}) collective-permute-start(bf16[32,1024]{1,0:T(8,128)(2,1)S(1)} %get-tuple-element.43), channel_id=1, source_target_pairs={{0,8},{8,16},{16,24},{24,0},{1,9},{9,17},{17,25},{25,1},{2,10},{10... | collective-permute-start | bytes 196616 | tf_op jit(solution)/shard_map/ppermute | solution.py:20
  145.4 7.3 %collective-permute-start.13 = (bf16[32,1024]{1,0:T(8,128)(2,1)S(1)}, bf16[32,1024]{1,0:T(8,128)(2,1)S(1)}, u32[]{:S(2)}, u32[]{:S(2)}) collective-permute-start(bf16[32,1024]{1,0:T(8,128)(2,1)S(1)} %get-tuple-element.44), channel_id=1, source_target_pairs={{0,24},{8,0},{16,8},{24,16},{1,25},{9,1},{17,9},{25,17},{2,26},{10... | collective-permute-start | bytes 196616 | tf_op jit(solution)/shard_map/ppermute | solution.py:20
  147.2 7.1 %collective-permute-start.14 = (bf16[32,1024]{1,0:T(8,128)(2,1)S(1)}, bf16[32,1024]{1,0:T(8,128)(2,1)S(1)}, u32[]{:S(2)}, u32[]{:S(2)}) collective-permute-start(bf16[32,1024]{1,0:T(8,128)(2,1)S(1)} %get-tuple-element.45), channel_id=1, source_target_pairs={{0,16},{8,24},{16,0},{24,8},{1,17},{9,25},{17,1},{25,9},{2,18},{10... | collective-permute-start | bytes 196616 | tf_op jit(solution)/shard_map/ppermute | solution.py:20
  (5 other events, 3.7 us)
Sparse Core Ops, SparseCore 0:
  10.9 38.2 all-gather.2
  91.9 41.8 reduce-scatter.1

commit v3 on v2

v3 whole, which is shorter than its diff:
```python
import jax
import jax.numpy as jnp
from jax import lax
from jax.experimental import pallas as pl
from jax.experimental.pallas import tpu as pltpu
from jax.sharding import Mesh, PartitionSpec as P

BF = jnp.bfloat16
F32 = jnp.float32
SHIFTS = (0, 1, -1, 2)
SIZES = {"y": 4, "c": 2, "x": 4, "z": 8}


def dot(a, b, da, db):
    return lax.dot_general(a, b, (((da,), (db,)), ((), ())), preferred_element_type=F32)


def shift(value, axis, by):
    n = SIZES[axis]
    return lax.ppermute(value, axis, [(i, (i + by) % n) for i in range(n)])


def mod(a, n):
    return lax.rem(a + n, n)


def run_copies(pairs, sems):
    copies = [pltpu.make_async_copy(a, b, sems.at[i]) for i, (a, b) in enumerate(pairs)]
    for copy in copies:
        copy.start()
    return copies


def wait_all(copies):
    for copy in copies:
        copy.wait()


def pack_kernel(pos, tok, cot, pattern, wk, wv, wq, out, kv_cut, q_cut, pat_s, mask_s, sems):
    cols = pl.ds(pl.multiple_of(256 * pos[2], 256), 256)
    copies = run_copies(
        [
            (pattern, pat_s),
            (wk.at[:, cols], kv_cut.at[:, pl.ds(0, 256)]),
            (wv.at[:, cols], kv_cut.at[:, pl.ds(256, 256)]),
            (tok, out.at[pl.ds(0, 128), :]),
            (cot, out.at[pl.ds(128, 128), :]),
            (wq.at[:, cols], q_cut),
        ],
        sems,
    )
    block = lax.broadcasted_iota(jnp.int32, (16, 1024), 0)
    key = lax.broadcasted_iota(jnp.int32, (16, 1024), 1)
    grow = jnp.where(block == 4 * ((key // 32) % 4) + key // 256, 1.0, 0.0).astype(BF)
    copies[0].wait()
    rows = jnp.where(pat_s[...] == 1, 1.0, 0.0).astype(BF)
    rows = jnp.concatenate([rows, jnp.zeros((14, 16), BF)], axis=0)
    mask_s[...] = dot(rows, grow, 1, 0).astype(BF)
    last = pltpu.make_async_copy(mask_s, out.at[pl.ds(256, 16), :], sems.at[6])
    last.start()
    wait_all(copies[1:] + [last])


def kv_kernel(pos, c0, c1, c2, c3, wa, wb, kv_out, w_out, ctx, kv_s, sems):
    y, c, x = pos[0], pos[1], pos[2]
    pairs = []
    for half, core in ((wa, c), (wb, 1 - c)):
        for slot, by in enumerate(SHIFTS):
            at = pl.multiple_of(128 * (2 * mod(y - by, 4) + core), 128)
            pairs.append((half.at[pl.ds(128 * slot, 128), :], w_out.at[pl.ds(at, 128), :]))
    for src, by in zip((c0, c1, c2, c3), SHIFTS):
        at = pl.multiple_of(32 * mod(x - by, 4), 32)
        pairs.append((src, ctx.at[pl.ds(at, 32), :]))
    wait_all(run_copies(pairs, sems))
    kv_s[...] = dot(ctx[...], w_out[...], 1, 0).astype(BF)
    wait_all(run_copies([(kv_s, kv_out.at[zd]) for zd in range(8)], sems))


def qd_kernel(pos, xg, wa, wb, qd_out, wq_out, wo_out, x_s, wq_s, wo_s, q_s, da_s, sems):
    y, c = pos[0], pos[1]
    pairs = []
    for half, core in ((wa, c), (wb, 1 - c)):
        for slot, by in enumerate(SHIFTS):
            rows = pl.ds(128 * slot, 128)
            at = pl.multiple_of(128 * (2 * mod(y - by, 4) + core), 128)
            pairs.append((half.at[rows, pl.ds(0, 256)], wq_s.at[pl.ds(at, 128), :]))
            at = pl.multiple_of(128 * core, 128)
            lanes = pl.ds(256 * slot, 256)
            pairs.append((half.at[rows, pl.ds(256, 256)], wo_s.at[pl.ds(at, 128), lanes]))
    for t in range(4):
        for k in range(2):
            rows = pl.ds(128 * t, 128)
            pairs.append((xg.at[t, pl.ds(128 * k, 128), :], x_s.at[k, rows, :]))
    wait_all(run_copies(pairs, sems))
    q = dot(x_s[0], wq_s[...], 1, 0).astype(BF)
    q_s[...] = q * jnp.asarray(0.125, BF)
    da_s[...] = dot(x_s[1], wo_s[...], 1, 1).astype(BF)
    pairs = [(q_s, qd_out.at[0]), (da_s, qd_out.at[1]), (wq_s, wq_out), (wo_s, wo_out)]
    wait_all(run_copies(pairs, sems))


def attn_kernel(xg, qd, kv, pay, att_out, dq_out, q_s, da_s,
                kt_s, vt_s, dk_s, dv_s, at_s, dqt_s, gq_s, go_s, pay_s, mask_s, x_s, sems):
    mask_copies = [
        pltpu.make_async_copy(xg.at[t, pl.ds(256, 16), :], mask_s.at[t], sems.at[t])
        for t in range(4)
    ]
    x_copies = [
        pltpu.make_async_copy(
            xg.at[t, pl.ds(128 * k, 128), :], x_s.at[k, pl.ds(128 * t, 128), :], sems.at[4 + 4 * k + t]
        )
        for t in range(4)
        for k in range(2)
    ]
    mask_copies.append(pltpu.make_async_copy(qd.at[0], q_s, sems.at[20]))
    mask_copies.append(pltpu.make_async_copy(qd.at[1], da_s, sems.at[21]))
    for copy in mask_copies + x_copies:
        copy.start()
    kt_s[...] = kv[:, 0:256].T
    vt_s[...] = kv[:, 256:512].T
    dk_s[...] = jnp.zeros_like(dk_s)
    dv_s[...] = jnp.zeros_like(dv_s)
    for copy in mask_copies:
        copy.wait()
    lane = lax.broadcasted_iota(jnp.int32, (256, 128), 1) // 64
    row16 = lax.broadcasted_iota(jnp.int32, (16, 128), 0)
    col16 = lax.broadcasted_iota(jnp.int32, (16, 128), 1) // 64
    pick = jnp.where(row16 == col16, 1.0, 0.0).astype(BF)

    allowed = [
        jnp.concatenate([dot(mask_s[2 * u + s], pick, 0, 0) for s in range(2)], axis=1) > 0.5
        for u in range(2)
    ]
    zero = jnp.zeros((256, 128), BF)

    def first(u, h):
        pair = slice(128 * (h // 2), 128 * (h // 2) + 128)
        vpair = slice(256 + 128 * (h // 2), 384 + 128 * (h // 2))
        qrows = slice(256 * u, 256 * u + 256)
        own = lane == (h % 2)
        qm = jnp.where(own, q_s[qrows, pair], zero)
        dam = jnp.where(own, da_s[qrows, pair], zero)
        s = dot(kv[:, pair], qm, 1, 1)
        dp = dot(kv[:, vpair], dam, 1, 1)
        return qm, dam, s, dp

    def second(u, h, qm, dam, s, dp):
        pair = slice(128 * (h // 2), 128 * (h // 2) + 128)
        head = slice(64 * h, 64 * h + 64)
        qrows = slice(256 * u, 256 * u + 256)
        s = jnp.where(allowed[u], s, -jnp.inf)
        e = jnp.exp(s - jnp.max(s, axis=0, keepdims=True))
        p = e * (1.0 / jnp.sum(e, axis=0, keepdims=True))
        plow = p.astype(BF)
        delta = jnp.sum(p * dp, axis=0, keepdims=True)
        ds = (p * (dp - delta)).astype(BF)
        return plow, ds

    def third(u, h, qm, dam, plow, ds):
        pair = slice(128 * (h // 2), 128 * (h // 2) + 128)
        head = slice(64 * h, 64 * h + 64)
        qrows = slice(256 * u, 256 * u + 256)
        at_s[head, qrows] = dot(vt_s[head, :], plow, 1, 0).astype(BF)
        dqt_s[head, qrows] = (0.125 * dot(kt_s[head, :], ds, 1, 0)).astype(BF)
        dv_s[:, pair] += dot(plow, dam, 1, 0)
        dk_s[:, pair] += dot(ds, qm, 1, 0)


    units = [(u, h) for h in range(4) for u in range(2)]

    now = first(*units[0])
    for n, (u, h) in enumerate(units):
        later = first(*units[n + 1]) if n < 7 else None
        plow, ds = second(u, h, *now)
        third(u, h, now[0], now[1], plow, ds)
        now = later
    for copy in x_copies:
        copy.wait()
    go = dot(at_s[...], x_s[1], 1, 0)
    gq = dot(dqt_s[...], x_s[0], 1, 0)
    for j in range(8):
        go_s[j] = go[:, 128 * j : 128 * j + 128]
    for j in range(2):
        gq_s[j] = gq[128 * j : 128 * j + 128, :].T
    outs = []
    for zd in range(8):
        block = slice(128 * zd, 128 * zd + 128)
        pay_s[block, 0:256] = dk_s[block, :].astype(BF)
        pay_s[block, 256:512] = dv_s[block, :].astype(BF)
        for b in range(4):
            rows = slice(128 * zd + 32 * b, 128 * zd + 32 * b + 32)
            for j in range(2):
                lanes = slice(512 + 128 * j, 640 + 128 * j)
                pay_s[rows, lanes] = gq_s[j, pl.ds(4 * zd + b, 32, stride=32), :].astype(BF)
                part = [go_s[2 * b + j, pl.ds(4 * zd + i, 8, stride=32), :] for i in range(4)]
                lanes = slice(768 + 128 * j, 896 + 128 * j)
                pay_s[rows, lanes] = jnp.concatenate(part, axis=0).astype(BF)
        outs.append(pltpu.make_async_copy(pay_s.at[block, :], pay.at[block, :], sems.at[12 + zd]))
        outs[-1].start()
    att_out[...] = at_s[...].T
    dq_out[...] = dqt_s[...].T
    for copy in outs:
        copy.wait()


def md_kernel(att, dq, wq, wo, out):
    for t in range(4):
        rows = slice(128 * t, 128 * t + 128)
        out[t, 0:128, :] = dot(att[rows, :], wo[...], 1, 0).astype(BF)
        out[t, 128:256, :] = dot(dq[rows, :], wq[...], 1, 1).astype(BF)


def part_kernel(pos, red, w, p0, p1, p2, p3, part):
    x = pos[2]
    part[...] = dot(red[:, 0:256], w[:, 0:256], 1, 1) + dot(red[:, 256:512], w[:, 256:512], 1, 1)
    for out, by in zip((p0, p1, p2, p3), SHIFTS):
        at = pl.multiple_of(32 * mod(x + by, 4), 32)
        out[...] = part[pl.ds(at, 32), :].astype(BF)


def split_kernel(pos, red, g_out, g_s):
    x = pos[2]
    g_s[...] = jnp.zeros_like(g_s)
    for i in range(4):
        for j in range(2):
            lanes = slice(512 + 128 * j, 640 + 128 * j)
            rows = slice(32 * i, 32 * i + 32)
            g_s[pl.ds(2 * i + j, 32, stride=40), :] = red[rows, lanes].astype(F32)
    for b in range(4):
        for j in range(2):
            block = red[32 * b : 32 * b + 32, 768 + 128 * j : 896 + 128 * j].astype(F32)
            for i in range(4):
                at = 320 * x + 8 + 8 * i + 2 * b + j
                g_s[pl.ds(at, 8, stride=40), :] = block[8 * i : 8 * i + 8, :]
    g_out[...] = g_s[...].astype(BF)


def finish_kernel(g, p0, p1, p2, p3, dctx, g_query, g_out):
    total = p0[...].astype(F32)
    for p in (p1, p2, p3):
        total += p[...].astype(F32)
    dctx[...] = total.astype(BF)
    for xs in range(4):
        acc = jnp.zeros((8, 128), F32)
        for yc in range(8):
            at = 40 * (4 * yc + xs)
            acc += g[at : at + 8, :].astype(F32)
        for i in range(4):
            for j in range(2):
                row = 2 * i + j
                lanes = slice(256 * xs + 128 * j, 256 * xs + 128 * j + 128)
                g_query[i : i + 1, lanes] = acc[row : row + 1, :]
    acc = jnp.zeros((32, 128), F32)
    for src in range(32):
        acc += g[40 * src + 8 : 40 * src + 40, :].astype(F32)
    for i in range(4):
        for m in range(8):
            row = 8 * i + m
            g_out[i : i + 1, 128 * m : 128 * m + 128] = acc[row : row + 1, :]


V = pl.BlockSpec(memory_space=pltpu.VMEM)
S = pl.BlockSpec(memory_space=pltpu.SMEM)
H = pl.BlockSpec(memory_space=pltpu.HBM)


def sds(shape, dtype=BF):
    return jax.ShapeDtypeStruct(shape, dtype)


def call(kernel, in_specs, outs, scratch, mflop, kib, limit, name, out_specs=None):
    return pl.pallas_call(
        kernel,
        out_shape=outs,
        in_specs=in_specs,
        out_specs=out_specs or [V] * len(outs),
        scratch_shapes=scratch,
        compiler_params=pltpu.CompilerParams(vmem_limit_bytes=limit * 2**20),
        cost_estimate=pl.CostEstimate(
            flops=mflop * 10**6, bytes_accessed=kib * 1024, transcendentals=0
        ),
        name=name,
    )


def local(tokens, context, pattern, w_query, w_key, w_value, w_out, cotangent):
    y, c, x, z = (lax.axis_index(n) for n in ("y", "c", "x", "z"))
    pos = jnp.stack([y, c, x, z]).astype(jnp.int32)
    tok, ctx, cot = tokens[0], context[0], cotangent[0]
    own, mine, mine_q = call(
        pack_kernel, [S] + [H] * 6, [sds((272, 1024)), sds((128, 512)), sds((128, 256))],
        [pltpu.VMEM((2, 16), jnp.int32), pltpu.VMEM((16, 1024), BF), pltpu.SemaphoreType.DMA((7,))],
        1, 1500, 61, "pack", [H] * 3,
    )(pos, tok, cot, pattern[0], w_key, w_value, w_query)
    xg = lax.all_gather(own, "x", axis=0, tiled=False)

    ctxs = [ctx] + [shift(ctx, "x", by) for by in SHIFTS[1:]]
    wa = jnp.concatenate([mine] + [shift(mine, "y", by) for by in SHIFTS[1:]], axis=0)
    wa, *ctxs = lax.optimization_barrier((wa, *ctxs))
    wb = shift(wa, "c", 1)
    kv8, wkv = call(
        kv_kernel, [S] + [H] * 6, [sds((8, 128, 512)), sds((1024, 512))],
        [pltpu.VMEM((128, 1024), BF), pltpu.VMEM((128, 512), BF), pltpu.SemaphoreType.DMA((12,))],
        134, 3000, 16, "kv", [H, V],
    )(pos, *ctxs, wa, wb)
    kvg = lax.all_to_all(kv8, "z", split_axis=0, concat_axis=0, tiled=True).reshape(1024, 512)

    mine_q, w_out, kv8 = lax.optimization_barrier((mine_q, w_out, kv8))
    wo = lax.ppermute(
        w_out, ("y", "x"), [(a * 4 + b, b * 4 + a) for a in range(4) for b in range(4)]
    )
    wo4 = jnp.concatenate([wo[:, 256 * j : 256 * j + 256] for j in range(4)], axis=0)
    wq4 = jnp.concatenate([mine_q] + [shift(mine_q, "y", by) for by in SHIFTS[1:]], axis=0)
    wa = jnp.concatenate([wq4, wo4], axis=1)
    wb = shift(wa, "c", 1)
    qd, wq, wo = call(
        qd_kernel, [S, H, H, H],
        [sds((2, 512, 256)), sds((1024, 256)), sds((256, 1024))],
        [pltpu.VMEM((2, 512, 1024), BF), pltpu.VMEM((1024, 256), BF), pltpu.VMEM((256, 1024), BF),
         pltpu.VMEM((512, 256), BF), pltpu.VMEM((512, 256), BF), pltpu.SemaphoreType.DMA((24,))],
        540, 5000, 61, "queries", [H] * 3,
    )(pos, xg, wa, wb)

    pay, att, dq = call(
        attn_kernel, [H, H, V],
        [sds((1024, 1024)), sds((512, 256)), sds((512, 256))],
        [pltpu.VMEM((512, 256), BF), pltpu.VMEM((512, 256), BF),
         pltpu.VMEM((256, 1024), BF), pltpu.VMEM((256, 1024), BF),
         pltpu.VMEM((1024, 256), F32), pltpu.VMEM((1024, 256), F32),
         pltpu.VMEM((256, 512), BF), pltpu.VMEM((256, 512), BF),
         pltpu.VMEM((2, 1024, 128), F32), pltpu.VMEM((8, 256, 128), F32),
         pltpu.VMEM((1024, 1024), BF), pltpu.VMEM((4, 16, 1024), BF),
         pltpu.VMEM((2, 512, 1024), BF), pltpu.SemaphoreType.DMA((22,))],
        2200, 8000, 48, "attention", [H, V, V],
    )(xg, qd, kvg)

    red = lax.psum_scatter(pay, "z", scatter_dimension=0, tiled=True)
    (md,) = call(md_kernel, [V] * 4, [sds((4, 256, 1024))], [], 540, 4000, 16, "md")(
        att, dq, wq, wo
    )
    md = lax.all_to_all(md, "x", split_axis=0, concat_axis=0, tiled=True)
    md = jnp.sum(md.astype(F32), axis=0)
    mixed = (tok.astype(F32) + md[0:128]).astype(BF)
    d_tokens = (cot.astype(F32) + md[128:256]).astype(BF)
    red, mixed, d_tokens = lax.optimization_barrier((red, mixed, d_tokens))

    parts = call(
        part_kernel, [S, V, V], [sds((32, 1024))] * 4,
        [pltpu.VMEM((128, 1024), F32)], 134, 2000, 16, "part",
    )(pos, red, wkv)
    red, *parts = lax.optimization_barrier((red, *parts))
    (g,) = call(
        split_kernel, [S, V], [sds((1280, 128))], [pltpu.VMEM((1280, 128), F32)],
        1, 600, 16, "split",
    )(pos, red)
    parts = [parts[0]] + [shift(p, "x", by) for p, by in zip(parts[1:], SHIFTS[1:])]
    g = lax.all_to_all(
        g.reshape(32, 40, 128), ("y", "c", "x"), split_axis=0, concat_axis=0, tiled=True
    ).reshape(1280, 128)
    d_context, g_query, g_out = call(
        finish_kernel, [V] * 5, [sds((32, 1024)), sds((4, 1024), F32), sds((4, 1024), F32)],
        [], 1, 700, 8, "finish",
    )(g, *parts)
    return mixed[None], d_tokens[None], d_context[None], g_query, g_out


def solution(mesh):
    fine = Mesh(mesh.devices.reshape(4, 2, 4, 8), ("y", "c", "x", "z"))
    seq = P(("y", "c"), ("x", "z"), None)
    wts = P(("y", "c"), None)
    grad = P(("y", "c", "x", "z"), None)
    return jax.shard_map(
        local,
        mesh=fine,
        in_specs=(seq, seq, seq, wts, wts, wts, wts, seq),
        out_specs=(seq, seq, seq, grad, grad),
        check_vma=False,
    )
```

time: 163 us -> 174 us (1.067)
  Pallas kernels: 27.1 us -> 49.4 us
  local copies, waits for them, and re-layouts: 13.7 us -> 4.8 us
  waiting for transfers between devices: 37.2 us -> 34.7 us
    pallas_call x5 -> x6, Pallas kernels: 25.3 us -> 47.6 us  [the longest x1 23.8 us: local(): call(pack_kernel, [S] + [H] * 6, [sds((272, 1024)), sds((128, 512)), sds(...]
    unnamed x36 -> x26, local copies, waits for them, and re-layouts: 12.8 us -> 4.78 us
    ppermute x14, waiting for transfers between devices: 22.6 us -> 15.6 us  [shift(): return lax.ppermute(value, axis, [(i, (i + by) % n) for i in range(n)])]
    ppermute x1, waiting for transfers between devices: 6.12 us -> 10.5 us  [local(): lax.ppermute(w_out, ('y', 'x'), [(a * 4 + b, b * 4 + a) for a in range(4)...]
    all_to_all x1, waiting for transfers between devices: 0.01 us -> 1.83 us  [local(): lax.all_to_all(kv8, 'z', split_axis=0, concat_axis=0, tiled=True)]
    reduce_scatter x1, waiting for transfers between devices: 8.48 us -> 6.71 us  [local(): red = lax.psum_scatter(pay, 'z', scatter_dimension=0, tiled=True)]
  transfers between devices with their start and end apart: 19 -> 19, of which waited for: 12 -> 12; matrix products, arithmetic and copies ran while one was open for 1% -> 1% of each run, Pallas kernels for 4% -> 6%
where the time goes in v3:
time: 174 us; the launch traced here: 173 us
  Pallas kernels  49.4 us (28%)
  starting transfers between devices  37.7 us (22%)
  waiting for transfers between devices  34.7 us (20%)
  blocking collectives  29.3 us (17%)
  between operations  14.2 us (8%)
  local copies, waits for them, and re-layouts  4.8 us (3%)
  other arithmetic  2.92 us (2%)
    all_to_all x1, blocking collectives, local(): md = lax.all_to_all(md, 'x', split_axis=0, concat_axis=0, tiled=True)  29.3 us
    pallas_call x1, Pallas kernels, local(): call(pack_kernel, [S] + [H] * 6, [sds((272, 1024)), sds((128, 512)), sds(...  23.8 us
    ppermute x14, starting transfers between devices, shift(): return lax.ppermute(value, axis, [(i, (i + by) % n) for i in range(n)])  19.5 us
    ppermute x14, waiting for transfers between devices, shift(): return lax.ppermute(value, axis, [(i, (i + by) % n) for i in range(n)])  15.6 us
    pallas_call x1, Pallas kernels, local(): call(attn_kernel, [H, H, V], [sds((1024, 1024)), sds((512, 256)), sds((51...  12.3 us
    ppermute x1, waiting for transfers between devices, local(): lax.ppermute(w_out, ('y', 'x'), [(a * 4 + b, b * 4 + a) for a in range(4)...  10.5 us
    all_to_all x1, starting transfers between devices, local(): lax.all_to_all(kv8, 'z', split_axis=0, concat_axis=0, tiled=True)  8.46 us
    all_to_all x1, starting transfers between devices, local(): lax.all_to_all(g.reshape(32, 40, 128), ('y', 'c', 'x'), split_axis=0, con...  7.25 us
  transfers between devices with their start and end apart: 19, of which 12 were waited for; matrix products, arithmetic and copies ran while one was open for 1% of the time, Pallas kernels for 6%

profile of v3, /device:TPU:8, one launch (start us, length us, event | category | flops | bytes accessed | tf_op | source)
XLA Modules:
  0.0 173.0 jit_solution(12874393856169312634)
XLA Ops:
  7.9 23.8 %pack.1 = (bf16[272,1024]{1,0:T(8,128)(2,1)}, bf16[128,512]{1,0:T(8,128)(2,1)}, bf16[128,256]{1,0:T(8,128)(2,1)}) custom-call(s32[4]{0:T(128)} %pad_add_fusion.pos, bf16[128,1024]{1,0:T(8,128)(2,1)} %bitcast.25, bf16[128,1024]{1,0:T(8,128)(2,1)} %bitcast.26, s32[2,16]{1,0:T(2,128)} %bitcast.29, bf16[128,1024]{1,0:T(8,128)(2,1)} %wk.1, bf16[128,1024]{1,0:T(8,128)(2,1)} %wv.1, ...), custom_call_target="tpu_custom_call" | custom-call | flops 1000000 | bytes 1536000 | tf_op jit(solution)/shard_map/pack/pallas_call | solution.py:290
  31.7 2.4 %collective-permute-start.2 = (bf16[128,512]{1,0:T(8,128)(2,1)}, bf16[128,512]{1,0:T(8,128)(2,1)S(1)}, u32[]{:S(2)}, u32[]{:S(2)}) collective-permute-start(bf16[128,512]{1,0:T(8,128)(2,1)} %get-tuple-element.40), channel_id=1, source_target_pairs={{0,128},{64,192},{128,0},{192,64},{1,129},{65,193},{129,1},{193,65... | collective-permute-start | bytes 393224 | tf_op jit(solution)/shard_map/ppermute | solution.py:20
  34.1 1.3 collective-permute-start.1
  36.1 3.0 %collective-permute-start.5 = (bf16[32,1024]{1,0:T(8,128)(2,1)}, bf16[32,1024]{1,0:T(8,128)(2,1)S(1)}, u32[]{:S(2)}, u32[]{:S(2)}) collective-permute-start(bf16[32,1024]{1,0:T(8,128)(2,1)} %bitcast.19), channel_id=1, source_target_pairs={{0,16},{8,24},{16,0},{24,8},{1,17},{9,25},{17,1},{25,9},{2,18},{10... | collective-permute-start | bytes 196616 | tf_op jit(solution)/shard_map/ppermute | solution.py:20
  39.1 1.1 collective-permute-start.4
  40.3 1.1 collective-permute-start.3
  42.6 1.0 collective-permute-done.4.c2
  43.6 2.4 %collective-permute-done.3.c1 = bf16[32,1024]{1,0:T(8,128)(2,1)S(1)} collective-permute-done((bf16[32,1024]{1,0:T(8,128)(2,1)}, bf16[32,1024]{1,0:T(8,128)(2,1)S(1)}, u32[]{:S(2)}, u32[]{:S(2)}) %collective-permute-start.3) | collective-permute-done | bytes 65568 | tf_op jit(solution)/shard_map/ppermute | solution.py:20
  46.0 1.9 %collective-permute-done.6.wb = bf16[512,512]{1,0:T(8,128)(2,1)S(1)} collective-permute-done((bf16[512,512]{1,0:T(8,128)(2,1)S(1)}, bf16[512,512]{1,0:T(8,128)(2,1)S(1)}, u32[]{:S(2)}, u32[]{:S(2)}) %collective-permute-start.6) | collective-permute-done | bytes 524320 | tf_op jit(solution)/shard_map/ppermute | solution.py:20
  47.9 4.4 %kv.1 = (bf16[8,128,512]{2,1,0:T(8,128)(2,1)S(1)}, bf16[1024,512]{1,0:T(8,128)(2,1)S(1)}) custom-call(s32[4]{0:T(128)S(1)} %copy-done.5, bf16[32,1024]{1,0:T(8,128)(2,1)S(1)} %bitcast.22, bf16[32,1024]{1,0:T(8,128)(2,1)S(1)} %collective-permute-done.3.c1, bf16[32,1024]{1,0:T(8,128)(2,1)S(1)} %collective-permute-done.4.c2, ...), custom_call_target="tpu_custom_call" | custom-call | flops 134000000 | bytes 3072000 | tf_op jit(solution)/shard_map/kv/pallas_call | solution.py:301
  53.3 8.5 %all-to-all-start = ((bf16[8,128,512]{2,1,0:T(8,128)(2,1)}), bf16[8,128,512]{2,1,0:T(8,128)(2,1)S(1)}, u32[]{:S(2)}, u32[]{:S(2)}) async-start(bf16[8,128,512]{2,1,0:T(8,128)(2,1)} %copy-done.1), calls=%async_computation | async-start | bytes 2097152 | tf_op jit(solution)/shard_map/all_to_all | solution.py:306
  61.8 2.4 %collective-permute-start.10 = (bf16[128,1024]{1,0:T(8,128)(2,1)S(1)}, bf16[128,1024]{1,0:T(8,128)(2,1)S(1)}, u32[]{:S(2)}, u32[]{:S(2)}) collective-permute-start(bf16[128,1024]{1,0:T(8,128)(2,1)S(1)} %copy-done.12), channel_id=1, source_target_pairs={{0,0},{8,64},{16,128},{24,192},{64,8},{72,72},{80,136},{88,200},{1... | collective-permute-start | bytes 786440 | tf_op jit(solution)/shard_map/ppermute | solution.py:309
  64.2 2.5 %collective-permute-start.9 = (bf16[128,256]{1,0:T(8,128)(2,1)S(1)}, bf16[128,256]{1,0:T(8,128)(2,1)S(1)}, u32[]{:S(2)}, u32[]{:S(2)}) collective-permute-start(bf16[128,256]{1,0:T(8,128)(2,1)S(1)} %copy-done.11), channel_id=1, source_target_pairs={{0,128},{64,192},{128,0},{192,64},{1,129},{65,193},{129,1},{193,65... | collective-permute-start | bytes 196616 | tf_op jit(solution)/shard_map/ppermute | solution.py:20
  66.6 1.8 %collective-permute-start.8 = (bf16[128,256]{1,0:T(8,128)(2,1)S(1)}, bf16[128,256]{1,0:T(8,128)(2,1)S(1)}, u32[]{:S(2)}, u32[]{:S(2)}) collective-permute-start(bf16[128,256]{1,0:T(8,128)(2,1)S(1)} %copy-done.11), channel_id=1, source_target_pairs={{0,192},{64,0},{128,64},{192,128},{1,193},{65,1},{129,65},{193,129... | collective-permute-start | bytes 196616 | tf_op jit(solution)/shard_map/ppermute | solution.py:20
  68.7 10.5 %collective-permute-done.10 = bf16[128,1024]{1,0:T(8,128)(2,1)S(1)} collective-permute-done((bf16[128,1024]{1,0:T(8,128)(2,1)S(1)}, bf16[128,1024]{1,0:T(8,128)(2,1)S(1)}, u32[]{:S(2)}, u32[]{:S(2)}) %collective-permute-start.10) | collective-permute-done | bytes 262176 | tf_op jit(solution)/shard_map/ppermute | solution.py:309
  79.2 2.7 %collective-permute-done.7 = bf16[128,256]{1,0:T(8,128)(2,1)S(1)} collective-permute-done((bf16[128,256]{1,0:T(8,128)(2,1)S(1)}, bf16[128,256]{1,0:T(8,128)(2,1)S(1)}, u32[]{:S(2)}, u32[]{:S(2)}) %collective-permute-start.7) | collective-permute-done | bytes 65568 | tf_op jit(solution)/shard_map/ppermute | solution.py:20
  82.2 2.0 %collective-permute-done.11.wb = bf16[512,512]{1,0:T(8,128)(2,1)} collective-permute-done((bf16[512,512]{1,0:T(8,128)(2,1)S(1)}, bf16[512,512]{1,0:T(8,128)(2,1)}, u32[]{:S(2)}, u32[]{:S(2)}) %collective-permute-start.11) | collective-permute-done | bytes 524320 | tf_op jit(solution)/shard_map/ppermute | solution.py:20
  84.3 4.7 %queries.1 = (bf16[2,512,256]{2,1,0:T(8,128)(2,1)}, bf16[1024,256]{1,0:T(8,128)(2,1)}, bf16[256,1024]{1,0:T(8,128)(2,1)}) custom-call(s32[4]{0:T(128)} %pad_add_fusion.pos, bf16[4,272,1024]{2,1,0:T(8,128)(2,1)} %bitcast.23, bf16[512,512]{1,0:T(8,128)(2,1)} %copy-done.8, bf16[512,512]{1,0:T(8,128)(2,1)} %collective-permute-done.11.wb), custom_call_target="tpu_custom_call" | custom-call | flops 540000000 | bytes 5120000 | tf_op jit(solution)/shard_map/queries/pallas_call | solution.py:316
  89.0 1.8 %all-to-all-done = bf16[8,128,512]{2,1,0:T(8,128)(2,1)S(1)} async-done(((bf16[8,128,512]{2,1,0:T(8,128)(2,1)}), bf16[8,128,512]{2,1,0:T(8,128)(2,1)S(1)}, u32[]{:S(2)}, u32[]{:S(2)}) %all-to-all-start) | async-done | bytes 1048608 | tf_op jit(solution)/shard_map/all_to_all | solution.py:306
  90.8 1.0 copy-done.7
  91.8 12.3 %attention.1 = (bf16[1024,1024]{1,0:T(8,128)(2,1)}, bf16[512,256]{1,0:T(8,128)(2,1)S(1)}, bf16[512,256]{1,0:T(8,128)(2,1)S(1)}) custom-call(bf16[4,272,1024]{2,1,0:T(8,128)(2,1)} %bitcast.24, bf16[2,512,256]{2,1,0:T(8,128)(2,1)S(1)} %copy-done.7, bf16[1024,512]{1,0:T(8,128)(2,1)S(1)} %bitcast.18), custom_call_target="tpu_custom_call" | custom-call | flops 2200000000 | bytes 8192000 | tf_op jit(solution)/shard_map/attention/pallas_call | solution.py:324
  105.3 1.2 md.1
  106.5 29.3 %all_to_all.15 = bf16[4,256,1024]{2,1,0:T(8,128)(2,1)S(1)} all-to-all(bf16[4,256,1024]{2,1,0:T(8,128)(2,1)S(1)} %md.1), channel_id=1, replica_groups=mesh['y'=4,'c'=2,'x'=4,'z'=8] {'x'}, dimensions={0} | all-to-all | bytes 4194304 | tf_op jit(solution)/shard_map/all_to_all | solution.py:341
  137.7 6.7 %reduce-scatter.2.cloned.1.call-done.red = bf16[128,1024]{1,0:T(8,128)(2,1)} async-done(((bf16[1024,1024]{1,0:T(8,128)(2,1)}), bf16[128,1024]{1,0:T(8,128)(2,1)}) %reduce-scatter.2.cloned.1.call-update) | async-done | bytes 262160 | tf_op jit(solution)/shard_map/reduce_scatter | solution.py:337
  145.4 1.0 part.1
  146.4 1.4 split.1
  147.8 7.2 %all-to-all-start.2 = ((bf16[32,40,128]{2,1,0:T(8,128)(2,1)}), bf16[32,40,128]{2,1,0:T(8,128)(2,1)S(1)}, u32[]{:S(2)}, u32[]{:S(2)}) async-start(bf16[32,40,128]{2,1,0:T(8,128)(2,1)} %bitcast.12), calls=%async_computation.3 | async-start | bytes 655360 | tf_op jit(solution)/shard_map/all_to_all | solution.py:357
  155.1 1.5 collective-permute-start.12
  156.6 1.8 %collective-permute-start.13 = (bf16[32,1024]{1,0:T(8,128)(2,1)S(1)}, bf16[32,1024]{1,0:T(8,128)(2,1)S(1)}, u32[]{:S(2)}, u32[]{:S(2)}) collective-permute-start(bf16[32,1024]{1,0:T(8,128)(2,1)S(1)} %get-tuple-element.66), channel_id=1, source_target_pairs={{0,24},{8,0},{16,8},{24,16},{1,25},{9,1},{17,9},{25,17},{2,26},{10... | collective-permute-start | bytes 196616 | tf_op jit(solution)/shard_map/ppermute | solution.py:20
  158.4 1.8 %collective-permute-start.14 = (bf16[32,1024]{1,0:T(8,128)(2,1)S(1)}, bf16[32,1024]{1,0:T(8,128)(2,1)S(1)}, u32[]{:S(2)}, u32[]{:S(2)}) collective-permute-start(bf16[32,1024]{1,0:T(8,128)(2,1)S(1)} %get-tuple-element.67), channel_id=1, source_target_pairs={{0,16},{8,24},{16,0},{24,8},{1,17},{9,25},{17,1},{25,9},{2,18},{10... | collective-permute-start | bytes 196616 | tf_op jit(solution)/shard_map/ppermute | solution.py:20
  160.1 3.8 %collective-permute-done.12.p1 = bf16[32,1024]{1,0:T(8,128)(2,1)S(1)} collective-permute-done((bf16[32,1024]{1,0:T(8,128)(2,1)S(1)}, bf16[32,1024]{1,0:T(8,128)(2,1)S(1)}, u32[]{:S(2)}, u32[]{:S(2)}) %collective-permute-start.12) | collective-permute-done | bytes 65568 | tf_op jit(solution)/shard_map/ppermute | solution.py:20
  163.9 1.5 collective-permute-done.14.p3
  (49 shorter events, 9.0 us)
Async XLA Ops:
  7.2 40.7 %copy-start.4 = (bf16[1,32,1024]{2,1,0:T(8,128)(2,1)S(1)}, bf16[1,32,1024]{2,1,0:T(8,128)(2,1)}, u32[]{:S(2)}) copy-start(bf16[1,32,1024]{2,1,0:T(8,128)(2,1)} %param.9) | copy-start | bytes 196612
  7.2 77.1 %all-gather.3.cloned.1.call-start = ((), (), s32[]{:S(2)}) async-start(), calls=%async_computation.5 | async-start | bytes 2785280 | tf_op jit(solution)/shard_map/all_gather | solution.py:295
  7.8 40.0 %copy-start.5 = (s32[4]{0:T(128)S(1)}, s32[4]{0:T(128)}, u32[]{:S(2)}) copy-start(s32[4]{0:T(128)} %pad_add_fusion.pos) | copy-start | bytes 52
  31.7 8.6 %collective-permute-start.2 = (bf16[128,512]{1,0:T(8,128)(2,1)}, bf16[128,512]{1,0:T(8,128)(2,1)S(1)}, u32[]{:S(2)}, u32[]{:S(2)}) collective-permute-start(bf16[128,512]{1,0:T(8,128)(2,1)} %get-tuple-element.40), channel_id=1, source_target_pairs={{0,128},{64,192},{128,0},{192,64},{1,129},{65,193},{129,1},{193,65... | collective-permute-start | bytes 393224 | tf_op jit(solution)/shard_map/ppermute | solution.py:20
  34.1 7.5 %collective-permute-start.1 = (bf16[128,512]{1,0:T(8,128)(2,1)}, bf16[128,512]{1,0:T(8,128)(2,1)S(1)}, u32[]{:S(2)}, u32[]{:S(2)}) collective-permute-start(bf16[128,512]{1,0:T(8,128)(2,1)} %get-tuple-element.40), channel_id=1, source_target_pairs={{0,192},{64,0},{128,64},{192,128},{1,193},{65,1},{129,65},{193,129... | collective-permute-start | bytes 393224 | tf_op jit(solution)/shard_map/ppermute | solution.py:20
  35.4 6.2 %collective-permute-start = (bf16[128,512]{1,0:T(8,128)(2,1)}, bf16[128,512]{1,0:T(8,128)(2,1)S(1)}, u32[]{:S(2)}, u32[]{:S(2)}) collective-permute-start(bf16[128,512]{1,0:T(8,128)(2,1)} %get-tuple-element.40), channel_id=1, source_target_pairs={{0,64},{64,128},{128,192},{192,0},{1,65},{65,129},{129,193},{193,1... | collective-permute-start | bytes 393224 | tf_op jit(solution)/shard_map/ppermute | solution.py:20
  36.1 25.7 %copy-start.12 = (bf16[128,1024]{1,0:T(8,128)(2,1)S(1)}, bf16[128,1024]{1,0:T(8,128)(2,1)}, u32[]{:S(2)}) copy-start(bf16[128,1024]{1,0:T(8,128)(2,1)} %param.14) | copy-start | bytes 786436
  36.1 28.1 %copy-start.11 = (bf16[128,256]{1,0:T(8,128)(2,1)S(1)}, bf16[128,256]{1,0:T(8,128)(2,1)}, u32[]{:S(2)}) copy-start(bf16[128,256]{1,0:T(8,128)(2,1)} %get-tuple-element.47) | copy-start | bytes 196612
  36.1 6.5 %collective-permute-start.5 = (bf16[32,1024]{1,0:T(8,128)(2,1)}, bf16[32,1024]{1,0:T(8,128)(2,1)S(1)}, u32[]{:S(2)}, u32[]{:S(2)}) collective-permute-start(bf16[32,1024]{1,0:T(8,128)(2,1)} %bitcast.19), channel_id=1, source_target_pairs={{0,16},{8,24},{16,0},{24,8},{1,17},{9,25},{17,1},{25,9},{2,18},{10... | collective-permute-start | bytes 196616 | tf_op jit(solution)/shard_map/ppermute | solution.py:20
  39.1 4.5 %collective-permute-start.4 = (bf16[32,1024]{1,0:T(8,128)(2,1)}, bf16[32,1024]{1,0:T(8,128)(2,1)S(1)}, u32[]{:S(2)}, u32[]{:S(2)}) collective-permute-start(bf16[32,1024]{1,0:T(8,128)(2,1)} %bitcast.20), channel_id=1, source_target_pairs={{0,24},{8,0},{16,8},{24,16},{1,25},{9,1},{17,9},{25,17},{2,26},{10... | collective-permute-start | bytes 196616 | tf_op jit(solution)/shard_map/ppermute | solution.py:20
  40.3 5.7 %collective-permute-start.3 = (bf16[32,1024]{1,0:T(8,128)(2,1)}, bf16[32,1024]{1,0:T(8,128)(2,1)S(1)}, u32[]{:S(2)}, u32[]{:S(2)}) collective-permute-start(bf16[32,1024]{1,0:T(8,128)(2,1)} %bitcast.21), channel_id=1, source_target_pairs={{0,8},{8,16},{16,24},{24,0},{1,9},{9,17},{17,25},{25,1},{2,10},{10... | collective-permute-start | bytes 196616 | tf_op jit(solution)/shard_map/ppermute | solution.py:20
  46.0 1.9 %collective-permute-start.6 = (bf16[512,512]{1,0:T(8,128)(2,1)S(1)}, bf16[512,512]{1,0:T(8,128)(2,1)S(1)}, u32[]{:S(2)}, u32[]{:S(2)}) collective-permute-start(bf16[512,512]{1,0:T(8,128)(2,1)S(1)} %pad_maximum_fusion.wa), channel_id=1, source_target_pairs={{0,32},{32,0},{1,33},{33,1},{2,34},{34,2},{3,35},{35,3},{4,36},{36... | collective-permute-start | bytes 1572872 | tf_op jit(solution)/shard_map/ppermute | solution.py:20
  52.3 1.0 copy-start.1
  53.3 37.5 %all-to-all-start = ((bf16[8,128,512]{2,1,0:T(8,128)(2,1)}), bf16[8,128,512]{2,1,0:T(8,128)(2,1)S(1)}, u32[]{:S(2)}, u32[]{:S(2)}) async-start(bf16[8,128,512]{2,1,0:T(8,128)(2,1)} %copy-done.1), calls=%async_computation | async-start | bytes 2097152 | tf_op jit(solution)/shard_map/all_to_all | solution.py:306
  61.7 82.7 %reduce-scatter.2.cloned.1.call-start = ((), (), s32[]{:S(2)}) async-start(), calls=%async_computation.4 | async-start | bytes 2359296 | tf_op jit(solution)/shard_map/reduce_scatter | solution.py:337
  61.8 17.4 %collective-permute-start.10 = (bf16[128,1024]{1,0:T(8,128)(2,1)S(1)}, bf16[128,1024]{1,0:T(8,128)(2,1)S(1)}, u32[]{:S(2)}, u32[]{:S(2)}) collective-permute-start(bf16[128,1024]{1,0:T(8,128)(2,1)S(1)} %copy-done.12), channel_id=1, source_target_pairs={{0,0},{8,64},{16,128},{24,192},{64,8},{72,72},{80,136},{88,200},{1... | collective-permute-start | bytes 786440 | tf_op jit(solution)/shard_map/ppermute | solution.py:309
  64.2 15.1 %collective-permute-start.9 = (bf16[128,256]{1,0:T(8,128)(2,1)S(1)}, bf16[128,256]{1,0:T(8,128)(2,1)S(1)}, u32[]{:S(2)}, u32[]{:S(2)}) collective-permute-start(bf16[128,256]{1,0:T(8,128)(2,1)S(1)} %copy-done.11), channel_id=1, source_target_pairs={{0,128},{64,192},{128,0},{192,64},{1,129},{65,193},{129,1},{193,65... | collective-permute-start | bytes 196616 | tf_op jit(solution)/shard_map/ppermute | solution.py:20
  66.6 12.6 %collective-permute-start.8 = (bf16[128,256]{1,0:T(8,128)(2,1)S(1)}, bf16[128,256]{1,0:T(8,128)(2,1)S(1)}, u32[]{:S(2)}, u32[]{:S(2)}) collective-permute-start(bf16[128,256]{1,0:T(8,128)(2,1)S(1)} %copy-done.11), channel_id=1, source_target_pairs={{0,192},{64,0},{128,64},{192,128},{1,193},{65,1},{129,65},{193,129... | collective-permute-start | bytes 196616 | tf_op jit(solution)/shard_map/ppermute | solution.py:20
  68.4 13.5 %collective-permute-start.7 = (bf16[128,256]{1,0:T(8,128)(2,1)S(1)}, bf16[128,256]{1,0:T(8,128)(2,1)S(1)}, u32[]{:S(2)}, u32[]{:S(2)}) collective-permute-start(bf16[128,256]{1,0:T(8,128)(2,1)S(1)} %copy-done.11), channel_id=1, source_target_pairs={{0,64},{64,128},{128,192},{192,0},{1,65},{65,129},{129,193},{193,1... | collective-permute-start | bytes 196616 | tf_op jit(solution)/shard_map/ppermute | solution.py:20
  81.9 2.3 %copy-start.8 = (bf16[512,512]{1,0:T(8,128)(2,1)}, bf16[512,512]{1,0:T(8,128)(2,1)S(1)}, u32[]{:S(2)}) copy-start(bf16[512,512]{1,0:T(8,128)(2,1)S(1)} %maximum_maximum_fusion.wa) | copy-start | bytes 1572868
  82.0 2.3 %collective-permute-start.11 = (bf16[512,512]{1,0:T(8,128)(2,1)S(1)}, bf16[512,512]{1,0:T(8,128)(2,1)}, u32[]{:S(2)}, u32[]{:S(2)}) collective-permute-start(bf16[512,512]{1,0:T(8,128)(2,1)S(1)} %maximum_maximum_fusion.wa), channel_id=1, source_target_pairs={{0,32},{32,0},{1,33},{33,1},{2,34},{34,2},{3,35},{35,3},{4,36},{36... | collective-permute-start | bytes 1572872 | tf_op jit(solution)/shard_map/ppermute | solution.py:20
  90.8 1.0 copy-start.7
  104.1 1.0 copy-start.2
  104.1 1.2 copy-start.3
  135.7 1.0 copy-start.9
  135.7 1.0 copy-start.10
  135.7 8.7 %copy-start.6 = (s32[4]{0:T(128)S(1)}, s32[4]{0:T(128)}, u32[]{:S(2)}) copy-start(s32[4]{0:T(128)} %pad_add_fusion.pos) | copy-start | bytes 52
  144.4 1.0 copy-start
  147.8 17.6 %all-to-all-start.2 = ((bf16[32,40,128]{2,1,0:T(8,128)(2,1)}), bf16[32,40,128]{2,1,0:T(8,128)(2,1)S(1)}, u32[]{:S(2)}, u32[]{:S(2)}) async-start(bf16[32,40,128]{2,1,0:T(8,128)(2,1)} %bitcast.12), calls=%async_computation.3 | async-start | bytes 655360 | tf_op jit(solution)/shard_map/all_to_all | solution.py:357
  155.1 8.9 %collective-permute-start.12 = (bf16[32,1024]{1,0:T(8,128)(2,1)S(1)}, bf16[32,1024]{1,0:T(8,128)(2,1)S(1)}, u32[]{:S(2)}, u32[]{:S(2)}) collective-permute-start(bf16[32,1024]{1,0:T(8,128)(2,1)S(1)} %get-tuple-element.65), channel_id=1, source_target_pairs={{0,8},{8,16},{16,24},{24,0},{1,9},{9,17},{17,25},{25,1},{2,10},{10... | collective-permute-start | bytes 196616 | tf_op jit(solution)/shard_map/ppermute | solution.py:20
  156.6 7.3 %collective-permute-start.13 = (bf16[32,1024]{1,0:T(8,128)(2,1)S(1)}, bf16[32,1024]{1,0:T(8,128)(2,1)S(1)}, u32[]{:S(2)}, u32[]{:S(2)}) collective-permute-start(bf16[32,1024]{1,0:T(8,128)(2,1)S(1)} %get-tuple-element.66), channel_id=1, source_target_pairs={{0,24},{8,0},{16,8},{24,16},{1,25},{9,1},{17,9},{25,17},{2,26},{10... | collective-permute-start | bytes 196616 | tf_op jit(solution)/shard_map/ppermute | solution.py:20
  158.4 7.1 %collective-permute-start.14 = (bf16[32,1024]{1,0:T(8,128)(2,1)S(1)}, bf16[32,1024]{1,0:T(8,128)(2,1)S(1)}, u32[]{:S(2)}, u32[]{:S(2)}) collective-permute-start(bf16[32,1024]{1,0:T(8,128)(2,1)S(1)} %get-tuple-element.67), channel_id=1, source_target_pairs={{0,16},{8,24},{16,0},{24,8},{1,17},{9,25},{17,1},{25,9},{2,18},{10... | collective-permute-start | bytes 196616 | tf_op jit(solution)/shard_map/ppermute | solution.py:20
Sparse Core Ops, SparseCore 0:
  31.8 37.3 all-gather.2
  104.3 40.1 reduce-scatter.1

commit v4 on v3

--- a/solution.py
+++ b/solution.py
@@ -36,16 +36,16 @@
         copy.wait()
 
 
-def pack_kernel(pos, tok, cot, pattern, wk, wv, wq, out, kv_cut, q_cut, pat_s, mask_s, sems):
+def pack_kernel(pos, tok, cot, pattern, wk, wv, wq, out, kv_cut, q_cut, pat_s, x_s, kv_s, q_s, sems):
     cols = pl.ds(pl.multiple_of(256 * pos[2], 256), 256)
     copies = run_copies(
         [
             (pattern, pat_s),
-            (wk.at[:, cols], kv_cut.at[:, pl.ds(0, 256)]),
-            (wv.at[:, cols], kv_cut.at[:, pl.ds(256, 256)]),
-            (tok, out.at[pl.ds(0, 128), :]),
-            (cot, out.at[pl.ds(128, 128), :]),
-            (wq.at[:, cols], q_cut),
+            (wk.at[:, cols], kv_s.at[:, pl.ds(0, 256)]),
+            (wv.at[:, cols], kv_s.at[:, pl.ds(256, 256)]),
+            (tok, x_s.at[pl.ds(0, 128), :]),
+            (cot, x_s.at[pl.ds(128, 128), :]),
+            (wq.at[:, cols], q_s),
         ],
         sems,
     )
@@ -55,25 +55,23 @@
     copies[0].wait()
     rows = jnp.where(pat_s[...] == 1, 1.0, 0.0).astype(BF)
     rows = jnp.concatenate([rows, jnp.zeros((14, 16), BF)], axis=0)
-    mask_s[...] = dot(rows, grow, 1, 0).astype(BF)
-    last = pltpu.make_async_copy(mask_s, out.at[pl.ds(256, 16), :], sems.at[6])
-    last.start()
-    wait_all(copies[1:] + [last])
-
-
-def kv_kernel(pos, c0, c1, c2, c3, wa, wb, kv_out, w_out, ctx, kv_s, sems):
+    x_s[256:272, :] = dot(rows, grow, 1, 0).astype(BF)
+    wait_all(copies[1:])
+    wait_all(run_copies([(x_s, out), (kv_s, kv_cut), (q_s, q_cut)], sems))
+
+
+def kv_kernel(pos, c0, c1, c2, c3, wa, wb, kv_out, w_out, ctx, w_s, kv_s, sems):
     y, c, x = pos[0], pos[1], pos[2]
-    pairs = []
     for half, core in ((wa, c), (wb, 1 - c)):
         for slot, by in enumerate(SHIFTS):
             at = pl.multiple_of(128 * (2 * mod(y - by, 4) + core), 128)
-            pairs.append((half.at[pl.ds(128 * slot, 128), :], w_out.at[pl.ds(at, 128), :]))
+            w_s[pl.ds(at, 128), :] = half[128 * slot : 128 * slot + 128, :]
     for src, by in zip((c0, c1, c2, c3), SHIFTS):
         at = pl.multiple_of(32 * mod(x - by, 4), 32)
-        pairs.append((src, ctx.at[pl.ds(at, 32), :]))
+        ctx[pl.ds(at, 32), :] = src[...]
+    kv_s[...] = dot(ctx[...], w_s[...], 1, 0).astype(BF)
+    pairs = [(kv_s, kv_out.at[zd]) for zd in range(8)] + [(w_s, w_out)]
     wait_all(run_copies(pairs, sems))
-    kv_s[...] = dot(ctx[...], w_out[...], 1, 0).astype(BF)
-    wait_all(run_copies([(kv_s, kv_out.at[zd]) for zd in range(8)], sems))
 
 
 def qd_kernel(pos, xg, wa, wb, qd_out, wq_out, wo_out, x_s, wq_s, wo_s, q_s, da_s, sems):
@@ -289,7 +287,8 @@
     tok, ctx, cot = tokens[0], context[0], cotangent[0]
     own, mine, mine_q = call(
         pack_kernel, [S] + [H] * 6, [sds((272, 1024)), sds((128, 512)), sds((128, 256))],
-        [pltpu.VMEM((2, 16), jnp.int32), pltpu.VMEM((16, 1024), BF), pltpu.SemaphoreType.DMA((7,))],
+        [pltpu.VMEM((2, 16), jnp.int32), pltpu.VMEM((272, 1024), BF), pltpu.VMEM((128, 512), BF),
+         pltpu.VMEM((128, 256), BF), pltpu.SemaphoreType.DMA((6,))],
         1, 1500, 61, "pack", [H] * 3,
     )(pos, tok, cot, pattern[0], w_key, w_value, w_query)
     xg = lax.all_gather(own, "x", axis=0, tiled=False)
@@ -299,9 +298,10 @@
     wa, *ctxs = lax.optimization_barrier((wa, *ctxs))
     wb = shift(wa, "c", 1)
     kv8, wkv = call(
-        kv_kernel, [S] + [H] * 6, [sds((8, 128, 512)), sds((1024, 512))],
-        [pltpu.VMEM((128, 1024), BF), pltpu.VMEM((128, 512), BF), pltpu.SemaphoreType.DMA((12,))],
-        134, 3000, 16, "kv", [H, V],
+        kv_kernel, [S] + [V] * 6, [sds((8, 128, 512)), sds((1024, 512))],
+        [pltpu.VMEM((128, 1024), BF), pltpu.VMEM((1024, 512), BF), pltpu.VMEM((128, 512), BF),
+         pltpu.SemaphoreType.DMA((9,))],
+        134, 3000, 16, "kv", [H, H],
     )(pos, *ctxs, wa, wb)
     kvg = lax.all_to_all(kv8, "z", split_axis=0, concat_axis=0, tiled=True).reshape(1024, 512)
 

time: 174 us -> 151 us (0.87)
  Pallas kernels: 49.4 us -> 26.5 us
    pallas_call x1, Pallas kernels: 23.8 us -> 2.82 us  [local(): call(pack_kernel, [S] + [H] * 6, [sds((272, 1024)), sds((128, 512)), sds(...]
    pallas_call x1, Pallas kernels: 4.4 us -> 2.44 us  [local(): call(kv_kernel, [S] + [V] * 6, [sds((8, 128, 512)), sds((1024, 512))], [p...]
  transfers between devices with their start and end apart: 19 -> 19, of which waited for: 12 -> 12; matrix products, arithmetic and copies ran while one was open for 1% -> 2% of each run, Pallas kernels for 6% -> 6%
where the time goes in v4:
time: 151 us; the launch traced here: 150 us
  starting transfers between devices  37.7 us (25%)
  waiting for transfers between devices  34.7 us (23%)
  blocking collectives  29.3 us (19%)
  Pallas kernels  26.5 us (18%)
  between operations  14.2 us (9%)
  local copies, waits for them, and re-layouts  4.8 us (3%)
  other arithmetic  2.92 us (2%)
    all_to_all x1, blocking collectives, local(): md = lax.all_to_all(md, 'x', split_axis=0, concat_axis=0, tiled=True)  29.3 us
    ppermute x14, starting transfers between devices, shift(): return lax.ppermute(value, axis, [(i, (i + by) % n) for i in range(n)])  19.5 us
    ppermute x14, waiting for transfers between devices, shift(): return lax.ppermute(value, axis, [(i, (i + by) % n) for i in range(n)])  14.9 us
    pallas_call x1, Pallas kernels, local(): call(attn_kernel, [H, H, V], [sds((1024, 1024)), sds((512, 256)), sds((51...  12.3 us
    ppermute x1, waiting for transfers between devices, local(): lax.ppermute(w_out, ('y', 'x'), [(a * 4 + b, b * 4 + a) for a in range(4)...  11.3 us
    all_to_all x1, starting transfers between devices, local(): lax.all_to_all(kv8, 'z', split_axis=0, concat_axis=0, tiled=True)  8.47 us
    all_to_all x1, starting transfers between devices, local(): lax.all_to_all(g.reshape(32, 40, 128), ('y', 'c', 'x'), split_axis=0, con...  7.25 us
    reduce_scatter x1, waiting for transfers between devices, local(): red = lax.psum_scatter(pay, 'z', scatter_dimension=0, tiled=True)  6.73 us
  transfers between devices with their start and end apart: 19, of which 12 were waited for; matrix products, arithmetic and copies ran while one was open for 2% of the time, Pallas kernels for 6%

profile of v4, /device:TPU:8, one launch (start us, length us, event | category | flops | bytes accessed | tf_op | source)
XLA Modules:
  0.0 150.1 jit_solution(15304756499700839125)
XLA Ops:
  7.9 2.8 %pack.1 = (bf16[272,1024]{1,0:T(8,128)(2,1)}, bf16[128,512]{1,0:T(8,128)(2,1)}, bf16[128,256]{1,0:T(8,128)(2,1)}) custom-call(s32[4]{0:T(128)} %pad_add_fusion.pos, bf16[128,1024]{1,0:T(8,128)(2,1)} %bitcast.25, bf16[128,1024]{1,0:T(8,128)(2,1)} %bitcast.26, s32[2,16]{1,0:T(2,128)} %bitcast.29, bf16[128,1024]{1,0:T(8,128)(2,1)} %wk.1, bf16[128,1024]{1,0:T(8,128)(2,1)} %wv.1, ...), custom_call_target="tpu_custom_call" | custom-call | flops 1000000 | bytes 1536000 | tf_op jit(solution)/shard_map/pack/pallas_call | solution.py:288
  10.7 2.4 %collective-permute-start.2 = (bf16[128,512]{1,0:T(8,128)(2,1)}, bf16[128,512]{1,0:T(8,128)(2,1)S(1)}, u32[]{:S(2)}, u32[]{:S(2)}) collective-permute-start(bf16[128,512]{1,0:T(8,128)(2,1)} %get-tuple-element.40), channel_id=1, source_target_pairs={{0,128},{64,192},{128,0},{192,64},{1,129},{65,193},{129,1},{193,65... | collective-permute-start | bytes 393224 | tf_op jit(solution)/shard_map/ppermute | solution.py:20
  13.1 1.3 collective-permute-start.1
  15.1 3.0 %collective-permute-start.5 = (bf16[32,1024]{1,0:T(8,128)(2,1)}, bf16[32,1024]{1,0:T(8,128)(2,1)S(1)}, u32[]{:S(2)}, u32[]{:S(2)}) collective-permute-start(bf16[32,1024]{1,0:T(8,128)(2,1)} %bitcast.19), channel_id=1, source_target_pairs={{0,16},{8,24},{16,0},{24,8},{1,17},{9,25},{17,1},{25,9},{2,18},{10... | collective-permute-start | bytes 196616 | tf_op jit(solution)/shard_map/ppermute | solution.py:20
  18.1 1.1 collective-permute-start.4
  19.3 1.1 collective-permute-start.3
  21.6 1.0 collective-permute-done.4.c2
  22.6 2.4 %collective-permute-done.3.c1 = bf16[32,1024]{1,0:T(8,128)(2,1)S(1)} collective-permute-done((bf16[32,1024]{1,0:T(8,128)(2,1)}, bf16[32,1024]{1,0:T(8,128)(2,1)S(1)}, u32[]{:S(2)}, u32[]{:S(2)}) %collective-permute-start.3) | collective-permute-done | bytes 65568 | tf_op jit(solution)/shard_map/ppermute | solution.py:20
  25.0 1.9 %collective-permute-done.6.wb = bf16[512,512]{1,0:T(8,128)(2,1)S(1)} collective-permute-done((bf16[512,512]{1,0:T(8,128)(2,1)S(1)}, bf16[512,512]{1,0:T(8,128)(2,1)S(1)}, u32[]{:S(2)}, u32[]{:S(2)}) %collective-permute-start.6) | collective-permute-done | bytes 524320 | tf_op jit(solution)/shard_map/ppermute | solution.py:20
  26.9 2.4 %kv.1 = (bf16[8,128,512]{2,1,0:T(8,128)(2,1)S(1)}, bf16[1024,512]{1,0:T(8,128)(2,1)S(1)}) custom-call(s32[4]{0:T(128)S(1)} %copy-done.5, bf16[32,1024]{1,0:T(8,128)(2,1)S(1)} %bitcast.22, bf16[32,1024]{1,0:T(8,128)(2,1)S(1)} %collective-permute-done.3.c1, bf16[32,1024]{1,0:T(8,128)(2,1)S(1)} %collective-permute-done.4.c2, ...), custom_call_target="tpu_custom_call" | custom-call | flops 134000000 | bytes 3072000 | tf_op jit(solution)/shard_map/kv/pallas_call | solution.py:300
  30.3 8.5 %all-to-all-start = ((bf16[8,128,512]{2,1,0:T(8,128)(2,1)}), bf16[8,128,512]{2,1,0:T(8,128)(2,1)S(1)}, u32[]{:S(2)}, u32[]{:S(2)}) async-start(bf16[8,128,512]{2,1,0:T(8,128)(2,1)} %copy-done.1), calls=%async_computation | async-start | bytes 2097152 | tf_op jit(solution)/shard_map/all_to_all | solution.py:306
  38.8 2.4 %collective-permute-start.10 = (bf16[128,1024]{1,0:T(8,128)(2,1)S(1)}, bf16[128,1024]{1,0:T(8,128)(2,1)S(1)}, u32[]{:S(2)}, u32[]{:S(2)}) collective-permute-start(bf16[128,1024]{1,0:T(8,128)(2,1)S(1)} %copy-done.12), channel_id=1, source_target_pairs={{0,0},{8,64},{16,128},{24,192},{64,8},{72,72},{80,136},{88,200},{1... | collective-permute-start | bytes 786440 | tf_op jit(solution)/shard_map/ppermute | solution.py:309
  41.2 2.5 %collective-permute-start.9 = (bf16[128,256]{1,0:T(8,128)(2,1)S(1)}, bf16[128,256]{1,0:T(8,128)(2,1)S(1)}, u32[]{:S(2)}, u32[]{:S(2)}) collective-permute-start(bf16[128,256]{1,0:T(8,128)(2,1)S(1)} %copy-done.11), channel_id=1, source_target_pairs={{0,128},{64,192},{128,0},{192,64},{1,129},{65,193},{129,1},{193,65... | collective-permute-start | bytes 196616 | tf_op jit(solution)/shard_map/ppermute | solution.py:20
  43.7 1.8 %collective-permute-start.8 = (bf16[128,256]{1,0:T(8,128)(2,1)S(1)}, bf16[128,256]{1,0:T(8,128)(2,1)S(1)}, u32[]{:S(2)}, u32[]{:S(2)}) collective-permute-start(bf16[128,256]{1,0:T(8,128)(2,1)S(1)} %copy-done.11), channel_id=1, source_target_pairs={{0,192},{64,0},{128,64},{192,128},{1,193},{65,1},{129,65},{193,129... | collective-permute-start | bytes 196616 | tf_op jit(solution)/shard_map/ppermute | solution.py:20
  45.7 11.3 %collective-permute-done.10 = bf16[128,1024]{1,0:T(8,128)(2,1)S(1)} collective-permute-done((bf16[128,1024]{1,0:T(8,128)(2,1)S(1)}, bf16[128,1024]{1,0:T(8,128)(2,1)S(1)}, u32[]{:S(2)}, u32[]{:S(2)}) %collective-permute-start.10) | collective-permute-done | bytes 262176 | tf_op jit(solution)/shard_map/ppermute | solution.py:309
  57.1 2.0 %collective-permute-done.7 = bf16[128,256]{1,0:T(8,128)(2,1)S(1)} collective-permute-done((bf16[128,256]{1,0:T(8,128)(2,1)S(1)}, bf16[128,256]{1,0:T(8,128)(2,1)S(1)}, u32[]{:S(2)}, u32[]{:S(2)}) %collective-permute-start.7) | collective-permute-done | bytes 65568 | tf_op jit(solution)/shard_map/ppermute | solution.py:20
  59.4 2.0 %collective-permute-done.11.wb = bf16[512,512]{1,0:T(8,128)(2,1)} collective-permute-done((bf16[512,512]{1,0:T(8,128)(2,1)S(1)}, bf16[512,512]{1,0:T(8,128)(2,1)}, u32[]{:S(2)}, u32[]{:S(2)}) %collective-permute-start.11) | collective-permute-done | bytes 524320 | tf_op jit(solution)/shard_map/ppermute | solution.py:20
  61.4 4.7 %queries.1 = (bf16[2,512,256]{2,1,0:T(8,128)(2,1)}, bf16[1024,256]{1,0:T(8,128)(2,1)}, bf16[256,1024]{1,0:T(8,128)(2,1)}) custom-call(s32[4]{0:T(128)} %pad_add_fusion.pos, bf16[4,272,1024]{2,1,0:T(8,128)(2,1)} %bitcast.23, bf16[512,512]{1,0:T(8,128)(2,1)} %copy-done.8, bf16[512,512]{1,0:T(8,128)(2,1)} %collective-permute-done.11.wb), custom_call_target="tpu_custom_call" | custom-call | flops 540000000 | bytes 5120000 | tf_op jit(solution)/shard_map/queries/pallas_call | solution.py:316
  66.1 1.7 %all-to-all-done = bf16[8,128,512]{2,1,0:T(8,128)(2,1)S(1)} async-done(((bf16[8,128,512]{2,1,0:T(8,128)(2,1)}), bf16[8,128,512]{2,1,0:T(8,128)(2,1)S(1)}, u32[]{:S(2)}, u32[]{:S(2)}) %all-to-all-start) | async-done | bytes 1048608 | tf_op jit(solution)/shard_map/all_to_all | solution.py:306
  67.9 1.0 copy-done.7
  68.9 12.3 %attention.1 = (bf16[1024,1024]{1,0:T(8,128)(2,1)}, bf16[512,256]{1,0:T(8,128)(2,1)S(1)}, bf16[512,256]{1,0:T(8,128)(2,1)S(1)}) custom-call(bf16[4,272,1024]{2,1,0:T(8,128)(2,1)} %bitcast.24, bf16[2,512,256]{2,1,0:T(8,128)(2,1)S(1)} %copy-done.7, bf16[1024,512]{1,0:T(8,128)(2,1)S(1)} %bitcast.18), custom_call_target="tpu_custom_call" | custom-call | flops 2200000000 | bytes 8192000 | tf_op jit(solution)/shard_map/attention/pallas_call | solution.py:324
  82.4 1.2 md.1
  83.5 29.3 %all_to_all.15 = bf16[4,256,1024]{2,1,0:T(8,128)(2,1)S(1)} all-to-all(bf16[4,256,1024]{2,1,0:T(8,128)(2,1)S(1)} %md.1), channel_id=1, replica_groups=mesh['y'=4,'c'=2,'x'=4,'z'=8] {'x'}, dimensions={0} | all-to-all | bytes 4194304 | tf_op jit(solution)/shard_map/all_to_all | solution.py:341
  114.8 6.7 %reduce-scatter.2.cloned.1.call-done.red = bf16[128,1024]{1,0:T(8,128)(2,1)} async-done(((bf16[1024,1024]{1,0:T(8,128)(2,1)}), bf16[128,1024]{1,0:T(8,128)(2,1)}) %reduce-scatter.2.cloned.1.call-update) | async-done | bytes 262160 | tf_op jit(solution)/shard_map/reduce_scatter | solution.py:337
  122.5 1.0 part.1
  123.5 1.4 split.1
  124.9 7.2 %all-to-all-start.2 = ((bf16[32,40,128]{2,1,0:T(8,128)(2,1)}), bf16[32,40,128]{2,1,0:T(8,128)(2,1)S(1)}, u32[]{:S(2)}, u32[]{:S(2)}) async-start(bf16[32,40,128]{2,1,0:T(8,128)(2,1)} %bitcast.12), calls=%async_computation.3 | async-start | bytes 655360 | tf_op jit(solution)/shard_map/all_to_all | solution.py:357
  132.2 1.5 %collective-permute-start.12 = (bf16[32,1024]{1,0:T(8,128)(2,1)S(1)}, bf16[32,1024]{1,0:T(8,128)(2,1)S(1)}, u32[]{:S(2)}, u32[]{:S(2)}) collective-permute-start(bf16[32,1024]{1,0:T(8,128)(2,1)S(1)} %get-tuple-element.65), channel_id=1, source_target_pairs={{0,8},{8,16},{16,24},{24,0},{1,9},{9,17},{17,25},{25,1},{2,10},{10... | collective-permute-start | bytes 196616 | tf_op jit(solution)/shard_map/ppermute | solution.py:20
  133.7 1.8 %collective-permute-start.13 = (bf16[32,1024]{1,0:T(8,128)(2,1)S(1)}, bf16[32,1024]{1,0:T(8,128)(2,1)S(1)}, u32[]{:S(2)}, u32[]{:S(2)}) collective-permute-start(bf16[32,1024]{1,0:T(8,128)(2,1)S(1)} %get-tuple-element.66), channel_id=1, source_target_pairs={{0,24},{8,0},{16,8},{24,16},{1,25},{9,1},{17,9},{25,17},{2,26},{10... | collective-permute-start | bytes 196616 | tf_op jit(solution)/shard_map/ppermute | solution.py:20
  135.5 1.8 %collective-permute-start.14 = (bf16[32,1024]{1,0:T(8,128)(2,1)S(1)}, bf16[32,1024]{1,0:T(8,128)(2,1)S(1)}, u32[]{:S(2)}, u32[]{:S(2)}) collective-permute-start(bf16[32,1024]{1,0:T(8,128)(2,1)S(1)} %get-tuple-element.67), channel_id=1, source_target_pairs={{0,16},{8,24},{16,0},{24,8},{1,17},{9,25},{17,1},{25,9},{2,18},{10... | collective-permute-start | bytes 196616 | tf_op jit(solution)/shard_map/ppermute | solution.py:20
  137.2 3.8 %collective-permute-done.12.p1 = bf16[32,1024]{1,0:T(8,128)(2,1)S(1)} collective-permute-done((bf16[32,1024]{1,0:T(8,128)(2,1)S(1)}, bf16[32,1024]{1,0:T(8,128)(2,1)S(1)}, u32[]{:S(2)}, u32[]{:S(2)}) %collective-permute-start.12) | collective-permute-done | bytes 65568 | tf_op jit(solution)/shard_map/ppermute | solution.py:20
  141.0 1.5 %collective-permute-done.14.p3 = bf16[32,1024]{1,0:T(8,128)(2,1)S(1)} collective-permute-done((bf16[32,1024]{1,0:T(8,128)(2,1)S(1)}, bf16[32,1024]{1,0:T(8,128)(2,1)S(1)}, u32[]{:S(2)}, u32[]{:S(2)}) %collective-permute-start.14) | collective-permute-done | bytes 65568 | tf_op jit(solution)/shard_map/ppermute | solution.py:20
  (49 shorter events, 9.0 us)
Async XLA Ops:
  7.2 19.7 %copy-start.4 = (bf16[1,32,1024]{2,1,0:T(8,128)(2,1)S(1)}, bf16[1,32,1024]{2,1,0:T(8,128)(2,1)}, u32[]{:S(2)}) copy-start(bf16[1,32,1024]{2,1,0:T(8,128)(2,1)} %param.9) | copy-start | bytes 196612
  7.2 54.3 %all-gather.3.cloned.1.call-start = ((), (), s32[]{:S(2)}) async-start(), calls=%async_computation.5 | async-start | bytes 2785280 | tf_op jit(solution)/shard_map/all_gather | solution.py:294
  7.8 19.0 %copy-start.5 = (s32[4]{0:T(128)S(1)}, s32[4]{0:T(128)}, u32[]{:S(2)}) copy-start(s32[4]{0:T(128)} %pad_add_fusion.pos) | copy-start | bytes 52
  10.7 8.6 %collective-permute-start.2 = (bf16[128,512]{1,0:T(8,128)(2,1)}, bf16[128,512]{1,0:T(8,128)(2,1)S(1)}, u32[]{:S(2)}, u32[]{:S(2)}) collective-permute-start(bf16[128,512]{1,0:T(8,128)(2,1)} %get-tuple-element.40), channel_id=1, source_target_pairs={{0,128},{64,192},{128,0},{192,64},{1,129},{65,193},{129,1},{193,65... | collective-permute-start | bytes 393224 | tf_op jit(solution)/shard_map/ppermute | solution.py:20
  13.1 7.5 %collective-permute-start.1 = (bf16[128,512]{1,0:T(8,128)(2,1)}, bf16[128,512]{1,0:T(8,128)(2,1)S(1)}, u32[]{:S(2)}, u32[]{:S(2)}) collective-permute-start(bf16[128,512]{1,0:T(8,128)(2,1)} %get-tuple-element.40), channel_id=1, source_target_pairs={{0,192},{64,0},{128,64},{192,128},{1,193},{65,1},{129,65},{193,129... | collective-permute-start | bytes 393224 | tf_op jit(solution)/shard_map/ppermute | solution.py:20
  14.4 6.2 %collective-permute-start = (bf16[128,512]{1,0:T(8,128)(2,1)}, bf16[128,512]{1,0:T(8,128)(2,1)S(1)}, u32[]{:S(2)}, u32[]{:S(2)}) collective-permute-start(bf16[128,512]{1,0:T(8,128)(2,1)} %get-tuple-element.40), channel_id=1, source_target_pairs={{0,64},{64,128},{128,192},{192,0},{1,65},{65,129},{129,193},{193,1... | collective-permute-start | bytes 393224 | tf_op jit(solution)/shard_map/ppermute | solution.py:20
  15.1 23.7 %copy-start.12 = (bf16[128,1024]{1,0:T(8,128)(2,1)S(1)}, bf16[128,1024]{1,0:T(8,128)(2,1)}, u32[]{:S(2)}) copy-start(bf16[128,1024]{1,0:T(8,128)(2,1)} %param.14) | copy-start | bytes 786436
  15.1 26.1 %copy-start.11 = (bf16[128,256]{1,0:T(8,128)(2,1)S(1)}, bf16[128,256]{1,0:T(8,128)(2,1)}, u32[]{:S(2)}) copy-start(bf16[128,256]{1,0:T(8,128)(2,1)} %get-tuple-element.47) | copy-start | bytes 196612
  15.1 6.5 %collective-permute-start.5 = (bf16[32,1024]{1,0:T(8,128)(2,1)}, bf16[32,1024]{1,0:T(8,128)(2,1)S(1)}, u32[]{:S(2)}, u32[]{:S(2)}) collective-permute-start(bf16[32,1024]{1,0:T(8,128)(2,1)} %bitcast.19), channel_id=1, source_target_pairs={{0,16},{8,24},{16,0},{24,8},{1,17},{9,25},{17,1},{25,9},{2,18},{10... | collective-permute-start | bytes 196616 | tf_op jit(solution)/shard_map/ppermute | solution.py:20
  18.1 4.5 %collective-permute-start.4 = (bf16[32,1024]{1,0:T(8,128)(2,1)}, bf16[32,1024]{1,0:T(8,128)(2,1)S(1)}, u32[]{:S(2)}, u32[]{:S(2)}) collective-permute-start(bf16[32,1024]{1,0:T(8,128)(2,1)} %bitcast.20), channel_id=1, source_target_pairs={{0,24},{8,0},{16,8},{24,16},{1,25},{9,1},{17,9},{25,17},{2,26},{10... | collective-permute-start | bytes 196616 | tf_op jit(solution)/shard_map/ppermute | solution.py:20
  19.3 5.7 %collective-permute-start.3 = (bf16[32,1024]{1,0:T(8,128)(2,1)}, bf16[32,1024]{1,0:T(8,128)(2,1)S(1)}, u32[]{:S(2)}, u32[]{:S(2)}) collective-permute-start(bf16[32,1024]{1,0:T(8,128)(2,1)} %bitcast.21), channel_id=1, source_target_pairs={{0,8},{8,16},{16,24},{24,0},{1,9},{9,17},{17,25},{25,1},{2,10},{10... | collective-permute-start | bytes 196616 | tf_op jit(solution)/shard_map/ppermute | solution.py:20
  25.0 1.9 %collective-permute-start.6 = (bf16[512,512]{1,0:T(8,128)(2,1)S(1)}, bf16[512,512]{1,0:T(8,128)(2,1)S(1)}, u32[]{:S(2)}, u32[]{:S(2)}) collective-permute-start(bf16[512,512]{1,0:T(8,128)(2,1)S(1)} %pad_maximum_fusion.wa), channel_id=1, source_target_pairs={{0,32},{32,0},{1,33},{33,1},{2,34},{34,2},{3,35},{35,3},{4,36},{36... | collective-permute-start | bytes 1572872 | tf_op jit(solution)/shard_map/ppermute | solution.py:20
  29.3 1.0 copy-start.1
  30.3 37.5 %all-to-all-start = ((bf16[8,128,512]{2,1,0:T(8,128)(2,1)}), bf16[8,128,512]{2,1,0:T(8,128)(2,1)S(1)}, u32[]{:S(2)}, u32[]{:S(2)}) async-start(bf16[8,128,512]{2,1,0:T(8,128)(2,1)} %copy-done.1), calls=%async_computation | async-start | bytes 2097152 | tf_op jit(solution)/shard_map/all_to_all | solution.py:306
  38.8 82.7 %reduce-scatter.2.cloned.1.call-start = ((), (), s32[]{:S(2)}) async-start(), calls=%async_computation.4 | async-start | bytes 2359296 | tf_op jit(solution)/shard_map/reduce_scatter | solution.py:337
  38.8 18.2 %collective-permute-start.10 = (bf16[128,1024]{1,0:T(8,128)(2,1)S(1)}, bf16[128,1024]{1,0:T(8,128)(2,1)S(1)}, u32[]{:S(2)}, u32[]{:S(2)}) collective-permute-start(bf16[128,1024]{1,0:T(8,128)(2,1)S(1)} %copy-done.12), channel_id=1, source_target_pairs={{0,0},{8,64},{16,128},{24,192},{64,8},{72,72},{80,136},{88,200},{1... | collective-permute-start | bytes 786440 | tf_op jit(solution)/shard_map/ppermute | solution.py:309
  41.2 15.8 %collective-permute-start.9 = (bf16[128,256]{1,0:T(8,128)(2,1)S(1)}, bf16[128,256]{1,0:T(8,128)(2,1)S(1)}, u32[]{:S(2)}, u32[]{:S(2)}) collective-permute-start(bf16[128,256]{1,0:T(8,128)(2,1)S(1)} %copy-done.11), channel_id=1, source_target_pairs={{0,128},{64,192},{128,0},{192,64},{1,129},{65,193},{129,1},{193,65... | collective-permute-start | bytes 196616 | tf_op jit(solution)/shard_map/ppermute | solution.py:20
  43.7 13.4 %collective-permute-start.8 = (bf16[128,256]{1,0:T(8,128)(2,1)S(1)}, bf16[128,256]{1,0:T(8,128)(2,1)S(1)}, u32[]{:S(2)}, u32[]{:S(2)}) collective-permute-start(bf16[128,256]{1,0:T(8,128)(2,1)S(1)} %copy-done.11), channel_id=1, source_target_pairs={{0,192},{64,0},{128,64},{192,128},{1,193},{65,1},{129,65},{193,129... | collective-permute-start | bytes 196616 | tf_op jit(solution)/shard_map/ppermute | solution.py:20
  45.5 13.6 %collective-permute-start.7 = (bf16[128,256]{1,0:T(8,128)(2,1)S(1)}, bf16[128,256]{1,0:T(8,128)(2,1)S(1)}, u32[]{:S(2)}, u32[]{:S(2)}) collective-permute-start(bf16[128,256]{1,0:T(8,128)(2,1)S(1)} %copy-done.11), channel_id=1, source_target_pairs={{0,64},{64,128},{128,192},{192,0},{1,65},{65,129},{129,193},{193,1... | collective-permute-start | bytes 196616 | tf_op jit(solution)/shard_map/ppermute | solution.py:20
  59.1 2.3 %copy-start.8 = (bf16[512,512]{1,0:T(8,128)(2,1)}, bf16[512,512]{1,0:T(8,128)(2,1)S(1)}, u32[]{:S(2)}) copy-start(bf16[512,512]{1,0:T(8,128)(2,1)S(1)} %maximum_maximum_fusion.wa) | copy-start | bytes 1572868
  59.1 2.3 %collective-permute-start.11 = (bf16[512,512]{1,0:T(8,128)(2,1)S(1)}, bf16[512,512]{1,0:T(8,128)(2,1)}, u32[]{:S(2)}, u32[]{:S(2)}) collective-permute-start(bf16[512,512]{1,0:T(8,128)(2,1)S(1)} %maximum_maximum_fusion.wa), channel_id=1, source_target_pairs={{0,32},{32,0},{1,33},{33,1},{2,34},{34,2},{3,35},{35,3},{4,36},{36... | collective-permute-start | bytes 1572872 | tf_op jit(solution)/shard_map/ppermute | solution.py:20
  67.9 1.0 copy-start.7
  81.2 1.0 copy-start.2
  81.2 1.2 copy-start.3
  112.8 1.0 copy-start.9
  112.8 1.0 copy-start.10
  112.8 8.7 %copy-start.6 = (s32[4]{0:T(128)S(1)}, s32[4]{0:T(128)}, u32[]{:S(2)}) copy-start(s32[4]{0:T(128)} %pad_add_fusion.pos) | copy-start | bytes 52
  121.5 1.0 copy-start
  124.9 17.6 %all-to-all-start.2 = ((bf16[32,40,128]{2,1,0:T(8,128)(2,1)}), bf16[32,40,128]{2,1,0:T(8,128)(2,1)S(1)}, u32[]{:S(2)}, u32[]{:S(2)}) async-start(bf16[32,40,128]{2,1,0:T(8,128)(2,1)} %bitcast.12), calls=%async_computation.3 | async-start | bytes 655360 | tf_op jit(solution)/shard_map/all_to_all | solution.py:357
  132.2 8.9 %collective-permute-start.12 = (bf16[32,1024]{1,0:T(8,128)(2,1)S(1)}, bf16[32,1024]{1,0:T(8,128)(2,1)S(1)}, u32[]{:S(2)}, u32[]{:S(2)}) collective-permute-start(bf16[32,1024]{1,0:T(8,128)(2,1)S(1)} %get-tuple-element.65), channel_id=1, source_target_pairs={{0,8},{8,16},{16,24},{24,0},{1,9},{9,17},{17,25},{25,1},{2,10},{10... | collective-permute-start | bytes 196616 | tf_op jit(solution)/shard_map/ppermute | solution.py:20
  133.7 7.3 %collective-permute-start.13 = (bf16[32,1024]{1,0:T(8,128)(2,1)S(1)}, bf16[32,1024]{1,0:T(8,128)(2,1)S(1)}, u32[]{:S(2)}, u32[]{:S(2)}) collective-permute-start(bf16[32,1024]{1,0:T(8,128)(2,1)S(1)} %get-tuple-element.66), channel_id=1, source_target_pairs={{0,24},{8,0},{16,8},{24,16},{1,25},{9,1},{17,9},{25,17},{2,26},{10... | collective-permute-start | bytes 196616 | tf_op jit(solution)/shard_map/ppermute | solution.py:20
  135.5 7.1 %collective-permute-start.14 = (bf16[32,1024]{1,0:T(8,128)(2,1)S(1)}, bf16[32,1024]{1,0:T(8,128)(2,1)S(1)}, u32[]{:S(2)}, u32[]{:S(2)}) collective-permute-start(bf16[32,1024]{1,0:T(8,128)(2,1)S(1)} %get-tuple-element.67), channel_id=1, source_target_pairs={{0,16},{8,24},{16,0},{24,8},{1,17},{9,25},{17,1},{25,9},{2,18},{10... | collective-permute-start | bytes 196616 | tf_op jit(solution)/shard_map/ppermute | solution.py:20
Sparse Core Ops, SparseCore 0:
  10.8 37.6 all-gather.2
  81.3 40.1 reduce-scatter.1

commit v5 on v4

--- a/solution.py
+++ b/solution.py
@@ -97,22 +97,15 @@
     wait_all(run_copies(pairs, sems))
 
 
-def attn_kernel(xg, qd, kv, pay, att_out, dq_out, q_s, da_s,
-                kt_s, vt_s, dk_s, dv_s, at_s, dqt_s, gq_s, go_s, pay_s, mask_s, x_s, sems):
+def attn_kernel(xg, qd, kv, pay, att_out, dq_out, at_s, dqt_s, q_s, da_s,
+                kt_s, vt_s, dk_s, dv_s, pay_s, mask_s, sems):
     mask_copies = [
         pltpu.make_async_copy(xg.at[t, pl.ds(256, 16), :], mask_s.at[t], sems.at[t])
         for t in range(4)
     ]
-    x_copies = [
-        pltpu.make_async_copy(
-            xg.at[t, pl.ds(128 * k, 128), :], x_s.at[k, pl.ds(128 * t, 128), :], sems.at[4 + 4 * k + t]
-        )
-        for t in range(4)
-        for k in range(2)
-    ]
-    mask_copies.append(pltpu.make_async_copy(qd.at[0], q_s, sems.at[20]))
-    mask_copies.append(pltpu.make_async_copy(qd.at[1], da_s, sems.at[21]))
-    for copy in mask_copies + x_copies:
+    mask_copies.append(pltpu.make_async_copy(qd.at[0], q_s, sems.at[4]))
+    mask_copies.append(pltpu.make_async_copy(qd.at[1], da_s, sems.at[5]))
+    for copy in mask_copies:
         copy.start()
     kt_s[...] = kv[:, 0:256].T
     vt_s[...] = kv[:, 256:512].T
@@ -172,40 +165,50 @@
         plow, ds = second(u, h, *now)
         third(u, h, now[0], now[1], plow, ds)
         now = later
-    for copy in x_copies:
-        copy.wait()
-    go = dot(at_s[...], x_s[1], 1, 0)
-    gq = dot(dqt_s[...], x_s[0], 1, 0)
-    for j in range(8):
-        go_s[j] = go[:, 128 * j : 128 * j + 128]
-    for j in range(2):
-        gq_s[j] = gq[128 * j : 128 * j + 128, :].T
     outs = []
     for zd in range(8):
         block = slice(128 * zd, 128 * zd + 128)
         pay_s[block, 0:256] = dk_s[block, :].astype(BF)
         pay_s[block, 256:512] = dv_s[block, :].astype(BF)
-        for b in range(4):
-            rows = slice(128 * zd + 32 * b, 128 * zd + 32 * b + 32)
-            for j in range(2):
-                lanes = slice(512 + 128 * j, 640 + 128 * j)
-                pay_s[rows, lanes] = gq_s[j, pl.ds(4 * zd + b, 32, stride=32), :].astype(BF)
-                part = [go_s[2 * b + j, pl.ds(4 * zd + i, 8, stride=32), :] for i in range(4)]
-                lanes = slice(768 + 128 * j, 896 + 128 * j)
-                pay_s[rows, lanes] = jnp.concatenate(part, axis=0).astype(BF)
-        outs.append(pltpu.make_async_copy(pay_s.at[block, :], pay.at[block, :], sems.at[12 + zd]))
+        outs.append(pltpu.make_async_copy(pay_s.at[block, :], pay.at[block, :], sems.at[6 + zd]))
         outs[-1].start()
     att_out[...] = at_s[...].T
     dq_out[...] = dqt_s[...].T
-    for copy in outs:
-        copy.wait()
-
-
-def md_kernel(att, dq, wq, wo, out):
+    wait_all(outs)
+
+
+def g_kernel(xg, at, dqt, out, x_s, o_s, sems):
+    pairs = []
     for t in range(4):
-        rows = slice(128 * t, 128 * t + 128)
-        out[t, 0:128, :] = dot(att[rows, :], wo[...], 1, 0).astype(BF)
-        out[t, 128:256, :] = dot(dq[rows, :], wq[...], 1, 1).astype(BF)
+        for k in range(2):
+            rows = pl.ds(128 * t, 128)
+            pairs.append((xg.at[t, pl.ds(128 * k, 128), :], x_s.at[k, rows, :]))
+    wait_all(run_copies(pairs, sems))
+    go = dot(at[...], x_s[1], 1, 0)
+    gq = dot(dqt[...], x_s[0], 1, 0).T
+    for d in range(8):
+        o_s[d, :, 0:256] = gq[128 * d : 128 * d + 128, :].astype(BF)
+        base = 32 * (4 * (d % 2) + d // 2)
+        for b in range(4):
+            part = go[base : base + 32, 256 * b : 256 * b + 256]
+            o_s[d, 32 * b : 32 * b + 32, 256:512] = part.astype(BF)
+    wait_all(run_copies([(o_s, out)], sems))
+
+
+def gsum_kernel(g, gq_out, go_out):
+    total = g[0].astype(F32)
+    for d in range(1, 8):
+        total += g[d].astype(F32)
+    gq_out[...] = total[:, 0:256].astype(BF)
+    for b in range(4):
+        go_out[:, 256 * b : 256 * b + 256] = total[32 * b : 32 * b + 32, 256:512].astype(BF)
+
+
+def md_kernel(pos, att, dq, wq, wo, m0, m1, m2, m3):
+    for out, by in zip((m0, m1, m2, m3), SHIFTS):
+        rows = pl.ds(pl.multiple_of(128 * mod(pos[2] + by, 4), 128), 128)
+        out[0:128, :] = dot(att[rows, :], wo[...], 1, 0).astype(BF)
+        out[128:256, :] = dot(dq[rows, :], wq[...], 1, 1).astype(BF)
 
 
 def part_kernel(pos, red, w, p0, p1, p2, p3, part):
@@ -216,20 +219,19 @@
         out[...] = part[pl.ds(at, 32), :].astype(BF)
 
 
-def split_kernel(pos, red, g_out, g_s):
+def split_kernel(pos, gq, go, g_out, g_s, gq_s, go_s):
     x = pos[2]
     g_s[...] = jnp.zeros_like(g_s)
+    for j in range(2):
+        gq_s[j] = gq[:, 128 * j : 128 * j + 128].astype(F32)
+    for m in range(8):
+        go_s[m] = go[:, 128 * m : 128 * m + 128].astype(F32)
     for i in range(4):
         for j in range(2):
-            lanes = slice(512 + 128 * j, 640 + 128 * j)
-            rows = slice(32 * i, 32 * i + 32)
-            g_s[pl.ds(2 * i + j, 32, stride=40), :] = red[rows, lanes].astype(F32)
-    for b in range(4):
-        for j in range(2):
-            block = red[32 * b : 32 * b + 32, 768 + 128 * j : 896 + 128 * j].astype(F32)
-            for i in range(4):
-                at = 320 * x + 8 + 8 * i + 2 * b + j
-                g_s[pl.ds(at, 8, stride=40), :] = block[8 * i : 8 * i + 8, :]
+            g_s[pl.ds(2 * i + j, 32, stride=40), :] = gq_s[j, pl.ds(i, 32, stride=4), :]
+        for m in range(8):
+            at = 320 * x + 8 + 8 * i + m
+            g_s[pl.ds(at, 8, stride=40), :] = go_s[m, pl.ds(i, 8, stride=4), :]
     g_out[...] = g_s[...].astype(BF)
 
 
@@ -240,8 +242,8 @@
     dctx[...] = total.astype(BF)
     for xs in range(4):
         acc = jnp.zeros((8, 128), F32)
-        for yc in range(8):
-            at = 40 * (4 * yc + xs)
+        for zs in range(8):
+            at = 40 * (8 * xs + zs)
             acc += g[at : at + 8, :].astype(F32)
         for i in range(4):
             for j in range(2):
@@ -321,41 +323,52 @@
         540, 5000, 61, "queries", [H] * 3,
     )(pos, xg, wa, wb)
 
-    pay, att, dq = call(
+    pay, att, dq, at, dqt = call(
         attn_kernel, [H, H, V],
-        [sds((1024, 1024)), sds((512, 256)), sds((512, 256))],
+        [sds((1024, 512)), sds((512, 256)), sds((512, 256)), sds((256, 512)), sds((256, 512))],
         [pltpu.VMEM((512, 256), BF), pltpu.VMEM((512, 256), BF),
          pltpu.VMEM((256, 1024), BF), pltpu.VMEM((256, 1024), BF),
          pltpu.VMEM((1024, 256), F32), pltpu.VMEM((1024, 256), F32),
-         pltpu.VMEM((256, 512), BF), pltpu.VMEM((256, 512), BF),
-         pltpu.VMEM((2, 1024, 128), F32), pltpu.VMEM((8, 256, 128), F32),
-         pltpu.VMEM((1024, 1024), BF), pltpu.VMEM((4, 16, 1024), BF),
-         pltpu.VMEM((2, 512, 1024), BF), pltpu.SemaphoreType.DMA((22,))],
-        2200, 8000, 48, "attention", [H, V, V],
+         pltpu.VMEM((1024, 512), BF), pltpu.VMEM((4, 16, 1024), BF),
+         pltpu.SemaphoreType.DMA((14,))],
+        1700, 6000, 56, "attention", [H, V, V, V, V],
     )(xg, qd, kvg)
 
     red = lax.psum_scatter(pay, "z", scatter_dimension=0, tiled=True)
-    (md,) = call(md_kernel, [V] * 4, [sds((4, 256, 1024))], [], 540, 4000, 16, "md")(
-        att, dq, wq, wo
-    )
-    md = lax.all_to_all(md, "x", split_axis=0, concat_axis=0, tiled=True)
-    md = jnp.sum(md.astype(F32), axis=0)
-    mixed = (tok.astype(F32) + md[0:128]).astype(BF)
-    d_tokens = (cot.astype(F32) + md[128:256]).astype(BF)
+    md = call(md_kernel, [S] + [V] * 4, [sds((256, 1024))] * 4, [], 540, 4000, 16, "md")(
+        pos, att, dq, wq, wo
+    )
+    md = [md[0]] + [shift(m, "x", by) for m, by in zip(md[1:], SHIFTS[1:])]
+    (g,) = call(
+        g_kernel, [H, V, V], [sds((8, 128, 512))],
+        [pltpu.VMEM((2, 512, 1024), BF), pltpu.VMEM((8, 128, 512), BF), pltpu.SemaphoreType.DMA((8,))],
+        540, 4000, 61, "grads", [H],
+    )(xg, at, dqt)
+    g = lax.all_to_all(g, ("y", "c"), split_axis=0, concat_axis=0, tiled=True)
+    gq, go = call(
+        gsum_kernel, [V], [sds((128, 256)), sds((32, 1024))], [], 1, 1200, 16, "gsum"
+    )(g)
+    go = lax.ppermute(
+        go, ("y", "x"), [(a * 4 + b, b * 4 + a) for a in range(4) for b in range(4)]
+    )
+    total = md[0].astype(F32) + md[1].astype(F32) + md[2].astype(F32) + md[3].astype(F32)
+    mixed = (tok.astype(F32) + total[0:128]).astype(BF)
+    d_tokens = (cot.astype(F32) + total[128:256]).astype(BF)
     red, mixed, d_tokens = lax.optimization_barrier((red, mixed, d_tokens))
 
     parts = call(
         part_kernel, [S, V, V], [sds((32, 1024))] * 4,
         [pltpu.VMEM((128, 1024), F32)], 134, 2000, 16, "part",
     )(pos, red, wkv)
-    red, *parts = lax.optimization_barrier((red, *parts))
+    gq, *parts = lax.optimization_barrier((gq, *parts))
     (g,) = call(
-        split_kernel, [S, V], [sds((1280, 128))], [pltpu.VMEM((1280, 128), F32)],
+        split_kernel, [S, V, V], [sds((1280, 128))],
+        [pltpu.VMEM((1280, 128), F32), pltpu.VMEM((2, 128, 128), F32), pltpu.VMEM((8, 32, 128), F32)],
         1, 600, 16, "split",
-    )(pos, red)
+    )(pos, gq, go)
     parts = [parts[0]] + [shift(p, "x", by) for p, by in zip(parts[1:], SHIFTS[1:])]
     g = lax.all_to_all(
-        g.reshape(32, 40, 128), ("y", "c", "x"), split_axis=0, concat_axis=0, tiled=True
+        g.reshape(32, 40, 128), ("x", "z"), split_axis=0, concat_axis=0, tiled=True
     ).reshape(1280, 128)
     d_context, g_query, g_out = call(
         finish_kernel, [V] * 5, [sds((32, 1024)), sds((4, 1024), F32), sds((4, 1024), F32)],

time: 151 us -> 160 us (1.060)
  blocking collectives: 29.3 us -> 0 us
  waiting for transfers between devices: 34.7 us -> 53.2 us
  starting transfers between devices: 37.7 us -> 54.1 us
  Pallas kernels: 26.5 us -> 30.9 us
  local copies, waits for them, and re-layouts: 4.8 us -> 2.93 us
    all_to_all x1 -> x0, blocking collectives: 29.3 us -> none  [local(): md = lax.all_to_all(md, 'x', split_axis=0, concat_axis=0, tiled=True)]
    ppermute x14 -> x17, waiting for transfers between devices: 14.9 us -> 36.9 us  [shift(): return lax.ppermute(value, axis, [(i, (i + by) % n) for i in range(n)])]
    all_to_all x1 -> x2, starting transfers between devices: 7.25 us -> 16.9 us  [the longest x1 12 us: local(): lax.all_to_all(g.reshape(32, 40, 128), ('x', 'z'), split_axis=0, concat_a...]
    reduce_scatter x1, waiting for transfers between devices: 6.73 us -> 0.01 us  [local(): red = lax.psum_scatter(pay, 'z', scatter_dimension=0, tiled=True)]
    pallas_call x3 -> x5, Pallas kernels: 14.8 us -> 19.7 us  [the longest x1 12 us: local(): call(attn_kernel, [H, H, V], [sds((1024, 512)), sds((512, 256)), sds((512...]
    ppermute x14 -> x17, starting transfers between devices: 19.5 us -> 23.4 us  [shift(): return lax.ppermute(value, axis, [(i, (i + by) % n) for i in range(n)])]
    all_to_all x1 -> x2, waiting for transfers between devices: 0.01 us -> 3.28 us  [the longest x1 3.28 us: local(): lax.all_to_all(g.reshape(32, 40, 128), ('x', 'z'), split_axis=0, concat_a...]
    ppermute x0 -> x1, starting transfers between devices: none -> 2.84 us  [local(): lax.ppermute(go, ('y', 'x'), [(a * 4 + b, b * 4 + a) for a in range(4) fo...]
  transfers between devices with their start and end apart: 19 -> 24, of which waited for: 12 -> 17; matrix products, arithmetic and copies ran while one was open for 2% -> 2% of each run, Pallas kernels for 6% -> 9%
where the time goes in v5:
time: 160 us; the launch traced here: 159 us
  starting transfers between devices  54.1 us (34%)
  waiting for transfers between devices  53.2 us (33%)
  Pallas kernels  30.9 us (19%)
  between operations  14.3 us (9%)
  other arithmetic  3.81 us (2%)
  local copies, waits for them, and re-layouts  2.93 us (2%)
    ppermute x17, waiting for transfers between devices, shift(): return lax.ppermute(value, axis, [(i, (i + by) % n) for i in range(n)])  36.9 us
    ppermute x17, starting transfers between devices, shift(): return lax.ppermute(value, axis, [(i, (i + by) % n) for i in range(n)])  23.4 us
    all_to_all x1, starting transfers between devices, local(): lax.all_to_all(g.reshape(32, 40, 128), ('x', 'z'), split_axis=0, concat_a...  12 us
    pallas_call x1, Pallas kernels, local(): call(attn_kernel, [H, H, V], [sds((1024, 512)), sds((512, 256)), sds((512...  12 us
    ppermute x1, waiting for transfers between devices, local(): lax.ppermute(w_out, ('y', 'x'), [(a * 4 + b, b * 4 + a) for a in range(4)...  10.8 us
    all_to_all x1, starting transfers between devices, local(): lax.all_to_all(kv8, 'z', split_axis=0, concat_axis=0, tiled=True)  8.48 us
    all_to_all x1, starting transfers between devices, local(): g = lax.all_to_all(g, ('y', 'c'), split_axis=0, concat_axis=0, tiled=True)  4.89 us
    pallas_call x1, Pallas kernels, local(): call(qd_kernel, [S, H, H, H], [sds((2, 512, 256)), sds((1024, 256)), sds(...  4.66 us
  transfers between devices with their start and end apart: 24, of which 17 were waited for; matrix products, arithmetic and copies ran while one was open for 2% of the time, Pallas kernels for 9%

profile of v5, /device:TPU:8, one launch (start us, length us, event | category | flops | bytes accessed | tf_op | source)
XLA Modules:
  0.0 159.2 jit_solution(5482622307659094796)
XLA Ops:
  7.8 2.8 %pack.1 = (bf16[272,1024]{1,0:T(8,128)(2,1)}, bf16[128,512]{1,0:T(8,128)(2,1)}, bf16[128,256]{1,0:T(8,128)(2,1)}) custom-call(s32[4]{0:T(128)} %pad_add_fusion.pos, bf16[128,1024]{1,0:T(8,128)(2,1)} %bitcast.26, bf16[128,1024]{1,0:T(8,128)(2,1)} %bitcast.27, s32[2,16]{1,0:T(2,128)} %bitcast.30, bf16[128,1024]{1,0:T(8,128)(2,1)} %wk.1, bf16[128,1024]{1,0:T(8,128)(2,1)} %wv.1, ...), custom_call_target="tpu_custom_call" | custom-call | flops 1000000 | bytes 1536000 | tf_op jit(solution)/shard_map/pack/pallas_call | solution.py:290
  10.7 2.4 %collective-permute-start.2 = (bf16[128,512]{1,0:T(8,128)(2,1)}, bf16[128,512]{1,0:T(8,128)(2,1)S(1)}, u32[]{:S(2)}, u32[]{:S(2)}) collective-permute-start(bf16[128,512]{1,0:T(8,128)(2,1)} %get-tuple-element.48), channel_id=1, source_target_pairs={{0,128},{64,192},{128,0},{192,64},{1,129},{65,193},{129,1},{193,65... | collective-permute-start | bytes 393224 | tf_op jit(solution)/shard_map/ppermute | solution.py:20
  13.1 1.3 collective-permute-start.1
  15.1 3.0 %collective-permute-start.5 = (bf16[32,1024]{1,0:T(8,128)(2,1)}, bf16[32,1024]{1,0:T(8,128)(2,1)S(1)}, u32[]{:S(2)}, u32[]{:S(2)}) collective-permute-start(bf16[32,1024]{1,0:T(8,128)(2,1)} %bitcast.18), channel_id=1, source_target_pairs={{0,16},{8,24},{16,0},{24,8},{1,17},{9,25},{17,1},{25,9},{2,18},{10... | collective-permute-start | bytes 196616 | tf_op jit(solution)/shard_map/ppermute | solution.py:20
  22.6 2.4 %collective-permute-done.3.c1 = bf16[32,1024]{1,0:T(8,128)(2,1)S(1)} collective-permute-done((bf16[32,1024]{1,0:T(8,128)(2,1)}, bf16[32,1024]{1,0:T(8,128)(2,1)S(1)}, u32[]{:S(2)}, u32[]{:S(2)}) %collective-permute-start.3) | collective-permute-done | bytes 65568 | tf_op jit(solution)/shard_map/ppermute | solution.py:20
  25.0 1.9 %collective-permute-done.6.wb = bf16[512,512]{1,0:T(8,128)(2,1)S(1)} collective-permute-done((bf16[512,512]{1,0:T(8,128)(2,1)S(1)}, bf16[512,512]{1,0:T(8,128)(2,1)S(1)}, u32[]{:S(2)}, u32[]{:S(2)}) %collective-permute-start.6) | collective-permute-done | bytes 524320 | tf_op jit(solution)/shard_map/ppermute | solution.py:20
  26.9 2.0 %kv.1 = (bf16[8,128,512]{2,1,0:T(8,128)(2,1)}, bf16[1024,512]{1,0:T(8,128)(2,1)S(1)}) custom-call(s32[4]{0:T(128)S(1)} %copy-done.2, bf16[32,1024]{1,0:T(8,128)(2,1)S(1)} %bitcast.21, bf16[32,1024]{1,0:T(8,128)(2,1)S(1)} %collective-permute-done.3.c1, bf16[32,1024]{1,0:T(8,128)(2,1)S(1)} %collective-permute-done.4.c2, ...), custom_call_target="tpu_custom_call" | custom-call | flops 134000000 | bytes 3072000 | tf_op jit(solution)/shard_map/kv/pallas_call | solution.py:302
  28.9 8.5 %all-to-all-start = ((bf16[8,128,512]{2,1,0:T(8,128)(2,1)}), bf16[8,128,512]{2,1,0:T(8,128)(2,1)S(1)}, u32[]{:S(2)}, u32[]{:S(2)}) async-start(bf16[8,128,512]{2,1,0:T(8,128)(2,1)} %get-tuple-element.54), calls=%async_computation | async-start | bytes 2097152 | tf_op jit(solution)/shard_map/all_to_all | solution.py:308
  37.4 2.4 %collective-permute-start.10 = (bf16[128,1024]{1,0:T(8,128)(2,1)S(1)}, bf16[128,1024]{1,0:T(8,128)(2,1)S(1)}, u32[]{:S(2)}, u32[]{:S(2)}) collective-permute-start(bf16[128,1024]{1,0:T(8,128)(2,1)S(1)} %copy-done.12), channel_id=1, source_target_pairs={{0,0},{8,64},{16,128},{24,192},{64,8},{72,72},{80,136},{88,200},{1... | collective-permute-start | bytes 786440 | tf_op jit(solution)/shard_map/ppermute | solution.py:311
  39.8 2.5 %collective-permute-start.9 = (bf16[128,256]{1,0:T(8,128)(2,1)S(1)}, bf16[128,256]{1,0:T(8,128)(2,1)S(1)}, u32[]{:S(2)}, u32[]{:S(2)}) collective-permute-start(bf16[128,256]{1,0:T(8,128)(2,1)S(1)} %copy-done.11), channel_id=1, source_target_pairs={{0,128},{64,192},{128,0},{192,64},{1,129},{65,193},{129,1},{193,65... | collective-permute-start | bytes 196616 | tf_op jit(solution)/shard_map/ppermute | solution.py:20
  42.3 1.8 %collective-permute-start.8 = (bf16[128,256]{1,0:T(8,128)(2,1)S(1)}, bf16[128,256]{1,0:T(8,128)(2,1)S(1)}, u32[]{:S(2)}, u32[]{:S(2)}) collective-permute-start(bf16[128,256]{1,0:T(8,128)(2,1)S(1)} %copy-done.11), channel_id=1, source_target_pairs={{0,192},{64,0},{128,64},{192,128},{1,193},{65,1},{129,65},{193,129... | collective-permute-start | bytes 196616 | tf_op jit(solution)/shard_map/ppermute | solution.py:20
  44.3 10.8 %collective-permute-done.10 = bf16[128,1024]{1,0:T(8,128)(2,1)S(1)} collective-permute-done((bf16[128,1024]{1,0:T(8,128)(2,1)S(1)}, bf16[128,1024]{1,0:T(8,128)(2,1)S(1)}, u32[]{:S(2)}, u32[]{:S(2)}) %collective-permute-start.10) | collective-permute-done | bytes 262176 | tf_op jit(solution)/shard_map/ppermute | solution.py:311
  55.2 2.5 %collective-permute-done.7 = bf16[128,256]{1,0:T(8,128)(2,1)S(1)} collective-permute-done((bf16[128,256]{1,0:T(8,128)(2,1)S(1)}, bf16[128,256]{1,0:T(8,128)(2,1)S(1)}, u32[]{:S(2)}, u32[]{:S(2)}) %collective-permute-start.7) | collective-permute-done | bytes 65568 | tf_op jit(solution)/shard_map/ppermute | solution.py:20
  58.0 2.0 %collective-permute-done.11.wb = bf16[512,512]{1,0:T(8,128)(2,1)} collective-permute-done((bf16[512,512]{1,0:T(8,128)(2,1)S(1)}, bf16[512,512]{1,0:T(8,128)(2,1)}, u32[]{:S(2)}, u32[]{:S(2)}) %collective-permute-start.11) | collective-permute-done | bytes 524320 | tf_op jit(solution)/shard_map/ppermute | solution.py:20
  60.0 4.7 %queries.1 = (bf16[2,512,256]{2,1,0:T(8,128)(2,1)}, bf16[1024,256]{1,0:T(8,128)(2,1)}, bf16[256,1024]{1,0:T(8,128)(2,1)}) custom-call(s32[4]{0:T(128)} %pad_add_fusion.pos, bf16[4,272,1024]{2,1,0:T(8,128)(2,1)} %bitcast.22, bf16[512,512]{1,0:T(8,128)(2,1)} %copy-done.8, bf16[512,512]{1,0:T(8,128)(2,1)} %collective-permute-done.11.wb), custom_call_target="tpu_custom_call" | custom-call | flops 540000000 | bytes 5120000 | tf_op jit(solution)/shard_map/queries/pallas_call | solution.py:318
  64.7 1.8 %all-to-all-done = bf16[8,128,512]{2,1,0:T(8,128)(2,1)S(1)} async-done(((bf16[8,128,512]{2,1,0:T(8,128)(2,1)}), bf16[8,128,512]{2,1,0:T(8,128)(2,1)S(1)}, u32[]{:S(2)}, u32[]{:S(2)}) %all-to-all-start) | async-done | bytes 1048608 | tf_op jit(solution)/shard_map/all_to_all | solution.py:308
  67.5 12.0 %attention.1 = (bf16[1024,512]{1,0:T(8,128)(2,1)}, bf16[512,256]{1,0:T(8,128)(2,1)}, bf16[512,256]{1,0:T(8,128)(2,1)}, bf16[256,512]{1,0:T(8,128)(2,1)}, bf16[256,512]{1,0:T(8,128)(2,1)}) custom-call(bf16[4,272,1024]{2,1,0:T(8,128)(2,1)} %bitcast.23, bf16[2,512,256]{2,1,0:T(8,128)(2,1)} %get-tuple-element.57.qd, bf16[1024,512]{1,0:T(8,128)(2,1)} %bitcast.25), custom_call_target="tpu_custom_call" | custom-call | flops 1700000000 | bytes 6144000 | tf_op jit(solution)/shard_map/attention/pallas_call | solution.py:326
  79.5 4.5 %grads.1 = bf16[8,128,512]{2,1,0:T(8,128)(2,1)} custom-call(bf16[4,272,1024]{2,1,0:T(8,128)(2,1)} %bitcast.24, bf16[256,512]{1,0:T(8,128)(2,1)} %get-tuple-element.69.at, bf16[256,512]{1,0:T(8,128)(2,1)} %get-tuple-element.70.dqt), custom_call_target="tpu_custom_call" | custom-call | flops 540000000 | bytes 4096000 | tf_op jit(solution)/shard_map/grads/pallas_call | solution.py:342
  84.0 4.9 %all-to-all-start.1 = ((bf16[8,128,512]{2,1,0:T(8,128)(2,1)}), bf16[8,128,512]{2,1,0:T(8,128)(2,1)S(1)}, u32[]{:S(2)}, u32[]{:S(2)}) async-start(bf16[8,128,512]{2,1,0:T(8,128)(2,1)} %grads.1), calls=%async_computation.2 | async-start | bytes 2097152 | tf_op jit(solution)/shard_map/all_to_all | solution.py:347
  89.9 1.7 %md.1 = (bf16[256,1024]{1,0:T(8,128)(2,1)S(1)}, bf16[256,1024]{1,0:T(8,128)(2,1)S(1)}, bf16[256,1024]{1,0:T(8,128)(2,1)S(1)}, bf16[256,1024]{1,0:T(8,128)(2,1)S(1)}) custom-call(s32[4]{0:T(128)S(1)} %copy-done.3, bf16[512,256]{1,0:T(8,128)(2,1)S(1)} %copy-done.6, bf16[512,256]{1,0:T(8,128)(2,1)S(1)} %copy-done.7, bf16[1024,256]{1,0:T(8,128)(2,1)S(1)} %copy-done.4, ...), custom_call_target="tpu_custom_call" | custom-call | flops 540000000 | bytes 4096000 | tf_op jit(solution)/shard_map/md/pallas_call | solution.py:338
  91.8 3.1 %collective-permute-start.13 = (bf16[256,1024]{1,0:T(8,128)(2,1)S(1)}, bf16[256,1024]{1,0:T(8,128)(2,1)S(1)}, u32[]{:S(2)}, u32[]{:S(2)}) collective-permute-start(bf16[256,1024]{1,0:T(8,128)(2,1)S(1)} %get-tuple-element.65), channel_id=1, source_target_pairs={{0,24},{8,0},{16,8},{24,16},{1,25},{9,1},{17,9},{25,17},{2,26},{10... | collective-permute-start | bytes 1572872 | tf_op jit(solution)/shard_map/ppermute | solution.py:20
  95.2 12.4 %collective-permute-done.12 = bf16[256,1024]{1,0:T(8,128)(2,1)S(1)} collective-permute-done((bf16[256,1024]{1,0:T(8,128)(2,1)S(1)}, bf16[256,1024]{1,0:T(8,128)(2,1)S(1)}, u32[]{:S(2)}, u32[]{:S(2)}) %collective-permute-start.12) | collective-permute-done | bytes 524320 | tf_op jit(solution)/shard_map/ppermute | solution.py:20
  107.6 9.8 %collective-permute-done.13 = bf16[256,1024]{1,0:T(8,128)(2,1)S(1)} collective-permute-done((bf16[256,1024]{1,0:T(8,128)(2,1)S(1)}, bf16[256,1024]{1,0:T(8,128)(2,1)S(1)}, u32[]{:S(2)}, u32[]{:S(2)}) %collective-permute-start.13) | collective-permute-done | bytes 524320 | tf_op jit(solution)/shard_map/ppermute | solution.py:20
  118.7 2.8 %collective-permute-start.15 = (bf16[32,1024]{1,0:T(8,128)(2,1)S(1)}, bf16[32,1024]{1,0:T(8,128)(2,1)S(1)}, u32[]{:S(2)}, u32[]{:S(2)}) collective-permute-start(bf16[32,1024]{1,0:T(8,128)(2,1)S(1)} %get-tuple-element.79), channel_id=1, source_target_pairs={{0,0},{8,64},{16,128},{24,192},{64,8},{72,72},{80,136},{88,200},{1... | collective-permute-start | bytes 196616 | tf_op jit(solution)/shard_map/ppermute | solution.py:351
  121.5 1.9 %fusion = (bf16[128,1024]{1,0:T(8,128)(2,1)}, bf16[128,1024]{1,0:T(8,128)(2,1)}) fusion(f32[256,1024]{1,0:T(8,128)S(1)} %convert_add_fusion, bf16[1,128,1024]{2,1,0:T(8,128)(2,1)} %param.15, bf16[1,128,1024]{2,1,0:T(8,128)(2,1)S(1)} %copy-done.10), kind=kLoop, calls=%fused_computation.2 | loop fusion | flops 786432 | bytes 2097152 | tf_op jit(solution)/shard_map/convert_element_type | solution.py:356
  125.7 1.4 split.1
  127.1 12.0 %all-to-all-start.2 = ((bf16[32,40,128]{2,1,0:T(8,128)(2,1)}), bf16[32,40,128]{2,1,0:T(8,128)(2,1)S(1)}, u32[]{:S(2)}, u32[]{:S(2)}) async-start(bf16[32,40,128]{2,1,0:T(8,128)(2,1)} %bitcast.12), calls=%async_computation.3 | async-start | bytes 655360 | tf_op jit(solution)/shard_map/all_to_all | solution.py:370
  139.1 1.9 %collective-permute-start.16 = (bf16[32,1024]{1,0:T(8,128)(2,1)S(1)}, bf16[32,1024]{1,0:T(8,128)(2,1)S(1)}, u32[]{:S(2)}, u32[]{:S(2)}) collective-permute-start(bf16[32,1024]{1,0:T(8,128)(2,1)S(1)} %get-tuple-element.81), channel_id=1, source_target_pairs={{0,8},{8,16},{16,24},{24,0},{1,9},{9,17},{17,25},{25,1},{2,10},{10... | collective-permute-start | bytes 196616 | tf_op jit(solution)/shard_map/ppermute | solution.py:20
  141.0 1.4 collective-permute-start.17
  142.4 2.1 %collective-permute-start.18 = (bf16[32,1024]{1,0:T(8,128)(2,1)S(1)}, bf16[32,1024]{1,0:T(8,128)(2,1)S(1)}, u32[]{:S(2)}, u32[]{:S(2)}) collective-permute-start(bf16[32,1024]{1,0:T(8,128)(2,1)S(1)} %get-tuple-element.83), channel_id=1, source_target_pairs={{0,16},{8,24},{16,0},{24,8},{1,17},{9,25},{17,1},{25,9},{2,18},{10... | collective-permute-start | bytes 196616 | tf_op jit(solution)/shard_map/ppermute | solution.py:20
  145.9 2.5 %collective-permute-done.18.p3 = bf16[32,1024]{1,0:T(8,128)(2,1)S(1)} collective-permute-done((bf16[32,1024]{1,0:T(8,128)(2,1)S(1)}, bf16[32,1024]{1,0:T(8,128)(2,1)S(1)}, u32[]{:S(2)}, u32[]{:S(2)}) %collective-permute-start.18) | collective-permute-done | bytes 65568 | tf_op jit(solution)/shard_map/ppermute | solution.py:20
  148.4 3.3 %all-to-all-done.2 = bf16[32,40,128]{2,1,0:T(8,128)(2,1)S(1)} async-done(((bf16[32,40,128]{2,1,0:T(8,128)(2,1)}), bf16[32,40,128]{2,1,0:T(8,128)(2,1)S(1)}, u32[]{:S(2)}, u32[]{:S(2)}) %all-to-all-start.2) | async-done | bytes 327712 | tf_op jit(solution)/shard_map/all_to_all | solution.py:370
  (60 shorter events, 14.6 us)
Async XLA Ops:
  7.2 19.7 %copy-start.1 = (bf16[1,32,1024]{2,1,0:T(8,128)(2,1)S(1)}, bf16[1,32,1024]{2,1,0:T(8,128)(2,1)}, u32[]{:S(2)}) copy-start(bf16[1,32,1024]{2,1,0:T(8,128)(2,1)} %param.9) | copy-start | bytes 196612
  7.2 52.8 %all-gather.3.cloned.1.call-start = ((), (), s32[]{:S(2)}) async-start(), calls=%async_computation.5 | async-start | bytes 2785280 | tf_op jit(solution)/shard_map/all_gather | solution.py:296
  7.8 19.0 %copy-start.2 = (s32[4]{0:T(128)S(1)}, s32[4]{0:T(128)}, u32[]{:S(2)}) copy-start(s32[4]{0:T(128)} %pad_add_fusion.pos) | copy-start | bytes 52
  10.7 8.6 %collective-permute-start.2 = (bf16[128,512]{1,0:T(8,128)(2,1)}, bf16[128,512]{1,0:T(8,128)(2,1)S(1)}, u32[]{:S(2)}, u32[]{:S(2)}) collective-permute-start(bf16[128,512]{1,0:T(8,128)(2,1)} %get-tuple-element.48), channel_id=1, source_target_pairs={{0,128},{64,192},{128,0},{192,64},{1,129},{65,193},{129,1},{193,65... | collective-permute-start | bytes 393224 | tf_op jit(solution)/shard_map/ppermute | solution.py:20
  13.1 7.5 %collective-permute-start.1 = (bf16[128,512]{1,0:T(8,128)(2,1)}, bf16[128,512]{1,0:T(8,128)(2,1)S(1)}, u32[]{:S(2)}, u32[]{:S(2)}) collective-permute-start(bf16[128,512]{1,0:T(8,128)(2,1)} %get-tuple-element.48), channel_id=1, source_target_pairs={{0,192},{64,0},{128,64},{192,128},{1,193},{65,1},{129,65},{193,129... | collective-permute-start | bytes 393224 | tf_op jit(solution)/shard_map/ppermute | solution.py:20
  14.4 6.2 %collective-permute-start = (bf16[128,512]{1,0:T(8,128)(2,1)}, bf16[128,512]{1,0:T(8,128)(2,1)S(1)}, u32[]{:S(2)}, u32[]{:S(2)}) collective-permute-start(bf16[128,512]{1,0:T(8,128)(2,1)} %get-tuple-element.48), channel_id=1, source_target_pairs={{0,64},{64,128},{128,192},{192,0},{1,65},{65,129},{129,193},{193,1... | collective-permute-start | bytes 393224 | tf_op jit(solution)/shard_map/ppermute | solution.py:20
  15.1 22.3 %copy-start.12 = (bf16[128,1024]{1,0:T(8,128)(2,1)S(1)}, bf16[128,1024]{1,0:T(8,128)(2,1)}, u32[]{:S(2)}) copy-start(bf16[128,1024]{1,0:T(8,128)(2,1)} %param.14) | copy-start | bytes 786436
  15.1 24.7 %copy-start.11 = (bf16[128,256]{1,0:T(8,128)(2,1)S(1)}, bf16[128,256]{1,0:T(8,128)(2,1)}, u32[]{:S(2)}) copy-start(bf16[128,256]{1,0:T(8,128)(2,1)} %get-tuple-element.55) | copy-start | bytes 196612
  15.1 6.5 %collective-permute-start.5 = (bf16[32,1024]{1,0:T(8,128)(2,1)}, bf16[32,1024]{1,0:T(8,128)(2,1)S(1)}, u32[]{:S(2)}, u32[]{:S(2)}) collective-permute-start(bf16[32,1024]{1,0:T(8,128)(2,1)} %bitcast.18), channel_id=1, source_target_pairs={{0,16},{8,24},{16,0},{24,8},{1,17},{9,25},{17,1},{25,9},{2,18},{10... | collective-permute-start | bytes 196616 | tf_op jit(solution)/shard_map/ppermute | solution.py:20
  18.1 4.5 %collective-permute-start.4 = (bf16[32,1024]{1,0:T(8,128)(2,1)}, bf16[32,1024]{1,0:T(8,128)(2,1)S(1)}, u32[]{:S(2)}, u32[]{:S(2)}) collective-permute-start(bf16[32,1024]{1,0:T(8,128)(2,1)} %bitcast.19), channel_id=1, source_target_pairs={{0,24},{8,0},{16,8},{24,16},{1,25},{9,1},{17,9},{25,17},{2,26},{10... | collective-permute-start | bytes 196616 | tf_op jit(solution)/shard_map/ppermute | solution.py:20
  19.3 5.7 %collective-permute-start.3 = (bf16[32,1024]{1,0:T(8,128)(2,1)}, bf16[32,1024]{1,0:T(8,128)(2,1)S(1)}, u32[]{:S(2)}, u32[]{:S(2)}) collective-permute-start(bf16[32,1024]{1,0:T(8,128)(2,1)} %bitcast.20), channel_id=1, source_target_pairs={{0,8},{8,16},{16,24},{24,0},{1,9},{9,17},{17,25},{25,1},{2,10},{10... | collective-permute-start | bytes 196616 | tf_op jit(solution)/shard_map/ppermute | solution.py:20
  25.0 1.9 %collective-permute-start.6 = (bf16[512,512]{1,0:T(8,128)(2,1)S(1)}, bf16[512,512]{1,0:T(8,128)(2,1)S(1)}, u32[]{:S(2)}, u32[]{:S(2)}) collective-permute-start(bf16[512,512]{1,0:T(8,128)(2,1)S(1)} %pad_maximum_fusion.wa), channel_id=1, source_target_pairs={{0,32},{32,0},{1,33},{33,1},{2,34},{34,2},{3,35},{35,3},{4,36},{36... | collective-permute-start | bytes 1572872 | tf_op jit(solution)/shard_map/ppermute | solution.py:20
  28.9 37.6 %all-to-all-start = ((bf16[8,128,512]{2,1,0:T(8,128)(2,1)}), bf16[8,128,512]{2,1,0:T(8,128)(2,1)S(1)}, u32[]{:S(2)}, u32[]{:S(2)}) async-start(bf16[8,128,512]{2,1,0:T(8,128)(2,1)} %get-tuple-element.54), calls=%async_computation | async-start | bytes 2097152 | tf_op jit(solution)/shard_map/all_to_all | solution.py:308
  37.4 86.0 %reduce-scatter.2.cloned.1.call-start = ((), (), s32[]{:S(2)}) async-start(), calls=%async_computation.4 | async-start | bytes 1179648 | tf_op jit(solution)/shard_map/reduce_scatter | solution.py:337
  37.4 17.7 %collective-permute-start.10 = (bf16[128,1024]{1,0:T(8,128)(2,1)S(1)}, bf16[128,1024]{1,0:T(8,128)(2,1)S(1)}, u32[]{:S(2)}, u32[]{:S(2)}) collective-permute-start(bf16[128,1024]{1,0:T(8,128)(2,1)S(1)} %copy-done.12), channel_id=1, source_target_pairs={{0,0},{8,64},{16,128},{24,192},{64,8},{72,72},{80,136},{88,200},{1... | collective-permute-start | bytes 786440 | tf_op jit(solution)/shard_map/ppermute | solution.py:311
  39.8 15.4 %collective-permute-start.9 = (bf16[128,256]{1,0:T(8,128)(2,1)S(1)}, bf16[128,256]{1,0:T(8,128)(2,1)S(1)}, u32[]{:S(2)}, u32[]{:S(2)}) collective-permute-start(bf16[128,256]{1,0:T(8,128)(2,1)S(1)} %copy-done.11), channel_id=1, source_target_pairs={{0,128},{64,192},{128,0},{192,64},{1,129},{65,193},{129,1},{193,65... | collective-permute-start | bytes 196616 | tf_op jit(solution)/shard_map/ppermute | solution.py:20
  42.3 12.9 %collective-permute-start.8 = (bf16[128,256]{1,0:T(8,128)(2,1)S(1)}, bf16[128,256]{1,0:T(8,128)(2,1)S(1)}, u32[]{:S(2)}, u32[]{:S(2)}) collective-permute-start(bf16[128,256]{1,0:T(8,128)(2,1)S(1)} %copy-done.11), channel_id=1, source_target_pairs={{0,192},{64,0},{128,64},{192,128},{1,193},{65,1},{129,65},{193,129... | collective-permute-start | bytes 196616 | tf_op jit(solution)/shard_map/ppermute | solution.py:20
  44.1 13.6 %collective-permute-start.7 = (bf16[128,256]{1,0:T(8,128)(2,1)S(1)}, bf16[128,256]{1,0:T(8,128)(2,1)S(1)}, u32[]{:S(2)}, u32[]{:S(2)}) collective-permute-start(bf16[128,256]{1,0:T(8,128)(2,1)S(1)} %copy-done.11), channel_id=1, source_target_pairs={{0,64},{64,128},{128,192},{192,0},{1,65},{65,129},{129,193},{193,1... | collective-permute-start | bytes 196616 | tf_op jit(solution)/shard_map/ppermute | solution.py:20
  57.7 2.3 %collective-permute-start.11 = (bf16[512,512]{1,0:T(8,128)(2,1)S(1)}, bf16[512,512]{1,0:T(8,128)(2,1)}, u32[]{:S(2)}, u32[]{:S(2)}) collective-permute-start(bf16[512,512]{1,0:T(8,128)(2,1)S(1)} %maximum_maximum_fusion.wa), channel_id=1, source_target_pairs={{0,32},{32,0},{1,33},{33,1},{2,34},{34,2},{3,35},{35,3},{4,36},{36... | collective-permute-start | bytes 1572872 | tf_op jit(solution)/shard_map/ppermute | solution.py:20
  79.5 9.4 %copy-start.3 = (s32[4]{0:T(128)S(1)}, s32[4]{0:T(128)}, u32[]{:S(2)}) copy-start(s32[4]{0:T(128)} %pad_add_fusion.pos) | copy-start | bytes 52
  79.5 9.4 %copy-start.4 = (bf16[1024,256]{1,0:T(8,128)(2,1)S(1)}, bf16[1024,256]{1,0:T(8,128)(2,1)}, u32[]{:S(2)}) copy-start(bf16[1024,256]{1,0:T(8,128)(2,1)} %get-tuple-element.61.wq) | copy-start | bytes 1572868
  79.5 9.4 %copy-start.5 = (bf16[256,1024]{1,0:T(8,128)(2,1)S(1)}, bf16[256,1024]{1,0:T(8,128)(2,1)}, u32[]{:S(2)}) copy-start(bf16[256,1024]{1,0:T(8,128)(2,1)} %get-tuple-element.62.wo) | copy-start | bytes 1572868
  84.0 34.5 %all-to-all-start.1 = ((bf16[8,128,512]{2,1,0:T(8,128)(2,1)}), bf16[8,128,512]{2,1,0:T(8,128)(2,1)S(1)}, u32[]{:S(2)}, u32[]{:S(2)}) async-start(bf16[8,128,512]{2,1,0:T(8,128)(2,1)} %grads.1), calls=%async_computation.2 | async-start | bytes 2097152 | tf_op jit(solution)/shard_map/all_to_all | solution.py:347
  91.6 29.9 %copy-start.10 = (bf16[1,128,1024]{2,1,0:T(8,128)(2,1)S(1)}, bf16[1,128,1024]{2,1,0:T(8,128)(2,1)}, u32[]{:S(2)}) copy-start(bf16[1,128,1024]{2,1,0:T(8,128)(2,1)} %param.8) | copy-start | bytes 786436
  91.6 16.0 %collective-permute-start.12 = (bf16[256,1024]{1,0:T(8,128)(2,1)S(1)}, bf16[256,1024]{1,0:T(8,128)(2,1)S(1)}, u32[]{:S(2)}, u32[]{:S(2)}) collective-permute-start(bf16[256,1024]{1,0:T(8,128)(2,1)S(1)} %get-tuple-element.64), channel_id=1, source_target_pairs={{0,8},{8,16},{16,24},{24,0},{1,9},{9,17},{17,25},{25,1},{2,10},{10... | collective-permute-start | bytes 1572872 | tf_op jit(solution)/shard_map/ppermute | solution.py:20
  91.8 25.5 %collective-permute-start.13 = (bf16[256,1024]{1,0:T(8,128)(2,1)S(1)}, bf16[256,1024]{1,0:T(8,128)(2,1)S(1)}, u32[]{:S(2)}, u32[]{:S(2)}) collective-permute-start(bf16[256,1024]{1,0:T(8,128)(2,1)S(1)} %get-tuple-element.65), channel_id=1, source_target_pairs={{0,24},{8,0},{16,8},{24,16},{1,25},{9,1},{17,9},{25,17},{2,26},{10... | collective-permute-start | bytes 1572872 | tf_op jit(solution)/shard_map/ppermute | solution.py:20
  94.9 23.3 %collective-permute-start.14 = (bf16[256,1024]{1,0:T(8,128)(2,1)S(1)}, bf16[256,1024]{1,0:T(8,128)(2,1)S(1)}, u32[]{:S(2)}, u32[]{:S(2)}) collective-permute-start(bf16[256,1024]{1,0:T(8,128)(2,1)S(1)} %get-tuple-element.66), channel_id=1, source_target_pairs={{0,16},{8,24},{16,0},{24,8},{1,17},{9,25},{17,1},{25,9},{2,18},{10... | collective-permute-start | bytes 1572872 | tf_op jit(solution)/shard_map/ppermute | solution.py:20
  118.7 7.1 %collective-permute-start.15 = (bf16[32,1024]{1,0:T(8,128)(2,1)S(1)}, bf16[32,1024]{1,0:T(8,128)(2,1)S(1)}, u32[]{:S(2)}, u32[]{:S(2)}) collective-permute-start(bf16[32,1024]{1,0:T(8,128)(2,1)S(1)} %get-tuple-element.79), channel_id=1, source_target_pairs={{0,0},{8,64},{16,128},{24,192},{64,8},{72,72},{80,136},{88,200},{1... | collective-permute-start | bytes 196616 | tf_op jit(solution)/shard_map/ppermute | solution.py:351
  127.1 24.6 %all-to-all-start.2 = ((bf16[32,40,128]{2,1,0:T(8,128)(2,1)}), bf16[32,40,128]{2,1,0:T(8,128)(2,1)S(1)}, u32[]{:S(2)}, u32[]{:S(2)}) async-start(bf16[32,40,128]{2,1,0:T(8,128)(2,1)} %bitcast.12), calls=%async_computation.3 | async-start | bytes 655360 | tf_op jit(solution)/shard_map/all_to_all | solution.py:370
  139.1 6.3 %collective-permute-start.16 = (bf16[32,1024]{1,0:T(8,128)(2,1)S(1)}, bf16[32,1024]{1,0:T(8,128)(2,1)S(1)}, u32[]{:S(2)}, u32[]{:S(2)}) collective-permute-start(bf16[32,1024]{1,0:T(8,128)(2,1)S(1)} %get-tuple-element.81), channel_id=1, source_target_pairs={{0,8},{8,16},{16,24},{24,0},{1,9},{9,17},{17,25},{25,1},{2,10},{10... | collective-permute-start | bytes 196616 | tf_op jit(solution)/shard_map/ppermute | solution.py:20
  141.0 4.9 %collective-permute-start.17 = (bf16[32,1024]{1,0:T(8,128)(2,1)S(1)}, bf16[32,1024]{1,0:T(8,128)(2,1)S(1)}, u32[]{:S(2)}, u32[]{:S(2)}) collective-permute-start(bf16[32,1024]{1,0:T(8,128)(2,1)S(1)} %get-tuple-element.82), channel_id=1, source_target_pairs={{0,24},{8,0},{16,8},{24,16},{1,25},{9,1},{17,9},{25,17},{2,26},{10... | collective-permute-start | bytes 196616 | tf_op jit(solution)/shard_map/ppermute | solution.py:20
  142.4 6.0 %collective-permute-start.18 = (bf16[32,1024]{1,0:T(8,128)(2,1)S(1)}, bf16[32,1024]{1,0:T(8,128)(2,1)S(1)}, u32[]{:S(2)}, u32[]{:S(2)}) collective-permute-start(bf16[32,1024]{1,0:T(8,128)(2,1)S(1)} %get-tuple-element.83), channel_id=1, source_target_pairs={{0,16},{8,24},{16,0},{24,8},{1,17},{9,25},{17,1},{25,9},{2,18},{10... | collective-permute-start | bytes 196616 | tf_op jit(solution)/shard_map/ppermute | solution.py:20
  (5 other events, 14.6 us)
Sparse Core Ops, SparseCore 0:
  10.8 38.8 all-gather.2
  79.6 37.1 reduce-scatter.1

commit v6 on v4

--- a/solution.py
+++ b/solution.py
@@ -8,6 +8,7 @@
 BF = jnp.bfloat16
 F32 = jnp.float32
 SHIFTS = (0, 1, -1, 2)
+Z_SHIFTS = (0, 4, 3, -3, 2, -2, 1, -1)
 SIZES = {"y": 4, "c": 2, "x": 4, "z": 8}
 
 
@@ -36,16 +37,16 @@
         copy.wait()
 
 
-def pack_kernel(pos, tok, cot, pattern, wk, wv, wq, out, kv_cut, q_cut, pat_s, x_s, kv_s, q_s, sems):
-    cols = pl.ds(pl.multiple_of(256 * pos[2], 256), 256)
+def pack_kernel(tok, cot, pattern, wk, wv, wq, out, cut, pat_s, x_s, w_s, sems):
+    cols = pl.ds(pl.multiple_of(256 * lax.axis_index("x"), 256), 256)
     copies = run_copies(
         [
             (pattern, pat_s),
-            (wk.at[:, cols], kv_s.at[:, pl.ds(0, 256)]),
-            (wv.at[:, cols], kv_s.at[:, pl.ds(256, 256)]),
+            (wk.at[:, cols], w_s.at[:, pl.ds(0, 256)]),
+            (wv.at[:, cols], w_s.at[:, pl.ds(256, 256)]),
             (tok, x_s.at[pl.ds(0, 128), :]),
             (cot, x_s.at[pl.ds(128, 128), :]),
-            (wq.at[:, cols], q_s),
+            (wq.at[:, cols], w_s.at[:, pl.ds(512, 256)]),
         ],
         sems,
     )
@@ -57,47 +58,41 @@
     rows = jnp.concatenate([rows, jnp.zeros((14, 16), BF)], axis=0)
     x_s[256:272, :] = dot(rows, grow, 1, 0).astype(BF)
     wait_all(copies[1:])
-    wait_all(run_copies([(x_s, out), (kv_s, kv_cut), (q_s, q_cut)], sems))
-
-
-def kv_kernel(pos, c0, c1, c2, c3, wa, wb, kv_out, w_out, ctx, w_s, kv_s, sems):
-    y, c, x = pos[0], pos[1], pos[2]
+    wait_all(run_copies([(w_s, cut), (x_s, out)], sems))
+
+
+def kv_kernel(c0, c1, c2, c3, wa, wb, kv_out, w_out, wq_out, wo_out, ctx, w_s, wq_s, wo_s, sems):
+    y, c, x = lax.axis_index("y"), lax.axis_index("c"), lax.axis_index("x")
     for half, core in ((wa, c), (wb, 1 - c)):
         for slot, by in enumerate(SHIFTS):
+            rows = slice(128 * slot, 128 * slot + 128)
             at = pl.multiple_of(128 * (2 * mod(y - by, 4) + core), 128)
-            w_s[pl.ds(at, 128), :] = half[128 * slot : 128 * slot + 128, :]
+            w_s[pl.ds(at, 128), :] = half[rows, 0:512]
+            wq_s[pl.ds(at, 128), :] = half[rows, 512:768]
+            at = pl.multiple_of(128 * core, 128)
+            wo_s[pl.ds(at, 128), 256 * slot : 256 * slot + 256] = half[rows, 768:1024]
+    copies = run_copies([(w_s, w_out), (wq_s, wq_out), (wo_s, wo_out)], sems)
     for src, by in zip((c0, c1, c2, c3), SHIFTS):
         at = pl.multiple_of(32 * mod(x - by, 4), 32)
         ctx[pl.ds(at, 32), :] = src[...]
-    kv_s[...] = dot(ctx[...], w_s[...], 1, 0).astype(BF)
-    pairs = [(kv_s, kv_out.at[zd]) for zd in range(8)] + [(w_s, w_out)]
-    wait_all(run_copies(pairs, sems))
-
-
-def qd_kernel(pos, xg, wa, wb, qd_out, wq_out, wo_out, x_s, wq_s, wo_s, q_s, da_s, sems):
-    y, c = pos[0], pos[1]
-    pairs = []
-    for half, core in ((wa, c), (wb, 1 - c)):
-        for slot, by in enumerate(SHIFTS):
-            rows = pl.ds(128 * slot, 128)
-            at = pl.multiple_of(128 * (2 * mod(y - by, 4) + core), 128)
-            pairs.append((half.at[rows, pl.ds(0, 256)], wq_s.at[pl.ds(at, 128), :]))
-            at = pl.multiple_of(128 * core, 128)
-            lanes = pl.ds(256 * slot, 256)
-            pairs.append((half.at[rows, pl.ds(256, 256)], wo_s.at[pl.ds(at, 128), lanes]))
+    kv_out[...] = dot(ctx[...], w_s[...], 1, 0).astype(BF)
+    wait_all(copies)
+
+
+def qd_kernel(xg, wq, wo, qd_out, x_s, wq_s, wo_s, qd_s, sems):
+    pairs = [(wq, wq_s), (wo, wo_s)]
     for t in range(4):
         for k in range(2):
             rows = pl.ds(128 * t, 128)
             pairs.append((xg.at[t, pl.ds(128 * k, 128), :], x_s.at[k, rows, :]))
     wait_all(run_copies(pairs, sems))
     q = dot(x_s[0], wq_s[...], 1, 0).astype(BF)
-    q_s[...] = q * jnp.asarray(0.125, BF)
-    da_s[...] = dot(x_s[1], wo_s[...], 1, 1).astype(BF)
-    pairs = [(q_s, qd_out.at[0]), (da_s, qd_out.at[1]), (wq_s, wq_out), (wo_s, wo_out)]
-    wait_all(run_copies(pairs, sems))
-
-
-def attn_kernel(xg, qd, kv, pay, att_out, dq_out, q_s, da_s,
+    qd_s[0] = q * jnp.asarray(0.125, BF)
+    qd_s[1] = dot(x_s[1], wo_s[...], 1, 1).astype(BF)
+    wait_all(run_copies([(qd_s, qd_out)], sems))
+
+
+def attn_kernel(xg, qd, kv0, kv1, kv2, kv3, kv4, kv5, kv6, kv7, pay, att_out, dq_out, kv, q_s, da_s,
                 kt_s, vt_s, dk_s, dv_s, at_s, dqt_s, gq_s, go_s, pay_s, mask_s, x_s, sems):
     mask_copies = [
         pltpu.make_async_copy(xg.at[t, pl.ds(256, 16), :], mask_s.at[t], sems.at[t])
@@ -114,6 +109,10 @@
     mask_copies.append(pltpu.make_async_copy(qd.at[1], da_s, sems.at[21]))
     for copy in mask_copies + x_copies:
         copy.start()
+    z = lax.axis_index("z")
+    for src, by in zip((kv0, kv1, kv2, kv3, kv4, kv5, kv6, kv7), Z_SHIFTS):
+        at = pl.multiple_of(128 * mod(z - by, 8), 128)
+        kv[pl.ds(at, 128), :] = src[...]
     kt_s[...] = kv[:, 0:256].T
     vt_s[...] = kv[:, 256:512].T
     dk_s[...] = jnp.zeros_like(dk_s)
@@ -208,16 +207,12 @@
         out[t, 128:256, :] = dot(dq[rows, :], wq[...], 1, 1).astype(BF)
 
 
-def part_kernel(pos, red, w, p0, p1, p2, p3, part):
-    x = pos[2]
+def split_kernel(red, w, p0, p1, p2, p3, g_out, part, g_s):
+    x = lax.axis_index("x")
     part[...] = dot(red[:, 0:256], w[:, 0:256], 1, 1) + dot(red[:, 256:512], w[:, 256:512], 1, 1)
     for out, by in zip((p0, p1, p2, p3), SHIFTS):
         at = pl.multiple_of(32 * mod(x + by, 4), 32)
         out[...] = part[pl.ds(at, 32), :].astype(BF)
-
-
-def split_kernel(pos, red, g_out, g_s):
-    x = pos[2]
     g_s[...] = jnp.zeros_like(g_s)
     for i in range(4):
         for j in range(2):
@@ -258,7 +253,6 @@
 
 
 V = pl.BlockSpec(memory_space=pltpu.VMEM)
-S = pl.BlockSpec(memory_space=pltpu.SMEM)
 H = pl.BlockSpec(memory_space=pltpu.HBM)
 
 
@@ -282,49 +276,43 @@
 
 
 def local(tokens, context, pattern, w_query, w_key, w_value, w_out, cotangent):
-    y, c, x, z = (lax.axis_index(n) for n in ("y", "c", "x", "z"))
-    pos = jnp.stack([y, c, x, z]).astype(jnp.int32)
     tok, ctx, cot = tokens[0], context[0], cotangent[0]
-    own, mine, mine_q = call(
-        pack_kernel, [S] + [H] * 6, [sds((272, 1024)), sds((128, 512)), sds((128, 256))],
-        [pltpu.VMEM((2, 16), jnp.int32), pltpu.VMEM((272, 1024), BF), pltpu.VMEM((128, 512), BF),
-         pltpu.VMEM((128, 256), BF), pltpu.SemaphoreType.DMA((6,))],
-        1, 1500, 61, "pack", [H] * 3,
-    )(pos, tok, cot, pattern[0], w_key, w_value, w_query)
+    own, mine = call(
+        pack_kernel, [H] * 6, [sds((272, 1024)), sds((128, 768))],
+        [pltpu.VMEM((2, 16), jnp.int32), pltpu.VMEM((272, 1024), BF), pltpu.VMEM((128, 768), BF),
+         pltpu.SemaphoreType.DMA((6,))],
+        1, 1500, 61, "pack", [H] * 2,
+    )(tok, cot, pattern[0], w_key, w_value, w_query)
     xg = lax.all_gather(own, "x", axis=0, tiled=False)
 
+    wo = lax.ppermute(
+        w_out, ("y", "x"), [(a * 4 + b, b * 4 + a) for a in range(4) for b in range(4)]
+    )
+    wo = jnp.concatenate([wo[:, 256 * j : 256 * j + 256] for j in range(4)], axis=0)
     ctxs = [ctx] + [shift(ctx, "x", by) for by in SHIFTS[1:]]
     wa = jnp.concatenate([mine] + [shift(mine, "y", by) for by in SHIFTS[1:]], axis=0)
+    wa = jnp.concatenate([wa, wo], axis=1)
     wa, *ctxs = lax.optimization_barrier((wa, *ctxs))
     wb = shift(wa, "c", 1)
-    kv8, wkv = call(
-        kv_kernel, [S] + [V] * 6, [sds((8, 128, 512)), sds((1024, 512))],
-        [pltpu.VMEM((128, 1024), BF), pltpu.VMEM((1024, 512), BF), pltpu.VMEM((128, 512), BF),
-         pltpu.SemaphoreType.DMA((9,))],
-        134, 3000, 16, "kv", [H, H],
-    )(pos, *ctxs, wa, wb)
-    kvg = lax.all_to_all(kv8, "z", split_axis=0, concat_axis=0, tiled=True).reshape(1024, 512)
-
-    mine_q, w_out, kv8 = lax.optimization_barrier((mine_q, w_out, kv8))
-    wo = lax.ppermute(
-        w_out, ("y", "x"), [(a * 4 + b, b * 4 + a) for a in range(4) for b in range(4)]
-    )
-    wo4 = jnp.concatenate([wo[:, 256 * j : 256 * j + 256] for j in range(4)], axis=0)
-    wq4 = jnp.concatenate([mine_q] + [shift(mine_q, "y", by) for by in SHIFTS[1:]], axis=0)
-    wa = jnp.concatenate([wq4, wo4], axis=1)
-    wb = shift(wa, "c", 1)
-    qd, wq, wo = call(
-        qd_kernel, [S, H, H, H],
-        [sds((2, 512, 256)), sds((1024, 256)), sds((256, 1024))],
+    kv, wkv, wq, wo = call(
+        kv_kernel, [V] * 6,
+        [sds((128, 512)), sds((1024, 512)), sds((1024, 256)), sds((256, 1024))],
+        [pltpu.VMEM((128, 1024), BF), pltpu.VMEM((1024, 512), BF), pltpu.VMEM((1024, 256), BF),
+         pltpu.VMEM((256, 1024), BF), pltpu.SemaphoreType.DMA((3,))],
+        134, 3000, 16, "kv", [V, H, H, H],
+    )(*ctxs, wa, wb)
+    kvs = [kv] + [shift(kv, "z", by) for by in Z_SHIFTS[1:]]
+    (qd,) = call(
+        qd_kernel, [H] * 3, [sds((2, 512, 256))],
         [pltpu.VMEM((2, 512, 1024), BF), pltpu.VMEM((1024, 256), BF), pltpu.VMEM((256, 1024), BF),
-         pltpu.VMEM((512, 256), BF), pltpu.VMEM((512, 256), BF), pltpu.SemaphoreType.DMA((24,))],
-        540, 5000, 61, "queries", [H] * 3,
-    )(pos, xg, wa, wb)
+         pltpu.VMEM((2, 512, 256), BF), pltpu.SemaphoreType.DMA((10,))],
+        540, 5000, 24, "queries", [H],
+    )(xg, wq, wo)
 
     pay, att, dq = call(
-        attn_kernel, [H, H, V],
+        attn_kernel, [H, H] + [V] * 8,
         [sds((1024, 1024)), sds((512, 256)), sds((512, 256))],
-        [pltpu.VMEM((512, 256), BF), pltpu.VMEM((512, 256), BF),
+        [pltpu.VMEM((1024, 512), BF), pltpu.VMEM((512, 256), BF), pltpu.VMEM((512, 256), BF),
          pltpu.VMEM((256, 1024), BF), pltpu.VMEM((256, 1024), BF),
          pltpu.VMEM((1024, 256), F32), pltpu.VMEM((1024, 256), F32),
          pltpu.VMEM((256, 512), BF), pltpu.VMEM((256, 512), BF),
@@ -332,7 +320,7 @@
          pltpu.VMEM((1024, 1024), BF), pltpu.VMEM((4, 16, 1024), BF),
          pltpu.VMEM((2, 512, 1024), BF), pltpu.SemaphoreType.DMA((22,))],
         2200, 8000, 48, "attention", [H, V, V],
-    )(xg, qd, kvg)
+    )(xg, qd, *kvs)
 
     red = lax.psum_scatter(pay, "z", scatter_dimension=0, tiled=True)
     (md,) = call(md_kernel, [V] * 4, [sds((4, 256, 1024))], [], 540, 4000, 16, "md")(
@@ -344,15 +332,10 @@
     d_tokens = (cot.astype(F32) + md[128:256]).astype(BF)
     red, mixed, d_tokens = lax.optimization_barrier((red, mixed, d_tokens))
 
-    parts = call(
-        part_kernel, [S, V, V], [sds((32, 1024))] * 4,
-        [pltpu.VMEM((128, 1024), F32)], 134, 2000, 16, "part",
-    )(pos, red, wkv)
-    red, *parts = lax.optimization_barrier((red, *parts))
-    (g,) = call(
-        split_kernel, [S, V], [sds((1280, 128))], [pltpu.VMEM((1280, 128), F32)],
-        1, 600, 16, "split",
-    )(pos, red)
+    *parts, g = call(
+        split_kernel, [V, V], [sds((32, 1024))] * 4 + [sds((1280, 128))],
+        [pltpu.VMEM((128, 1024), F32), pltpu.VMEM((1280, 128), F32)], 134, 2000, 16, "split",
+    )(red, wkv)
     parts = [parts[0]] + [shift(p, "x", by) for p, by in zip(parts[1:], SHIFTS[1:])]
     g = lax.all_to_all(
         g.reshape(32, 40, 128), ("y", "c", "x"), split_axis=0, concat_axis=0, tiled=True

time: 151 us -> 158 us (1.046)
  starting transfers between devices: 37.7 us -> 48.5 us
  Pallas kernels: 26.5 us -> 19.2 us
  waiting for transfers between devices: 34.7 us -> 36.7 us
  blocking collectives: 29.3 us -> 31.1 us
    ppermute x14 -> x17, starting transfers between devices: 19.5 us -> 37.9 us  [shift(): return lax.ppermute(value, axis, [(i, (i + by) % n) for i in range(n)])]
    ppermute x14 -> x17, waiting for transfers between devices: 14.9 us -> 23.9 us  [shift(): return lax.ppermute(value, axis, [(i, (i + by) % n) for i in range(n)])]
    all_to_all x1 -> x0, starting transfers between devices: 8.47 us -> none  [local(): lax.all_to_all(kv8, 'z', split_axis=0, concat_axis=0, tiled=True)]
    ppermute x1, waiting for transfers between devices: 11.3 us -> 3.51 us  [local(): lax.ppermute(w_out, ('y', 'x'), [(a * 4 + b, b * 4 + a) for a in range(4)...]
    pallas_call x6 -> x5, Pallas kernels: 24.6 us -> 17.3 us  [the longest x1 12.3 us: local(): call(attn_kernel, [H, H] + [V] * 8, [sds((1024, 1024)), sds((512, 256)),...]
    reduce_scatter x1, waiting for transfers between devices: 6.73 us -> 9.22 us  [local(): red = lax.psum_scatter(pay, 'z', scatter_dimension=0, tiled=True)]
    all_to_all x1, blocking collectives: 29.3 us -> 31.1 us  [local(): md = lax.all_to_all(md, 'x', split_axis=0, concat_axis=0, tiled=True)]
    all_to_all x1 -> x0, waiting for transfers between devices: 1.73 us -> none  [local(): lax.all_to_all(kv8, 'z', split_axis=0, concat_axis=0, tiled=True)]
  transfers between devices with their start and end apart: 19 -> 21, of which waited for: 12 -> 9; matrix products, arithmetic and copies ran while one was open for 2% -> 2% of each run, Pallas kernels for 6% -> 2%
where the time goes in v6:
time: 158 us; the launch traced here: 157 us
  starting transfers between devices  48.5 us (31%)
  waiting for transfers between devices  36.7 us (23%)
  blocking collectives  31.1 us (20%)
  Pallas kernels  19.2 us (12%)
  between operations  14.2 us (9%)
  local copies, waits for them, and re-layouts  4.8 us (3%)
  other arithmetic  2.38 us (2%)
    ppermute x17, starting transfers between devices, shift(): return lax.ppermute(value, axis, [(i, (i + by) % n) for i in range(n)])  37.9 us
    all_to_all x1, blocking collectives, local(): md = lax.all_to_all(md, 'x', split_axis=0, concat_axis=0, tiled=True)  31.1 us
    ppermute x17, waiting for transfers between devices, shift(): return lax.ppermute(value, axis, [(i, (i + by) % n) for i in range(n)])  23.9 us
    pallas_call x1, Pallas kernels, local(): call(attn_kernel, [H, H] + [V] * 8, [sds((1024, 1024)), sds((512, 256)),...  12.3 us
    reduce_scatter x1, waiting for transfers between devices, local(): red = lax.psum_scatter(pay, 'z', scatter_dimension=0, tiled=True)  9.22 us
    all_to_all x1, starting transfers between devices, local(): lax.all_to_all(g.reshape(32, 40, 128), ('y', 'c', 'x'), split_axis=0, con...  7.25 us
    unnamed x14, local copies, waits for them, and re-layouts  4.78 us
    ppermute x1, waiting for transfers between devices, local(): lax.ppermute(w_out, ('y', 'x'), [(a * 4 + b, b * 4 + a) for a in range(4)...  3.51 us
  transfers between devices with their start and end apart: 21, of which 9 were waited for; matrix products, arithmetic and copies ran while one was open for 2% of the time, Pallas kernels for 2%

profile of v6, /device:TPU:8, one launch (start us, length us, event | category | flops | bytes accessed | tf_op | source)
XLA Modules:
  0.0 156.8 jit_solution(11999882826674802941)
XLA Ops:
  7.2 2.1 %pack.1 = (bf16[272,1024]{1,0:T(8,128)(2,1)}, bf16[128,768]{1,0:T(8,128)(2,1)}) custom-call(bf16[128,1024]{1,0:T(8,128)(2,1)} %bitcast.19, bf16[128,1024]{1,0:T(8,128)(2,1)} %bitcast.20, s32[2,16]{1,0:T(2,128)} %bitcast.23, bf16[128,1024]{1,0:T(8,128)(2,1)} %wk.1, bf16[128,1024]{1,0:T(8,128)(2,1)} %wv.1, bf16[128,1024]{1,0:T(8,128)(2,1)} %wq.1), custom_call_target="tpu_custom_call" | custom-call | flops 1000000 | bytes 1536000 | tf_op jit(solution)/shard_map/pack/pallas_call | solution.py:280
  9.4 3.3 %collective-permute-start.3 = (bf16[128,1024]{1,0:T(8,128)(2,1)}, bf16[128,1024]{1,0:T(8,128)(2,1)S(1)}, u32[]{:S(2)}, u32[]{:S(2)}) collective-permute-start(bf16[128,1024]{1,0:T(8,128)(2,1)} %param.14), channel_id=1, source_target_pairs={{0,0},{8,64},{16,128},{24,192},{64,8},{72,72},{80,136},{88,200},{1... | collective-permute-start | bytes 786440 | tf_op jit(solution)/shard_map/ppermute | solution.py:288
  12.7 3.3 %collective-permute-start.6 = (bf16[32,1024]{1,0:T(8,128)(2,1)}, bf16[32,1024]{1,0:T(8,128)(2,1)S(1)}, u32[]{:S(2)}, u32[]{:S(2)}) collective-permute-start(bf16[32,1024]{1,0:T(8,128)(2,1)} %bitcast.15), channel_id=1, source_target_pairs={{0,16},{8,24},{16,0},{24,8},{1,17},{9,25},{17,1},{25,9},{2,18},{10... | collective-permute-start | bytes 196616 | tf_op jit(solution)/shard_map/ppermute | solution.py:21
  15.9 1.4 collective-permute-start.5
  17.4 3.3 %collective-permute-start.2 = (bf16[128,768]{1,0:T(8,128)(2,1)}, bf16[128,768]{1,0:T(8,128)(2,1)S(1)}, u32[]{:S(2)}, u32[]{:S(2)}) collective-permute-start(bf16[128,768]{1,0:T(8,128)(2,1)} %get-tuple-element.31), channel_id=1, source_target_pairs={{0,128},{64,192},{128,0},{192,64},{1,129},{65,193},{129,1},{193,65... | collective-permute-start | bytes 589832 | tf_op jit(solution)/shard_map/ppermute | solution.py:21
  20.6 3.5 %collective-permute-done.3 = bf16[128,1024]{1,0:T(8,128)(2,1)S(1)} collective-permute-done((bf16[128,1024]{1,0:T(8,128)(2,1)}, bf16[128,1024]{1,0:T(8,128)(2,1)S(1)}, u32[]{:S(2)}, u32[]{:S(2)}) %collective-permute-start.3) | collective-permute-done | bytes 262176 | tf_op jit(solution)/shard_map/ppermute | solution.py:288
  24.1 3.5 %collective-permute-start = (bf16[128,768]{1,0:T(8,128)(2,1)}, bf16[128,768]{1,0:T(8,128)(2,1)S(1)}, u32[]{:S(2)}, u32[]{:S(2)}) collective-permute-start(bf16[128,768]{1,0:T(8,128)(2,1)} %get-tuple-element.31), channel_id=1, source_target_pairs={{0,64},{64,128},{128,192},{192,0},{1,65},{65,129},{129,193},{193,1... | collective-permute-start | bytes 589832 | tf_op jit(solution)/shard_map/ppermute | solution.py:21
  27.6 4.1 %collective-permute-start.4 = (bf16[32,1024]{1,0:T(8,128)(2,1)S(1)}, bf16[32,1024]{1,0:T(8,128)(2,1)S(1)}, u32[]{:S(2)}, u32[]{:S(2)}) collective-permute-start(bf16[32,1024]{1,0:T(8,128)(2,1)S(1)} %bitcast.17), channel_id=1, source_target_pairs={{0,8},{8,16},{16,24},{24,0},{1,9},{9,17},{17,25},{25,1},{2,10},{10... | collective-permute-start | bytes 196616 | tf_op jit(solution)/shard_map/ppermute | solution.py:21
  31.8 2.7 %collective-permute-done = bf16[128,768]{1,0:T(8,128)(2,1)S(1)} collective-permute-done((bf16[128,768]{1,0:T(8,128)(2,1)}, bf16[128,768]{1,0:T(8,128)(2,1)S(1)}, u32[]{:S(2)}, u32[]{:S(2)}) %collective-permute-start) | collective-permute-done | bytes 196640 | tf_op jit(solution)/shard_map/ppermute | solution.py:21
  34.5 1.1 maximum_maximum_fusion.wa
  35.6 2.6 %collective-permute-done.4.c1 = bf16[32,1024]{1,0:T(8,128)(2,1)S(1)} collective-permute-done((bf16[32,1024]{1,0:T(8,128)(2,1)S(1)}, bf16[32,1024]{1,0:T(8,128)(2,1)S(1)}, u32[]{:S(2)}, u32[]{:S(2)}) %collective-permute-start.4) | collective-permute-done | bytes 65568 | tf_op jit(solution)/shard_map/ppermute | solution.py:21
  38.2 2.7 %collective-permute-done.7.wb = bf16[512,1024]{1,0:T(8,128)(2,1)S(1)} collective-permute-done((bf16[512,1024]{1,0:T(8,128)(2,1)S(1)}, bf16[512,1024]{1,0:T(8,128)(2,1)S(1)}, u32[]{:S(2)}, u32[]{:S(2)}) %collective-permute-start.7) | collective-permute-done | bytes 1048608 | tf_op jit(solution)/shard_map/ppermute | solution.py:21
  41.6 5.9 %collective-permute-start.14 = (bf16[128,512]{1,0:T(8,128)(2,1)S(1)}, bf16[128,512]{1,0:T(8,128)(2,1)S(1)}, u32[]{:S(2)}, u32[]{:S(2)}) collective-permute-start(bf16[128,512]{1,0:T(8,128)(2,1)S(1)} %get-tuple-element.39.kv0), channel_id=1, source_target_pairs={{0,7},{1,0},{2,1},{3,2},{4,3},{5,4},{6,5},{7,6},{8,15},{9,8},{10,9... | collective-permute-start | bytes 393224 | tf_op jit(solution)/shard_map/ppermute | solution.py:21
  47.5 2.5 %collective-permute-start.12 = (bf16[128,512]{1,0:T(8,128)(2,1)S(1)}, bf16[128,512]{1,0:T(8,128)(2,1)S(1)}, u32[]{:S(2)}, u32[]{:S(2)}) collective-permute-start(bf16[128,512]{1,0:T(8,128)(2,1)S(1)} %get-tuple-element.39.kv0), channel_id=1, source_target_pairs={{0,6},{1,7},{2,0},{3,1},{4,2},{5,3},{6,4},{7,5},{8,14},{9,15},{10,... | collective-permute-start | bytes 393224 | tf_op jit(solution)/shard_map/ppermute | solution.py:21
  50.4 2.9 %collective-permute-start.10 = (bf16[128,512]{1,0:T(8,128)(2,1)S(1)}, bf16[128,512]{1,0:T(8,128)(2,1)S(1)}, u32[]{:S(2)}, u32[]{:S(2)}) collective-permute-start(bf16[128,512]{1,0:T(8,128)(2,1)S(1)} %get-tuple-element.39.kv0), channel_id=1, source_target_pairs={{0,5},{1,6},{2,7},{3,0},{4,1},{5,2},{6,3},{7,4},{8,13},{9,14},{10,... | collective-permute-start | bytes 393224 | tf_op jit(solution)/shard_map/ppermute | solution.py:21
  54.2 4.6 %collective-permute-start.8 = (bf16[128,512]{1,0:T(8,128)(2,1)S(1)}, bf16[128,512]{1,0:T(8,128)(2,1)S(1)}, u32[]{:S(2)}, u32[]{:S(2)}) collective-permute-start(bf16[128,512]{1,0:T(8,128)(2,1)S(1)} %get-tuple-element.39.kv0), channel_id=1, source_target_pairs={{0,4},{1,5},{2,6},{3,7},{4,0},{5,1},{6,2},{7,3},{8,12},{9,13},{10,... | collective-permute-start | bytes 393224 | tf_op jit(solution)/shard_map/ppermute | solution.py:21
  58.8 1.6 %copy-done = bf16[1088,1024]{1,0:T(8,128)(2,1)S(1)} copy-done((bf16[1088,1024]{1,0:T(8,128)(2,1)S(1)}, bf16[1088,1024]{1,0:T(8,128)(2,1)}, u32[]{:S(2)}) %copy-start) | copy-done | bytes 2228248
  60.5 1.1 queries.1.qd
  61.6 8.4 %collective-permute-done.9.kv2 = bf16[128,512]{1,0:T(8,128)(2,1)S(1)} collective-permute-done((bf16[128,512]{1,0:T(8,128)(2,1)S(1)}, bf16[128,512]{1,0:T(8,128)(2,1)S(1)}, u32[]{:S(2)}, u32[]{:S(2)}) %collective-permute-start.9) | collective-permute-done | bytes 131104 | tf_op jit(solution)/shard_map/ppermute | solution.py:21
  70.0 2.2 %collective-permute-done.8.kv1 = bf16[128,512]{1,0:T(8,128)(2,1)S(1)} collective-permute-done((bf16[128,512]{1,0:T(8,128)(2,1)S(1)}, bf16[128,512]{1,0:T(8,128)(2,1)S(1)}, u32[]{:S(2)}, u32[]{:S(2)}) %collective-permute-start.8) | collective-permute-done | bytes 131104 | tf_op jit(solution)/shard_map/ppermute | solution.py:21
  73.7 12.3 %attention.1 = (bf16[1024,1024]{1,0:T(8,128)(2,1)}, bf16[512,256]{1,0:T(8,128)(2,1)S(1)}, bf16[512,256]{1,0:T(8,128)(2,1)S(1)}) custom-call(bf16[4,272,1024]{2,1,0:T(8,128)(2,1)} %bitcast.12, bf16[2,512,256]{2,1,0:T(8,128)(2,1)S(1)} %queries.1.qd, bf16[128,512]{1,0:T(8,128)(2,1)S(1)} %get-tuple-element.39.kv0, bf16[128,512]{1,0:T(8,128)(2,1)S(1)} %copy-done.4, ...), custom_call_target="tpu_custom_call" | custom-call | flops 2200000000 | bytes 8192000 | tf_op jit(solution)/shard_map/attention/pallas_call | solution.py:312
  86.0 1.2 md.1
  87.2 31.1 %all_to_all.10 = bf16[4,256,1024]{2,1,0:T(8,128)(2,1)S(1)} all-to-all(bf16[4,256,1024]{2,1,0:T(8,128)(2,1)S(1)} %md.1), channel_id=1, replica_groups=mesh['y'=4,'c'=2,'x'=4,'z'=8] {'x'}, dimensions={0} | all-to-all | bytes 4194304 | tf_op jit(solution)/shard_map/all_to_all | solution.py:329
  120.2 9.2 %reduce-scatter.2.cloned.1.call-done.red = bf16[128,1024]{1,0:T(8,128)(2,1)} async-done(((bf16[1024,1024]{1,0:T(8,128)(2,1)}), bf16[128,1024]{1,0:T(8,128)(2,1)}) %reduce-scatter.2.cloned.1.call-update) | async-done | bytes 262160 | tf_op jit(solution)/shard_map/reduce_scatter | solution.py:325
  129.4 0.9 copy-done.1
  130.4 1.3 split.1
  131.7 7.3 %all-to-all-start.1 = ((bf16[32,40,128]{2,1,0:T(8,128)(2,1)}), bf16[32,40,128]{2,1,0:T(8,128)(2,1)S(1)}, u32[]{:S(2)}, u32[]{:S(2)}) async-start(bf16[32,40,128]{2,1,0:T(8,128)(2,1)} %bitcast.7), calls=%async_computation.2 | async-start | bytes 655360 | tf_op jit(solution)/shard_map/all_to_all | solution.py:340
  138.9 1.5 collective-permute-start.15
  140.5 1.8 %collective-permute-start.16 = (bf16[32,1024]{1,0:T(8,128)(2,1)S(1)}, bf16[32,1024]{1,0:T(8,128)(2,1)S(1)}, u32[]{:S(2)}, u32[]{:S(2)}) collective-permute-start(bf16[32,1024]{1,0:T(8,128)(2,1)S(1)} %get-tuple-element.50), channel_id=1, source_target_pairs={{0,24},{8,0},{16,8},{24,16},{1,25},{9,1},{17,9},{25,17},{2,26},{10... | collective-permute-start | bytes 196616 | tf_op jit(solution)/shard_map/ppermute | solution.py:21
  142.2 1.8 %collective-permute-start.17 = (bf16[32,1024]{1,0:T(8,128)(2,1)S(1)}, bf16[32,1024]{1,0:T(8,128)(2,1)S(1)}, u32[]{:S(2)}, u32[]{:S(2)}) collective-permute-start(bf16[32,1024]{1,0:T(8,128)(2,1)S(1)} %get-tuple-element.51), channel_id=1, source_target_pairs={{0,16},{8,24},{16,0},{24,8},{1,17},{9,25},{17,1},{25,9},{2,18},{10... | collective-permute-start | bytes 196616 | tf_op jit(solution)/shard_map/ppermute | solution.py:21
  144.0 3.8 %collective-permute-done.15.p1 = bf16[32,1024]{1,0:T(8,128)(2,1)S(1)} collective-permute-done((bf16[32,1024]{1,0:T(8,128)(2,1)S(1)}, bf16[32,1024]{1,0:T(8,128)(2,1)S(1)}, u32[]{:S(2)}, u32[]{:S(2)}) %collective-permute-start.15) | collective-permute-done | bytes 65568 | tf_op jit(solution)/shard_map/ppermute | solution.py:21
  147.8 1.5 collective-permute-done.17.p3
  (38 shorter events, 6.4 us)
Async XLA Ops:
  7.2 20.5 %copy-start.2 = (bf16[1,32,1024]{2,1,0:T(8,128)(2,1)S(1)}, bf16[1,32,1024]{2,1,0:T(8,128)(2,1)}, u32[]{:S(2)}) copy-start(bf16[1,32,1024]{2,1,0:T(8,128)(2,1)} %param.9) | copy-start | bytes 196612
  7.2 51.7 %all-gather.3.cloned.1.call-start = ((), (), s32[]{:S(2)}) async-start(), calls=%async_computation.4 | async-start | bytes 2785280 | tf_op jit(solution)/shard_map/all_gather | solution.py:286
  9.3 120.1 %reduce-scatter.2.cloned.1.call-start = ((), (), s32[]{:S(2)}) async-start(), calls=%async_computation.3 | async-start | bytes 2359296 | tf_op jit(solution)/shard_map/reduce_scatter | solution.py:325
  9.4 14.8 %collective-permute-start.3 = (bf16[128,1024]{1,0:T(8,128)(2,1)}, bf16[128,1024]{1,0:T(8,128)(2,1)S(1)}, u32[]{:S(2)}, u32[]{:S(2)}) collective-permute-start(bf16[128,1024]{1,0:T(8,128)(2,1)} %param.14), channel_id=1, source_target_pairs={{0,0},{8,64},{16,128},{24,192},{64,8},{72,72},{80,136},{88,200},{1... | collective-permute-start | bytes 786440 | tf_op jit(solution)/shard_map/ppermute | solution.py:288
  12.7 22.9 %collective-permute-start.6 = (bf16[32,1024]{1,0:T(8,128)(2,1)}, bf16[32,1024]{1,0:T(8,128)(2,1)S(1)}, u32[]{:S(2)}, u32[]{:S(2)}) collective-permute-start(bf16[32,1024]{1,0:T(8,128)(2,1)} %bitcast.15), channel_id=1, source_target_pairs={{0,16},{8,24},{16,0},{24,8},{1,17},{9,25},{17,1},{25,9},{2,18},{10... | collective-permute-start | bytes 196616 | tf_op jit(solution)/shard_map/ppermute | solution.py:21
  15.9 19.6 %collective-permute-start.5 = (bf16[32,1024]{1,0:T(8,128)(2,1)}, bf16[32,1024]{1,0:T(8,128)(2,1)S(1)}, u32[]{:S(2)}, u32[]{:S(2)}) collective-permute-start(bf16[32,1024]{1,0:T(8,128)(2,1)} %bitcast.16), channel_id=1, source_target_pairs={{0,24},{8,0},{16,8},{24,16},{1,25},{9,1},{17,9},{25,17},{2,26},{10... | collective-permute-start | bytes 196616 | tf_op jit(solution)/shard_map/ppermute | solution.py:21
  17.4 10.3 %collective-permute-start.2 = (bf16[128,768]{1,0:T(8,128)(2,1)}, bf16[128,768]{1,0:T(8,128)(2,1)S(1)}, u32[]{:S(2)}, u32[]{:S(2)}) collective-permute-start(bf16[128,768]{1,0:T(8,128)(2,1)} %get-tuple-element.31), channel_id=1, source_target_pairs={{0,128},{64,192},{128,0},{192,64},{1,129},{65,193},{129,1},{193,65... | collective-permute-start | bytes 589832 | tf_op jit(solution)/shard_map/ppermute | solution.py:21
  20.6 11.2 %collective-permute-start.1 = (bf16[128,768]{1,0:T(8,128)(2,1)}, bf16[128,768]{1,0:T(8,128)(2,1)S(1)}, u32[]{:S(2)}, u32[]{:S(2)}) collective-permute-start(bf16[128,768]{1,0:T(8,128)(2,1)} %get-tuple-element.31), channel_id=1, source_target_pairs={{0,192},{64,0},{128,64},{192,128},{1,193},{65,1},{129,65},{193,129... | collective-permute-start | bytes 589832 | tf_op jit(solution)/shard_map/ppermute | solution.py:21
  24.1 10.4 %collective-permute-start = (bf16[128,768]{1,0:T(8,128)(2,1)}, bf16[128,768]{1,0:T(8,128)(2,1)S(1)}, u32[]{:S(2)}, u32[]{:S(2)}) collective-permute-start(bf16[128,768]{1,0:T(8,128)(2,1)} %get-tuple-element.31), channel_id=1, source_target_pairs={{0,64},{64,128},{128,192},{192,0},{1,65},{65,129},{129,193},{193,1... | collective-permute-start | bytes 589832 | tf_op jit(solution)/shard_map/ppermute | solution.py:21
  27.6 10.6 %collective-permute-start.4 = (bf16[32,1024]{1,0:T(8,128)(2,1)S(1)}, bf16[32,1024]{1,0:T(8,128)(2,1)S(1)}, u32[]{:S(2)}, u32[]{:S(2)}) collective-permute-start(bf16[32,1024]{1,0:T(8,128)(2,1)S(1)} %bitcast.17), channel_id=1, source_target_pairs={{0,8},{8,16},{16,24},{24,0},{1,9},{9,17},{17,25},{25,1},{2,10},{10... | collective-permute-start | bytes 196616 | tf_op jit(solution)/shard_map/ppermute | solution.py:21
  38.2 2.7 %collective-permute-start.7 = (bf16[512,1024]{1,0:T(8,128)(2,1)S(1)}, bf16[512,1024]{1,0:T(8,128)(2,1)S(1)}, u32[]{:S(2)}, u32[]{:S(2)}) collective-permute-start(bf16[512,1024]{1,0:T(8,128)(2,1)S(1)} %maximum_maximum_fusion.wa), channel_id=1, source_target_pairs={{0,32},{32,0},{1,33},{33,1},{2,34},{34,2},{3,35},{35,3},{4,36},{36... | collective-permute-start | bytes 3145736 | tf_op jit(solution)/shard_map/ppermute | solution.py:21
  41.6 11.8 %collective-permute-start.14 = (bf16[128,512]{1,0:T(8,128)(2,1)S(1)}, bf16[128,512]{1,0:T(8,128)(2,1)S(1)}, u32[]{:S(2)}, u32[]{:S(2)}) collective-permute-start(bf16[128,512]{1,0:T(8,128)(2,1)S(1)} %get-tuple-element.39.kv0), channel_id=1, source_target_pairs={{0,7},{1,0},{2,1},{3,2},{4,3},{5,4},{6,5},{7,6},{8,15},{9,8},{10,9... | collective-permute-start | bytes 393224 | tf_op jit(solution)/shard_map/ppermute | solution.py:21
  47.5 6.8 %collective-permute-start.13 = (bf16[128,512]{1,0:T(8,128)(2,1)S(1)}, bf16[128,512]{1,0:T(8,128)(2,1)S(1)}, u32[]{:S(2)}, u32[]{:S(2)}) collective-permute-start(bf16[128,512]{1,0:T(8,128)(2,1)S(1)} %get-tuple-element.39.kv0), channel_id=1, source_target_pairs={{0,1},{1,2},{2,3},{3,4},{4,5},{5,6},{6,7},{7,0},{8,9},{9,10},{10,1... | collective-permute-start | bytes 393224 | tf_op jit(solution)/shard_map/ppermute | solution.py:21
  47.5 14.1 %collective-permute-start.12 = (bf16[128,512]{1,0:T(8,128)(2,1)S(1)}, bf16[128,512]{1,0:T(8,128)(2,1)S(1)}, u32[]{:S(2)}, u32[]{:S(2)}) collective-permute-start(bf16[128,512]{1,0:T(8,128)(2,1)S(1)} %get-tuple-element.39.kv0), channel_id=1, source_target_pairs={{0,6},{1,7},{2,0},{3,1},{4,2},{5,3},{6,4},{7,5},{8,14},{9,15},{10,... | collective-permute-start | bytes 393224 | tf_op jit(solution)/shard_map/ppermute | solution.py:21
  50.0 11.6 %collective-permute-start.11 = (bf16[128,512]{1,0:T(8,128)(2,1)S(1)}, bf16[128,512]{1,0:T(8,128)(2,1)S(1)}, u32[]{:S(2)}, u32[]{:S(2)}) collective-permute-start(bf16[128,512]{1,0:T(8,128)(2,1)S(1)} %get-tuple-element.39.kv0), channel_id=1, source_target_pairs={{0,2},{1,3},{2,4},{3,5},{4,6},{5,7},{6,0},{7,1},{8,10},{9,11},{10,... | collective-permute-start | bytes 393224 | tf_op jit(solution)/shard_map/ppermute | solution.py:21
  50.4 11.2 %collective-permute-start.10 = (bf16[128,512]{1,0:T(8,128)(2,1)S(1)}, bf16[128,512]{1,0:T(8,128)(2,1)S(1)}, u32[]{:S(2)}, u32[]{:S(2)}) collective-permute-start(bf16[128,512]{1,0:T(8,128)(2,1)S(1)} %get-tuple-element.39.kv0), channel_id=1, source_target_pairs={{0,5},{1,6},{2,7},{3,0},{4,1},{5,2},{6,3},{7,4},{8,13},{9,14},{10,... | collective-permute-start | bytes 393224 | tf_op jit(solution)/shard_map/ppermute | solution.py:21
  53.3 16.6 %collective-permute-start.9 = (bf16[128,512]{1,0:T(8,128)(2,1)S(1)}, bf16[128,512]{1,0:T(8,128)(2,1)S(1)}, u32[]{:S(2)}, u32[]{:S(2)}) collective-permute-start(bf16[128,512]{1,0:T(8,128)(2,1)S(1)} %get-tuple-element.39.kv0), channel_id=1, source_target_pairs={{0,3},{1,4},{2,5},{3,6},{4,7},{5,0},{6,1},{7,2},{8,11},{9,12},{10,... | collective-permute-start | bytes 393224 | tf_op jit(solution)/shard_map/ppermute | solution.py:21
  54.2 17.9 %collective-permute-start.8 = (bf16[128,512]{1,0:T(8,128)(2,1)S(1)}, bf16[128,512]{1,0:T(8,128)(2,1)S(1)}, u32[]{:S(2)}, u32[]{:S(2)}) collective-permute-start(bf16[128,512]{1,0:T(8,128)(2,1)S(1)} %get-tuple-element.39.kv0), channel_id=1, source_target_pairs={{0,4},{1,5},{2,6},{3,7},{4,0},{5,1},{6,2},{7,3},{8,12},{9,13},{10,... | collective-permute-start | bytes 393224 | tf_op jit(solution)/shard_map/ppermute | solution.py:21
  58.8 1.6 %copy-start = (bf16[1088,1024]{1,0:T(8,128)(2,1)S(1)}, bf16[1088,1024]{1,0:T(8,128)(2,1)}, u32[]{:S(2)}) copy-start(bf16[1088,1024]{1,0:T(8,128)(2,1)} %all-gather.3.cloned.1.call-done) | copy-start | bytes 6684676
  72.2 0.7 copy-start.3
  72.8 0.9 copy-start.4
  118.3 1.0 copy-start.5
  118.3 1.0 copy-start.6
  129.4 0.9 copy-start.1
  131.7 17.6 %all-to-all-start.1 = ((bf16[32,40,128]{2,1,0:T(8,128)(2,1)}), bf16[32,40,128]{2,1,0:T(8,128)(2,1)S(1)}, u32[]{:S(2)}, u32[]{:S(2)}) async-start(bf16[32,40,128]{2,1,0:T(8,128)(2,1)} %bitcast.7), calls=%async_computation.2 | async-start | bytes 655360 | tf_op jit(solution)/shard_map/all_to_all | solution.py:340
  138.9 8.9 %collective-permute-start.15 = (bf16[32,1024]{1,0:T(8,128)(2,1)S(1)}, bf16[32,1024]{1,0:T(8,128)(2,1)S(1)}, u32[]{:S(2)}, u32[]{:S(2)}) collective-permute-start(bf16[32,1024]{1,0:T(8,128)(2,1)S(1)} %get-tuple-element.49), channel_id=1, source_target_pairs={{0,8},{8,16},{16,24},{24,0},{1,9},{9,17},{17,25},{25,1},{2,10},{10... | collective-permute-start | bytes 196616 | tf_op jit(solution)/shard_map/ppermute | solution.py:21
  140.5 7.3 %collective-permute-start.16 = (bf16[32,1024]{1,0:T(8,128)(2,1)S(1)}, bf16[32,1024]{1,0:T(8,128)(2,1)S(1)}, u32[]{:S(2)}, u32[]{:S(2)}) collective-permute-start(bf16[32,1024]{1,0:T(8,128)(2,1)S(1)} %get-tuple-element.50), channel_id=1, source_target_pairs={{0,24},{8,0},{16,8},{24,16},{1,25},{9,1},{17,9},{25,17},{2,26},{10... | collective-permute-start | bytes 196616 | tf_op jit(solution)/shard_map/ppermute | solution.py:21
  142.2 7.1 %collective-permute-start.17 = (bf16[32,1024]{1,0:T(8,128)(2,1)S(1)}, bf16[32,1024]{1,0:T(8,128)(2,1)S(1)}, u32[]{:S(2)}, u32[]{:S(2)}) collective-permute-start(bf16[32,1024]{1,0:T(8,128)(2,1)S(1)} %get-tuple-element.51), channel_id=1, source_target_pairs={{0,16},{8,24},{16,0},{24,8},{1,17},{9,25},{17,1},{25,9},{2,18},{10... | collective-permute-start | bytes 196616 | tf_op jit(solution)/shard_map/ppermute | solution.py:21
Sparse Core Ops, SparseCore 0:
  9.8 38.7 all-gather.2
  86.1 43.2 reduce-scatter.1

commit v7 on v4

--- a/solution.py
+++ b/solution.py
@@ -36,8 +36,8 @@
         copy.wait()
 
 
-def pack_kernel(pos, tok, cot, pattern, wk, wv, wq, out, kv_cut, q_cut, pat_s, x_s, kv_s, q_s, sems):
-    cols = pl.ds(pl.multiple_of(256 * pos[2], 256), 256)
+def pack_kernel(tok, cot, pattern, wk, wv, wq, out, kv_cut, q_cut, pat_s, x_s, kv_s, q_s, sems):
+    cols = pl.ds(pl.multiple_of(256 * lax.axis_index("x"), 256), 256)
     copies = run_copies(
         [
             (pattern, pat_s),
@@ -60,8 +60,8 @@
     wait_all(run_copies([(x_s, out), (kv_s, kv_cut), (q_s, q_cut)], sems))
 
 
-def kv_kernel(pos, c0, c1, c2, c3, wa, wb, kv_out, w_out, ctx, w_s, kv_s, sems):
-    y, c, x = pos[0], pos[1], pos[2]
+def kv_kernel(c0, c1, c2, c3, wa, wb, kv_out, w_out, ctx, w_s, kv_s, sems):
+    y, c, x = (lax.axis_index(n) for n in ("y", "c", "x"))
     for half, core in ((wa, c), (wb, 1 - c)):
         for slot, by in enumerate(SHIFTS):
             at = pl.multiple_of(128 * (2 * mod(y - by, 4) + core), 128)
@@ -74,8 +74,8 @@
     wait_all(run_copies(pairs, sems))
 
 
-def qd_kernel(pos, xg, wa, wb, qd_out, wq_out, wo_out, x_s, wq_s, wo_s, q_s, da_s, sems):
-    y, c = pos[0], pos[1]
+def qd_kernel(xg, wa, wb, qd_out, wq_out, wo_out, x_s, wq_s, wo_s, q_s, da_s, sems):
+    y, c = lax.axis_index("y"), lax.axis_index("c")
     pairs = []
     for half, core in ((wa, c), (wb, 1 - c)):
         for slot, by in enumerate(SHIFTS):
@@ -208,16 +208,12 @@
         out[t, 128:256, :] = dot(dq[rows, :], wq[...], 1, 1).astype(BF)
 
 
-def part_kernel(pos, red, w, p0, p1, p2, p3, part):
-    x = pos[2]
+def split_kernel(red, w, p0, p1, p2, p3, g_out, part, g_s):
+    x = lax.axis_index("x")
     part[...] = dot(red[:, 0:256], w[:, 0:256], 1, 1) + dot(red[:, 256:512], w[:, 256:512], 1, 1)
     for out, by in zip((p0, p1, p2, p3), SHIFTS):
         at = pl.multiple_of(32 * mod(x + by, 4), 32)
         out[...] = part[pl.ds(at, 32), :].astype(BF)
-
-
-def split_kernel(pos, red, g_out, g_s):
-    x = pos[2]
     g_s[...] = jnp.zeros_like(g_s)
     for i in range(4):
         for j in range(2):
@@ -258,7 +254,6 @@
 
 
 V = pl.BlockSpec(memory_space=pltpu.VMEM)
-S = pl.BlockSpec(memory_space=pltpu.SMEM)
 H = pl.BlockSpec(memory_space=pltpu.HBM)
 
 
@@ -282,15 +277,13 @@
 
 
 def local(tokens, context, pattern, w_query, w_key, w_value, w_out, cotangent):
-    y, c, x, z = (lax.axis_index(n) for n in ("y", "c", "x", "z"))
-    pos = jnp.stack([y, c, x, z]).astype(jnp.int32)
     tok, ctx, cot = tokens[0], context[0], cotangent[0]
     own, mine, mine_q = call(
-        pack_kernel, [S] + [H] * 6, [sds((272, 1024)), sds((128, 512)), sds((128, 256))],
+        pack_kernel, [H] * 6, [sds((272, 1024)), sds((128, 512)), sds((128, 256))],
         [pltpu.VMEM((2, 16), jnp.int32), pltpu.VMEM((272, 1024), BF), pltpu.VMEM((128, 512), BF),
          pltpu.VMEM((128, 256), BF), pltpu.SemaphoreType.DMA((6,))],
         1, 1500, 61, "pack", [H] * 3,
-    )(pos, tok, cot, pattern[0], w_key, w_value, w_query)
+    )(tok, cot, pattern[0], w_key, w_value, w_query)
     xg = lax.all_gather(own, "x", axis=0, tiled=False)
 
     ctxs = [ctx] + [shift(ctx, "x", by) for by in SHIFTS[1:]]
@@ -298,11 +291,11 @@
     wa, *ctxs = lax.optimization_barrier((wa, *ctxs))
     wb = shift(wa, "c", 1)
     kv8, wkv = call(
-        kv_kernel, [S] + [V] * 6, [sds((8, 128, 512)), sds((1024, 512))],
+        kv_kernel, [V] * 6, [sds((8, 128, 512)), sds((1024, 512))],
         [pltpu.VMEM((128, 1024), BF), pltpu.VMEM((1024, 512), BF), pltpu.VMEM((128, 512), BF),
          pltpu.SemaphoreType.DMA((9,))],
         134, 3000, 16, "kv", [H, H],
-    )(pos, *ctxs, wa, wb)
+    )(*ctxs, wa, wb)
     kvg = lax.all_to_all(kv8, "z", split_axis=0, concat_axis=0, tiled=True).reshape(1024, 512)
 
     mine_q, w_out, kv8 = lax.optimization_barrier((mine_q, w_out, kv8))
@@ -314,12 +307,12 @@
     wa = jnp.concatenate([wq4, wo4], axis=1)
     wb = shift(wa, "c", 1)
     qd, wq, wo = call(
-        qd_kernel, [S, H, H, H],
+        qd_kernel, [H, H, H],
         [sds((2, 512, 256)), sds((1024, 256)), sds((256, 1024))],
         [pltpu.VMEM((2, 512, 1024), BF), pltpu.VMEM((1024, 256), BF), pltpu.VMEM((256, 1024), BF),
          pltpu.VMEM((512, 256), BF), pltpu.VMEM((512, 256), BF), pltpu.SemaphoreType.DMA((24,))],
         540, 5000, 61, "queries", [H] * 3,
-    )(pos, xg, wa, wb)
+    )(xg, wa, wb)
 
     pay, att, dq = call(
         attn_kernel, [H, H, V],
@@ -344,15 +337,10 @@
     d_tokens = (cot.astype(F32) + md[128:256]).astype(BF)
     red, mixed, d_tokens = lax.optimization_barrier((red, mixed, d_tokens))
 
-    parts = call(
-        part_kernel, [S, V, V], [sds((32, 1024))] * 4,
-        [pltpu.VMEM((128, 1024), F32)], 134, 2000, 16, "part",
-    )(pos, red, wkv)
-    red, *parts = lax.optimization_barrier((red, *parts))
-    (g,) = call(
-        split_kernel, [S, V], [sds((1280, 128))], [pltpu.VMEM((1280, 128), F32)],
-        1, 600, 16, "split",
-    )(pos, red)
+    *parts, g = call(
+        split_kernel, [V, V], [sds((32, 1024))] * 4 + [sds((1280, 128))],
+        [pltpu.VMEM((128, 1024), F32), pltpu.VMEM((1280, 128), F32)], 134, 2000, 16, "split",
+    )(red, wkv)
     parts = [parts[0]] + [shift(p, "x", by) for p, by in zip(parts[1:], SHIFTS[1:])]
     g = lax.all_to_all(
         g.reshape(32, 40, 128), ("y", "c", "x"), split_axis=0, concat_axis=0, tiled=True

time: 151 us -> 148 us (0.980)
  Pallas kernels: 26.5 us -> 23.3 us
    pallas_call x5 -> x4, Pallas kernels: 12.4 us -> 9.21 us  [the longest x1 4.03 us: local(): call(qd_kernel, [H, H, H], [sds((2, 512, 256)), sds((1024, 256)), sds((25...]
    unnamed x26 -> x22, local copies, waits for them, and re-layouts: 4.78 us -> 4.78 us
  transfers between devices with their start and end apart: 19 -> 19, of which waited for: 12 -> 12; matrix products, arithmetic and copies ran while one was open for 2% -> 2% of each run, Pallas kernels for 6% -> 5%
where the time goes in v7:
time: 148 us; the launch traced here: 146 us
  starting transfers between devices  37.7 us (25%)
  waiting for transfers between devices  34.8 us (24%)
  blocking collectives  29.3 us (20%)
  Pallas kernels  23.3 us (16%)
  between operations  14.2 us (10%)
  local copies, waits for them, and re-layouts  4.8 us (3%)
  other arithmetic  2.3 us (2%)
    all_to_all x1, blocking collectives, local(): md = lax.all_to_all(md, 'x', split_axis=0, concat_axis=0, tiled=True)  29.3 us
    ppermute x14, starting transfers between devices, shift(): return lax.ppermute(value, axis, [(i, (i + by) % n) for i in range(n)])  19.5 us
    ppermute x14, waiting for transfers between devices, shift(): return lax.ppermute(value, axis, [(i, (i + by) % n) for i in range(n)])  15 us
    pallas_call x1, Pallas kernels, local(): call(attn_kernel, [H, H, V], [sds((1024, 1024)), sds((512, 256)), sds((51...  12.3 us
    ppermute x1, waiting for transfers between devices, local(): lax.ppermute(w_out, ('y', 'x'), [(a * 4 + b, b * 4 + a) for a in range(4)...  11.2 us
    all_to_all x1, starting transfers between devices, local(): lax.all_to_all(kv8, 'z', split_axis=0, concat_axis=0, tiled=True)  8.46 us
    all_to_all x1, starting transfers between devices, local(): lax.all_to_all(g.reshape(32, 40, 128), ('y', 'c', 'x'), split_axis=0, con...  7.3 us
    reduce_scatter x1, waiting for transfers between devices, local(): red = lax.psum_scatter(pay, 'z', scatter_dimension=0, tiled=True)  6.14 us
  transfers between devices with their start and end apart: 19, of which 12 were waited for; matrix products, arithmetic and copies ran while one was open for 2% of the time, Pallas kernels for 5%

profile of v7, /device:TPU:8, one launch (start us, length us, event | category | flops | bytes accessed | tf_op | source)
XLA Modules:
  0.0 146.4 jit_solution(11611024328409122756)
XLA Ops:
  7.2 2.0 %pack.1 = (bf16[272,1024]{1,0:T(8,128)(2,1)}, bf16[128,512]{1,0:T(8,128)(2,1)}, bf16[128,256]{1,0:T(8,128)(2,1)}) custom-call(bf16[128,1024]{1,0:T(8,128)(2,1)} %bitcast.21, bf16[128,1024]{1,0:T(8,128)(2,1)} %bitcast.22, s32[2,16]{1,0:T(2,128)} %bitcast.25, bf16[128,1024]{1,0:T(8,128)(2,1)} %wk.1, bf16[128,1024]{1,0:T(8,128)(2,1)} %wv.1, bf16[128,1024]{1,0:T(8,128)(2,1)} %wq.1), custom_call_target="tpu_custom_call" | custom-call | flops 1000000 | bytes 1536000 | tf_op jit(solution)/shard_map/pack/pallas_call | solution.py:281
  9.3 2.4 %collective-permute-start.2 = (bf16[128,512]{1,0:T(8,128)(2,1)}, bf16[128,512]{1,0:T(8,128)(2,1)S(1)}, u32[]{:S(2)}, u32[]{:S(2)}) collective-permute-start(bf16[128,512]{1,0:T(8,128)(2,1)} %get-tuple-element.36), channel_id=1, source_target_pairs={{0,128},{64,192},{128,0},{192,64},{1,129},{65,193},{129,1},{193,65... | collective-permute-start | bytes 393224 | tf_op jit(solution)/shard_map/ppermute | solution.py:20
  11.7 1.3 collective-permute-start.1
  13.7 3.0 %collective-permute-start.5 = (bf16[32,1024]{1,0:T(8,128)(2,1)}, bf16[32,1024]{1,0:T(8,128)(2,1)S(1)}, u32[]{:S(2)}, u32[]{:S(2)}) collective-permute-start(bf16[32,1024]{1,0:T(8,128)(2,1)} %bitcast.15), channel_id=1, source_target_pairs={{0,16},{8,24},{16,0},{24,8},{1,17},{9,25},{17,1},{25,9},{2,18},{10... | collective-permute-start | bytes 196616 | tf_op jit(solution)/shard_map/ppermute | solution.py:20
  16.7 1.1 collective-permute-start.4
  17.9 1.1 collective-permute-start.3
  20.2 1.0 collective-permute-done.4.c2
  21.2 2.4 %collective-permute-done.3.c1 = bf16[32,1024]{1,0:T(8,128)(2,1)S(1)} collective-permute-done((bf16[32,1024]{1,0:T(8,128)(2,1)}, bf16[32,1024]{1,0:T(8,128)(2,1)S(1)}, u32[]{:S(2)}, u32[]{:S(2)}) %collective-permute-start.3) | collective-permute-done | bytes 65568 | tf_op jit(solution)/shard_map/ppermute | solution.py:20
  23.6 1.9 %collective-permute-done.6.wb = bf16[512,512]{1,0:T(8,128)(2,1)S(1)} collective-permute-done((bf16[512,512]{1,0:T(8,128)(2,1)S(1)}, bf16[512,512]{1,0:T(8,128)(2,1)S(1)}, u32[]{:S(2)}, u32[]{:S(2)}) %collective-permute-start.6) | collective-permute-done | bytes 524320 | tf_op jit(solution)/shard_map/ppermute | solution.py:20
  25.5 1.9 %kv.1 = (bf16[8,128,512]{2,1,0:T(8,128)(2,1)S(1)}, bf16[1024,512]{1,0:T(8,128)(2,1)S(1)}) custom-call(bf16[32,1024]{1,0:T(8,128)(2,1)S(1)} %bitcast.18, bf16[32,1024]{1,0:T(8,128)(2,1)S(1)} %collective-permute-done.3.c1, bf16[32,1024]{1,0:T(8,128)(2,1)S(1)} %collective-permute-done.4.c2, bf16[32,1024]{1,0:T(8,128)(2,1)S(1)} %collective-permute-done.5.c3, ...), custom_call_target="tpu_custom_call" | custom-call | flops 134000000 | bytes 3072000 | tf_op jit(solution)/shard_map/kv/pallas_call | solution.py:293
  28.4 8.5 %all-to-all-start = ((bf16[8,128,512]{2,1,0:T(8,128)(2,1)}), bf16[8,128,512]{2,1,0:T(8,128)(2,1)S(1)}, u32[]{:S(2)}, u32[]{:S(2)}) async-start(bf16[8,128,512]{2,1,0:T(8,128)(2,1)} %copy-done), calls=%async_computation | async-start | bytes 2097152 | tf_op jit(solution)/shard_map/all_to_all | solution.py:299
  36.9 2.4 %collective-permute-start.10 = (bf16[128,1024]{1,0:T(8,128)(2,1)S(1)}, bf16[128,1024]{1,0:T(8,128)(2,1)S(1)}, u32[]{:S(2)}, u32[]{:S(2)}) collective-permute-start(bf16[128,1024]{1,0:T(8,128)(2,1)S(1)} %copy-done.10), channel_id=1, source_target_pairs={{0,0},{8,64},{16,128},{24,192},{64,8},{72,72},{80,136},{88,200},{1... | collective-permute-start | bytes 786440 | tf_op jit(solution)/shard_map/ppermute | solution.py:302
  39.3 2.5 %collective-permute-start.9 = (bf16[128,256]{1,0:T(8,128)(2,1)S(1)}, bf16[128,256]{1,0:T(8,128)(2,1)S(1)}, u32[]{:S(2)}, u32[]{:S(2)}) collective-permute-start(bf16[128,256]{1,0:T(8,128)(2,1)S(1)} %copy-done.9), channel_id=1, source_target_pairs={{0,128},{64,192},{128,0},{192,64},{1,129},{65,193},{129,1},{193,65... | collective-permute-start | bytes 196616 | tf_op jit(solution)/shard_map/ppermute | solution.py:20
  41.7 1.8 %collective-permute-start.8 = (bf16[128,256]{1,0:T(8,128)(2,1)S(1)}, bf16[128,256]{1,0:T(8,128)(2,1)S(1)}, u32[]{:S(2)}, u32[]{:S(2)}) collective-permute-start(bf16[128,256]{1,0:T(8,128)(2,1)S(1)} %copy-done.9), channel_id=1, source_target_pairs={{0,192},{64,0},{128,64},{192,128},{1,193},{65,1},{129,65},{193,129... | collective-permute-start | bytes 196616 | tf_op jit(solution)/shard_map/ppermute | solution.py:20
  43.8 11.2 %collective-permute-done.10 = bf16[128,1024]{1,0:T(8,128)(2,1)S(1)} collective-permute-done((bf16[128,1024]{1,0:T(8,128)(2,1)S(1)}, bf16[128,1024]{1,0:T(8,128)(2,1)S(1)}, u32[]{:S(2)}, u32[]{:S(2)}) %collective-permute-start.10) | collective-permute-done | bytes 262176 | tf_op jit(solution)/shard_map/ppermute | solution.py:302
  55.0 2.1 %collective-permute-done.7 = bf16[128,256]{1,0:T(8,128)(2,1)S(1)} collective-permute-done((bf16[128,256]{1,0:T(8,128)(2,1)S(1)}, bf16[128,256]{1,0:T(8,128)(2,1)S(1)}, u32[]{:S(2)}, u32[]{:S(2)}) %collective-permute-start.7) | collective-permute-done | bytes 65568 | tf_op jit(solution)/shard_map/ppermute | solution.py:20
  57.4 2.0 %collective-permute-done.11.wb = bf16[512,512]{1,0:T(8,128)(2,1)} collective-permute-done((bf16[512,512]{1,0:T(8,128)(2,1)S(1)}, bf16[512,512]{1,0:T(8,128)(2,1)}, u32[]{:S(2)}, u32[]{:S(2)}) %collective-permute-start.11) | collective-permute-done | bytes 524320 | tf_op jit(solution)/shard_map/ppermute | solution.py:20
  59.5 4.0 %queries.1 = (bf16[2,512,256]{2,1,0:T(8,128)(2,1)}, bf16[1024,256]{1,0:T(8,128)(2,1)}, bf16[256,1024]{1,0:T(8,128)(2,1)}) custom-call(bf16[4,272,1024]{2,1,0:T(8,128)(2,1)} %bitcast.19, bf16[512,512]{1,0:T(8,128)(2,1)} %copy-done.6, bf16[512,512]{1,0:T(8,128)(2,1)} %collective-permute-done.11.wb), custom_call_target="tpu_custom_call" | custom-call | flops 540000000 | bytes 5120000 | tf_op jit(solution)/shard_map/queries/pallas_call | solution.py:309
  63.5 2.4 %all-to-all-done = bf16[8,128,512]{2,1,0:T(8,128)(2,1)S(1)} async-done(((bf16[8,128,512]{2,1,0:T(8,128)(2,1)}), bf16[8,128,512]{2,1,0:T(8,128)(2,1)S(1)}, u32[]{:S(2)}, u32[]{:S(2)}) %all-to-all-start) | async-done | bytes 1048608 | tf_op jit(solution)/shard_map/all_to_all | solution.py:299
  65.9 1.0 copy-done.5
  66.9 12.3 %attention.1 = (bf16[1024,1024]{1,0:T(8,128)(2,1)}, bf16[512,256]{1,0:T(8,128)(2,1)S(1)}, bf16[512,256]{1,0:T(8,128)(2,1)S(1)}) custom-call(bf16[4,272,1024]{2,1,0:T(8,128)(2,1)} %bitcast.20, bf16[2,512,256]{2,1,0:T(8,128)(2,1)S(1)} %copy-done.5, bf16[1024,512]{1,0:T(8,128)(2,1)S(1)} %bitcast.14), custom_call_target="tpu_custom_call" | custom-call | flops 2200000000 | bytes 8192000 | tf_op jit(solution)/shard_map/attention/pallas_call | solution.py:317
  79.3 1.0 copy-done.1
  80.4 1.2 md.1
  81.6 29.3 %all_to_all.15 = bf16[4,256,1024]{2,1,0:T(8,128)(2,1)S(1)} all-to-all(bf16[4,256,1024]{2,1,0:T(8,128)(2,1)S(1)} %md.1), channel_id=1, replica_groups=mesh['y'=4,'c'=2,'x'=4,'z'=8] {'x'}, dimensions={0} | all-to-all | bytes 4194304 | tf_op jit(solution)/shard_map/all_to_all | solution.py:334
  112.8 6.1 %reduce-scatter.2.cloned.1.call-done.red = bf16[128,1024]{1,0:T(8,128)(2,1)} async-done(((bf16[1024,1024]{1,0:T(8,128)(2,1)}), bf16[128,1024]{1,0:T(8,128)(2,1)}) %reduce-scatter.2.cloned.1.call-update) | async-done | bytes 262160 | tf_op jit(solution)/shard_map/reduce_scatter | solution.py:330
  119.9 1.2 split.1
  121.2 7.3 %all-to-all-start.2 = ((bf16[32,40,128]{2,1,0:T(8,128)(2,1)}), bf16[32,40,128]{2,1,0:T(8,128)(2,1)S(1)}, u32[]{:S(2)}, u32[]{:S(2)}) async-start(bf16[32,40,128]{2,1,0:T(8,128)(2,1)} %bitcast.8), calls=%async_computation.3 | async-start | bytes 655360 | tf_op jit(solution)/shard_map/all_to_all | solution.py:345
  128.5 1.5 %collective-permute-start.12 = (bf16[32,1024]{1,0:T(8,128)(2,1)S(1)}, bf16[32,1024]{1,0:T(8,128)(2,1)S(1)}, u32[]{:S(2)}, u32[]{:S(2)}) collective-permute-start(bf16[32,1024]{1,0:T(8,128)(2,1)S(1)} %get-tuple-element.57), channel_id=1, source_target_pairs={{0,8},{8,16},{16,24},{24,0},{1,9},{9,17},{17,25},{25,1},{2,10},{10... | collective-permute-start | bytes 196616 | tf_op jit(solution)/shard_map/ppermute | solution.py:20
  130.0 1.8 %collective-permute-start.13 = (bf16[32,1024]{1,0:T(8,128)(2,1)S(1)}, bf16[32,1024]{1,0:T(8,128)(2,1)S(1)}, u32[]{:S(2)}, u32[]{:S(2)}) collective-permute-start(bf16[32,1024]{1,0:T(8,128)(2,1)S(1)} %get-tuple-element.58), channel_id=1, source_target_pairs={{0,24},{8,0},{16,8},{24,16},{1,25},{9,1},{17,9},{25,17},{2,26},{10... | collective-permute-start | bytes 196616 | tf_op jit(solution)/shard_map/ppermute | solution.py:20
  131.8 1.8 %collective-permute-start.14 = (bf16[32,1024]{1,0:T(8,128)(2,1)S(1)}, bf16[32,1024]{1,0:T(8,128)(2,1)S(1)}, u32[]{:S(2)}, u32[]{:S(2)}) collective-permute-start(bf16[32,1024]{1,0:T(8,128)(2,1)S(1)} %get-tuple-element.59), channel_id=1, source_target_pairs={{0,16},{8,24},{16,0},{24,8},{1,17},{9,25},{17,1},{25,9},{2,18},{10... | collective-permute-start | bytes 196616 | tf_op jit(solution)/shard_map/ppermute | solution.py:20
  133.5 3.8 %collective-permute-done.12.p1 = bf16[32,1024]{1,0:T(8,128)(2,1)S(1)} collective-permute-done((bf16[32,1024]{1,0:T(8,128)(2,1)S(1)}, bf16[32,1024]{1,0:T(8,128)(2,1)S(1)}, u32[]{:S(2)}, u32[]{:S(2)}) %collective-permute-start.12) | collective-permute-done | bytes 65568 | tf_op jit(solution)/shard_map/ppermute | solution.py:20
  137.3 1.5 %collective-permute-done.14.p3 = bf16[32,1024]{1,0:T(8,128)(2,1)S(1)} collective-permute-done((bf16[32,1024]{1,0:T(8,128)(2,1)S(1)}, bf16[32,1024]{1,0:T(8,128)(2,1)S(1)}, u32[]{:S(2)}, u32[]{:S(2)}) %collective-permute-start.14) | collective-permute-done | bytes 65568 | tf_op jit(solution)/shard_map/ppermute | solution.py:20
  (43 shorter events, 7.4 us)
Async XLA Ops:
  7.2 18.3 %copy-start.4 = (bf16[1,32,1024]{2,1,0:T(8,128)(2,1)S(1)}, bf16[1,32,1024]{2,1,0:T(8,128)(2,1)}, u32[]{:S(2)}) copy-start(bf16[1,32,1024]{2,1,0:T(8,128)(2,1)} %param.9) | copy-start | bytes 196612
  7.2 52.3 %all-gather.3.cloned.1.call-start = ((), (), s32[]{:S(2)}) async-start(), calls=%async_computation.5 | async-start | bytes 2785280 | tf_op jit(solution)/shard_map/all_gather | solution.py:287
  9.3 8.6 %collective-permute-start.2 = (bf16[128,512]{1,0:T(8,128)(2,1)}, bf16[128,512]{1,0:T(8,128)(2,1)S(1)}, u32[]{:S(2)}, u32[]{:S(2)}) collective-permute-start(bf16[128,512]{1,0:T(8,128)(2,1)} %get-tuple-element.36), channel_id=1, source_target_pairs={{0,128},{64,192},{128,0},{192,64},{1,129},{65,193},{129,1},{193,65... | collective-permute-start | bytes 393224 | tf_op jit(solution)/shard_map/ppermute | solution.py:20
  11.7 7.5 %collective-permute-start.1 = (bf16[128,512]{1,0:T(8,128)(2,1)}, bf16[128,512]{1,0:T(8,128)(2,1)S(1)}, u32[]{:S(2)}, u32[]{:S(2)}) collective-permute-start(bf16[128,512]{1,0:T(8,128)(2,1)} %get-tuple-element.36), channel_id=1, source_target_pairs={{0,192},{64,0},{128,64},{192,128},{1,193},{65,1},{129,65},{193,129... | collective-permute-start | bytes 393224 | tf_op jit(solution)/shard_map/ppermute | solution.py:20
  13.0 6.2 %collective-permute-start = (bf16[128,512]{1,0:T(8,128)(2,1)}, bf16[128,512]{1,0:T(8,128)(2,1)S(1)}, u32[]{:S(2)}, u32[]{:S(2)}) collective-permute-start(bf16[128,512]{1,0:T(8,128)(2,1)} %get-tuple-element.36), channel_id=1, source_target_pairs={{0,64},{64,128},{128,192},{192,0},{1,65},{65,129},{129,193},{193,1... | collective-permute-start | bytes 393224 | tf_op jit(solution)/shard_map/ppermute | solution.py:20
  13.7 23.2 %copy-start.10 = (bf16[128,1024]{1,0:T(8,128)(2,1)S(1)}, bf16[128,1024]{1,0:T(8,128)(2,1)}, u32[]{:S(2)}) copy-start(bf16[128,1024]{1,0:T(8,128)(2,1)} %param.14) | copy-start | bytes 786436
  13.7 25.6 %copy-start.9 = (bf16[128,256]{1,0:T(8,128)(2,1)S(1)}, bf16[128,256]{1,0:T(8,128)(2,1)}, u32[]{:S(2)}) copy-start(bf16[128,256]{1,0:T(8,128)(2,1)} %get-tuple-element.43) | copy-start | bytes 196612
  13.7 6.5 %collective-permute-start.5 = (bf16[32,1024]{1,0:T(8,128)(2,1)}, bf16[32,1024]{1,0:T(8,128)(2,1)S(1)}, u32[]{:S(2)}, u32[]{:S(2)}) collective-permute-start(bf16[32,1024]{1,0:T(8,128)(2,1)} %bitcast.15), channel_id=1, source_target_pairs={{0,16},{8,24},{16,0},{24,8},{1,17},{9,25},{17,1},{25,9},{2,18},{10... | collective-permute-start | bytes 196616 | tf_op jit(solution)/shard_map/ppermute | solution.py:20
  16.7 4.5 %collective-permute-start.4 = (bf16[32,1024]{1,0:T(8,128)(2,1)}, bf16[32,1024]{1,0:T(8,128)(2,1)S(1)}, u32[]{:S(2)}, u32[]{:S(2)}) collective-permute-start(bf16[32,1024]{1,0:T(8,128)(2,1)} %bitcast.16), channel_id=1, source_target_pairs={{0,24},{8,0},{16,8},{24,16},{1,25},{9,1},{17,9},{25,17},{2,26},{10... | collective-permute-start | bytes 196616 | tf_op jit(solution)/shard_map/ppermute | solution.py:20
  17.9 5.7 %collective-permute-start.3 = (bf16[32,1024]{1,0:T(8,128)(2,1)}, bf16[32,1024]{1,0:T(8,128)(2,1)S(1)}, u32[]{:S(2)}, u32[]{:S(2)}) collective-permute-start(bf16[32,1024]{1,0:T(8,128)(2,1)} %bitcast.17), channel_id=1, source_target_pairs={{0,8},{8,16},{16,24},{24,0},{1,9},{9,17},{17,25},{25,1},{2,10},{10... | collective-permute-start | bytes 196616 | tf_op jit(solution)/shard_map/ppermute | solution.py:20
  23.6 1.9 %collective-permute-start.6 = (bf16[512,512]{1,0:T(8,128)(2,1)S(1)}, bf16[512,512]{1,0:T(8,128)(2,1)S(1)}, u32[]{:S(2)}, u32[]{:S(2)}) collective-permute-start(bf16[512,512]{1,0:T(8,128)(2,1)S(1)} %pad_maximum_fusion.wa), channel_id=1, source_target_pairs={{0,32},{32,0},{1,33},{33,1},{2,34},{34,2},{3,35},{35,3},{4,36},{36... | collective-permute-start | bytes 1572872 | tf_op jit(solution)/shard_map/ppermute | solution.py:20
  27.4 1.0 copy-start
  28.4 37.5 %all-to-all-start = ((bf16[8,128,512]{2,1,0:T(8,128)(2,1)}), bf16[8,128,512]{2,1,0:T(8,128)(2,1)S(1)}, u32[]{:S(2)}, u32[]{:S(2)}) async-start(bf16[8,128,512]{2,1,0:T(8,128)(2,1)} %copy-done), calls=%async_computation | async-start | bytes 2097152 | tf_op jit(solution)/shard_map/all_to_all | solution.py:299
  36.8 82.1 %reduce-scatter.2.cloned.1.call-start = ((), (), s32[]{:S(2)}) async-start(), calls=%async_computation.4 | async-start | bytes 2359296 | tf_op jit(solution)/shard_map/reduce_scatter | solution.py:330
  36.9 18.1 %collective-permute-start.10 = (bf16[128,1024]{1,0:T(8,128)(2,1)S(1)}, bf16[128,1024]{1,0:T(8,128)(2,1)S(1)}, u32[]{:S(2)}, u32[]{:S(2)}) collective-permute-start(bf16[128,1024]{1,0:T(8,128)(2,1)S(1)} %copy-done.10), channel_id=1, source_target_pairs={{0,0},{8,64},{16,128},{24,192},{64,8},{72,72},{80,136},{88,200},{1... | collective-permute-start | bytes 786440 | tf_op jit(solution)/shard_map/ppermute | solution.py:302
  39.3 15.8 %collective-permute-start.9 = (bf16[128,256]{1,0:T(8,128)(2,1)S(1)}, bf16[128,256]{1,0:T(8,128)(2,1)S(1)}, u32[]{:S(2)}, u32[]{:S(2)}) collective-permute-start(bf16[128,256]{1,0:T(8,128)(2,1)S(1)} %copy-done.9), channel_id=1, source_target_pairs={{0,128},{64,192},{128,0},{192,64},{1,129},{65,193},{129,1},{193,65... | collective-permute-start | bytes 196616 | tf_op jit(solution)/shard_map/ppermute | solution.py:20
  41.7 13.3 %collective-permute-start.8 = (bf16[128,256]{1,0:T(8,128)(2,1)S(1)}, bf16[128,256]{1,0:T(8,128)(2,1)S(1)}, u32[]{:S(2)}, u32[]{:S(2)}) collective-permute-start(bf16[128,256]{1,0:T(8,128)(2,1)S(1)} %copy-done.9), channel_id=1, source_target_pairs={{0,192},{64,0},{128,64},{192,128},{1,193},{65,1},{129,65},{193,129... | collective-permute-start | bytes 196616 | tf_op jit(solution)/shard_map/ppermute | solution.py:20
  43.5 13.6 %collective-permute-start.7 = (bf16[128,256]{1,0:T(8,128)(2,1)S(1)}, bf16[128,256]{1,0:T(8,128)(2,1)S(1)}, u32[]{:S(2)}, u32[]{:S(2)}) collective-permute-start(bf16[128,256]{1,0:T(8,128)(2,1)S(1)} %copy-done.9), channel_id=1, source_target_pairs={{0,64},{64,128},{128,192},{192,0},{1,65},{65,129},{129,193},{193,1... | collective-permute-start | bytes 196616 | tf_op jit(solution)/shard_map/ppermute | solution.py:20
  57.1 2.3 %copy-start.6 = (bf16[512,512]{1,0:T(8,128)(2,1)}, bf16[512,512]{1,0:T(8,128)(2,1)S(1)}, u32[]{:S(2)}) copy-start(bf16[512,512]{1,0:T(8,128)(2,1)S(1)} %maximum_maximum_fusion.wa) | copy-start | bytes 1572868
  57.2 2.3 %collective-permute-start.11 = (bf16[512,512]{1,0:T(8,128)(2,1)S(1)}, bf16[512,512]{1,0:T(8,128)(2,1)}, u32[]{:S(2)}, u32[]{:S(2)}) collective-permute-start(bf16[512,512]{1,0:T(8,128)(2,1)S(1)} %maximum_maximum_fusion.wa), channel_id=1, source_target_pairs={{0,32},{32,0},{1,33},{33,1},{2,34},{34,2},{3,35},{35,3},{4,36},{36... | collective-permute-start | bytes 1572872 | tf_op jit(solution)/shard_map/ppermute | solution.py:20
  65.9 1.0 copy-start.5
  79.2 1.0 copy-start.1
  79.2 1.2 copy-start.2
  110.8 1.0 copy-start.7
  110.8 1.0 copy-start.8
  119.0 0.9 copy-start.3
  121.2 17.7 %all-to-all-start.2 = ((bf16[32,40,128]{2,1,0:T(8,128)(2,1)}), bf16[32,40,128]{2,1,0:T(8,128)(2,1)S(1)}, u32[]{:S(2)}, u32[]{:S(2)}) async-start(bf16[32,40,128]{2,1,0:T(8,128)(2,1)} %bitcast.8), calls=%async_computation.3 | async-start | bytes 655360 | tf_op jit(solution)/shard_map/all_to_all | solution.py:345
  128.5 8.9 %collective-permute-start.12 = (bf16[32,1024]{1,0:T(8,128)(2,1)S(1)}, bf16[32,1024]{1,0:T(8,128)(2,1)S(1)}, u32[]{:S(2)}, u32[]{:S(2)}) collective-permute-start(bf16[32,1024]{1,0:T(8,128)(2,1)S(1)} %get-tuple-element.57), channel_id=1, source_target_pairs={{0,8},{8,16},{16,24},{24,0},{1,9},{9,17},{17,25},{25,1},{2,10},{10... | collective-permute-start | bytes 196616 | tf_op jit(solution)/shard_map/ppermute | solution.py:20
  130.0 7.3 %collective-permute-start.13 = (bf16[32,1024]{1,0:T(8,128)(2,1)S(1)}, bf16[32,1024]{1,0:T(8,128)(2,1)S(1)}, u32[]{:S(2)}, u32[]{:S(2)}) collective-permute-start(bf16[32,1024]{1,0:T(8,128)(2,1)S(1)} %get-tuple-element.58), channel_id=1, source_target_pairs={{0,24},{8,0},{16,8},{24,16},{1,25},{9,1},{17,9},{25,17},{2,26},{10... | collective-permute-start | bytes 196616 | tf_op jit(solution)/shard_map/ppermute | solution.py:20
  131.8 7.1 %collective-permute-start.14 = (bf16[32,1024]{1,0:T(8,128)(2,1)S(1)}, bf16[32,1024]{1,0:T(8,128)(2,1)S(1)}, u32[]{:S(2)}, u32[]{:S(2)}) collective-permute-start(bf16[32,1024]{1,0:T(8,128)(2,1)S(1)} %get-tuple-element.59), channel_id=1, source_target_pairs={{0,16},{8,24},{16,0},{24,8},{1,17},{9,25},{17,1},{25,9},{2,18},{10... | collective-permute-start | bytes 196616 | tf_op jit(solution)/shard_map/ppermute | solution.py:20
Sparse Core Ops, SparseCore 0:
  9.8 38.2 all-gather.2
  79.4 39.5 reduce-scatter.1

commit v8 on v7

--- a/solution.py
+++ b/solution.py
@@ -208,12 +208,13 @@
         out[t, 128:256, :] = dot(dq[rows, :], wq[...], 1, 1).astype(BF)
 
 
-def split_kernel(red, w, p0, p1, p2, p3, g_out, part, g_s):
+def part_kernel(red, w, part):
+    total = dot(red[:, 0:256], w[:, 0:256], 1, 1) + dot(red[:, 256:512], w[:, 256:512], 1, 1)
+    part[...] = total.astype(BF)
+
+
+def split_kernel(red, g_out, g_s):
     x = lax.axis_index("x")
-    part[...] = dot(red[:, 0:256], w[:, 0:256], 1, 1) + dot(red[:, 256:512], w[:, 256:512], 1, 1)
-    for out, by in zip((p0, p1, p2, p3), SHIFTS):
-        at = pl.multiple_of(32 * mod(x + by, 4), 32)
-        out[...] = part[pl.ds(at, 32), :].astype(BF)
     g_s[...] = jnp.zeros_like(g_s)
     for i in range(4):
         for j in range(2):
@@ -229,11 +230,7 @@
     g_out[...] = g_s[...].astype(BF)
 
 
-def finish_kernel(g, p0, p1, p2, p3, dctx, g_query, g_out):
-    total = p0[...].astype(F32)
-    for p in (p1, p2, p3):
-        total += p[...].astype(F32)
-    dctx[...] = total.astype(BF)
+def finish_kernel(g, g_query, g_out):
     for xs in range(4):
         acc = jnp.zeros((8, 128), F32)
         for yc in range(8):
@@ -337,18 +334,17 @@
     d_tokens = (cot.astype(F32) + md[128:256]).astype(BF)
     red, mixed, d_tokens = lax.optimization_barrier((red, mixed, d_tokens))
 
-    *parts, g = call(
-        split_kernel, [V, V], [sds((32, 1024))] * 4 + [sds((1280, 128))],
-        [pltpu.VMEM((128, 1024), F32), pltpu.VMEM((1280, 128), F32)], 134, 2000, 16, "split",
-    )(red, wkv)
-    parts = [parts[0]] + [shift(p, "x", by) for p, by in zip(parts[1:], SHIFTS[1:])]
+    (part,) = call(part_kernel, [V, V], [sds((128, 1024))], [], 134, 2000, 16, "part")(red, wkv)
+    d_context = lax.psum_scatter(part, "x", scatter_dimension=0, tiled=True)
+    (g,) = call(
+        split_kernel, [V], [sds((1280, 128))], [pltpu.VMEM((1280, 128), F32)], 1, 600, 16, "split"
+    )(red)
     g = lax.all_to_all(
         g.reshape(32, 40, 128), ("y", "c", "x"), split_axis=0, concat_axis=0, tiled=True
     ).reshape(1280, 128)
-    d_context, g_query, g_out = call(
-        finish_kernel, [V] * 5, [sds((32, 1024)), sds((4, 1024), F32), sds((4, 1024), F32)],
-        [], 1, 700, 8, "finish",
-    )(g, *parts)
+    g_query, g_out = call(
+        finish_kernel, [V], [sds((4, 1024), F32), sds((4, 1024), F32)], [], 1, 700, 8, "finish"
+    )(g)
     return mixed[None], d_tokens[None], d_context[None], g_query, g_out
 
 

time: 148 us -> 152 us (1.027)
  blocking collectives: 29.3 us -> 45.9 us
  starting transfers between devices: 37.7 us -> 25.4 us
    all_to_all x0 -> x1, blocking collectives: none -> 16.7 us  [local(): lax.all_to_all(g.reshape(32, 40, 128), ('y', 'c', 'x'), split_axis=0, con...]
    all_to_all x1 -> x0, starting transfers between devices: 7.3 us -> none  [local(): lax.all_to_all(g.reshape(32, 40, 128), ('y', 'c', 'x'), split_axis=0, con...]
    reduce_scatter x0 -> x1, waiting for transfers between devices: none -> 5.36 us  [local(): d_context = lax.psum_scatter(part, 'x', scatter_dimension=0, tiled=True)]
    ppermute x14 -> x11, waiting for transfers between devices: 15 us -> 9.64 us  [shift(): return lax.ppermute(value, axis, [(i, (i + by) % n) for i in range(n)])]
    ppermute x14 -> x11, starting transfers between devices: 19.5 us -> 14.4 us  [shift(): return lax.ppermute(value, axis, [(i, (i + by) % n) for i in range(n)])]
    unnamed x22 -> x24, local copies, waits for them, and re-layouts: 4.78 us -> 5.69 us
  transfers between devices with their start and end apart: 19 -> 16, of which waited for: 12 -> 11; matrix products, arithmetic and copies ran while one was open for 2% -> 2% of each run, Pallas kernels for 5% -> 5%
where the time goes in v8:
time: 152 us; the launch traced here: 151 us
  blocking collectives  45.9 us (30%)
  waiting for transfers between devices  34.8 us (23%)
  starting transfers between devices  25.4 us (17%)
  Pallas kernels  23.4 us (15%)
  between operations  13.9 us (9%)
  local copies, waits for them, and re-layouts  5.71 us (4%)
  other arithmetic  2.3 us (2%)
    all_to_all x1, blocking collectives, local(): md = lax.all_to_all(md, 'x', split_axis=0, concat_axis=0, tiled=True)  29.3 us
    all_to_all x1, blocking collectives, local(): lax.all_to_all(g.reshape(32, 40, 128), ('y', 'c', 'x'), split_axis=0, con...  16.7 us
    ppermute x11, starting transfers between devices, shift(): return lax.ppermute(value, axis, [(i, (i + by) % n) for i in range(n)])  14.4 us
    pallas_call x1, Pallas kernels, local(): call(attn_kernel, [H, H, V], [sds((1024, 1024)), sds((512, 256)), sds((51...  12.3 us
    ppermute x1, waiting for transfers between devices, local(): lax.ppermute(w_out, ('y', 'x'), [(a * 4 + b, b * 4 + a) for a in range(4)...  11.2 us
    ppermute x11, waiting for transfers between devices, shift(): return lax.ppermute(value, axis, [(i, (i + by) % n) for i in range(n)])  9.64 us
    all_to_all x1, starting transfers between devices, local(): lax.all_to_all(kv8, 'z', split_axis=0, concat_axis=0, tiled=True)  8.46 us
    reduce_scatter x1, waiting for transfers between devices, local(): red = lax.psum_scatter(pay, 'z', scatter_dimension=0, tiled=True)  6.09 us
  transfers between devices with their start and end apart: 16, of which 11 were waited for; matrix products, arithmetic and copies ran while one was open for 2% of the time, Pallas kernels for 5%

profile of v8, /device:TPU:8, one launch (start us, length us, event | category | flops | bytes accessed | tf_op | source)
XLA Modules:
  0.0 151.4 jit_solution(10648927593437207345)
XLA Ops:
  7.2 2.0 %pack.1 = (bf16[272,1024]{1,0:T(8,128)(2,1)}, bf16[128,512]{1,0:T(8,128)(2,1)}, bf16[128,256]{1,0:T(8,128)(2,1)}) custom-call(bf16[128,1024]{1,0:T(8,128)(2,1)} %bitcast.22, bf16[128,1024]{1,0:T(8,128)(2,1)} %bitcast.23, s32[2,16]{1,0:T(2,128)} %bitcast.26, bf16[128,1024]{1,0:T(8,128)(2,1)} %wk.1, bf16[128,1024]{1,0:T(8,128)(2,1)} %wv.1, bf16[128,1024]{1,0:T(8,128)(2,1)} %wq.1), custom_call_target="tpu_custom_call" | custom-call | flops 1000000 | bytes 1536000 | tf_op jit(solution)/shard_map/pack/pallas_call | solution.py:278
  9.3 2.4 %collective-permute-start.2 = (bf16[128,512]{1,0:T(8,128)(2,1)}, bf16[128,512]{1,0:T(8,128)(2,1)S(1)}, u32[]{:S(2)}, u32[]{:S(2)}) collective-permute-start(bf16[128,512]{1,0:T(8,128)(2,1)} %get-tuple-element.30), channel_id=1, source_target_pairs={{0,128},{64,192},{128,0},{192,64},{1,129},{65,193},{129,1},{193,65... | collective-permute-start | bytes 393224 | tf_op jit(solution)/shard_map/ppermute | solution.py:20
  11.7 1.3 collective-permute-start.1
  13.7 3.0 %collective-permute-start.5 = (bf16[32,1024]{1,0:T(8,128)(2,1)}, bf16[32,1024]{1,0:T(8,128)(2,1)S(1)}, u32[]{:S(2)}, u32[]{:S(2)}) collective-permute-start(bf16[32,1024]{1,0:T(8,128)(2,1)} %bitcast.16), channel_id=1, source_target_pairs={{0,16},{8,24},{16,0},{24,8},{1,17},{9,25},{17,1},{25,9},{2,18},{10... | collective-permute-start | bytes 196616 | tf_op jit(solution)/shard_map/ppermute | solution.py:20
  16.7 1.1 collective-permute-start.4
  17.9 1.1 collective-permute-start.3
  19.3 0.9 pad_maximum_fusion.wa
  20.2 1.0 collective-permute-done.4.c2
  21.2 2.4 %collective-permute-done.3.c1 = bf16[32,1024]{1,0:T(8,128)(2,1)S(1)} collective-permute-done((bf16[32,1024]{1,0:T(8,128)(2,1)}, bf16[32,1024]{1,0:T(8,128)(2,1)S(1)}, u32[]{:S(2)}, u32[]{:S(2)}) %collective-permute-start.3) | collective-permute-done | bytes 65568 | tf_op jit(solution)/shard_map/ppermute | solution.py:20
  23.6 1.9 %collective-permute-done.6.wb = bf16[512,512]{1,0:T(8,128)(2,1)S(1)} collective-permute-done((bf16[512,512]{1,0:T(8,128)(2,1)S(1)}, bf16[512,512]{1,0:T(8,128)(2,1)S(1)}, u32[]{:S(2)}, u32[]{:S(2)}) %collective-permute-start.6) | collective-permute-done | bytes 524320 | tf_op jit(solution)/shard_map/ppermute | solution.py:20
  25.5 1.9 %kv.1 = (bf16[8,128,512]{2,1,0:T(8,128)(2,1)S(1)}, bf16[1024,512]{1,0:T(8,128)(2,1)S(1)}) custom-call(bf16[32,1024]{1,0:T(8,128)(2,1)S(1)} %bitcast.19, bf16[32,1024]{1,0:T(8,128)(2,1)S(1)} %collective-permute-done.3.c1, bf16[32,1024]{1,0:T(8,128)(2,1)S(1)} %collective-permute-done.4.c2, bf16[32,1024]{1,0:T(8,128)(2,1)S(1)} %collective-permute-done.5.c3, ...), custom_call_target="tpu_custom_call" | custom-call | flops 134000000 | bytes 3072000 | tf_op jit(solution)/shard_map/kv/pallas_call | solution.py:290
  27.4 1.0 copy-done
  28.4 8.5 %all-to-all-start = ((bf16[8,128,512]{2,1,0:T(8,128)(2,1)}), bf16[8,128,512]{2,1,0:T(8,128)(2,1)S(1)}, u32[]{:S(2)}, u32[]{:S(2)}) async-start(bf16[8,128,512]{2,1,0:T(8,128)(2,1)} %copy-done), calls=%async_computation | async-start | bytes 2097152 | tf_op jit(solution)/shard_map/all_to_all | solution.py:296
  36.9 2.4 %collective-permute-start.10 = (bf16[128,1024]{1,0:T(8,128)(2,1)S(1)}, bf16[128,1024]{1,0:T(8,128)(2,1)S(1)}, u32[]{:S(2)}, u32[]{:S(2)}) collective-permute-start(bf16[128,1024]{1,0:T(8,128)(2,1)S(1)} %copy-done.11), channel_id=1, source_target_pairs={{0,0},{8,64},{16,128},{24,192},{64,8},{72,72},{80,136},{88,200},{1... | collective-permute-start | bytes 786440 | tf_op jit(solution)/shard_map/ppermute | solution.py:299
  39.3 2.5 %collective-permute-start.9 = (bf16[128,256]{1,0:T(8,128)(2,1)S(1)}, bf16[128,256]{1,0:T(8,128)(2,1)S(1)}, u32[]{:S(2)}, u32[]{:S(2)}) collective-permute-start(bf16[128,256]{1,0:T(8,128)(2,1)S(1)} %copy-done.10), channel_id=1, source_target_pairs={{0,128},{64,192},{128,0},{192,64},{1,129},{65,193},{129,1},{193,65... | collective-permute-start | bytes 196616 | tf_op jit(solution)/shard_map/ppermute | solution.py:20
  41.8 1.8 %collective-permute-start.8 = (bf16[128,256]{1,0:T(8,128)(2,1)S(1)}, bf16[128,256]{1,0:T(8,128)(2,1)S(1)}, u32[]{:S(2)}, u32[]{:S(2)}) collective-permute-start(bf16[128,256]{1,0:T(8,128)(2,1)S(1)} %copy-done.10), channel_id=1, source_target_pairs={{0,192},{64,0},{128,64},{192,128},{1,193},{65,1},{129,65},{193,129... | collective-permute-start | bytes 196616 | tf_op jit(solution)/shard_map/ppermute | solution.py:20
  43.8 11.2 %collective-permute-done.10 = bf16[128,1024]{1,0:T(8,128)(2,1)S(1)} collective-permute-done((bf16[128,1024]{1,0:T(8,128)(2,1)S(1)}, bf16[128,1024]{1,0:T(8,128)(2,1)S(1)}, u32[]{:S(2)}, u32[]{:S(2)}) %collective-permute-start.10) | collective-permute-done | bytes 262176 | tf_op jit(solution)/shard_map/ppermute | solution.py:299
  55.1 2.1 %collective-permute-done.7 = bf16[128,256]{1,0:T(8,128)(2,1)S(1)} collective-permute-done((bf16[128,256]{1,0:T(8,128)(2,1)S(1)}, bf16[128,256]{1,0:T(8,128)(2,1)S(1)}, u32[]{:S(2)}, u32[]{:S(2)}) %collective-permute-start.7) | collective-permute-done | bytes 65568 | tf_op jit(solution)/shard_map/ppermute | solution.py:20
  57.5 2.0 %collective-permute-done.11.wb = bf16[512,512]{1,0:T(8,128)(2,1)} collective-permute-done((bf16[512,512]{1,0:T(8,128)(2,1)S(1)}, bf16[512,512]{1,0:T(8,128)(2,1)}, u32[]{:S(2)}, u32[]{:S(2)}) %collective-permute-start.11) | collective-permute-done | bytes 524320 | tf_op jit(solution)/shard_map/ppermute | solution.py:20
  59.5 4.0 %queries.1 = (bf16[2,512,256]{2,1,0:T(8,128)(2,1)}, bf16[1024,256]{1,0:T(8,128)(2,1)}, bf16[256,1024]{1,0:T(8,128)(2,1)}) custom-call(bf16[4,272,1024]{2,1,0:T(8,128)(2,1)} %bitcast.20, bf16[512,512]{1,0:T(8,128)(2,1)} %copy-done.7, bf16[512,512]{1,0:T(8,128)(2,1)} %collective-permute-done.11.wb), custom_call_target="tpu_custom_call" | custom-call | flops 540000000 | bytes 5120000 | tf_op jit(solution)/shard_map/queries/pallas_call | solution.py:306
  63.5 2.4 %all-to-all-done = bf16[8,128,512]{2,1,0:T(8,128)(2,1)S(1)} async-done(((bf16[8,128,512]{2,1,0:T(8,128)(2,1)}), bf16[8,128,512]{2,1,0:T(8,128)(2,1)S(1)}, u32[]{:S(2)}, u32[]{:S(2)}) %all-to-all-start) | async-done | bytes 1048608 | tf_op jit(solution)/shard_map/all_to_all | solution.py:296
  65.9 1.0 copy-done.6
  67.0 12.3 %attention.1 = (bf16[1024,1024]{1,0:T(8,128)(2,1)}, bf16[512,256]{1,0:T(8,128)(2,1)S(1)}, bf16[512,256]{1,0:T(8,128)(2,1)S(1)}) custom-call(bf16[4,272,1024]{2,1,0:T(8,128)(2,1)} %bitcast.21, bf16[2,512,256]{2,1,0:T(8,128)(2,1)S(1)} %copy-done.6, bf16[1024,512]{1,0:T(8,128)(2,1)S(1)} %bitcast.15), custom_call_target="tpu_custom_call" | custom-call | flops 2200000000 | bytes 8192000 | tf_op jit(solution)/shard_map/attention/pallas_call | solution.py:314
  79.3 0.9 copy-done.3
  80.4 1.2 md.1
  81.6 29.3 %all_to_all.15 = bf16[4,256,1024]{2,1,0:T(8,128)(2,1)S(1)} all-to-all(bf16[4,256,1024]{2,1,0:T(8,128)(2,1)S(1)} %md.1), channel_id=1, replica_groups=mesh['y'=4,'c'=2,'x'=4,'z'=8] {'x'}, dimensions={0} | all-to-all | bytes 4194304 | tf_op jit(solution)/shard_map/all_to_all | solution.py:331
  112.8 6.1 %reduce-scatter.3.cloned.1.call-done.red = bf16[128,1024]{1,0:T(8,128)(2,1)} async-done(((bf16[1024,1024]{1,0:T(8,128)(2,1)}), bf16[128,1024]{1,0:T(8,128)(2,1)}) %reduce-scatter.3.cloned.1.call-update) | async-done | bytes 262160 | tf_op jit(solution)/shard_map/reduce_scatter | solution.py:327
  118.9 0.9 copy-done.1
  119.9 1.2 part.1
  121.1 0.9 copy-done.2
  122.2 16.7 %all_to_all.16 = bf16[32,40,128]{2,1,0:T(8,128)(2,1)S(1)} all-to-all(bf16[32,40,128]{2,1,0:T(8,128)(2,1)S(1)} %bitcast.14), channel_id=1, replica_groups=mesh['y'=4,'c'=2,'x'=4,'z'=8] {'y','c','x'}, dimensions={0} | all-to-all | bytes 655360 | tf_op jit(solution)/shard_map/all_to_all | solution.py:342
  139.5 5.4 %reduce-scatter.5.cloned.1.call-done = bf16[32,1024]{1,0:T(8,128)(2,1)} async-done(((bf16[128,1024]{1,0:T(8,128)(2,1)}), bf16[32,1024]{1,0:T(8,128)(2,1)}) %reduce-scatter.5.cloned.1.call-update) | async-done | bytes 65552 | tf_op jit(solution)/shard_map/reduce_scatter | solution.py:338
  (42 shorter events, 4.7 us)
Async XLA Ops:
  7.2 18.3 %copy-start.5 = (bf16[1,32,1024]{2,1,0:T(8,128)(2,1)S(1)}, bf16[1,32,1024]{2,1,0:T(8,128)(2,1)}, u32[]{:S(2)}) copy-start(bf16[1,32,1024]{2,1,0:T(8,128)(2,1)} %param.9) | copy-start | bytes 196612
  7.2 52.3 %all-gather.3.cloned.1.call-start = ((), (), s32[]{:S(2)}) async-start(), calls=%async_computation.7 | async-start | bytes 2785280 | tf_op jit(solution)/shard_map/all_gather | solution.py:284
  9.3 8.6 %collective-permute-start.2 = (bf16[128,512]{1,0:T(8,128)(2,1)}, bf16[128,512]{1,0:T(8,128)(2,1)S(1)}, u32[]{:S(2)}, u32[]{:S(2)}) collective-permute-start(bf16[128,512]{1,0:T(8,128)(2,1)} %get-tuple-element.30), channel_id=1, source_target_pairs={{0,128},{64,192},{128,0},{192,64},{1,129},{65,193},{129,1},{193,65... | collective-permute-start | bytes 393224 | tf_op jit(solution)/shard_map/ppermute | solution.py:20
  11.7 7.5 %collective-permute-start.1 = (bf16[128,512]{1,0:T(8,128)(2,1)}, bf16[128,512]{1,0:T(8,128)(2,1)S(1)}, u32[]{:S(2)}, u32[]{:S(2)}) collective-permute-start(bf16[128,512]{1,0:T(8,128)(2,1)} %get-tuple-element.30), channel_id=1, source_target_pairs={{0,192},{64,0},{128,64},{192,128},{1,193},{65,1},{129,65},{193,129... | collective-permute-start | bytes 393224 | tf_op jit(solution)/shard_map/ppermute | solution.py:20
  13.0 6.2 %collective-permute-start = (bf16[128,512]{1,0:T(8,128)(2,1)}, bf16[128,512]{1,0:T(8,128)(2,1)S(1)}, u32[]{:S(2)}, u32[]{:S(2)}) collective-permute-start(bf16[128,512]{1,0:T(8,128)(2,1)} %get-tuple-element.30), channel_id=1, source_target_pairs={{0,64},{64,128},{128,192},{192,0},{1,65},{65,129},{129,193},{193,1... | collective-permute-start | bytes 393224 | tf_op jit(solution)/shard_map/ppermute | solution.py:20
  13.7 23.2 %copy-start.11 = (bf16[128,1024]{1,0:T(8,128)(2,1)S(1)}, bf16[128,1024]{1,0:T(8,128)(2,1)}, u32[]{:S(2)}) copy-start(bf16[128,1024]{1,0:T(8,128)(2,1)} %param.14) | copy-start | bytes 786436
  13.7 25.6 %copy-start.10 = (bf16[128,256]{1,0:T(8,128)(2,1)S(1)}, bf16[128,256]{1,0:T(8,128)(2,1)}, u32[]{:S(2)}) copy-start(bf16[128,256]{1,0:T(8,128)(2,1)} %get-tuple-element.37) | copy-start | bytes 196612
  13.7 6.5 %collective-permute-start.5 = (bf16[32,1024]{1,0:T(8,128)(2,1)}, bf16[32,1024]{1,0:T(8,128)(2,1)S(1)}, u32[]{:S(2)}, u32[]{:S(2)}) collective-permute-start(bf16[32,1024]{1,0:T(8,128)(2,1)} %bitcast.16), channel_id=1, source_target_pairs={{0,16},{8,24},{16,0},{24,8},{1,17},{9,25},{17,1},{25,9},{2,18},{10... | collective-permute-start | bytes 196616 | tf_op jit(solution)/shard_map/ppermute | solution.py:20
  16.7 4.5 %collective-permute-start.4 = (bf16[32,1024]{1,0:T(8,128)(2,1)}, bf16[32,1024]{1,0:T(8,128)(2,1)S(1)}, u32[]{:S(2)}, u32[]{:S(2)}) collective-permute-start(bf16[32,1024]{1,0:T(8,128)(2,1)} %bitcast.17), channel_id=1, source_target_pairs={{0,24},{8,0},{16,8},{24,16},{1,25},{9,1},{17,9},{25,17},{2,26},{10... | collective-permute-start | bytes 196616 | tf_op jit(solution)/shard_map/ppermute | solution.py:20
  17.9 5.7 %collective-permute-start.3 = (bf16[32,1024]{1,0:T(8,128)(2,1)}, bf16[32,1024]{1,0:T(8,128)(2,1)S(1)}, u32[]{:S(2)}, u32[]{:S(2)}) collective-permute-start(bf16[32,1024]{1,0:T(8,128)(2,1)} %bitcast.18), channel_id=1, source_target_pairs={{0,8},{8,16},{16,24},{24,0},{1,9},{9,17},{17,25},{25,1},{2,10},{10... | collective-permute-start | bytes 196616 | tf_op jit(solution)/shard_map/ppermute | solution.py:20
  23.6 1.9 %collective-permute-start.6 = (bf16[512,512]{1,0:T(8,128)(2,1)S(1)}, bf16[512,512]{1,0:T(8,128)(2,1)S(1)}, u32[]{:S(2)}, u32[]{:S(2)}) collective-permute-start(bf16[512,512]{1,0:T(8,128)(2,1)S(1)} %pad_maximum_fusion.wa), channel_id=1, source_target_pairs={{0,32},{32,0},{1,33},{33,1},{2,34},{34,2},{3,35},{35,3},{4,36},{36... | collective-permute-start | bytes 1572872 | tf_op jit(solution)/shard_map/ppermute | solution.py:20
  27.4 1.0 copy-start
  28.4 37.5 %all-to-all-start = ((bf16[8,128,512]{2,1,0:T(8,128)(2,1)}), bf16[8,128,512]{2,1,0:T(8,128)(2,1)S(1)}, u32[]{:S(2)}, u32[]{:S(2)}) async-start(bf16[8,128,512]{2,1,0:T(8,128)(2,1)} %copy-done), calls=%async_computation | async-start | bytes 2097152 | tf_op jit(solution)/shard_map/all_to_all | solution.py:296
  36.8 82.1 %reduce-scatter.3.cloned.1.call-start = ((), (), s32[]{:S(2)}) async-start(), calls=%async_computation.5 | async-start | bytes 2359296 | tf_op jit(solution)/shard_map/reduce_scatter | solution.py:327
  36.9 18.1 %collective-permute-start.10 = (bf16[128,1024]{1,0:T(8,128)(2,1)S(1)}, bf16[128,1024]{1,0:T(8,128)(2,1)S(1)}, u32[]{:S(2)}, u32[]{:S(2)}) collective-permute-start(bf16[128,1024]{1,0:T(8,128)(2,1)S(1)} %copy-done.11), channel_id=1, source_target_pairs={{0,0},{8,64},{16,128},{24,192},{64,8},{72,72},{80,136},{88,200},{1... | collective-permute-start | bytes 786440 | tf_op jit(solution)/shard_map/ppermute | solution.py:299
  39.3 15.8 %collective-permute-start.9 = (bf16[128,256]{1,0:T(8,128)(2,1)S(1)}, bf16[128,256]{1,0:T(8,128)(2,1)S(1)}, u32[]{:S(2)}, u32[]{:S(2)}) collective-permute-start(bf16[128,256]{1,0:T(8,128)(2,1)S(1)} %copy-done.10), channel_id=1, source_target_pairs={{0,128},{64,192},{128,0},{192,64},{1,129},{65,193},{129,1},{193,65... | collective-permute-start | bytes 196616 | tf_op jit(solution)/shard_map/ppermute | solution.py:20
  41.8 13.3 %collective-permute-start.8 = (bf16[128,256]{1,0:T(8,128)(2,1)S(1)}, bf16[128,256]{1,0:T(8,128)(2,1)S(1)}, u32[]{:S(2)}, u32[]{:S(2)}) collective-permute-start(bf16[128,256]{1,0:T(8,128)(2,1)S(1)} %copy-done.10), channel_id=1, source_target_pairs={{0,192},{64,0},{128,64},{192,128},{1,193},{65,1},{129,65},{193,129... | collective-permute-start | bytes 196616 | tf_op jit(solution)/shard_map/ppermute | solution.py:20
  43.5 13.6 %collective-permute-start.7 = (bf16[128,256]{1,0:T(8,128)(2,1)S(1)}, bf16[128,256]{1,0:T(8,128)(2,1)S(1)}, u32[]{:S(2)}, u32[]{:S(2)}) collective-permute-start(bf16[128,256]{1,0:T(8,128)(2,1)S(1)} %copy-done.10), channel_id=1, source_target_pairs={{0,64},{64,128},{128,192},{192,0},{1,65},{65,129},{129,193},{193,1... | collective-permute-start | bytes 196616 | tf_op jit(solution)/shard_map/ppermute | solution.py:20
  57.2 2.3 %copy-start.7 = (bf16[512,512]{1,0:T(8,128)(2,1)}, bf16[512,512]{1,0:T(8,128)(2,1)S(1)}, u32[]{:S(2)}) copy-start(bf16[512,512]{1,0:T(8,128)(2,1)S(1)} %maximum_maximum_fusion.wa) | copy-start | bytes 1572868
  57.2 2.3 %collective-permute-start.11 = (bf16[512,512]{1,0:T(8,128)(2,1)S(1)}, bf16[512,512]{1,0:T(8,128)(2,1)}, u32[]{:S(2)}, u32[]{:S(2)}) collective-permute-start(bf16[512,512]{1,0:T(8,128)(2,1)S(1)} %maximum_maximum_fusion.wa), channel_id=1, source_target_pairs={{0,32},{32,0},{1,33},{33,1},{2,34},{34,2},{3,35},{35,3},{4,36},{36... | collective-permute-start | bytes 1572872 | tf_op jit(solution)/shard_map/ppermute | solution.py:20
  65.9 1.0 copy-start.6
  79.2 1.0 copy-start.3
  79.2 1.2 copy-start.4
  79.3 65.6 %reduce-scatter.5.cloned.1.call-start = ((), (), s32[]{:S(2)}) async-start(), calls=%async_computation.6 | async-start | bytes 327680 | tf_op jit(solution)/shard_map/reduce_scatter | solution.py:338
  110.9 1.0 copy-start.8
  110.9 1.0 copy-start.9
  118.9 0.9 copy-start.1
  121.1 1.0 copy-start.2
Sparse Core Ops, SparseCore 0:
  9.8 38.2 all-gather.2
  79.4 39.4 reduce-scatter.2
  122.0 22.7 reduce-scatter.4

commit v9 on v7

--- a/solution.py
+++ b/solution.py
@@ -97,8 +97,8 @@
     wait_all(run_copies(pairs, sems))
 
 
-def attn_kernel(xg, qd, kv, pay, att_out, dq_out, q_s, da_s,
-                kt_s, vt_s, dk_s, dv_s, at_s, dqt_s, gq_s, go_s, pay_s, mask_s, x_s, sems):
+def attn_kernel(xg, qd, kv, pay, at_s, dqt_s, q_s, da_s,
+                kt_s, vt_s, dk_s, dv_s, gq_s, go_s, pay_s, mask_s, x_s, sems):
     mask_copies = [
         pltpu.make_async_copy(xg.at[t, pl.ds(256, 16), :], mask_s.at[t], sems.at[t])
         for t in range(4)
@@ -195,8 +195,6 @@
                 pay_s[rows, lanes] = jnp.concatenate(part, axis=0).astype(BF)
         outs.append(pltpu.make_async_copy(pay_s.at[block, :], pay.at[block, :], sems.at[12 + zd]))
         outs[-1].start()
-    att_out[...] = at_s[...].T
-    dq_out[...] = dqt_s[...].T
     for copy in outs:
         copy.wait()
 
@@ -204,8 +202,8 @@
 def md_kernel(att, dq, wq, wo, out):
     for t in range(4):
         rows = slice(128 * t, 128 * t + 128)
-        out[t, 0:128, :] = dot(att[rows, :], wo[...], 1, 0).astype(BF)
-        out[t, 128:256, :] = dot(dq[rows, :], wq[...], 1, 1).astype(BF)
+        out[t, 0:128, :] = dot(att[:, rows], wo[...], 0, 0).astype(BF)
+        out[t, 128:256, :] = dot(dq[:, rows], wq[...], 0, 1).astype(BF)
 
 
 def split_kernel(red, w, p0, p1, p2, p3, g_out, part, g_s):
@@ -316,11 +314,10 @@
 
     pay, att, dq = call(
         attn_kernel, [H, H, V],
-        [sds((1024, 1024)), sds((512, 256)), sds((512, 256))],
+        [sds((1024, 1024)), sds((256, 512)), sds((256, 512))],
         [pltpu.VMEM((512, 256), BF), pltpu.VMEM((512, 256), BF),
          pltpu.VMEM((256, 1024), BF), pltpu.VMEM((256, 1024), BF),
          pltpu.VMEM((1024, 256), F32), pltpu.VMEM((1024, 256), F32),
-         pltpu.VMEM((256, 512), BF), pltpu.VMEM((256, 512), BF),
          pltpu.VMEM((2, 1024, 128), F32), pltpu.VMEM((8, 256, 128), F32),
          pltpu.VMEM((1024, 1024), BF), pltpu.VMEM((4, 16, 1024), BF),
          pltpu.VMEM((2, 512, 1024), BF), pltpu.SemaphoreType.DMA((22,))],

time: 148 us -> 148 us (level)
  no operation moved by 1% of the time
where the time goes in v9:
time: 148 us; the launch traced here: 147 us
  starting transfers between devices  37.9 us (26%)
  waiting for transfers between devices  34.7 us (23%)
  blocking collectives  29.3 us (20%)
  Pallas kernels  23.4 us (16%)
  between operations  14.2 us (10%)
  local copies, waits for them, and re-layouts  4.8 us (3%)
  other arithmetic  2.3 us (2%)
    all_to_all x1, blocking collectives, local(): md = lax.all_to_all(md, 'x', split_axis=0, concat_axis=0, tiled=True)  29.3 us
    ppermute x14, starting transfers between devices, shift(): return lax.ppermute(value, axis, [(i, (i + by) % n) for i in range(n)])  19.5 us
    ppermute x14, waiting for transfers between devices, shift(): return lax.ppermute(value, axis, [(i, (i + by) % n) for i in range(n)])  15 us
    pallas_call x1, Pallas kernels, local(): call(attn_kernel, [H, H, V], [sds((1024, 1024)), sds((256, 512)), sds((25...  12.3 us
    ppermute x1, waiting for transfers between devices, local(): lax.ppermute(w_out, ('y', 'x'), [(a * 4 + b, b * 4 + a) for a in range(4)...  11.2 us
    all_to_all x1, starting transfers between devices, local(): lax.all_to_all(kv8, 'z', split_axis=0, concat_axis=0, tiled=True)  8.46 us
    all_to_all x1, starting transfers between devices, local(): lax.all_to_all(g.reshape(32, 40, 128), ('y', 'c', 'x'), split_axis=0, con...  7.49 us
    reduce_scatter x1, waiting for transfers between devices, local(): red = lax.psum_scatter(pay, 'z', scatter_dimension=0, tiled=True)  6.09 us
  transfers between devices with their start and end apart: 19, of which 12 were waited for; matrix products, arithmetic and copies ran while one was open for 2% of the time, Pallas kernels for 5%

profile of v9, /device:TPU:8, one launch (start us, length us, event | category | flops | bytes accessed | tf_op | source)
XLA Modules:
  0.0 146.6 jit_solution(13361411905971158022)
XLA Ops:
  7.2 2.0 %pack.1 = (bf16[272,1024]{1,0:T(8,128)(2,1)}, bf16[128,512]{1,0:T(8,128)(2,1)}, bf16[128,256]{1,0:T(8,128)(2,1)}) custom-call(bf16[128,1024]{1,0:T(8,128)(2,1)} %bitcast.21, bf16[128,1024]{1,0:T(8,128)(2,1)} %bitcast.22, s32[2,16]{1,0:T(2,128)} %bitcast.25, bf16[128,1024]{1,0:T(8,128)(2,1)} %wk.1, bf16[128,1024]{1,0:T(8,128)(2,1)} %wv.1, bf16[128,1024]{1,0:T(8,128)(2,1)} %wq.1), custom_call_target="tpu_custom_call" | custom-call | flops 1000000 | bytes 1536000 | tf_op jit(solution)/shard_map/pack/pallas_call | solution.py:279
  9.3 2.4 %collective-permute-start.2 = (bf16[128,512]{1,0:T(8,128)(2,1)}, bf16[128,512]{1,0:T(8,128)(2,1)S(1)}, u32[]{:S(2)}, u32[]{:S(2)}) collective-permute-start(bf16[128,512]{1,0:T(8,128)(2,1)} %get-tuple-element.36), channel_id=1, source_target_pairs={{0,128},{64,192},{128,0},{192,64},{1,129},{65,193},{129,1},{193,65... | collective-permute-start | bytes 393224 | tf_op jit(solution)/shard_map/ppermute | solution.py:20
  11.7 1.3 collective-permute-start.1
  13.7 3.0 %collective-permute-start.5 = (bf16[32,1024]{1,0:T(8,128)(2,1)}, bf16[32,1024]{1,0:T(8,128)(2,1)S(1)}, u32[]{:S(2)}, u32[]{:S(2)}) collective-permute-start(bf16[32,1024]{1,0:T(8,128)(2,1)} %bitcast.15), channel_id=1, source_target_pairs={{0,16},{8,24},{16,0},{24,8},{1,17},{9,25},{17,1},{25,9},{2,18},{10... | collective-permute-start | bytes 196616 | tf_op jit(solution)/shard_map/ppermute | solution.py:20
  16.7 1.1 collective-permute-start.4
  17.9 1.1 collective-permute-start.3
  20.2 1.0 collective-permute-done.4.c2
  21.2 2.4 %collective-permute-done.3.c1 = bf16[32,1024]{1,0:T(8,128)(2,1)S(1)} collective-permute-done((bf16[32,1024]{1,0:T(8,128)(2,1)}, bf16[32,1024]{1,0:T(8,128)(2,1)S(1)}, u32[]{:S(2)}, u32[]{:S(2)}) %collective-permute-start.3) | collective-permute-done | bytes 65568 | tf_op jit(solution)/shard_map/ppermute | solution.py:20
  23.6 1.9 %collective-permute-done.6.wb = bf16[512,512]{1,0:T(8,128)(2,1)S(1)} collective-permute-done((bf16[512,512]{1,0:T(8,128)(2,1)S(1)}, bf16[512,512]{1,0:T(8,128)(2,1)S(1)}, u32[]{:S(2)}, u32[]{:S(2)}) %collective-permute-start.6) | collective-permute-done | bytes 524320 | tf_op jit(solution)/shard_map/ppermute | solution.py:20
  25.5 1.9 %kv.1 = (bf16[8,128,512]{2,1,0:T(8,128)(2,1)S(1)}, bf16[1024,512]{1,0:T(8,128)(2,1)S(1)}) custom-call(bf16[32,1024]{1,0:T(8,128)(2,1)S(1)} %bitcast.18, bf16[32,1024]{1,0:T(8,128)(2,1)S(1)} %collective-permute-done.3.c1, bf16[32,1024]{1,0:T(8,128)(2,1)S(1)} %collective-permute-done.4.c2, bf16[32,1024]{1,0:T(8,128)(2,1)S(1)} %collective-permute-done.5.c3, ...), custom_call_target="tpu_custom_call" | custom-call | flops 134000000 | bytes 3072000 | tf_op jit(solution)/shard_map/kv/pallas_call | solution.py:291
  28.4 8.5 %all-to-all-start = ((bf16[8,128,512]{2,1,0:T(8,128)(2,1)}), bf16[8,128,512]{2,1,0:T(8,128)(2,1)S(1)}, u32[]{:S(2)}, u32[]{:S(2)}) async-start(bf16[8,128,512]{2,1,0:T(8,128)(2,1)} %copy-done), calls=%async_computation | async-start | bytes 2097152 | tf_op jit(solution)/shard_map/all_to_all | solution.py:297
  36.9 2.4 %collective-permute-start.10 = (bf16[128,1024]{1,0:T(8,128)(2,1)S(1)}, bf16[128,1024]{1,0:T(8,128)(2,1)S(1)}, u32[]{:S(2)}, u32[]{:S(2)}) collective-permute-start(bf16[128,1024]{1,0:T(8,128)(2,1)S(1)} %copy-done.10), channel_id=1, source_target_pairs={{0,0},{8,64},{16,128},{24,192},{64,8},{72,72},{80,136},{88,200},{1... | collective-permute-start | bytes 786440 | tf_op jit(solution)/shard_map/ppermute | solution.py:300
  39.3 2.5 %collective-permute-start.9 = (bf16[128,256]{1,0:T(8,128)(2,1)S(1)}, bf16[128,256]{1,0:T(8,128)(2,1)S(1)}, u32[]{:S(2)}, u32[]{:S(2)}) collective-permute-start(bf16[128,256]{1,0:T(8,128)(2,1)S(1)} %copy-done.9), channel_id=1, source_target_pairs={{0,128},{64,192},{128,0},{192,64},{1,129},{65,193},{129,1},{193,65... | collective-permute-start | bytes 196616 | tf_op jit(solution)/shard_map/ppermute | solution.py:20
  41.7 1.8 %collective-permute-start.8 = (bf16[128,256]{1,0:T(8,128)(2,1)S(1)}, bf16[128,256]{1,0:T(8,128)(2,1)S(1)}, u32[]{:S(2)}, u32[]{:S(2)}) collective-permute-start(bf16[128,256]{1,0:T(8,128)(2,1)S(1)} %copy-done.9), channel_id=1, source_target_pairs={{0,192},{64,0},{128,64},{192,128},{1,193},{65,1},{129,65},{193,129... | collective-permute-start | bytes 196616 | tf_op jit(solution)/shard_map/ppermute | solution.py:20
  43.8 11.2 %collective-permute-done.10 = bf16[128,1024]{1,0:T(8,128)(2,1)S(1)} collective-permute-done((bf16[128,1024]{1,0:T(8,128)(2,1)S(1)}, bf16[128,1024]{1,0:T(8,128)(2,1)S(1)}, u32[]{:S(2)}, u32[]{:S(2)}) %collective-permute-start.10) | collective-permute-done | bytes 262176 | tf_op jit(solution)/shard_map/ppermute | solution.py:300
  55.0 2.1 %collective-permute-done.7 = bf16[128,256]{1,0:T(8,128)(2,1)S(1)} collective-permute-done((bf16[128,256]{1,0:T(8,128)(2,1)S(1)}, bf16[128,256]{1,0:T(8,128)(2,1)S(1)}, u32[]{:S(2)}, u32[]{:S(2)}) %collective-permute-start.7) | collective-permute-done | bytes 65568 | tf_op jit(solution)/shard_map/ppermute | solution.py:20
  57.4 2.0 %collective-permute-done.11.wb = bf16[512,512]{1,0:T(8,128)(2,1)} collective-permute-done((bf16[512,512]{1,0:T(8,128)(2,1)S(1)}, bf16[512,512]{1,0:T(8,128)(2,1)}, u32[]{:S(2)}, u32[]{:S(2)}) %collective-permute-start.11) | collective-permute-done | bytes 524320 | tf_op jit(solution)/shard_map/ppermute | solution.py:20
  59.5 4.0 %queries.1 = (bf16[2,512,256]{2,1,0:T(8,128)(2,1)}, bf16[1024,256]{1,0:T(8,128)(2,1)}, bf16[256,1024]{1,0:T(8,128)(2,1)}) custom-call(bf16[4,272,1024]{2,1,0:T(8,128)(2,1)} %bitcast.19, bf16[512,512]{1,0:T(8,128)(2,1)} %copy-done.6, bf16[512,512]{1,0:T(8,128)(2,1)} %collective-permute-done.11.wb), custom_call_target="tpu_custom_call" | custom-call | flops 540000000 | bytes 5120000 | tf_op jit(solution)/shard_map/queries/pallas_call | solution.py:307
  63.5 2.4 %all-to-all-done = bf16[8,128,512]{2,1,0:T(8,128)(2,1)S(1)} async-done(((bf16[8,128,512]{2,1,0:T(8,128)(2,1)}), bf16[8,128,512]{2,1,0:T(8,128)(2,1)S(1)}, u32[]{:S(2)}, u32[]{:S(2)}) %all-to-all-start) | async-done | bytes 1048608 | tf_op jit(solution)/shard_map/all_to_all | solution.py:297
  65.9 1.0 copy-done.5
  66.9 12.3 %attention.1 = (bf16[1024,1024]{1,0:T(8,128)(2,1)}, bf16[256,512]{1,0:T(8,128)(2,1)S(1)}, bf16[256,512]{1,0:T(8,128)(2,1)S(1)}) custom-call(bf16[4,272,1024]{2,1,0:T(8,128)(2,1)} %bitcast.20, bf16[2,512,256]{2,1,0:T(8,128)(2,1)S(1)} %copy-done.5, bf16[1024,512]{1,0:T(8,128)(2,1)S(1)} %bitcast.14), custom_call_target="tpu_custom_call" | custom-call | flops 2200000000 | bytes 8192000 | tf_op jit(solution)/shard_map/attention/pallas_call | solution.py:315
  79.3 1.0 copy-done.1
  80.4 1.2 md.1
  81.6 29.3 %all_to_all.15 = bf16[4,256,1024]{2,1,0:T(8,128)(2,1)S(1)} all-to-all(bf16[4,256,1024]{2,1,0:T(8,128)(2,1)S(1)} %md.1), channel_id=1, replica_groups=mesh['y'=4,'c'=2,'x'=4,'z'=8] {'x'}, dimensions={0} | all-to-all | bytes 4194304 | tf_op jit(solution)/shard_map/all_to_all | solution.py:331
  112.9 6.1 %reduce-scatter.2.cloned.1.call-done.red = bf16[128,1024]{1,0:T(8,128)(2,1)} async-done(((bf16[1024,1024]{1,0:T(8,128)(2,1)}), bf16[128,1024]{1,0:T(8,128)(2,1)}) %reduce-scatter.2.cloned.1.call-update) | async-done | bytes 262160 | tf_op jit(solution)/shard_map/reduce_scatter | solution.py:327
  119.9 1.2 split.1
  121.1 7.5 %all-to-all-start.2 = ((bf16[32,40,128]{2,1,0:T(8,128)(2,1)}), bf16[32,40,128]{2,1,0:T(8,128)(2,1)S(1)}, u32[]{:S(2)}, u32[]{:S(2)}) async-start(bf16[32,40,128]{2,1,0:T(8,128)(2,1)} %bitcast.8), calls=%async_computation.3 | async-start | bytes 655360 | tf_op jit(solution)/shard_map/all_to_all | solution.py:342
  128.6 1.5 %collective-permute-start.12 = (bf16[32,1024]{1,0:T(8,128)(2,1)S(1)}, bf16[32,1024]{1,0:T(8,128)(2,1)S(1)}, u32[]{:S(2)}, u32[]{:S(2)}) collective-permute-start(bf16[32,1024]{1,0:T(8,128)(2,1)S(1)} %get-tuple-element.57), channel_id=1, source_target_pairs={{0,8},{8,16},{16,24},{24,0},{1,9},{9,17},{17,25},{25,1},{2,10},{10... | collective-permute-start | bytes 196616 | tf_op jit(solution)/shard_map/ppermute | solution.py:20
  130.2 1.8 %collective-permute-start.13 = (bf16[32,1024]{1,0:T(8,128)(2,1)S(1)}, bf16[32,1024]{1,0:T(8,128)(2,1)S(1)}, u32[]{:S(2)}, u32[]{:S(2)}) collective-permute-start(bf16[32,1024]{1,0:T(8,128)(2,1)S(1)} %get-tuple-element.58), channel_id=1, source_target_pairs={{0,24},{8,0},{16,8},{24,16},{1,25},{9,1},{17,9},{25,17},{2,26},{10... | collective-permute-start | bytes 196616 | tf_op jit(solution)/shard_map/ppermute | solution.py:20
  132.0 1.8 %collective-permute-start.14 = (bf16[32,1024]{1,0:T(8,128)(2,1)S(1)}, bf16[32,1024]{1,0:T(8,128)(2,1)S(1)}, u32[]{:S(2)}, u32[]{:S(2)}) collective-permute-start(bf16[32,1024]{1,0:T(8,128)(2,1)S(1)} %get-tuple-element.59), channel_id=1, source_target_pairs={{0,16},{8,24},{16,0},{24,8},{1,17},{9,25},{17,1},{25,9},{2,18},{10... | collective-permute-start | bytes 196616 | tf_op jit(solution)/shard_map/ppermute | solution.py:20
  133.7 3.8 %collective-permute-done.12.p1 = bf16[32,1024]{1,0:T(8,128)(2,1)S(1)} collective-permute-done((bf16[32,1024]{1,0:T(8,128)(2,1)S(1)}, bf16[32,1024]{1,0:T(8,128)(2,1)S(1)}, u32[]{:S(2)}, u32[]{:S(2)}) %collective-permute-start.12) | collective-permute-done | bytes 65568 | tf_op jit(solution)/shard_map/ppermute | solution.py:20
  137.5 1.5 %collective-permute-done.14.p3 = bf16[32,1024]{1,0:T(8,128)(2,1)S(1)} collective-permute-done((bf16[32,1024]{1,0:T(8,128)(2,1)S(1)}, bf16[32,1024]{1,0:T(8,128)(2,1)S(1)}, u32[]{:S(2)}, u32[]{:S(2)}) %collective-permute-start.14) | collective-permute-done | bytes 65568 | tf_op jit(solution)/shard_map/ppermute | solution.py:20
  (43 shorter events, 7.4 us)
Async XLA Ops:
  7.2 18.3 %copy-start.4 = (bf16[1,32,1024]{2,1,0:T(8,128)(2,1)S(1)}, bf16[1,32,1024]{2,1,0:T(8,128)(2,1)}, u32[]{:S(2)}) copy-start(bf16[1,32,1024]{2,1,0:T(8,128)(2,1)} %param.9) | copy-start | bytes 196612
  7.2 52.3 %all-gather.3.cloned.1.call-start = ((), (), s32[]{:S(2)}) async-start(), calls=%async_computation.5 | async-start | bytes 2785280 | tf_op jit(solution)/shard_map/all_gather | solution.py:285
  9.3 8.6 %collective-permute-start.2 = (bf16[128,512]{1,0:T(8,128)(2,1)}, bf16[128,512]{1,0:T(8,128)(2,1)S(1)}, u32[]{:S(2)}, u32[]{:S(2)}) collective-permute-start(bf16[128,512]{1,0:T(8,128)(2,1)} %get-tuple-element.36), channel_id=1, source_target_pairs={{0,128},{64,192},{128,0},{192,64},{1,129},{65,193},{129,1},{193,65... | collective-permute-start | bytes 393224 | tf_op jit(solution)/shard_map/ppermute | solution.py:20
  11.7 7.5 %collective-permute-start.1 = (bf16[128,512]{1,0:T(8,128)(2,1)}, bf16[128,512]{1,0:T(8,128)(2,1)S(1)}, u32[]{:S(2)}, u32[]{:S(2)}) collective-permute-start(bf16[128,512]{1,0:T(8,128)(2,1)} %get-tuple-element.36), channel_id=1, source_target_pairs={{0,192},{64,0},{128,64},{192,128},{1,193},{65,1},{129,65},{193,129... | collective-permute-start | bytes 393224 | tf_op jit(solution)/shard_map/ppermute | solution.py:20
  13.0 6.2 %collective-permute-start = (bf16[128,512]{1,0:T(8,128)(2,1)}, bf16[128,512]{1,0:T(8,128)(2,1)S(1)}, u32[]{:S(2)}, u32[]{:S(2)}) collective-permute-start(bf16[128,512]{1,0:T(8,128)(2,1)} %get-tuple-element.36), channel_id=1, source_target_pairs={{0,64},{64,128},{128,192},{192,0},{1,65},{65,129},{129,193},{193,1... | collective-permute-start | bytes 393224 | tf_op jit(solution)/shard_map/ppermute | solution.py:20
  13.7 23.2 %copy-start.10 = (bf16[128,1024]{1,0:T(8,128)(2,1)S(1)}, bf16[128,1024]{1,0:T(8,128)(2,1)}, u32[]{:S(2)}) copy-start(bf16[128,1024]{1,0:T(8,128)(2,1)} %param.14) | copy-start | bytes 786436
  13.7 25.6 %copy-start.9 = (bf16[128,256]{1,0:T(8,128)(2,1)S(1)}, bf16[128,256]{1,0:T(8,128)(2,1)}, u32[]{:S(2)}) copy-start(bf16[128,256]{1,0:T(8,128)(2,1)} %get-tuple-element.43) | copy-start | bytes 196612
  13.7 6.5 %collective-permute-start.5 = (bf16[32,1024]{1,0:T(8,128)(2,1)}, bf16[32,1024]{1,0:T(8,128)(2,1)S(1)}, u32[]{:S(2)}, u32[]{:S(2)}) collective-permute-start(bf16[32,1024]{1,0:T(8,128)(2,1)} %bitcast.15), channel_id=1, source_target_pairs={{0,16},{8,24},{16,0},{24,8},{1,17},{9,25},{17,1},{25,9},{2,18},{10... | collective-permute-start | bytes 196616 | tf_op jit(solution)/shard_map/ppermute | solution.py:20
  16.7 4.5 %collective-permute-start.4 = (bf16[32,1024]{1,0:T(8,128)(2,1)}, bf16[32,1024]{1,0:T(8,128)(2,1)S(1)}, u32[]{:S(2)}, u32[]{:S(2)}) collective-permute-start(bf16[32,1024]{1,0:T(8,128)(2,1)} %bitcast.16), channel_id=1, source_target_pairs={{0,24},{8,0},{16,8},{24,16},{1,25},{9,1},{17,9},{25,17},{2,26},{10... | collective-permute-start | bytes 196616 | tf_op jit(solution)/shard_map/ppermute | solution.py:20
  17.9 5.7 %collective-permute-start.3 = (bf16[32,1024]{1,0:T(8,128)(2,1)}, bf16[32,1024]{1,0:T(8,128)(2,1)S(1)}, u32[]{:S(2)}, u32[]{:S(2)}) collective-permute-start(bf16[32,1024]{1,0:T(8,128)(2,1)} %bitcast.17), channel_id=1, source_target_pairs={{0,8},{8,16},{16,24},{24,0},{1,9},{9,17},{17,25},{25,1},{2,10},{10... | collective-permute-start | bytes 196616 | tf_op jit(solution)/shard_map/ppermute | solution.py:20
  23.6 1.9 %collective-permute-start.6 = (bf16[512,512]{1,0:T(8,128)(2,1)S(1)}, bf16[512,512]{1,0:T(8,128)(2,1)S(1)}, u32[]{:S(2)}, u32[]{:S(2)}) collective-permute-start(bf16[512,512]{1,0:T(8,128)(2,1)S(1)} %pad_maximum_fusion.wa), channel_id=1, source_target_pairs={{0,32},{32,0},{1,33},{33,1},{2,34},{34,2},{3,35},{35,3},{4,36},{36... | collective-permute-start | bytes 1572872 | tf_op jit(solution)/shard_map/ppermute | solution.py:20
  27.4 1.0 copy-start
  28.4 37.5 %all-to-all-start = ((bf16[8,128,512]{2,1,0:T(8,128)(2,1)}), bf16[8,128,512]{2,1,0:T(8,128)(2,1)S(1)}, u32[]{:S(2)}, u32[]{:S(2)}) async-start(bf16[8,128,512]{2,1,0:T(8,128)(2,1)} %copy-done), calls=%async_computation | async-start | bytes 2097152 | tf_op jit(solution)/shard_map/all_to_all | solution.py:297
  36.8 82.1 %reduce-scatter.2.cloned.1.call-start = ((), (), s32[]{:S(2)}) async-start(), calls=%async_computation.4 | async-start | bytes 2359296 | tf_op jit(solution)/shard_map/reduce_scatter | solution.py:327
  36.9 18.1 %collective-permute-start.10 = (bf16[128,1024]{1,0:T(8,128)(2,1)S(1)}, bf16[128,1024]{1,0:T(8,128)(2,1)S(1)}, u32[]{:S(2)}, u32[]{:S(2)}) collective-permute-start(bf16[128,1024]{1,0:T(8,128)(2,1)S(1)} %copy-done.10), channel_id=1, source_target_pairs={{0,0},{8,64},{16,128},{24,192},{64,8},{72,72},{80,136},{88,200},{1... | collective-permute-start | bytes 786440 | tf_op jit(solution)/shard_map/ppermute | solution.py:300
  39.3 15.8 %collective-permute-start.9 = (bf16[128,256]{1,0:T(8,128)(2,1)S(1)}, bf16[128,256]{1,0:T(8,128)(2,1)S(1)}, u32[]{:S(2)}, u32[]{:S(2)}) collective-permute-start(bf16[128,256]{1,0:T(8,128)(2,1)S(1)} %copy-done.9), channel_id=1, source_target_pairs={{0,128},{64,192},{128,0},{192,64},{1,129},{65,193},{129,1},{193,65... | collective-permute-start | bytes 196616 | tf_op jit(solution)/shard_map/ppermute | solution.py:20
  41.7 13.3 %collective-permute-start.8 = (bf16[128,256]{1,0:T(8,128)(2,1)S(1)}, bf16[128,256]{1,0:T(8,128)(2,1)S(1)}, u32[]{:S(2)}, u32[]{:S(2)}) collective-permute-start(bf16[128,256]{1,0:T(8,128)(2,1)S(1)} %copy-done.9), channel_id=1, source_target_pairs={{0,192},{64,0},{128,64},{192,128},{1,193},{65,1},{129,65},{193,129... | collective-permute-start | bytes 196616 | tf_op jit(solution)/shard_map/ppermute | solution.py:20
  43.5 13.6 %collective-permute-start.7 = (bf16[128,256]{1,0:T(8,128)(2,1)S(1)}, bf16[128,256]{1,0:T(8,128)(2,1)S(1)}, u32[]{:S(2)}, u32[]{:S(2)}) collective-permute-start(bf16[128,256]{1,0:T(8,128)(2,1)S(1)} %copy-done.9), channel_id=1, source_target_pairs={{0,64},{64,128},{128,192},{192,0},{1,65},{65,129},{129,193},{193,1... | collective-permute-start | bytes 196616 | tf_op jit(solution)/shard_map/ppermute | solution.py:20
  57.1 2.3 %copy-start.6 = (bf16[512,512]{1,0:T(8,128)(2,1)}, bf16[512,512]{1,0:T(8,128)(2,1)S(1)}, u32[]{:S(2)}) copy-start(bf16[512,512]{1,0:T(8,128)(2,1)S(1)} %maximum_maximum_fusion.wa) | copy-start | bytes 1572868
  57.2 2.3 %collective-permute-start.11 = (bf16[512,512]{1,0:T(8,128)(2,1)S(1)}, bf16[512,512]{1,0:T(8,128)(2,1)}, u32[]{:S(2)}, u32[]{:S(2)}) collective-permute-start(bf16[512,512]{1,0:T(8,128)(2,1)S(1)} %maximum_maximum_fusion.wa), channel_id=1, source_target_pairs={{0,32},{32,0},{1,33},{33,1},{2,34},{34,2},{3,35},{35,3},{4,36},{36... | collective-permute-start | bytes 1572872 | tf_op jit(solution)/shard_map/ppermute | solution.py:20
  65.9 1.0 copy-start.5
  79.2 1.0 copy-start.1
  79.2 1.2 copy-start.2
  110.9 1.0 copy-start.7
  110.9 1.0 copy-start.8
  118.9 0.9 copy-start.3
  121.1 17.9 %all-to-all-start.2 = ((bf16[32,40,128]{2,1,0:T(8,128)(2,1)}), bf16[32,40,128]{2,1,0:T(8,128)(2,1)S(1)}, u32[]{:S(2)}, u32[]{:S(2)}) async-start(bf16[32,40,128]{2,1,0:T(8,128)(2,1)} %bitcast.8), calls=%async_computation.3 | async-start | bytes 655360 | tf_op jit(solution)/shard_map/all_to_all | solution.py:342
  128.6 8.9 %collective-permute-start.12 = (bf16[32,1024]{1,0:T(8,128)(2,1)S(1)}, bf16[32,1024]{1,0:T(8,128)(2,1)S(1)}, u32[]{:S(2)}, u32[]{:S(2)}) collective-permute-start(bf16[32,1024]{1,0:T(8,128)(2,1)S(1)} %get-tuple-element.57), channel_id=1, source_target_pairs={{0,8},{8,16},{16,24},{24,0},{1,9},{9,17},{17,25},{25,1},{2,10},{10... | collective-permute-start | bytes 196616 | tf_op jit(solution)/shard_map/ppermute | solution.py:20
  130.2 7.3 %collective-permute-start.13 = (bf16[32,1024]{1,0:T(8,128)(2,1)S(1)}, bf16[32,1024]{1,0:T(8,128)(2,1)S(1)}, u32[]{:S(2)}, u32[]{:S(2)}) collective-permute-start(bf16[32,1024]{1,0:T(8,128)(2,1)S(1)} %get-tuple-element.58), channel_id=1, source_target_pairs={{0,24},{8,0},{16,8},{24,16},{1,25},{9,1},{17,9},{25,17},{2,26},{10... | collective-permute-start | bytes 196616 | tf_op jit(solution)/shard_map/ppermute | solution.py:20
  132.0 7.1 %collective-permute-start.14 = (bf16[32,1024]{1,0:T(8,128)(2,1)S(1)}, bf16[32,1024]{1,0:T(8,128)(2,1)S(1)}, u32[]{:S(2)}, u32[]{:S(2)}) collective-permute-start(bf16[32,1024]{1,0:T(8,128)(2,1)S(1)} %get-tuple-element.59), channel_id=1, source_target_pairs={{0,16},{8,24},{16,0},{24,8},{1,17},{9,25},{17,1},{25,9},{2,18},{10... | collective-permute-start | bytes 196616 | tf_op jit(solution)/shard_map/ppermute | solution.py:20
Sparse Core Ops, SparseCore 0:
  9.8 38.2 all-gather.2
  79.4 39.5 reduce-scatter.1

commit v10 on v9

--- a/solution.py
+++ b/solution.py
@@ -309,7 +309,7 @@
         [sds((2, 512, 256)), sds((1024, 256)), sds((256, 1024))],
         [pltpu.VMEM((2, 512, 1024), BF), pltpu.VMEM((1024, 256), BF), pltpu.VMEM((256, 1024), BF),
          pltpu.VMEM((512, 256), BF), pltpu.VMEM((512, 256), BF), pltpu.SemaphoreType.DMA((24,))],
-        540, 5000, 61, "queries", [H] * 3,
+        540, 5000, 24, "queries", [H] * 3,
     )(xg, wa, wb)
 
     pay, att, dq = call(

time: 148 us -> 150 us (1.014)
  local copies, waits for them, and re-layouts: 4.8 us -> 8.75 us
  Pallas kernels: 23.4 us -> 20.2 us
  blocking collectives: 29.3 us -> 31.6 us
    unnamed x22 -> x26, local copies, waits for them, and re-layouts: 4.78 us -> 8.73 us
    pallas_call x1, Pallas kernels: 4.03 us -> 1.33 us  [local(): call(qd_kernel, [H, H, H], [sds((2, 512, 256)), sds((1024, 256)), sds((25...]
    all_to_all x1, blocking collectives: 29.3 us -> 31.6 us  [local(): md = lax.all_to_all(md, 'x', split_axis=0, concat_axis=0, tiled=True)]
    all_to_all x1, waiting for transfers between devices: 2.39 us -> 0.33 us  [local(): lax.all_to_all(kv8, 'z', split_axis=0, concat_axis=0, tiled=True)]
  transfers between devices with their start and end apart: 19 -> 19, of which waited for: 12 -> 12; matrix products, arithmetic and copies ran while one was open for 2% -> 2% of each run, Pallas kernels for 5% -> 3%
where the time goes in v10:
time: 150 us; the launch traced here: 148 us
  starting transfers between devices  37.5 us (25%)
  waiting for transfers between devices  33.9 us (23%)
  blocking collectives  31.6 us (21%)
  Pallas kernels  20.2 us (13%)
  between operations  14.2 us (9%)
  local copies, waits for them, and re-layouts  8.75 us (6%)
  other arithmetic  2.3 us (2%)
    all_to_all x1, blocking collectives, local(): md = lax.all_to_all(md, 'x', split_axis=0, concat_axis=0, tiled=True)  31.6 us
    ppermute x14, starting transfers between devices, shift(): return lax.ppermute(value, axis, [(i, (i + by) % n) for i in range(n)])  19.3 us
    ppermute x14, waiting for transfers between devices, shift(): return lax.ppermute(value, axis, [(i, (i + by) % n) for i in range(n)])  15.9 us
    pallas_call x1, Pallas kernels, local(): call(attn_kernel, [H, H, V], [sds((1024, 1024)), sds((256, 512)), sds((25...  12.3 us
    ppermute x1, waiting for transfers between devices, local(): lax.ppermute(w_out, ('y', 'x'), [(a * 4 + b, b * 4 + a) for a in range(4)...  10.1 us
    unnamed x26, local copies, waits for them, and re-layouts  8.73 us
    all_to_all x1, starting transfers between devices, local(): lax.all_to_all(kv8, 'z', split_axis=0, concat_axis=0, tiled=True)  8.48 us
    reduce_scatter x1, waiting for transfers between devices, local(): red = lax.psum_scatter(pay, 'z', scatter_dimension=0, tiled=True)  7.47 us
  transfers between devices with their start and end apart: 19, of which 12 were waited for; matrix products, arithmetic and copies ran while one was open for 2% of the time, Pallas kernels for 3%

profile of v10, /device:TPU:8, one launch (start us, length us, event | category | flops | bytes accessed | tf_op | source)
XLA Modules:
  0.0 148.5 jit_solution(15524766764560956682)
XLA Ops:
  7.2 2.0 %pack.1 = (bf16[272,1024]{1,0:T(8,128)(2,1)}, bf16[128,512]{1,0:T(8,128)(2,1)}, bf16[128,256]{1,0:T(8,128)(2,1)}) custom-call(bf16[128,1024]{1,0:T(8,128)(2,1)} %bitcast.21, bf16[128,1024]{1,0:T(8,128)(2,1)} %bitcast.22, s32[2,16]{1,0:T(2,128)} %bitcast.25, bf16[128,1024]{1,0:T(8,128)(2,1)} %wk.1, bf16[128,1024]{1,0:T(8,128)(2,1)} %wv.1, bf16[128,1024]{1,0:T(8,128)(2,1)} %wq.1), custom_call_target="tpu_custom_call" | custom-call | flops 1000000 | bytes 1536000 | tf_op jit(solution)/shard_map/pack/pallas_call | solution.py:279
  9.3 2.4 %collective-permute-start.2 = (bf16[128,512]{1,0:T(8,128)(2,1)}, bf16[128,512]{1,0:T(8,128)(2,1)S(1)}, u32[]{:S(2)}, u32[]{:S(2)}) collective-permute-start(bf16[128,512]{1,0:T(8,128)(2,1)} %get-tuple-element.36), channel_id=1, source_target_pairs={{0,128},{64,192},{128,0},{192,64},{1,129},{65,193},{129,1},{193,65... | collective-permute-start | bytes 393224 | tf_op jit(solution)/shard_map/ppermute | solution.py:20
  11.7 1.3 collective-permute-start.1
  13.7 3.0 %collective-permute-start.5 = (bf16[32,1024]{1,0:T(8,128)(2,1)}, bf16[32,1024]{1,0:T(8,128)(2,1)S(1)}, u32[]{:S(2)}, u32[]{:S(2)}) collective-permute-start(bf16[32,1024]{1,0:T(8,128)(2,1)} %bitcast.17), channel_id=1, source_target_pairs={{0,16},{8,24},{16,0},{24,8},{1,17},{9,25},{17,1},{25,9},{2,18},{10... | collective-permute-start | bytes 196616 | tf_op jit(solution)/shard_map/ppermute | solution.py:20
  16.7 1.1 collective-permute-start.4
  17.9 1.1 collective-permute-start.3
  21.2 2.4 %collective-permute-done.3.c1 = bf16[32,1024]{1,0:T(8,128)(2,1)S(1)} collective-permute-done((bf16[32,1024]{1,0:T(8,128)(2,1)}, bf16[32,1024]{1,0:T(8,128)(2,1)S(1)}, u32[]{:S(2)}, u32[]{:S(2)}) %collective-permute-start.3) | collective-permute-done | bytes 65568 | tf_op jit(solution)/shard_map/ppermute | solution.py:20
  23.6 1.9 %collective-permute-done.6.wb = bf16[512,512]{1,0:T(8,128)(2,1)S(1)} collective-permute-done((bf16[512,512]{1,0:T(8,128)(2,1)S(1)}, bf16[512,512]{1,0:T(8,128)(2,1)S(1)}, u32[]{:S(2)}, u32[]{:S(2)}) %collective-permute-start.6) | collective-permute-done | bytes 524320 | tf_op jit(solution)/shard_map/ppermute | solution.py:20
  25.5 1.5 kv.1
  26.9 8.5 %all-to-all-start = ((bf16[8,128,512]{2,1,0:T(8,128)(2,1)}), bf16[8,128,512]{2,1,0:T(8,128)(2,1)S(1)}, u32[]{:S(2)}, u32[]{:S(2)}) async-start(bf16[8,128,512]{2,1,0:T(8,128)(2,1)} %get-tuple-element.42), calls=%async_computation | async-start | bytes 2097152 | tf_op jit(solution)/shard_map/all_to_all | solution.py:297
  35.5 2.4 %collective-permute-start.10 = (bf16[128,1024]{1,0:T(8,128)(2,1)S(1)}, bf16[128,1024]{1,0:T(8,128)(2,1)S(1)}, u32[]{:S(2)}, u32[]{:S(2)}) collective-permute-start(bf16[128,1024]{1,0:T(8,128)(2,1)S(1)} %copy-done.12), channel_id=1, source_target_pairs={{0,0},{8,64},{16,128},{24,192},{64,8},{72,72},{80,136},{88,200},{1... | collective-permute-start | bytes 786440 | tf_op jit(solution)/shard_map/ppermute | solution.py:300
  37.9 2.5 %collective-permute-start.9 = (bf16[128,256]{1,0:T(8,128)(2,1)S(1)}, bf16[128,256]{1,0:T(8,128)(2,1)S(1)}, u32[]{:S(2)}, u32[]{:S(2)}) collective-permute-start(bf16[128,256]{1,0:T(8,128)(2,1)S(1)} %copy-done.11), channel_id=1, source_target_pairs={{0,128},{64,192},{128,0},{192,64},{1,129},{65,193},{129,1},{193,65... | collective-permute-start | bytes 196616 | tf_op jit(solution)/shard_map/ppermute | solution.py:20
  40.3 1.8 %collective-permute-start.8 = (bf16[128,256]{1,0:T(8,128)(2,1)S(1)}, bf16[128,256]{1,0:T(8,128)(2,1)S(1)}, u32[]{:S(2)}, u32[]{:S(2)}) collective-permute-start(bf16[128,256]{1,0:T(8,128)(2,1)S(1)} %copy-done.11), channel_id=1, source_target_pairs={{0,192},{64,0},{128,64},{192,128},{1,193},{65,1},{129,65},{193,129... | collective-permute-start | bytes 196616 | tf_op jit(solution)/shard_map/ppermute | solution.py:20
  42.4 10.1 %collective-permute-done.10 = bf16[128,1024]{1,0:T(8,128)(2,1)S(1)} collective-permute-done((bf16[128,1024]{1,0:T(8,128)(2,1)S(1)}, bf16[128,1024]{1,0:T(8,128)(2,1)S(1)}, u32[]{:S(2)}, u32[]{:S(2)}) %collective-permute-start.10) | collective-permute-done | bytes 262176 | tf_op jit(solution)/shard_map/ppermute | solution.py:300
  52.5 3.2 %collective-permute-done.7 = bf16[128,256]{1,0:T(8,128)(2,1)S(1)} collective-permute-done((bf16[128,256]{1,0:T(8,128)(2,1)S(1)}, bf16[128,256]{1,0:T(8,128)(2,1)S(1)}, u32[]{:S(2)}, u32[]{:S(2)}) %collective-permute-start.7) | collective-permute-done | bytes 65568 | tf_op jit(solution)/shard_map/ppermute | solution.py:20
  55.8 1.9 %collective-permute-done.11.wb = bf16[512,512]{1,0:T(8,128)(2,1)S(1)} collective-permute-done((bf16[512,512]{1,0:T(8,128)(2,1)S(1)}, bf16[512,512]{1,0:T(8,128)(2,1)S(1)}, u32[]{:S(2)}, u32[]{:S(2)}) %collective-permute-start.11) | collective-permute-done | bytes 524320 | tf_op jit(solution)/shard_map/ppermute | solution.py:20
  58.5 1.6 %copy-done = bf16[1088,1024]{1,0:T(8,128)(2,1)S(1)} copy-done((bf16[1088,1024]{1,0:T(8,128)(2,1)S(1)}, bf16[1088,1024]{1,0:T(8,128)(2,1)}, u32[]{:S(2)}) %copy-start) | copy-done | bytes 2228248
  60.2 1.0 copy-done.4
  61.2 1.3 queries.1
  64.5 1.0 copy-done.8
  65.5 12.3 %attention.1 = (bf16[1024,1024]{1,0:T(8,128)(2,1)}, bf16[256,512]{1,0:T(8,128)(2,1)S(1)}, bf16[256,512]{1,0:T(8,128)(2,1)S(1)}) custom-call(bf16[4,272,1024]{2,1,0:T(8,128)(2,1)} %bitcast.13, bf16[2,512,256]{2,1,0:T(8,128)(2,1)S(1)} %copy-done.8, bf16[1024,512]{1,0:T(8,128)(2,1)S(1)} %bitcast.16), custom_call_target="tpu_custom_call" | custom-call | flops 2200000000 | bytes 8192000 | tf_op jit(solution)/shard_map/attention/pallas_call | solution.py:315
  77.9 1.0 copy-done.2
  78.9 1.2 md.1
  80.1 31.6 %all_to_all.15 = bf16[4,256,1024]{2,1,0:T(8,128)(2,1)S(1)} all-to-all(bf16[4,256,1024]{2,1,0:T(8,128)(2,1)S(1)} %md.1), channel_id=1, replica_groups=mesh['y'=4,'c'=2,'x'=4,'z'=8] {'x'}, dimensions={0} | all-to-all | bytes 4194304 | tf_op jit(solution)/shard_map/all_to_all | solution.py:331
  113.6 7.5 %reduce-scatter.2.cloned.1.call-done.red = bf16[128,1024]{1,0:T(8,128)(2,1)} async-done(((bf16[1024,1024]{1,0:T(8,128)(2,1)}), bf16[128,1024]{1,0:T(8,128)(2,1)}) %reduce-scatter.2.cloned.1.call-update) | async-done | bytes 262160 | tf_op jit(solution)/shard_map/reduce_scatter | solution.py:327
  122.0 1.3 split.1
  123.3 7.2 %all-to-all-start.2 = ((bf16[32,40,128]{2,1,0:T(8,128)(2,1)}), bf16[32,40,128]{2,1,0:T(8,128)(2,1)S(1)}, u32[]{:S(2)}, u32[]{:S(2)}) async-start(bf16[32,40,128]{2,1,0:T(8,128)(2,1)} %bitcast.8), calls=%async_computation.3 | async-start | bytes 655360 | tf_op jit(solution)/shard_map/all_to_all | solution.py:342
  130.5 1.5 %collective-permute-start.12 = (bf16[32,1024]{1,0:T(8,128)(2,1)S(1)}, bf16[32,1024]{1,0:T(8,128)(2,1)S(1)}, u32[]{:S(2)}, u32[]{:S(2)}) collective-permute-start(bf16[32,1024]{1,0:T(8,128)(2,1)S(1)} %get-tuple-element.57), channel_id=1, source_target_pairs={{0,8},{8,16},{16,24},{24,0},{1,9},{9,17},{17,25},{25,1},{2,10},{10... | collective-permute-start | bytes 196616 | tf_op jit(solution)/shard_map/ppermute | solution.py:20
  132.1 1.8 %collective-permute-start.13 = (bf16[32,1024]{1,0:T(8,128)(2,1)S(1)}, bf16[32,1024]{1,0:T(8,128)(2,1)S(1)}, u32[]{:S(2)}, u32[]{:S(2)}) collective-permute-start(bf16[32,1024]{1,0:T(8,128)(2,1)S(1)} %get-tuple-element.58), channel_id=1, source_target_pairs={{0,24},{8,0},{16,8},{24,16},{1,25},{9,1},{17,9},{25,17},{2,26},{10... | collective-permute-start | bytes 196616 | tf_op jit(solution)/shard_map/ppermute | solution.py:20
  133.9 1.8 %collective-permute-start.14 = (bf16[32,1024]{1,0:T(8,128)(2,1)S(1)}, bf16[32,1024]{1,0:T(8,128)(2,1)S(1)}, u32[]{:S(2)}, u32[]{:S(2)}) collective-permute-start(bf16[32,1024]{1,0:T(8,128)(2,1)S(1)} %get-tuple-element.59), channel_id=1, source_target_pairs={{0,16},{8,24},{16,0},{24,8},{1,17},{9,25},{17,1},{25,9},{2,18},{10... | collective-permute-start | bytes 196616 | tf_op jit(solution)/shard_map/ppermute | solution.py:20
  135.6 3.8 %collective-permute-done.12.p1 = bf16[32,1024]{1,0:T(8,128)(2,1)S(1)} collective-permute-done((bf16[32,1024]{1,0:T(8,128)(2,1)S(1)}, bf16[32,1024]{1,0:T(8,128)(2,1)S(1)}, u32[]{:S(2)}, u32[]{:S(2)}) %collective-permute-start.12) | collective-permute-done | bytes 65568 | tf_op jit(solution)/shard_map/ppermute | solution.py:20
  139.4 1.5 %collective-permute-done.14.p3 = bf16[32,1024]{1,0:T(8,128)(2,1)S(1)} collective-permute-done((bf16[32,1024]{1,0:T(8,128)(2,1)S(1)}, bf16[32,1024]{1,0:T(8,128)(2,1)S(1)}, u32[]{:S(2)}, u32[]{:S(2)}) %collective-permute-start.14) | collective-permute-done | bytes 65568 | tf_op jit(solution)/shard_map/ppermute | solution.py:20
  (47 shorter events, 9.8 us)
Async XLA Ops:
  7.2 18.3 %copy-start.6 = (bf16[1,32,1024]{2,1,0:T(8,128)(2,1)S(1)}, bf16[1,32,1024]{2,1,0:T(8,128)(2,1)}, u32[]{:S(2)}) copy-start(bf16[1,32,1024]{2,1,0:T(8,128)(2,1)} %param.9) | copy-start | bytes 196612
  7.2 51.4 %all-gather.3.cloned.1.call-start = ((), (), s32[]{:S(2)}) async-start(), calls=%async_computation.5 | async-start | bytes 2785280 | tf_op jit(solution)/shard_map/all_gather | solution.py:285
  9.3 8.6 %collective-permute-start.2 = (bf16[128,512]{1,0:T(8,128)(2,1)}, bf16[128,512]{1,0:T(8,128)(2,1)S(1)}, u32[]{:S(2)}, u32[]{:S(2)}) collective-permute-start(bf16[128,512]{1,0:T(8,128)(2,1)} %get-tuple-element.36), channel_id=1, source_target_pairs={{0,128},{64,192},{128,0},{192,64},{1,129},{65,193},{129,1},{193,65... | collective-permute-start | bytes 393224 | tf_op jit(solution)/shard_map/ppermute | solution.py:20
  11.7 7.5 %collective-permute-start.1 = (bf16[128,512]{1,0:T(8,128)(2,1)}, bf16[128,512]{1,0:T(8,128)(2,1)S(1)}, u32[]{:S(2)}, u32[]{:S(2)}) collective-permute-start(bf16[128,512]{1,0:T(8,128)(2,1)} %get-tuple-element.36), channel_id=1, source_target_pairs={{0,192},{64,0},{128,64},{192,128},{1,193},{65,1},{129,65},{193,129... | collective-permute-start | bytes 393224 | tf_op jit(solution)/shard_map/ppermute | solution.py:20
  13.0 6.2 %collective-permute-start = (bf16[128,512]{1,0:T(8,128)(2,1)}, bf16[128,512]{1,0:T(8,128)(2,1)S(1)}, u32[]{:S(2)}, u32[]{:S(2)}) collective-permute-start(bf16[128,512]{1,0:T(8,128)(2,1)} %get-tuple-element.36), channel_id=1, source_target_pairs={{0,64},{64,128},{128,192},{192,0},{1,65},{65,129},{129,193},{193,1... | collective-permute-start | bytes 393224 | tf_op jit(solution)/shard_map/ppermute | solution.py:20
  13.7 21.8 %copy-start.12 = (bf16[128,1024]{1,0:T(8,128)(2,1)S(1)}, bf16[128,1024]{1,0:T(8,128)(2,1)}, u32[]{:S(2)}) copy-start(bf16[128,1024]{1,0:T(8,128)(2,1)} %param.14) | copy-start | bytes 786436
  13.7 24.2 %copy-start.11 = (bf16[128,256]{1,0:T(8,128)(2,1)S(1)}, bf16[128,256]{1,0:T(8,128)(2,1)}, u32[]{:S(2)}) copy-start(bf16[128,256]{1,0:T(8,128)(2,1)} %get-tuple-element.43) | copy-start | bytes 196612
  13.7 6.5 %collective-permute-start.5 = (bf16[32,1024]{1,0:T(8,128)(2,1)}, bf16[32,1024]{1,0:T(8,128)(2,1)S(1)}, u32[]{:S(2)}, u32[]{:S(2)}) collective-permute-start(bf16[32,1024]{1,0:T(8,128)(2,1)} %bitcast.17), channel_id=1, source_target_pairs={{0,16},{8,24},{16,0},{24,8},{1,17},{9,25},{17,1},{25,9},{2,18},{10... | collective-permute-start | bytes 196616 | tf_op jit(solution)/shard_map/ppermute | solution.py:20
  16.7 4.5 %collective-permute-start.4 = (bf16[32,1024]{1,0:T(8,128)(2,1)}, bf16[32,1024]{1,0:T(8,128)(2,1)S(1)}, u32[]{:S(2)}, u32[]{:S(2)}) collective-permute-start(bf16[32,1024]{1,0:T(8,128)(2,1)} %bitcast.18), channel_id=1, source_target_pairs={{0,24},{8,0},{16,8},{24,16},{1,25},{9,1},{17,9},{25,17},{2,26},{10... | collective-permute-start | bytes 196616 | tf_op jit(solution)/shard_map/ppermute | solution.py:20
  17.9 5.7 %collective-permute-start.3 = (bf16[32,1024]{1,0:T(8,128)(2,1)}, bf16[32,1024]{1,0:T(8,128)(2,1)S(1)}, u32[]{:S(2)}, u32[]{:S(2)}) collective-permute-start(bf16[32,1024]{1,0:T(8,128)(2,1)} %bitcast.19), channel_id=1, source_target_pairs={{0,8},{8,16},{16,24},{24,0},{1,9},{9,17},{17,25},{25,1},{2,10},{10... | collective-permute-start | bytes 196616 | tf_op jit(solution)/shard_map/ppermute | solution.py:20
  23.6 1.9 %collective-permute-start.6 = (bf16[512,512]{1,0:T(8,128)(2,1)S(1)}, bf16[512,512]{1,0:T(8,128)(2,1)S(1)}, u32[]{:S(2)}, u32[]{:S(2)}) collective-permute-start(bf16[512,512]{1,0:T(8,128)(2,1)S(1)} %pad_maximum_fusion.wa), channel_id=1, source_target_pairs={{0,32},{32,0},{1,33},{33,1},{2,34},{34,2},{3,35},{35,3},{4,36},{36... | collective-permute-start | bytes 1572872 | tf_op jit(solution)/shard_map/ppermute | solution.py:20
  26.9 37.6 %all-to-all-start = ((bf16[8,128,512]{2,1,0:T(8,128)(2,1)}), bf16[8,128,512]{2,1,0:T(8,128)(2,1)S(1)}, u32[]{:S(2)}, u32[]{:S(2)}) async-start(bf16[8,128,512]{2,1,0:T(8,128)(2,1)} %get-tuple-element.42), calls=%async_computation | async-start | bytes 2097152 | tf_op jit(solution)/shard_map/all_to_all | solution.py:297
  35.4 85.7 %reduce-scatter.2.cloned.1.call-start = ((), (), s32[]{:S(2)}) async-start(), calls=%async_computation.4 | async-start | bytes 2359296 | tf_op jit(solution)/shard_map/reduce_scatter | solution.py:327
  35.5 17.0 %collective-permute-start.10 = (bf16[128,1024]{1,0:T(8,128)(2,1)S(1)}, bf16[128,1024]{1,0:T(8,128)(2,1)S(1)}, u32[]{:S(2)}, u32[]{:S(2)}) collective-permute-start(bf16[128,1024]{1,0:T(8,128)(2,1)S(1)} %copy-done.12), channel_id=1, source_target_pairs={{0,0},{8,64},{16,128},{24,192},{64,8},{72,72},{80,136},{88,200},{1... | collective-permute-start | bytes 786440 | tf_op jit(solution)/shard_map/ppermute | solution.py:300
  37.9 14.6 %collective-permute-start.9 = (bf16[128,256]{1,0:T(8,128)(2,1)S(1)}, bf16[128,256]{1,0:T(8,128)(2,1)S(1)}, u32[]{:S(2)}, u32[]{:S(2)}) collective-permute-start(bf16[128,256]{1,0:T(8,128)(2,1)S(1)} %copy-done.11), channel_id=1, source_target_pairs={{0,128},{64,192},{128,0},{192,64},{1,129},{65,193},{129,1},{193,65... | collective-permute-start | bytes 196616 | tf_op jit(solution)/shard_map/ppermute | solution.py:20
  40.3 12.2 %collective-permute-start.8 = (bf16[128,256]{1,0:T(8,128)(2,1)S(1)}, bf16[128,256]{1,0:T(8,128)(2,1)S(1)}, u32[]{:S(2)}, u32[]{:S(2)}) collective-permute-start(bf16[128,256]{1,0:T(8,128)(2,1)S(1)} %copy-done.11), channel_id=1, source_target_pairs={{0,192},{64,0},{128,64},{192,128},{1,193},{65,1},{129,65},{193,129... | collective-permute-start | bytes 196616 | tf_op jit(solution)/shard_map/ppermute | solution.py:20
  42.1 13.6 %collective-permute-start.7 = (bf16[128,256]{1,0:T(8,128)(2,1)S(1)}, bf16[128,256]{1,0:T(8,128)(2,1)S(1)}, u32[]{:S(2)}, u32[]{:S(2)}) collective-permute-start(bf16[128,256]{1,0:T(8,128)(2,1)S(1)} %copy-done.11), channel_id=1, source_target_pairs={{0,64},{64,128},{128,192},{192,0},{1,65},{65,129},{129,193},{193,1... | collective-permute-start | bytes 196616 | tf_op jit(solution)/shard_map/ppermute | solution.py:20
  55.7 2.0 %collective-permute-start.11 = (bf16[512,512]{1,0:T(8,128)(2,1)S(1)}, bf16[512,512]{1,0:T(8,128)(2,1)S(1)}, u32[]{:S(2)}, u32[]{:S(2)}) collective-permute-start(bf16[512,512]{1,0:T(8,128)(2,1)S(1)} %maximum_maximum_fusion.wa), channel_id=1, source_target_pairs={{0,32},{32,0},{1,33},{33,1},{2,34},{34,2},{3,35},{35,3},{4,36},{36... | collective-permute-start | bytes 1572872 | tf_op jit(solution)/shard_map/ppermute | solution.py:20
  57.7 0.8 copy-start.3
  58.5 1.6 %copy-start = (bf16[1088,1024]{1,0:T(8,128)(2,1)S(1)}, bf16[1088,1024]{1,0:T(8,128)(2,1)}, u32[]{:S(2)}) copy-start(bf16[1088,1024]{1,0:T(8,128)(2,1)} %all-gather.3.cloned.1.call-done) | copy-start | bytes 6684676
  60.2 1.0 copy-start.4
  62.6 0.8 copy-start.1
  63.4 0.8 copy-start.7
  64.5 1.0 copy-start.8
  77.8 1.0 copy-start.2
  111.7 1.0 copy-start.9
  111.7 1.0 copy-start.10
  121.1 0.9 copy-start.5
  123.3 17.6 %all-to-all-start.2 = ((bf16[32,40,128]{2,1,0:T(8,128)(2,1)}), bf16[32,40,128]{2,1,0:T(8,128)(2,1)S(1)}, u32[]{:S(2)}, u32[]{:S(2)}) async-start(bf16[32,40,128]{2,1,0:T(8,128)(2,1)} %bitcast.8), calls=%async_computation.3 | async-start | bytes 655360 | tf_op jit(solution)/shard_map/all_to_all | solution.py:342
  130.5 8.9 %collective-permute-start.12 = (bf16[32,1024]{1,0:T(8,128)(2,1)S(1)}, bf16[32,1024]{1,0:T(8,128)(2,1)S(1)}, u32[]{:S(2)}, u32[]{:S(2)}) collective-permute-start(bf16[32,1024]{1,0:T(8,128)(2,1)S(1)} %get-tuple-element.57), channel_id=1, source_target_pairs={{0,8},{8,16},{16,24},{24,0},{1,9},{9,17},{17,25},{25,1},{2,10},{10... | collective-permute-start | bytes 196616 | tf_op jit(solution)/shard_map/ppermute | solution.py:20
  132.1 7.3 %collective-permute-start.13 = (bf16[32,1024]{1,0:T(8,128)(2,1)S(1)}, bf16[32,1024]{1,0:T(8,128)(2,1)S(1)}, u32[]{:S(2)}, u32[]{:S(2)}) collective-permute-start(bf16[32,1024]{1,0:T(8,128)(2,1)S(1)} %get-tuple-element.58), channel_id=1, source_target_pairs={{0,24},{8,0},{16,8},{24,16},{1,25},{9,1},{17,9},{25,17},{2,26},{10... | collective-permute-start | bytes 196616 | tf_op jit(solution)/shard_map/ppermute | solution.py:20
  133.9 7.1 %collective-permute-start.14 = (bf16[32,1024]{1,0:T(8,128)(2,1)S(1)}, bf16[32,1024]{1,0:T(8,128)(2,1)S(1)}, u32[]{:S(2)}, u32[]{:S(2)}) collective-permute-start(bf16[32,1024]{1,0:T(8,128)(2,1)S(1)} %get-tuple-element.59), channel_id=1, source_target_pairs={{0,16},{8,24},{16,0},{24,8},{1,17},{9,25},{17,1},{25,9},{2,18},{10... | collective-permute-start | bytes 196616 | tf_op jit(solution)/shard_map/ppermute | solution.py:20
Sparse Core Ops, SparseCore 0:
  9.8 39.4 all-gather.2
  78.0 43.0 reduce-scatter.1
